TPU v7x, 32 devices: a whole 2x2x4 slice. The times are simulated.
32 devices in a mesh: rep: 8 (over z, y), tp: 4 (over x, core).
Axes of the slice: x: 2, y: 2, z: 4, core: 2. Of those that a mesh axis runs over, the one named last changes fastest.
Arguments:
- grads: bfloat16 [8, 12, 768, 2048], P('rep', None, None, 'tp'), may hold values from -6 to 6
- error: float32 [8, 12, 768, 2048], P('rep', None, None, 'tp'), may hold values from -2 to 2
- query: float32 [12, 32, 2048], P(None, None, 'tp'), may hold values from -6 to 6
- momentum: float32 [9216, 2048], P(('rep', 'tp')), may hold values from -0.8 to 0.8
- master: float32 [9216, 2048], P(('rep', 'tp')), may hold values from -0.8 to 0.8
Outputs:
- new_error: float32 [8, 12, 768, 2048], P('rep', None, None, 'tp')
- new_query: float32 [12, 32, 2048], P(None, None, 'tp')
- new_momentum: float32 [9216, 2048], P(('rep', 'tp'))
- new_master: float32 [9216, 2048], P(('rep', 'tp'))
- weights: bfloat16 [12, 768, 2048], P(None, None, 'tp')
All inputs are finite; a program needn't handle non-finite values.
Results may differ from a plain program's by a relative error of at most 0.0004.
Values may be sent and summed in bfloat16 or wider, within the bound.
No kernel may reach another device: no remote copies, remote signals or barrier semaphores. Data moves between devices by JAX's collectives and lax.ppermute only.
A program may use at most 128 MiB of HBM per device.

v0:
```python
import jax
import jax.numpy as jnp
from jax import lax
from jax.sharding import PartitionSpec as P

ROUNDS = 2
NS_STEPS = 5


NORM_EPSILON = 1e-06
MOMENTUM_DECAY = 0.9
LEARNING_RATE = 0.5


def local_gram(factor):
    return jnp.einsum("krd,ksd->krs", factor, factor, precision=lax.Precision.HIGHEST)


def orthonormal(factor, gram_of):
    gram_now = gram_of(factor)
    sum_squares = jnp.trace(gram_now, axis1=1, axis2=2)[:, None, None]
    factor_scale = lax.rsqrt(sum_squares + NORM_EPSILON)
    ortho_basis = factor * factor_scale
    gram_now = gram_now * (factor_scale * factor_scale)
    for iteration in range(NS_STEPS):
        if iteration > 0:
            gram_now = gram_of(ortho_basis)
        ortho_basis = 1.5 * ortho_basis - 0.5 * jnp.einsum(
            "krs,ksd->krd", gram_now, ortho_basis, precision=lax.Precision.HIGHEST
        )
    return ortho_basis


def local(grads, error, query, momentum, master):
    corrected = grads[0].astype(jnp.float32) + error[0]
    current = query
    replicas = lax.axis_size("rep")
    for power_pass in range(ROUNDS):
        partial_factor = jnp.einsum(
            "kdf,krf->krd", corrected, current, precision=lax.Precision.HIGHEST
        )
        summed = lax.psum(partial_factor, ("rep", "tp"))
        ortho_basis = orthonormal(summed, local_gram)
        partial_query = jnp.einsum(
            "kdf,krd->krf", corrected, ortho_basis, precision=lax.Precision.HIGHEST
        )
        current = lax.psum(partial_query, "rep") / replicas
    approx = jnp.einsum("krd,krf->kdf", ortho_basis, current, precision=lax.Precision.HIGHEST)
    new_error = (corrected - approx)[None]
    matrices, model_width, shard_cols = approx.shape
    block_rows = matrices * model_width // replicas
    approx_rows = approx.reshape(matrices * model_width, shard_cols)
    own_block = lax.dynamic_slice_in_dim(
        approx_rows, lax.axis_index("rep") * block_rows, block_rows, 0
    )
    flat_approx = lax.all_to_all(own_block, "tp", split_axis=0, concat_axis=1, tiled=True)
    new_momentum = MOMENTUM_DECAY * momentum + flat_approx
    new_master = master - LEARNING_RATE * new_momentum
    working = new_master.astype(jnp.bfloat16)
    by_columns = lax.all_to_all(working, "tp", split_axis=1, concat_axis=0, tiled=True)
    weight_rows = lax.all_gather(by_columns, "rep", axis=0, tiled=True)
    weights = weight_rows.reshape(matrices, model_width, shard_cols)
    return (new_error, current, new_momentum, new_master, weights)


def solution(mesh):
    placed = (
        P("rep", None, None, "tp"),
        P("rep", None, None, "tp"),
        P(None, None, "tp"),
        P(("rep", "tp"), None),
        P(("rep", "tp"), None),
    )
    return jax.shard_map(
        local,
        mesh=mesh,
        in_specs=placed,
        out_specs=(
            P("rep", None, None, "tp"),
            P(None, None, "tp"),
            P(("rep", "tp"), None),
            P(("rep", "tp"), None),
            P(None, None, "tp"),
        ),
        check_vma=False,
    )
```

profile of v0, /device:TPU:0, one launch (start us, length us, event | category | flops | bytes accessed | tf_op | source)
XLA Modules:
  0.0 752.0 jit_solution(18014886156988979553)
XLA Ops:
  7.2 0.0 all-reduce.5.cloned.1.call-start
  7.2 1.1 copy-done
  8.3 24.0 %fusion.19 = f32[12,32,768]{2,1,0:T(8,128)} fusion(f32[12,32,512]{2,1,0:T(8,128)S(1)} %copy-done, f32[1,12,768,512]{3,2,1,0:T(8,128)} %param.6, bf16[1,12,768,512]{3,2,1,0:T(8,128)(2,1)} %param.5), kind=kOutput, calls=%fused_computation.33 | convolution fusion | flops 1821376512 | bytes 30277632 | tf_op jit(solution)/shard_map/kdf,krf->krd/dot_general | solution.py:39
  32.3 0.3 all-reduce.7.cloned.1.call-start
  32.6 133.6 %all-reduce.5.cloned.1.call-done = f32[12,32,768]{2,1,0:T(8,128)} async-done(((f32[12,32,768]{2,1,0:T(8,128)}), f32[12,32,768]{2,1,0:T(8,128)}) %all-reduce.5.cloned.1.call-update) | async-done | bytes 1179664 | tf_op jit(solution)/shard_map/psum | solution.py:42
  166.2 3.0 select_reduce_fusion.1
  169.2 1.3 fusion.18
  170.5 1.2 fusion.36
  171.7 1.2 fusion.17
  172.9 1.2 fusion.37
  174.1 1.2 fusion.16
  175.3 1.2 fusion.38
  176.5 1.2 fusion.15
  177.7 1.2 fusion.39
  178.9 1.2 fusion.14
  180.2 16.8 %fusion.4 = f32[12,32,512]{2,1,0:T(8,128)} fusion(f32[12,32,768]{2,1,0:T(8,128)S(1)} %fusion.14, f32[1,12,768,512]{3,2,1,0:T(8,128)} %param.6, bf16[1,12,768,512]{3,2,1,0:T(8,128)(2,1)S(1)} %bitcast.73), kind=kOutput, calls=%fused_computation.5 | convolution fusion | flops 1821376512 | bytes 30277632 | tf_op jit(solution)/shard_map/kdf,krd->krf/dot_general | solution.py:44
  196.9 0.0 all-reduce.9.cloned.1.call-start
  197.0 73.8 %all-reduce.7.cloned.1.call-done = f32[12,32,512]{2,1,0:T(8,128)} async-done(((f32[12,32,512]{2,1,0:T(8,128)}), f32[12,32,512]{2,1,0:T(8,128)}) %all-reduce.7.cloned.1.call-update) | async-done | bytes 786448 | tf_op jit(solution)/shard_map/psum | solution.py:47
  270.8 23.1 %fusion.2 = f32[12,32,768]{2,1,0:T(8,128)} fusion(f32[12,32,512]{2,1,0:T(8,128)} %all-reduce.7.cloned.1.call-done, f32[1,12,768,512]{3,2,1,0:T(8,128)} %param.6, bf16[1,12,768,512]{3,2,1,0:T(8,128)(2,1)} %param.5), kind=kOutput, calls=%fused_computation.3 | convolution fusion | flops 1821573120 | bytes 30277632 | tf_op jit(solution)/shard_map/kdf,krf->krd/dot_general | solution.py:39
  293.9 0.2 all-reduce.11.cloned.1.call-start
  294.1 130.1 %all-reduce.9.cloned.1.call-done = f32[12,32,768]{2,1,0:T(8,128)} async-done(((f32[12,32,768]{2,1,0:T(8,128)}), f32[12,32,768]{2,1,0:T(8,128)}) %all-reduce.9.cloned.1.call-update) | async-done | bytes 1179664 | tf_op jit(solution)/shard_map/psum | solution.py:42
  424.2 3.0 select_reduce_fusion
  427.2 1.3 fusion.13
  428.5 1.2 fusion.40
  429.7 1.2 fusion.12
  430.9 1.2 fusion.41
  432.2 1.2 fusion.11
  433.3 1.2 fusion.42
  434.6 1.2 fusion.10
  435.7 1.2 fusion.43
  436.9 1.2 fusion.9
  438.2 16.2 %fusion = f32[12,32,512]{2,1,0:T(8,128)} fusion(f32[12,32,768]{2,1,0:T(8,128)S(1)} %fusion.9, f32[1,12,768,512]{3,2,1,0:T(8,128)} %param.6, bf16[1,12,768,512]{3,2,1,0:T(8,128)(2,1)S(1)} %bitcast.75), kind=kOutput, calls=%fused_computation.1 | convolution fusion | flops 1821376512 | bytes 30277632 | tf_op jit(solution)/shard_map/kdf,krd->krf/dot_general | solution.py:44
  454.4 0.3 all-gather.2.cloned.1.call-start
  454.7 73.5 %all-reduce.11.cloned.1.call-done = f32[12,32,512]{2,1,0:T(8,128)} async-done(((f32[12,32,512]{2,1,0:T(8,128)}), f32[12,32,512]{2,1,0:T(8,128)}) %all-reduce.11.cloned.1.call-update) | async-done | bytes 786448 | tf_op jit(solution)/shard_map/psum | solution.py:47
  528.2 1.2 broadcast_multiply_fusion
  529.5 15.4 %fusion.44 = f32[12,768,512]{2,1,0:T(8,128)S(1)} fusion(f32[12,32,768]{2,1,0:T(8,128)S(1)} %fusion.9, f32[12,32,512]{2,1,0:T(8,128)S(1)} %broadcast_multiply_fusion), kind=kOutput, calls=%fused_computation.64 | convolution fusion | flops 1811939328 | bytes 20840448 | tf_op jit(solution)/shard_map/krd,krf->kdf/dot_general | solution.py:48
  545.0 0.2 constant_dynamic-slice_fusion
  545.2 31.0 %all_to_all.38 = f32[4,288,512]{2,1,0:T(8,128)S(1)} all-to-all(f32[4,288,512]{2,1,0:T(8,128)S(1)} %bitcast.79), channel_id=1, replica_groups=mesh['rep'=8,'tp'=4] {'tp'}, dimensions={0} | all-to-all | bytes 4718592 | tf_op jit(solution)/shard_map/all_to_all | solution.py:56
  576.2 0.2 copy.16
  576.5 1.5 copy-done.6
  577.9 0.7 copy-done.7
  578.6 3.0 fusion.35
  581.6 0.1 copy.18
  581.7 19.0 %all_to_all.39 = bf16[288,4,512]{2,0,1:T(8,128)(2,1)} all-to-all(bf16[288,4,512]{2,0,1:T(8,128)(2,1)S(1)} %bitcast.83), channel_id=1, replica_groups=mesh['rep'=8,'tp'=4] {'tp'}, dimensions={1} | all-to-all | bytes 2359296 | tf_op jit(solution)/shard_map/all_to_all | solution.py:60
  600.7 0.0 all-gather.2.cloned.1.call-update
  600.8 22.7 %fusion.8 = f32[1,12,768,512]{3,2,1,0:T(8,128)} fusion(f32[12,768,512]{2,1,0:T(8,128)} %copy-done.2, f32[1,12,768,512]{3,2,1,0:T(8,128)} %param.6, bf16[1,12,768,512]{3,2,1,0:T(8,128)(2,1)} %param.5), kind=kLoop, calls=%fused_computation.9 | loop fusion | flops 14155776 | bytes 66060288 | tf_op jit(solution)/shard_map/broadcast_in_dim | solution.py:49
  623.4 113.8 %all-gather.2.cloned.1.call-done = bf16[9216,512]{1,0:T(8,128)(2,1)} async-done(((bf16[1152,512]{1,0:T(8,128)(2,1)}), bf16[9216,512]{1,0:T(8,128)(2,1)}) %all-gather.2.cloned.1.call-update) | async-done | bytes 9437200 | tf_op jit(solution)/shard_map/all_gather | solution.py:61
  737.2 8.1 %copy.24 = bf16[12,768,512]{2,1,0:T(8,128)(2,1)} copy(bf16[12,768,512]{2,1,0:T(8,128)(2,1)} %bitcast.78) | data formatting | bytes 18874368
  (34 shorter events, 0.2 us)
Async XLA Ops:
  7.2 1.1 copy-start
  7.2 159.0 %all-reduce.5.cloned.1.call-start = ((), (), s32[]{:S(2)}) async-start(), calls=%async_computation.2 | async-start | bytes 2359296 | tf_op jit(solution)/shard_map/psum | solution.py:42
  32.3 238.5 %all-reduce.7.cloned.1.call-start = ((), (), s32[]{:S(2)}) async-start(), calls=%async_computation.3 | async-start | bytes 1572864 | tf_op jit(solution)/shard_map/psum | solution.py:47
  166.2 3.0 copy-start.3
  170.5 9.6 %slice-start = ((s8[9437184]{0:T(1024)(128)(4,1)}), s8[4194304]{0:T(1024)(128)(4,1)S(1)}, s32[]{:S(2)}) async-start(s8[9437184]{0:T(1024)(128)(4,1)} %bitcast.72), calls=%async_computation.7 | async-start | bytes 8388608
  172.9 7.2 slice-start.1
  176.5 3.6 slice-start.2
  196.9 227.3 %all-reduce.9.cloned.1.call-start = ((), (), s32[]{:S(2)}) async-start(), calls=%async_computation.4 | async-start | bytes 2359296 | tf_op jit(solution)/shard_map/psum | solution.py:42
  293.9 234.4 %all-reduce.11.cloned.1.call-start = ((), (), s32[]{:S(2)}) async-start(), calls=%async_computation.5 | async-start | bytes 1572864 | tf_op jit(solution)/shard_map/psum | solution.py:47
  424.2 3.0 copy-start.4
  428.5 9.6 %slice-start.3 = ((s8[9437184]{0:T(1024)(128)(4,1)}), s8[4194304]{0:T(1024)(128)(4,1)S(1)}, s32[]{:S(2)}) async-start(s8[9437184]{0:T(1024)(128)(4,1)} %bitcast.74), calls=%async_computation.10 | async-start | bytes 8388608
  430.9 7.2 slice-start.4
  434.5 3.6 slice-start.5
  454.4 282.8 %all-gather.2.cloned.1.call-start = ((), (), s32[]{:S(2)}) async-start(), calls=%async_computation.6 | async-start | bytes 10616832 | tf_op jit(solution)/shard_map/all_gather | solution.py:61
  529.5 15.5 %copy-start.5 = (f32[12,32,512]{2,1,0:T(8,128)}, f32[12,32,512]{2,1,0:T(8,128)S(1)}, u32[]{:S(2)}) copy-start(f32[12,32,512]{2,1,0:T(8,128)S(1)} %broadcast_multiply_fusion) | copy-start | bytes 2359300
  545.0 31.3 %copy-start.2 = (f32[12,768,512]{2,1,0:T(8,128)}, f32[12,768,512]{2,1,0:T(8,128)S(1)}, u32[]{:S(2)}) copy-start(f32[12,768,512]{2,1,0:T(8,128)S(1)} %fusion.44) | copy-start | bytes 56623108
  576.2 1.7 copy-start.6
  576.2 2.4 copy-start.7
  737.2 8.1 %copy-start.1 = (f32[12,32,512]{2,1,0:T(8,128)S(1)}, f32[12,32,512]{2,1,0:T(8,128)}, u32[]{:S(2)}) copy-start(f32[12,32,512]{2,1,0:T(8,128)} %param.7) | copy-start | bytes 2359300
Sparse Core Ops, SparseCore 0:
  32.4 133.7 all-reduce.4
  197.1 73.6 all-reduce.6
  294.0 130.1 all-reduce.8
  454.6 73.6 all-reduce.10
  600.9 136.2 all-gather.1
where the time goes:
time: 758 us; the launch traced here: 752 us
  waiting for transfers between devices  525 us (69%)
  matrix products  123 us (16%)
  blocking collectives  50.1 us (7%)
  other arithmetic  26.9 us (4%)
  between operations  14.2 us (2%)
  local copies, waits for them, and re-layouts  11.9 us (2%)
    psum x2, waiting for transfers between devices, local(): summed = lax.psum(partial_factor, ('rep', 'tp'))  264 us
    psum x2, waiting for transfers between devices, local(): current = lax.psum(partial_query, 'rep') / replicas  147 us
    all_gather x1, waiting for transfers between devices, local(): weight_rows = lax.all_gather(by_columns, 'rep', axis=0, tiled=True)  114 us
    dot_general x2, matrix products, local(): jnp.einsum('kdf,krf->krd', corrected, current, precision=lax.Precision.HI...  47.1 us
    dot_general x2, matrix products, local(): jnp.einsum('kdf,krd->krf', corrected, ortho_basis, precision=lax.Precisio...  33 us
    all_to_all x1, blocking collectives, local(): lax.all_to_all(own_block, 'tp', split_axis=0, concat_axis=1, tiled=True)  31 us
    broadcast_in_dim x1, other arithmetic, local(): new_error = (corrected - approx)[None]  22.7 us
    all_to_all x1, blocking collectives, local(): lax.all_to_all(working, 'tp', split_axis=1, concat_axis=0, tiled=True)  19 us
  transfers between devices with their start and end apart: 5, of which 5 were waited for; matrix products, arithmetic and copies ran while one was open for 3% of the time, Pallas kernels for 0%

commit v1 on v0

v1 whole, which is shorter than its diff:
```python
import functools
import math

import jax
import jax.numpy as jnp
from jax import lax
from jax.experimental import pallas as pl
from jax.experimental.pallas import tpu as pltpu
from jax.sharding import PartitionSpec as P

ROUNDS = 2
NS_STEPS = 5


NORM_EPSILON = 1e-06
MOMENTUM_DECAY = 0.9
LEARNING_RATE = 0.5
HIGHEST = lax.Precision.HIGHEST
LANES = 128
EARLY = 2
F32, BF16 = jnp.float32, jnp.bfloat16
PARAMS = pltpu.CompilerParams(vmem_limit_bytes=60 * 2**20)
SCALARS = pl.BlockSpec(memory_space=pltpu.SMEM)


def two_terms(x):
    high = x.astype(BF16)
    return high, (x - high.astype(F32)).astype(BF16)


def dot(a, b, transposed=False):
    dims = (((1,), (1 if transposed else 0,)), ((), ()))
    return lax.dot_general(a, b, dims, preferred_element_type=F32)


def small_by_large(small, high, low, transposed):
    rows = small.shape[0]
    small_high, small_low = two_terms(small)
    both = dot(jnp.concatenate([small_high, small_low], axis=0), high, transposed)
    return both[:rows] + both[rows:] + dot(small_high, low, transposed)


def dot3(a, b):
    a_high, a_low = two_terms(a)
    b_high, b_low = two_terms(b)
    return dot(
        jnp.concatenate([a_high, a_low, a_high], axis=1),
        jnp.concatenate([b_high, b_high, b_low], axis=0),
    )


def stacked(right):
    right_high, right_low = two_terms(right)
    return jnp.concatenate([right_high, right_high, right_low], axis=0)


def lay_lanes(scratch, value):
    rows = value.shape[0]
    for block in range(value.shape[1] // LANES):
        scratch[block * rows : (block + 1) * rows] = value[:, block * LANES : (block + 1) * LANES]


def read_lanes(scratch, rows):
    blocks = scratch.shape[0] // rows
    return jnp.concatenate([scratch[block * rows : (block + 1) * rows] for block in range(blocks)], axis=1)


def part_at(index, rows):
    return pl.ds(pl.multiple_of(index * rows, 8), rows)


def split_parts(scratch, me, part_refs):
    rows = part_refs[0].shape[0]
    for offset, part_ref in enumerate(part_refs):
        part_ref[...] = scratch[part_at(me ^ offset, rows), :]


def join_parts(scratch, me, part_refs):
    rows = part_refs[0].shape[0]
    for offset, part_ref in enumerate(part_refs):
        scratch[part_at(me ^ offset, rows), :] = part_ref[...]


def sum_of(refs):
    values = [ref[...] for ref in refs]
    while len(values) > 1:
        values = [sum(values[at : at + 2][1:], values[at]) for at in range(0, len(values), 2)]
    return values[0]


def put_left(left, step, left_refs, per_tp):
    for which, left_ref in enumerate(left_refs):

        @pl.when(step // per_tp == which)
        def _():
            left_ref[...] = left


def first_left_kernel(per_tp, ids_ref, grads_ref, error_ref, query_ref, high_ref, low_ref, *left_refs):
    high, low = two_terms(grads_ref[0, 0].astype(F32) + error_ref[0, 0])
    high_ref[0] = high
    low_ref[0] = low
    put_left(small_by_large(query_ref[0], high, low, True), pl.program_id(0), left_refs, per_tp)


def left_kernel(per_tp, ids_ref, high_ref, low_ref, *refs):
    parts, left_refs, (scratch, current) = refs[:-4], refs[-4:-2], refs[-2:]
    step = pl.program_id(0)
    rank = left_refs[0].shape[0]

    @pl.when(step == 0)
    def _():
        join_parts(scratch, ids_ref[0], parts)
        current[...] = read_lanes(scratch, current.shape[0])

    own = current[part_at(step, rank), :]
    put_left(small_by_large(own, high_ref[0], low_ref[0], True), step, left_refs, per_tp)


def split_kernel(tps, ids_ref, *refs):
    scratch = refs[-1]
    lay_lanes(scratch, sum_of(refs[:tps]))
    split_parts(scratch, ids_ref[0], refs[tps:-1])


def sum_kernel(scale, *refs):
    summed = sum_of(refs[:-1])
    refs[-1][...] = summed if scale == 1.0 else summed * scale


def mixing(left, rank):
    rows = left.shape[0]
    row_id = lax.broadcasted_iota(jnp.int32, (rows, rows), 0)
    col_id = lax.broadcasted_iota(jnp.int32, (rows, rows), 1)
    same = (row_id // rank) == (col_id // rank)
    eye = (row_id == col_id).astype(F32)
    left_high, left_low = two_terms(left)
    cross = dot(left_high, left_low, True)
    gram = jnp.where(same, dot(left_high, left_high, True) + cross + cross.T, 0.0)
    diagonal = jnp.sum(gram * eye, axis=0, keepdims=True)
    trace = jnp.sum(jnp.where(same, diagonal, 0.0), axis=1, keepdims=True) + NORM_EPSILON
    scale = lax.rsqrt(trace)
    scale = scale * (1.5 - 0.5 * trace * scale * scale)
    gram = gram * (scale * scale)
    step = 1.5 * eye - 0.5 * gram
    mixed = step * scale
    for _ in range(NS_STEPS - 1):
        gram = dot3(dot3(step, gram), step)
        step = 1.5 * eye - 0.5 * gram
        mixed = dot3(step, mixed)
    return mixed


def basis_kernel(rank, ids_ref, *refs):
    basis_ref, scratch = refs[-2:]
    join_parts(scratch, ids_ref[0], refs[:-2])
    rows = basis_ref.shape[0]
    left = read_lanes(scratch, rows)
    padded = jnp.concatenate([left, jnp.zeros((-rows % LANES, left.shape[1]), F32)], axis=0)
    basis_ref[...] = dot3(mixing(padded, rank), padded)[:rows]


def right_kernel(per_tp, ids_ref, first_ref, second_ref, high_ref, low_ref, *refs):
    part_refs, (scratch, right) = refs[:-2], refs[-2:]
    step = pl.program_id(0)
    rank = first_ref.shape[0] // per_tp
    at = part_at(step % per_tp, rank)
    own = jnp.where(step // per_tp == 0, first_ref[at, :], second_ref[at, :])
    right[part_at(step, rank), :] = small_by_large(own, high_ref[0], low_ref[0], False)

    @pl.when(step == pl.num_programs(0) - 1)
    def _():
        lay_lanes(scratch, right[...])
        split_parts(scratch, ids_ref[0], part_refs)


def factor_kernel(ids_ref, basis_ref, factors_ref):
    high, low = two_terms(basis_ref[0].T)
    factors_ref[...] = jnp.concatenate([high, low, high], axis=1)


def query_kernel(tps, ids_ref, *refs):
    query_ref, scratch = refs[-2:]
    halves = tps // 2
    per_half = (len(refs) - 2) // halves
    rows = query_ref.shape[0] // halves
    for half in range(halves):
        join_parts(scratch, ids_ref[0], refs[half * per_half : (half + 1) * per_half])
        value = read_lanes(scratch, rows)
        for which in range(2):
            owner = ids_ref[1] ^ (2 * half + which)
            query_ref[part_at(owner, rows // 2), :] = value[which * (rows // 2) : (which + 1) * (rows // 2)]


def weight_kernel(ids_ref, factors_ref, right_ref, base_ref, weights_ref):
    approx = dot(factors_ref[...], stacked(right_ref[...]))
    weights = (base_ref[...].reshape(approx.shape) - LEARNING_RATE * approx).astype(BF16)
    weights_ref[...] = weights.reshape(weights_ref.shape)


def place_kernel(ids_ref, part_ref, _, weights_ref):
    weights_ref[...] = part_ref[...].reshape(weights_ref.shape)


def error_kernel(per_half, ids_ref, factors_ref, right_ref, *refs):
    new_error_ref = refs[-1]
    approx = dot(factors_ref[...], stacked(right_ref[...]))
    for half in range(len(refs) // 2):
        high_ref, low_ref = refs[2 * half : 2 * half + 2]

        @pl.when(pl.program_id(0) // per_half == half)
        def _():
            new_error_ref[0, 0] = high_ref[0].astype(F32) + low_ref[0].astype(F32) - approx


def flat_kernel(ids_ref, factors_ref, right_ref, momentum_ref, master_ref, new_momentum_ref, new_master_ref):
    approx = dot(factors_ref[...], stacked(right_ref[...].reshape(right_ref.shape[-2:])))
    new_momentum = MOMENTUM_DECAY * momentum_ref[...] + approx
    new_momentum_ref[...] = new_momentum
    new_master_ref[...] = master_ref[...] - LEARNING_RATE * new_momentum


def shape(*dims, dtype=F32):
    return jax.ShapeDtypeStruct(dims, dtype)


def whole_call(kernel, name, out_shape, operands, ids=None, scratch=()):
    specs = [pl.BlockSpec(memory_space=pltpu.VMEM)] * len(operands)
    many = isinstance(out_shape, (list, tuple))
    out_spec = pl.BlockSpec(memory_space=pltpu.VMEM)
    moved = sum(4 * x.size for x in operands)
    if ids is not None:
        operands, specs = [ids, *operands], [SCALARS, *specs]
    return pl.pallas_call(
        kernel,
        in_specs=specs,
        out_specs=[out_spec] * len(out_shape) if many else out_spec,
        out_shape=out_shape,
        scratch_shapes=list(scratch),
        compiler_params=PARAMS,
        name=name,
        cost_estimate=pl.CostEstimate(flops=moved, bytes_accessed=2 * moved, transcendentals=0),
    )(*operands)


def grid_call(kernel, name, ids, grid, in_specs, out_specs, out_shape, operands, scratch=(), aliases=None, flops=0, moved=0):
    return pl.pallas_call(
        kernel,
        grid_spec=pltpu.PrefetchScalarGridSpec(
            num_scalar_prefetch=1,
            grid=grid,
            in_specs=in_specs,
            out_specs=out_specs,
            scratch_shapes=list(scratch),
        ),
        out_shape=out_shape,
        input_output_aliases=aliases or {},
        compiler_params=PARAMS,
        name=name,
        cost_estimate=pl.CostEstimate(flops=flops, bytes_accessed=moved, transcendentals=0),
    )(ids, *operands)


def swap(x, axis, size, offset):
    return lax.ppermute(x, axis, [(index, index ^ offset) for index in range(size)])


def scattered(parts, replicas):
    return [parts[0]] + [swap(parts[offset], "rep", replicas, offset) for offset in range(1, replicas)]


def spread(part, axis, size):
    return [part] + [swap(part, axis, size, offset) for offset in range(1, size)]


def local(grads, error, query, momentum, master):
    replicas, tps = lax.axis_size("rep"), lax.axis_size("tp")
    rep, tp = lax.axis_index("rep"), lax.axis_index("tp")
    ids = jnp.stack([rep, tp]).astype(jnp.int32)
    _, matrices, width, cols = grads.shape
    rank = query.shape[1]
    per_tp = matrices // tps
    per_half = 2 * per_tp
    halves = tps // 2
    tp_rows = per_tp * rank
    left_part = tp_rows * width // LANES // replicas
    right_part = 2 * tp_rows * cols // LANES // replicas
    own_rows = momentum.shape[0]
    flops = 2 * 3 * per_half * rank * width * cols
    elements = per_half * width * cols

    def matrix_of(half, k, at):
        return (at[1] ^ (2 * half + k // per_tp)) * per_tp + k % per_tp

    term_spec = pl.BlockSpec((1, width, cols), lambda k, at: (k, 0, 0))
    term_shape = shape(per_half, width, cols, dtype=BF16)
    left_specs = [
        pl.BlockSpec((rank, width), lambda k, at, which=which: (jnp.clip(k - which * per_tp, 0, per_tp - 1), 0))
        for which in range(2)
    ]
    left_shapes = [shape(tp_rows, width)] * 2

    def whole_spec(*dims):
        return pl.BlockSpec(dims, lambda k, at: (0,) * len(dims))

    terms, lefts = [None] * halves, [None] * tps
    for half in reversed(range(halves)):
        picked = functools.partial(matrix_of, half)
        high, low, *out = grid_call(
            functools.partial(first_left_kernel, per_tp),
            "first_left",
            ids,
            (per_half,),
            [
                pl.BlockSpec((1, 1, width, cols), lambda k, at, picked=picked: (0, picked(k, at), 0, 0)),
                pl.BlockSpec((1, 1, width, cols), lambda k, at, picked=picked: (0, picked(k, at), 0, 0)),
                pl.BlockSpec((1, rank, cols), lambda k, at, picked=picked: (picked(k, at), 0, 0)),
            ],
            [term_spec, term_spec, *left_specs],
            [term_shape, term_shape, *left_shapes],
            (grads, error, query),
            flops=flops,
            moved=10 * elements,
        )
        terms[half] = (high, low)
        lefts[2 * half : 2 * half + 2] = out

    gathered = []
    for power_pass in range(ROUNDS):
        met = [lefts[0]] + [swap(lefts[offset], "tp", tps, offset) for offset in range(1, tps)]
        parts = whole_call(
            functools.partial(split_kernel, tps),
            "left_split",
            [shape(left_part, LANES)] * replicas,
            met,
            ids,
            [pltpu.VMEM((left_part * replicas, LANES), F32)],
        )
        if power_pass == 0:
            base = []
            tied = lax.optimization_barrier((master, momentum, *parts))
            parts = list(tied[2:])
            for offset in range(tps):
                column = (tp ^ offset) * cols
                piece = lax.dynamic_slice_in_dim(tied[0], column, cols, 1)
                piece = piece - (LEARNING_RATE * MOMENTUM_DECAY) * lax.dynamic_slice_in_dim(tied[1], column, cols, 1)
                base.append(piece if offset == 0 else swap(piece, "tp", tps, offset))
            gathered = [lax.all_gather(base[offset], "rep") for offset in range(EARLY)]
        met = scattered(parts, replicas)
        part = whole_call(functools.partial(sum_kernel, 1.0), "left_sum", shape(left_part, LANES), met)
        basis = whole_call(
            functools.partial(basis_kernel, rank),
            "basis",
            shape(tp_rows, width),
            spread(part, "rep", replicas),
            ids,
            [pltpu.VMEM((left_part * replicas, LANES), F32)],
        )
        bases = spread(basis, "tp", tps)
        rights = []
        for half in range(halves):
            parts = grid_call(
                functools.partial(right_kernel, per_tp),
                "right",
                ids,
                (per_half,),
                [whole_spec(tp_rows, width), whole_spec(tp_rows, width), term_spec, term_spec],
                [whole_spec(right_part, LANES)] * replicas,
                [shape(right_part, LANES)] * replicas,
                (*bases[2 * half : 2 * half + 2], *terms[half]),
                [pltpu.VMEM((right_part * replicas, LANES), F32), pltpu.VMEM((2 * tp_rows, cols), F32)],
                flops=flops,
                moved=4 * elements,
            )
            met = scattered(parts, replicas)
            part = whole_call(functools.partial(sum_kernel, 1.0 / replicas), "right_sum", shape(right_part, LANES), met)
            rights.append(spread(part, "rep", replicas))
        if power_pass < ROUNDS - 1:
            for half in range(halves):
                lefts[2 * half : 2 * half + 2] = grid_call(
                    functools.partial(left_kernel, per_tp),
                    "left",
                    ids,
                    (per_half,),
                    [term_spec, term_spec] + [whole_spec(right_part, LANES)] * replicas,
                    left_specs,
                    left_shapes,
                    (*terms[half], *rights[half]),
                    [pltpu.VMEM((right_part * replicas, LANES), F32), pltpu.VMEM((2 * tp_rows, cols), F32)],
                    flops=flops,
                    moved=4 * elements,
                )

    factors = grid_call(
        factor_kernel,
        "factors",
        ids,
        (matrices,),
        [pl.BlockSpec((1, rank, width), lambda k, at: ((at[1] ^ (k // per_tp)) * per_tp + k % per_tp, 0, 0))],
        pl.BlockSpec((width, 3 * rank), lambda k, at: (k, 0)),
        shape(matrices * width, 3 * rank, dtype=BF16),
        (jnp.concatenate(bases, axis=0).reshape(matrices, rank, width),),
    )
    right = whole_call(
        functools.partial(query_kernel, tps),
        "new_query",
        shape(matrices * rank, cols),
        [part for parts in rights for part in parts],
        ids,
        [pltpu.VMEM((right_part * replicas, LANES), F32)],
    )

    chunk = math.gcd(own_rows, width)
    chunks = own_rows // chunk

    def chunk_at(replica, owner, b):
        return (replica * tps + owner) * chunks + b

    late = tps - EARLY
    block = grid_call(
        weight_kernel,
        "late_weights",
        ids,
        (late, chunks),
        [
            pl.BlockSpec((chunk, 3 * rank), lambda s, b, at: (chunk_at(at[0], at[1] ^ (EARLY + s), b), 0)),
            pl.BlockSpec((rank, cols), lambda s, b, at: (chunk_at(at[0], at[1] ^ (EARLY + s), b) * chunk // width, 0)),
            pl.BlockSpec((1, chunk, cols), lambda s, b, at: (s, b, 0)),
        ],
        pl.BlockSpec((1, chunk, cols), lambda s, b, at: (s, b, 0)),
        shape(late, own_rows, cols, dtype=BF16),
        (factors, right, jnp.stack(base[EARLY:])),
    )
    late_rows = lax.all_gather(block, "rep")

    weights_shape = shape(replicas, tps, own_rows, cols, dtype=BF16)
    weights = None
    for offset in range(EARLY):
        kernel = weight_kernel if weights is None else lambda ids_ref, a, b, c, _, out: weight_kernel(ids_ref, a, b, c, out)
        weights = grid_call(
            kernel,
            "early_weights",
            ids,
            (replicas, chunks),
            [
                pl.BlockSpec((chunk, 3 * rank), lambda q, b, at, offset=offset: (chunk_at(q, at[1] ^ offset, b), 0)),
                pl.BlockSpec((rank, cols), lambda q, b, at, offset=offset: (chunk_at(q, at[1] ^ offset, b) * chunk // width, 0)),
                pl.BlockSpec((1, chunk, cols), lambda q, b, at: (q, b, 0)),
            ]
            + ([] if weights is None else [pl.BlockSpec(memory_space=pl.ANY)]),
            pl.BlockSpec((1, 1, chunk, cols), lambda q, b, at, offset=offset: (q, at[1] ^ offset, b, 0)),
            weights_shape,
            (factors, right, gathered[offset]) + (() if weights is None else (weights,)),
            aliases=None if weights is None else {4: 0},
            flops=2 * 3 * rank * replicas * own_rows * cols,
            moved=6 * replicas * own_rows * cols,
        )
    weights = grid_call(
        place_kernel,
        "place_late",
        ids,
        (replicas, late),
        [
            pl.BlockSpec((1, 1, own_rows, cols), lambda q, s, at: (q, s, 0, 0)),
            pl.BlockSpec(memory_space=pl.ANY),
        ],
        pl.BlockSpec((1, 1, own_rows, cols), lambda q, s, at: (q, at[1] ^ (EARLY + s), 0, 0)),
        weights_shape,
        (late_rows, weights),
        aliases={2: 0},
    )
    weights = weights.reshape(matrices, width, cols)

    def picked(k, at):
        return matrix_of(k // per_half, k % per_half, at)

    new_error = grid_call(
        functools.partial(error_kernel, per_half),
        "new_error",
        ids,
        (matrices,),
        [
            pl.BlockSpec((width, 3 * rank), lambda k, at: (picked(k, at), 0)),
            pl.BlockSpec((rank, cols), lambda k, at: (picked(k, at), 0)),
        ]
        + [
            pl.BlockSpec((1, width, cols), lambda k, at, half=half: (jnp.clip(k - half * per_half, 0, per_half - 1), 0, 0))
            for half in range(halves)
            for _ in range(2)
        ],
        pl.BlockSpec((1, 1, width, cols), lambda k, at: (0, picked(k, at), 0, 0)),
        shape(*error.shape),
        (factors, right, *[term for pair in terms for term in pair]),
        flops=2 * 3 * rank * error.size,
        moved=8 * error.size,
    )

    rep_rows = tps * own_rows
    spans = -(-(width - math.gcd(rep_rows, width) + rep_rows) // width)

    def first_near(at):
        return jnp.minimum(at[0] * rep_rows // width, matrices - spans)

    near = lax.dynamic_slice_in_dim(right.reshape(matrices, rank, cols), first_near(ids), spans, 0)
    near = jnp.stack(spread(near, "tp", tps))
    wide = pl.BlockSpec((chunk, cols), lambda b, s, at: (b, at[1] ^ s))
    new_momentum, new_master = grid_call(
        flat_kernel,
        "flat_rows",
        ids,
        (chunks, tps),
        [
            pl.BlockSpec((chunk, 3 * rank), lambda b, s, at: (chunk_at(at[0], at[1], b), 0)),
            pl.BlockSpec(
                (1, 1, rank, cols),
                lambda b, s, at: (s, chunk_at(at[0], at[1], b) * chunk // width - first_near(at), 0, 0),
            ),
            wide,
            wide,
        ],
        [wide, wide],
        [shape(*momentum.shape), shape(*master.shape)],
        (factors, near, momentum, master),
        flops=2 * 3 * rank * momentum.size,
        moved=16 * momentum.size,
    )
    return (new_error, right.reshape(matrices, rank, cols), new_momentum, new_master, weights)


def plain_orthonormal(factor):
    def gram_of(x):
        return jnp.einsum("krd,ksd->krs", x, x, precision=HIGHEST)

    gram_now = gram_of(factor)
    factor_scale = lax.rsqrt(jnp.trace(gram_now, axis1=1, axis2=2)[:, None, None] + NORM_EPSILON)
    ortho_basis = factor * factor_scale
    gram_now = gram_now * (factor_scale * factor_scale)
    for iteration in range(NS_STEPS):
        if iteration > 0:
            gram_now = gram_of(ortho_basis)
        ortho_basis = 1.5 * ortho_basis - 0.5 * jnp.einsum("krs,ksd->krd", gram_now, ortho_basis, precision=HIGHEST)
    return ortho_basis


def plain_local(grads, error, query, momentum, master):
    corrected = grads[0].astype(F32) + error[0]
    current = query
    replicas = lax.axis_size("rep")
    for _ in range(ROUNDS):
        partial_factor = jnp.einsum("kdf,krf->krd", corrected, current, precision=HIGHEST)
        ortho_basis = plain_orthonormal(lax.psum(partial_factor, ("rep", "tp")))
        partial_query = jnp.einsum("kdf,krd->krf", corrected, ortho_basis, precision=HIGHEST)
        current = lax.psum(partial_query, "rep") / replicas
    approx = jnp.einsum("krd,krf->kdf", ortho_basis, current, precision=HIGHEST)
    new_error = (corrected - approx)[None]
    matrices, width, cols = approx.shape
    block_rows = matrices * width // replicas
    own_block = lax.dynamic_slice_in_dim(
        approx.reshape(matrices * width, cols), lax.axis_index("rep") * block_rows, block_rows, 0
    )
    flat_approx = lax.all_to_all(own_block, "tp", split_axis=0, concat_axis=1, tiled=True)
    new_momentum = MOMENTUM_DECAY * momentum + flat_approx
    new_master = master - LEARNING_RATE * new_momentum
    by_columns = lax.all_to_all(new_master.astype(BF16), "tp", split_axis=1, concat_axis=0, tiled=True)
    weights = lax.all_gather(by_columns, "rep", axis=0, tiled=True).reshape(matrices, width, cols)
    return (new_error, current, new_momentum, new_master, weights)


def divides(mesh, matrices, rank, width, cols):
    replicas, tps = mesh.shape["rep"], mesh.shape["tp"]
    if replicas & (replicas - 1) or tps & (tps - 1) or tps < 4 or matrices % tps or cols % (tps * LANES) or width % LANES:
        return False
    tp_rows = matrices // tps * rank
    tiles = 8 * LANES * replicas
    return tp_rows * width % tiles == 0 and 2 * tp_rows * (cols // tps) % tiles == 0


def solution(mesh):
    placed = (
        P("rep", None, None, "tp"),
        P("rep", None, None, "tp"),
        P(None, None, "tp"),
        P(("rep", "tp"), None),
        P(("rep", "tp"), None),
    )

    def step(grads, error, query, momentum, master):
        fits = divides(mesh, grads.shape[1], query.shape[1], grads.shape[2], grads.shape[3])
        return jax.shard_map(
            local if fits else plain_local,
            mesh=mesh,
            in_specs=placed,
            out_specs=(
                P("rep", None, None, "tp"),
                P(None, None, "tp"),
                P(("rep", "tp"), None),
                P(("rep", "tp"), None),
                P(None, None, "tp"),
            ),
            check_vma=False,
        )(grads, error, query, momentum, master)

    return step
```

time: 758 us -> 445 us (0.59)
  waiting for transfers between devices: 525 us -> 70.7 us
  Pallas kernels: 0 us -> 183 us
  starting transfers between devices: 0.85 us -> 155 us
  matrix products: 123 us -> 0 us
  blocking collectives: 50.1 us -> 0 us
  other arithmetic: 26.9 us -> 6.86 us
    psum x4 -> x0, waiting for transfers between devices: 411 us -> none  [the longest x2 264 us: local(): summed = lax.psum(partial_factor, ('rep', 'tp'))]
    pallas_call x0 -> x26, Pallas kernels: none -> 183 us  [the longest x15 160 us: grid_call(): pl.pallas_call(kernel, grid_spec=pltpu.PrefetchScalarGridSpec(num_scalar_...]
    ppermute x0 -> x102, starting transfers between devices: none -> 155 us  [swap(): lax.ppermute(x, axis, [(index, index ^ offset) for index in range(size)])]
    dot_general x25 -> x0, matrix products: 123 us -> none  [the longest x2 47.1 us: local(): jnp.einsum('kdf,krf->krd', corrected, current, precision=lax.Precision.HI...]
    all_gather x1 -> x3, waiting for transfers between devices: 114 us -> 11.7 us  [the longest x1 11.7 us: local(): late_rows = lax.all_gather(block, 'rep')]
    ppermute x0 -> x102, waiting for transfers between devices: none -> 59 us  [swap(): lax.ppermute(x, axis, [(index, index ^ offset) for index in range(size)])]
    all_to_all x2 -> x0, blocking collectives: 50.1 us -> none  [the longest x1 31 us: local(): lax.all_to_all(own_block, 'tp', split_axis=0, concat_axis=1, tiled=True)]
    broadcast_in_dim x1 -> x0, other arithmetic: 22.7 us -> none  [local(): new_error = (corrected - approx)[None]]
  transfers between devices with their start and end apart: 5 -> 105, of which waited for: 5 -> 25; matrix products, arithmetic and copies ran while one was open for 3% -> 1% of each run, Pallas kernels for 0% -> 36%
where the time goes in v1:
time: 445 us; the launch traced here: 442 us
  Pallas kernels  183 us (41%)
  starting transfers between devices  155 us (35%)
  waiting for transfers between devices  70.7 us (16%)
  between operations  14.6 us (3%)
  local copies, waits for them, and re-layouts  11.6 us (3%)
  other arithmetic  6.86 us (2%)
    pallas_call x15, Pallas kernels, grid_call(): pl.pallas_call(kernel, grid_spec=pltpu.PrefetchScalarGridSpec(num_scalar_...  160 us
    ppermute x102, starting transfers between devices, swap(): lax.ppermute(x, axis, [(index, index ^ offset) for index in range(size)])  155 us
    ppermute x102, waiting for transfers between devices, swap(): lax.ppermute(x, axis, [(index, index ^ offset) for index in range(size)])  59 us
    pallas_call x11, Pallas kernels, whole_call(): pl.pallas_call(kernel, in_specs=specs, out_specs=[out_spec] * len(out_sha...  22.9 us
    all_gather x1, waiting for transfers between devices, local(): late_rows = lax.all_gather(block, 'rep')  11.7 us
    unnamed x212, local copies, waits for them, and re-layouts  9.79 us
  transfers between devices with their start and end apart: 105, of which 25 were waited for; matrix products, arithmetic and copies ran while one was open for 1% of the time, Pallas kernels for 36%

profile of v1, /device:TPU:0, one launch (start us, length us, event | category | flops | bytes accessed | tf_op | source)
XLA Modules:
  0.0 441.7 jit_solution(17606578367615736016)
XLA Ops:
  7.9 11.8 %first_left.3 = (bf16[6,768,512]{2,1,0:T(8,128)(2,1)}, bf16[6,768,512]{2,1,0:T(8,128)(2,1)}, f32[96,768]{1,0:T(8,128)}, f32[96,768]{1,0:T(8,128)}) custom-call(s32[2]{0:T(128)} %pad_add_fusion.ids_ref, bf16[1,12,768,512]{3,2,1,0:T(8,128)(2,1)} %grads_ref.3, f32[1,12,768,512]{3,2,1,0:T(8,128)} %error_ref.3, f32[12,32,512]{2,1,0:T(8,128)} %query_ref.3), custom_call_target="tpu_custom_call" | custom-call | flops 452984832 | bytes 23592960 | tf_op jit(solution)/shard_map/first_left/pallas_call | solution.py:247
  19.7 3.0 collective-permute-start.1
  22.6 11.9 %first_left.2 = (bf16[6,768,512]{2,1,0:T(8,128)(2,1)}, bf16[6,768,512]{2,1,0:T(8,128)(2,1)}, f32[96,768]{1,0:T(8,128)}, f32[96,768]{1,0:T(8,128)}) custom-call(s32[2]{0:T(128)} %pad_add_fusion.ids_ref, bf16[1,12,768,512]{3,2,1,0:T(8,128)(2,1)} %grads_ref.3, f32[1,12,768,512]{3,2,1,0:T(8,128)} %error_ref.3, f32[12,32,512]{2,1,0:T(8,128)} %query_ref.3), custom_call_target="tpu_custom_call" | custom-call | flops 452984832 | bytes 23592960 | tf_op jit(solution)/shard_map/first_left/pallas_call | solution.py:247
  39.1 3.2 multiply_subtract_fusion
  49.2 2.9 collective-permute-start.6
  53.3 3.6 collective-permute-start.8
  57.0 5.0 %collective-permute-done.7.refs_5_ = f32[72,128]{1,0:T(8,128)S(1)} collective-permute-done((f32[72,128]{1,0:T(8,128)}, f32[72,128]{1,0:T(8,128)S(1)}, u32[]{:S(2)}, u32[]{:S(2)}) %collective-permute-start.7) | collective-permute-done | bytes 36896 | tf_op jit(solution)/shard_map/ppermute | solution.py:265
  66.7 3.2 collective-permute-start.16
  70.5 6.2 %collective-permute-start.14 = (f32[72,128]{1,0:T(8,128)}, f32[72,128]{1,0:T(8,128)S(1)}, u32[]{:S(2)}, u32[]{:S(2)}) collective-permute-start(f32[72,128]{1,0:T(8,128)} %left_sum.2.refs_0_), channel_id=1, source_target_pairs={{0,20},{4,16},{8,28},{12,24},{16,4},{20,0},{24,12},{28,8},{1,21},{... | collective-permute-start | bytes 110600 | tf_op jit(solution)/shard_map/ppermute | solution.py:265
  81.2 3.4 collective-permute-done.14.refs_5_
  87.4 3.6 basis.2.first_ref
  92.8 7.6 %collective-permute-done.34.second_ref = f32[96,768]{1,0:T(8,128)S(1)} collective-permute-done((f32[96,768]{1,0:T(8,128)}, f32[96,768]{1,0:T(8,128)S(1)}, u32[]{:S(2)}, u32[]{:S(2)}) %collective-permute-start.34) | collective-permute-done | bytes 294944 | tf_op jit(solution)/shard_map/ppermute | solution.py:265
  100.5 6.3 %collective-permute-done.33.first_ref = f32[96,768]{1,0:T(8,128)S(1)} collective-permute-done((f32[96,768]{1,0:T(8,128)}, f32[96,768]{1,0:T(8,128)S(1)}, u32[]{:S(2)}, u32[]{:S(2)}) %collective-permute-start.33) | collective-permute-done | bytes 294944 | tf_op jit(solution)/shard_map/ppermute | solution.py:265
  107.5 7.8 %right.5 = (f32[96,128]{1,0:T(8,128)}, f32[96,128]{1,0:T(8,128)}, f32[96,128]{1,0:T(8,128)}, f32[96,128]{1,0:T(8,128)}, f32[96,128]{1,0:T(8,128)}, /*index=5*/f3...) custom-call(s32[2]{0:T(128)} %pad_add_fusion.ids_ref, f32[96,768]{1,0:T(8,128)} %copy-done.11, f32[96,768]{1,0:T(8,128)} %copy-done.10, ...), custom_call_target="tpu_custom_call" | custom-call | flops 452984832 | bytes 9437184 | tf_op jit(solution)/shard_map/right/pallas_call | solution.py:247
  121.4 7.7 %right.4 = (f32[96,128]{1,0:T(8,128)}, f32[96,128]{1,0:T(8,128)}, f32[96,128]{1,0:T(8,128)}, f32[96,128]{1,0:T(8,128)}, f32[96,128]{1,0:T(8,128)}, /*index=5*/f3...) custom-call(s32[2]{0:T(128)} %pad_add_fusion.ids_ref, f32[96,768]{1,0:T(8,128)} %basis.2.first_ref, ...), custom_call_target="tpu_custom_call" | custom-call | flops 452984832 | bytes 9437184 | tf_op jit(solution)/shard_map/right/pallas_call | solution.py:247
  129.2 3.4 collective-permute-start.40
  134.6 3.3 collective-permute-start.20
  140.9 3.0 collective-permute-start.22
  154.3 2.7 collective-permute-start.45
  170.7 3.0 collective-permute-start.26
  174.4 8.3 %left.3 = (f32[96,768]{1,0:T(8,128)}, f32[96,768]{1,0:T(8,128)}) custom-call(s32[2]{0:T(128)} %pad_add_fusion.ids_ref, bf16[6,768,512]{2,1,0:T(8,128)(2,1)} %get-tuple-element.109.high_ref.refs_2_, bf16[6,768,512]{2,1,0:T(8,128)(2,1)} %get-tuple-element.110.low_ref.refs_3_, f32[96,128]{1,0:T(8,128)} %right_sum.5.refs_0_, f32[96,128]{1,0:T(8,128)} %copy-done.29, ...), custom_call_target="tpu_custom_call" | custom-call | flops 452984832 | bytes 9437184 | tf_op jit(solution)/shard_map/left/pallas_call | solution.py:247
  184.6 8.2 %left.2 = (f32[96,768]{1,0:T(8,128)}, f32[96,768]{1,0:T(8,128)}) custom-call(s32[2]{0:T(128)} %pad_add_fusion.ids_ref, bf16[6,768,512]{2,1,0:T(8,128)(2,1)} %get-tuple-element.77.high_ref.refs_0_, bf16[6,768,512]{2,1,0:T(8,128)(2,1)} %get-tuple-element.78.low_ref.refs_1_, f32[96,128]{1,0:T(8,128)} %right_sum.4.refs_0_, f32[96,128]{1,0:T(8,128)} %copy-done.32, ...), custom_call_target="tpu_custom_call" | custom-call | flops 452984832 | bytes 9437184 | tf_op jit(solution)/shard_map/left/pallas_call | solution.py:247
  200.1 4.1 collective-permute-start.52
  204.3 2.8 collective-permute-start.54
  217.4 3.5 collective-permute-done.57.refs_7_
  224.4 3.2 collective-permute-start.63
  230.7 5.6 %collective-permute-start.60 = (f32[72,128]{1,0:T(8,128)}, f32[72,128]{1,0:T(8,128)S(1)}, u32[]{:S(2)}, u32[]{:S(2)}) collective-permute-start(f32[72,128]{1,0:T(8,128)} %left_sum.3.refs_0_), channel_id=1, source_target_pairs={{0,12},{4,8},{8,4},{12,0},{16,28},{20,24},{24,20},{28,16},{1,13},{... | collective-permute-start | bytes 110600 | tf_op jit(solution)/shard_map/ppermute | solution.py:265
  238.0 3.0 collective-permute-done.62.refs_5_
  245.8 3.6 basis.3.first_ref
  252.3 7.6 %right.6 = (f32[96,128]{1,0:T(8,128)}, f32[96,128]{1,0:T(8,128)}, f32[96,128]{1,0:T(8,128)}, f32[96,128]{1,0:T(8,128)}, f32[96,128]{1,0:T(8,128)}, /*index=5*/f3...) custom-call(s32[2]{0:T(128)} %pad_add_fusion.ids_ref, f32[96,768]{1,0:T(8,128)} %basis.3.first_ref, ...), custom_call_target="tpu_custom_call" | custom-call | flops 452984832 | bytes 9437184 | tf_op jit(solution)/shard_map/right/pallas_call | solution.py:247
  260.8 3.8 collective-permute-done.67.second_ref
  264.6 7.0 %collective-permute-done.66.first_ref = f32[96,768]{1,0:T(8,128)S(1)} collective-permute-done((f32[96,768]{1,0:T(8,128)}, f32[96,768]{1,0:T(8,128)S(1)}, u32[]{:S(2)}, u32[]{:S(2)}) %collective-permute-start.66) | collective-permute-done | bytes 294944 | tf_op jit(solution)/shard_map/ppermute | solution.py:265
  271.7 3.3 collective-permute-start.72
  275.3 7.6 %right.7 = (f32[96,128]{1,0:T(8,128)}, f32[96,128]{1,0:T(8,128)}, f32[96,128]{1,0:T(8,128)}, f32[96,128]{1,0:T(8,128)}, f32[96,128]{1,0:T(8,128)}, /*index=5*/f3...) custom-call(s32[2]{0:T(128)} %pad_add_fusion.ids_ref, f32[96,768]{1,0:T(8,128)} %copy-done.6, f32[96,768]{1,0:T(8,128)} %copy-done.4, ...), custom_call_target="tpu_custom_call" | custom-call | flops 452984832 | bytes 9437184 | tf_op jit(solution)/shard_map/right/pallas_call | solution.py:247
  283.0 4.1 collective-permute-start.74
  293.9 3.0 collective-permute-start.87
  299.9 3.5 collective-permute-start.81
  304.2 3.4 collective-permute-start.78
  312.8 3.4 collective-permute-start.95
  318.5 3.2 collective-permute-start.92
  326.3 9.6 %factors.1.factors_ref.a = bf16[9216,96]{1,0:T(8,128)(2,1)} custom-call(s32[2]{0:T(128)} %pad_add_fusion.ids_ref, f32[12,32,768]{2,1,0:T(8,128)} %bitcast.21), custom_call_target="tpu_custom_call" | custom-call | tf_op jit(solution)/shard_map/factors/pallas_call | solution.py:247
  339.4 5.5 %late_weights.1 = bf16[2,288,512]{2,1,0:T(8,128)(2,1)} custom-call(s32[2]{0:T(128)} %pad_add_fusion.ids_ref, bf16[9216,96]{1,0:T(8,128)(2,1)} %factors.1.factors_ref.a, f32[384,512]{1,0:T(8,128)} %new_query.1.right_ref.b, f32[2,288,512]{2,1,0:T(8,128)} %pad_maximum_fusion.1.base_ref), custom_call_target="tpu_custom_call" | custom-call | tf_op jit(solution)/shard_map/late_weights/pallas_call | solution.py:247
  348.1 19.6 %new_error.1 = f32[1,12,768,512]{3,2,1,0:T(8,128)} custom-call(s32[2]{0:T(128)} %pad_add_fusion.ids_ref, bf16[9216,96]{1,0:T(8,128)(2,1)} %factors.1.factors_ref.a, f32[384,512]{1,0:T(8,128)} %new_query.1.right_ref.b, bf16[6,768,512]{2,1,0:T(8,128)(2,1)} %get-tuple-element.77.high_ref.refs_0_, bf16[6,768,512]{2,1,0:T(8,128)(2,1)} %get-tuple-element.78.low_ref.refs_1_, ...), custom_call_target="tpu_custom_call" | custom-call | flops 905969664 | bytes 37748736 | tf_op jit(solution)/shard_map/new_error/pallas_call | solution.py:247
  369.4 10.3 %flat_rows.1 = (f32[288,2048]{1,0:T(8,128)}, f32[288,2048]{1,0:T(8,128)}) custom-call(s32[2]{0:T(128)} %pad_add_fusion.ids_ref, bf16[9216,96]{1,0:T(8,128)(2,1)} %factors.1.factors_ref.a, f32[4,2,32,512]{3,2,1,0:T(8,128)} %pad_maximum_fusion.2.right_ref, f32[288,2048]{1,0:T(8,128)} %momentum_ref.1, f32[288,2048]{1,0:T(8,128)} %master_ref.1), custom_call_target="tpu_custom_call" | custom-call | flops 113246208 | bytes 9437184 | tf_op jit(solution)/shard_map/flat_rows/pallas_call | solution.py:247
  379.8 16.3 %early_weights.2._ = bf16[8,4,288,512]{3,2,1,0:T(8,128)(2,1)} custom-call(s32[2]{0:T(128)} %pad_add_fusion.ids_ref, bf16[9216,96]{1,0:T(8,128)(2,1)} %factors.1.factors_ref.a, f32[384,512]{1,0:T(8,128)} %new_query.1.right_ref.b, f32[8,288,512]{2,1,0:T(8,128)} %bitcast.19), custom_call_target="tpu_custom_call" | custom-call | flops 226492416 | bytes 7077888 | tf_op jit(solution)/shard_map/early_weights/pallas_call | solution.py:247
  396.1 16.4 %early_weights.3._ = bf16[8,4,288,512]{3,2,1,0:T(8,128)(2,1)} custom-call(s32[2]{0:T(128)} %pad_add_fusion.ids_ref, bf16[9216,96]{1,0:T(8,128)(2,1)} %factors.1.factors_ref.a, f32[384,512]{1,0:T(8,128)} %new_query.1.right_ref.b, f32[8,288,512]{2,1,0:T(8,128)} %bitcast.22, bf16[8,4,288,512]{3,2,1,0:T(8,128)(2,1)} %early_weights.2._), custom_call_target="tpu_custom_call", output_to_operand_aliasing={{}: (4, {})} | custom-call | flops 226492416 | bytes 7077888 | tf_op jit(solution)/shard_map/early_weights/pallas_call | solution.py:247
  412.5 11.7 %all-gather.7.cloned.1.call-done = bf16[16,288,512]{2,1,0:T(8,128)(2,1)} async-done(((bf16[2,288,512]{2,1,0:T(8,128)(2,1)}), bf16[16,288,512]{2,1,0:T(8,128)(2,1)}) %all-gather.7.cloned.1.call-update) | async-done | bytes 4718608 | tf_op jit(solution)/shard_map/all_gather | solution.py:434
  424.2 11.0 %place_late.1 = bf16[8,4,288,512]{3,2,1,0:T(8,128)(2,1)} custom-call(s32[2]{0:T(128)} %pad_add_fusion.ids_ref, bf16[8,2,288,512]{3,2,1,0:T(8,128)(2,1)} %bitcast.20, bf16[8,4,288,512]{3,2,1,0:T(8,128)(2,1)} %early_weights.3._), custom_call_target="tpu_custom_call", output_to_operand_aliasing={{}: (2, {})} | custom-call | tf_op jit(solution)/shard_map/place_late/pallas_call | solution.py:247
  (410 shorter events, 131.9 us)
Async XLA Ops:
  7.2 372.6 %all-gather.11.cloned.1.call-start = ((), (), s32[]{:S(2)}) async-start(), calls=%async_computation.2 | async-start | bytes 5308416 | tf_op jit(solution)/shard_map/all_gather | solution.py:348
  19.7 15.1 %collective-permute-start.1 = (f32[96,768]{1,0:T(8,128)}, f32[96,768]{1,0:T(8,128)S(1)}, u32[]{:S(2)}, u32[]{:S(2)}) collective-permute-start(f32[96,768]{1,0:T(8,128)} %get-tuple-element.81), channel_id=1, source_target_pairs={{0,2},{1,3},{2,0},{3,1},{4,6},{5,7},{6,4},{7,5},{8,10},{9,11},{10,... | collective-permute-start | bytes 884744 | tf_op jit(solution)/shard_map/ppermute | solution.py:265
  22.6 12.9 %collective-permute-start.2 = (f32[96,768]{1,0:T(8,128)}, f32[96,768]{1,0:T(8,128)S(1)}, u32[]{:S(2)}, u32[]{:S(2)}) collective-permute-start(f32[96,768]{1,0:T(8,128)} %get-tuple-element.82), channel_id=1, source_target_pairs={{0,3},{1,2},{2,1},{3,0},{4,7},{5,6},{6,5},{7,4},{8,11},{9,10},{10,... | collective-permute-start | bytes 884744 | tf_op jit(solution)/shard_map/ppermute | solution.py:265
  42.3 353.8 %all-gather.9.cloned.1.call-start = ((), (), s32[]{:S(2)}) async-start(), calls=%async_computation.1 | async-start | bytes 5308416 | tf_op jit(solution)/shard_map/all_gather | solution.py:348
  45.5 378.6 %all-gather.7.cloned.1.call-start = ((), (), s32[]{:S(2)}) async-start(), calls=%async_computation | async-start | bytes 5308416 | tf_op jit(solution)/shard_map/all_gather | solution.py:434
  66.7 11.6 %collective-permute-start.16 = (f32[72,128]{1,0:T(8,128)}, f32[72,128]{1,0:T(8,128)S(1)}, u32[]{:S(2)}, u32[]{:S(2)}) collective-permute-start(f32[72,128]{1,0:T(8,128)} %left_sum.2.refs_0_), channel_id=1, source_target_pairs={{0,28},{4,24},{8,20},{12,16},{16,12},{20,8},{24,4},{28,0},{1,29},{... | collective-permute-start | bytes 110600 | tf_op jit(solution)/shard_map/ppermute | solution.py:265
  70.5 14.1 %collective-permute-start.14 = (f32[72,128]{1,0:T(8,128)}, f32[72,128]{1,0:T(8,128)S(1)}, u32[]{:S(2)}, u32[]{:S(2)}) collective-permute-start(f32[72,128]{1,0:T(8,128)} %left_sum.2.refs_0_), channel_id=1, source_target_pairs={{0,20},{4,16},{8,28},{12,24},{16,4},{20,0},{24,12},{28,8},{1,21},{... | collective-permute-start | bytes 110600 | tf_op jit(solution)/shard_map/ppermute | solution.py:265
  91.0 15.8 %collective-permute-start.33 = (f32[96,768]{1,0:T(8,128)}, f32[96,768]{1,0:T(8,128)S(1)}, u32[]{:S(2)}, u32[]{:S(2)}) collective-permute-start(f32[96,768]{1,0:T(8,128)} %basis.2.first_ref), channel_id=1, source_target_pairs={{0,2},{1,3},{2,0},{3,1},{4,6},{5,7},{6,4},{7,5},{8,10},{9,11},{10,... | collective-permute-start | bytes 884744 | tf_op jit(solution)/shard_map/ppermute | solution.py:265
  92.5 27.3 %collective-permute-start.17 = (f32[96,768]{1,0:T(8,128)}, f32[96,768]{1,0:T(8,128)S(1)}, u32[]{:S(2)}, u32[]{:S(2)}) collective-permute-start(f32[96,768]{1,0:T(8,128)} %basis.2.first_ref), channel_id=1, source_target_pairs={{0,1},{1,0},{2,3},{3,2},{4,5},{5,4},{6,7},{7,6},{8,9},{9,8},{10,11... | collective-permute-start | bytes 884744 | tf_op jit(solution)/shard_map/ppermute | solution.py:265
  115.3 13.8 %collective-permute-start.35 = (f32[96,128]{1,0:T(8,128)}, f32[96,128]{1,0:T(8,128)S(1)}, u32[]{:S(2)}, u32[]{:S(2)}) collective-permute-start(f32[96,128]{1,0:T(8,128)} %get-tuple-element.112), channel_id=1, source_target_pairs={{0,4},{4,0},{8,12},{12,8},{16,20},{20,16},{24,28},{28,24},{1,5},{5... | collective-permute-start | bytes 147464 | tf_op jit(solution)/shard_map/ppermute | solution.py:265
  115.6 16.9 %collective-permute-start.36 = (f32[96,128]{1,0:T(8,128)}, f32[96,128]{1,0:T(8,128)S(1)}, u32[]{:S(2)}, u32[]{:S(2)}) collective-permute-start(f32[96,128]{1,0:T(8,128)} %get-tuple-element.113), channel_id=1, source_target_pairs={{0,8},{4,12},{8,0},{12,4},{16,24},{20,28},{24,16},{28,20},{1,9},{5... | collective-permute-start | bytes 147464 | tf_op jit(solution)/shard_map/ppermute | solution.py:265
  116.4 18.0 %collective-permute-start.37 = (f32[96,128]{1,0:T(8,128)}, f32[96,128]{1,0:T(8,128)S(1)}, u32[]{:S(2)}, u32[]{:S(2)}) collective-permute-start(f32[96,128]{1,0:T(8,128)} %get-tuple-element.114), channel_id=1, source_target_pairs={{0,12},{4,8},{8,4},{12,0},{16,28},{20,24},{24,20},{28,16},{1,13},{... | collective-permute-start | bytes 147464 | tf_op jit(solution)/shard_map/ppermute | solution.py:265
  118.9 15.7 %collective-permute-start.38 = (f32[96,128]{1,0:T(8,128)}, f32[96,128]{1,0:T(8,128)S(1)}, u32[]{:S(2)}, u32[]{:S(2)}) collective-permute-start(f32[96,128]{1,0:T(8,128)} %get-tuple-element.115), channel_id=1, source_target_pairs={{0,16},{4,20},{8,24},{12,28},{16,0},{20,4},{24,8},{28,12},{1,17},{... | collective-permute-start | bytes 147464 | tf_op jit(solution)/shard_map/ppermute | solution.py:265
  119.8 14.8 %collective-permute-start.39 = (f32[96,128]{1,0:T(8,128)}, f32[96,128]{1,0:T(8,128)S(1)}, u32[]{:S(2)}, u32[]{:S(2)}) collective-permute-start(f32[96,128]{1,0:T(8,128)} %get-tuple-element.116), channel_id=1, source_target_pairs={{0,20},{4,16},{8,28},{12,24},{16,4},{20,0},{24,12},{28,8},{1,21},{... | collective-permute-start | bytes 147464 | tf_op jit(solution)/shard_map/ppermute | solution.py:265
  134.6 14.6 %collective-permute-start.20 = (f32[96,128]{1,0:T(8,128)}, f32[96,128]{1,0:T(8,128)S(1)}, u32[]{:S(2)}, u32[]{:S(2)}) collective-permute-start(f32[96,128]{1,0:T(8,128)} %get-tuple-element.102), channel_id=1, source_target_pairs={{0,12},{4,8},{8,4},{12,0},{16,28},{20,24},{24,20},{28,16},{1,13},{... | collective-permute-start | bytes 147464 | tf_op jit(solution)/shard_map/ppermute | solution.py:265
  137.9 13.9 %collective-permute-start.21 = (f32[96,128]{1,0:T(8,128)}, f32[96,128]{1,0:T(8,128)S(1)}, u32[]{:S(2)}, u32[]{:S(2)}) collective-permute-start(f32[96,128]{1,0:T(8,128)} %get-tuple-element.103), channel_id=1, source_target_pairs={{0,16},{4,20},{8,24},{12,28},{16,0},{20,4},{24,8},{28,12},{1,17},{... | collective-permute-start | bytes 147464 | tf_op jit(solution)/shard_map/ppermute | solution.py:265
  140.9 13.3 %collective-permute-start.22 = (f32[96,128]{1,0:T(8,128)}, f32[96,128]{1,0:T(8,128)S(1)}, u32[]{:S(2)}, u32[]{:S(2)}) collective-permute-start(f32[96,128]{1,0:T(8,128)} %get-tuple-element.104), channel_id=1, source_target_pairs={{0,20},{4,16},{8,28},{12,24},{16,4},{20,0},{24,12},{28,8},{1,21},{... | collective-permute-start | bytes 147464 | tf_op jit(solution)/shard_map/ppermute | solution.py:265
  145.3 11.6 %collective-permute-start.24 = (f32[96,128]{1,0:T(8,128)}, f32[96,128]{1,0:T(8,128)S(1)}, u32[]{:S(2)}, u32[]{:S(2)}) collective-permute-start(f32[96,128]{1,0:T(8,128)} %get-tuple-element.106), channel_id=1, source_target_pairs={{0,28},{4,24},{8,20},{12,16},{16,12},{20,8},{24,4},{28,0},{1,29},{... | collective-permute-start | bytes 147464 | tf_op jit(solution)/shard_map/ppermute | solution.py:265
  167.1 15.7 %collective-permute-start.29 = (f32[96,128]{1,0:T(8,128)}, f32[96,128]{1,0:T(8,128)S(1)}, u32[]{:S(2)}, u32[]{:S(2)}) collective-permute-start(f32[96,128]{1,0:T(8,128)} %right_sum.4.refs_0_), channel_id=1, source_target_pairs={{0,20},{4,16},{8,28},{12,24},{16,4},{20,0},{24,12},{28,8},{1,21},{... | collective-permute-start | bytes 147464 | tf_op jit(solution)/shard_map/ppermute | solution.py:265
  167.5 15.8 %collective-permute-start.28 = (f32[96,128]{1,0:T(8,128)}, f32[96,128]{1,0:T(8,128)S(1)}, u32[]{:S(2)}, u32[]{:S(2)}) collective-permute-start(f32[96,128]{1,0:T(8,128)} %right_sum.4.refs_0_), channel_id=1, source_target_pairs={{0,16},{4,20},{8,24},{12,28},{16,0},{20,4},{24,8},{28,12},{1,17},{... | collective-permute-start | bytes 147464 | tf_op jit(solution)/shard_map/ppermute | solution.py:265
  169.8 13.5 %collective-permute-start.27 = (f32[96,128]{1,0:T(8,128)}, f32[96,128]{1,0:T(8,128)S(1)}, u32[]{:S(2)}, u32[]{:S(2)}) collective-permute-start(f32[96,128]{1,0:T(8,128)} %right_sum.4.refs_0_), channel_id=1, source_target_pairs={{0,12},{4,8},{8,4},{12,0},{16,28},{20,24},{24,20},{28,16},{1,13},{... | collective-permute-start | bytes 147464 | tf_op jit(solution)/shard_map/ppermute | solution.py:265
  170.7 12.7 %collective-permute-start.26 = (f32[96,128]{1,0:T(8,128)}, f32[96,128]{1,0:T(8,128)S(1)}, u32[]{:S(2)}, u32[]{:S(2)}) collective-permute-start(f32[96,128]{1,0:T(8,128)} %right_sum.4.refs_0_), channel_id=1, source_target_pairs={{0,8},{4,12},{8,0},{12,4},{16,24},{20,28},{24,16},{28,20},{1,9},{5... | collective-permute-start | bytes 147464 | tf_op jit(solution)/shard_map/ppermute | solution.py:265
  182.8 11.9 %collective-permute-start.49 = (f32[96,768]{1,0:T(8,128)}, f32[96,768]{1,0:T(8,128)S(1)}, u32[]{:S(2)}, u32[]{:S(2)}) collective-permute-start(f32[96,768]{1,0:T(8,128)} %get-tuple-element.119), channel_id=1, source_target_pairs={{0,2},{1,3},{2,0},{3,1},{4,6},{5,7},{6,4},{7,5},{8,10},{9,11},{10,... | collective-permute-start | bytes 884744 | tf_op jit(solution)/shard_map/ppermute | solution.py:265
  183.3 11.3 %collective-permute-start.50 = (f32[96,768]{1,0:T(8,128)}, f32[96,768]{1,0:T(8,128)S(1)}, u32[]{:S(2)}, u32[]{:S(2)}) collective-permute-start(f32[96,768]{1,0:T(8,128)} %get-tuple-element.120), channel_id=1, source_target_pairs={{0,3},{1,2},{2,1},{3,0},{4,7},{5,6},{6,5},{7,4},{8,11},{9,10},{10,... | collective-permute-start | bytes 884744 | tf_op jit(solution)/shard_map/ppermute | solution.py:265
  194.5 66.3 %collective-permute-start.100 = (f32[288,512]{1,0:T(8,128)S(1)}, f32[288,512]{1,0:T(8,128)S(1)}, u32[]{:S(2)}, u32[]{:S(2)}) collective-permute-start(f32[288,512]{1,0:T(8,128)S(1)} %get-tuple-element.151), channel_id=1, source_target_pairs={{0,3},{1,2},{2,1},{3,0},{4,7},{5,6},{6,5},{7,4},{8,11},{9,10},{10,... | collective-permute-start | bytes 1769480 | tf_op jit(solution)/shard_map/ppermute | solution.py:265
  224.4 11.9 %collective-permute-start.63 = (f32[72,128]{1,0:T(8,128)}, f32[72,128]{1,0:T(8,128)S(1)}, u32[]{:S(2)}, u32[]{:S(2)}) collective-permute-start(f32[72,128]{1,0:T(8,128)} %left_sum.3.refs_0_), channel_id=1, source_target_pairs={{0,24},{4,28},{8,16},{12,20},{16,8},{20,12},{24,0},{28,4},{1,25},{... | collective-permute-start | bytes 110600 | tf_op jit(solution)/shard_map/ppermute | solution.py:265
  227.6 13.4 %collective-permute-start.62 = (f32[72,128]{1,0:T(8,128)}, f32[72,128]{1,0:T(8,128)S(1)}, u32[]{:S(2)}, u32[]{:S(2)}) collective-permute-start(f32[72,128]{1,0:T(8,128)} %left_sum.3.refs_0_), channel_id=1, source_target_pairs={{0,20},{4,16},{8,28},{12,24},{16,4},{20,0},{24,12},{28,8},{1,21},{... | collective-permute-start | bytes 110600 | tf_op jit(solution)/shard_map/ppermute | solution.py:265
  229.7 13.8 %collective-permute-start.61 = (f32[72,128]{1,0:T(8,128)}, f32[72,128]{1,0:T(8,128)S(1)}, u32[]{:S(2)}, u32[]{:S(2)}) collective-permute-start(f32[72,128]{1,0:T(8,128)} %left_sum.3.refs_0_), channel_id=1, source_target_pairs={{0,16},{4,20},{8,24},{12,28},{16,0},{20,4},{24,8},{28,12},{1,17},{... | collective-permute-start | bytes 110600 | tf_op jit(solution)/shard_map/ppermute | solution.py:265
  230.7 12.9 %collective-permute-start.60 = (f32[72,128]{1,0:T(8,128)}, f32[72,128]{1,0:T(8,128)S(1)}, u32[]{:S(2)}, u32[]{:S(2)}) collective-permute-start(f32[72,128]{1,0:T(8,128)} %left_sum.3.refs_0_), channel_id=1, source_target_pairs={{0,12},{4,8},{8,4},{12,0},{16,28},{20,24},{24,20},{28,16},{1,13},{... | collective-permute-start | bytes 110600 | tf_op jit(solution)/shard_map/ppermute | solution.py:265
  243.6 65.7 %collective-permute-start.99 = (f32[288,512]{1,0:T(8,128)S(1)}, f32[288,512]{1,0:T(8,128)S(1)}, u32[]{:S(2)}, u32[]{:S(2)}) collective-permute-start(f32[288,512]{1,0:T(8,128)S(1)} %get-tuple-element.152), channel_id=1, source_target_pairs={{0,2},{1,3},{2,0},{3,1},{4,6},{5,7},{6,4},{7,5},{8,10},{9,11},{10,... | collective-permute-start | bytes 1769480 | tf_op jit(solution)/shard_map/ppermute | solution.py:265
  249.4 15.2 %collective-permute-start.67 = (f32[96,768]{1,0:T(8,128)}, f32[96,768]{1,0:T(8,128)S(1)}, u32[]{:S(2)}, u32[]{:S(2)}) collective-permute-start(f32[96,768]{1,0:T(8,128)} %basis.3.first_ref), channel_id=1, source_target_pairs={{0,3},{1,2},{2,1},{3,0},{4,7},{5,6},{6,5},{7,4},{8,11},{9,10},{10,... | collective-permute-start | bytes 884744 | tf_op jit(solution)/shard_map/ppermute | solution.py:265
  250.9 20.7 %collective-permute-start.66 = (f32[96,768]{1,0:T(8,128)}, f32[96,768]{1,0:T(8,128)S(1)}, u32[]{:S(2)}, u32[]{:S(2)}) collective-permute-start(f32[96,768]{1,0:T(8,128)} %basis.3.first_ref), channel_id=1, source_target_pairs={{0,2},{1,3},{2,0},{3,1},{4,6},{5,7},{6,4},{7,5},{8,10},{9,11},{10,... | collective-permute-start | bytes 884744 | tf_op jit(solution)/shard_map/ppermute | solution.py:265
  259.9 11.8 %collective-permute-start.68 = (f32[96,128]{1,0:T(8,128)}, f32[96,128]{1,0:T(8,128)S(1)}, u32[]{:S(2)}, u32[]{:S(2)}) collective-permute-start(f32[96,128]{1,0:T(8,128)} %get-tuple-element.130), channel_id=1, source_target_pairs={{0,4},{4,0},{8,12},{12,8},{16,20},{20,16},{24,28},{28,24},{1,5},{5... | collective-permute-start | bytes 147464 | tf_op jit(solution)/shard_map/ppermute | solution.py:265
  260.8 14.2 %collective-permute-start.69 = (f32[96,128]{1,0:T(8,128)}, f32[96,128]{1,0:T(8,128)S(1)}, u32[]{:S(2)}, u32[]{:S(2)}) collective-permute-start(f32[96,128]{1,0:T(8,128)} %get-tuple-element.131), channel_id=1, source_target_pairs={{0,8},{4,12},{8,0},{12,4},{16,24},{20,28},{24,16},{28,20},{1,9},{5... | collective-permute-start | bytes 147464 | tf_op jit(solution)/shard_map/ppermute | solution.py:265
  264.6 18.3 %collective-permute-start.70 = (f32[96,128]{1,0:T(8,128)}, f32[96,128]{1,0:T(8,128)S(1)}, u32[]{:S(2)}, u32[]{:S(2)}) collective-permute-start(f32[96,128]{1,0:T(8,128)} %get-tuple-element.132), channel_id=1, source_target_pairs={{0,12},{4,8},{8,4},{12,0},{16,28},{20,24},{24,20},{28,16},{1,13},{... | collective-permute-start | bytes 147464 | tf_op jit(solution)/shard_map/ppermute | solution.py:265
  271.6 15.4 %collective-permute-start.71 = (f32[96,128]{1,0:T(8,128)}, f32[96,128]{1,0:T(8,128)S(1)}, u32[]{:S(2)}, u32[]{:S(2)}) collective-permute-start(f32[96,128]{1,0:T(8,128)} %get-tuple-element.133), channel_id=1, source_target_pairs={{0,16},{4,20},{8,24},{12,28},{16,0},{20,4},{24,8},{28,12},{1,17},{... | collective-permute-start | bytes 147464 | tf_op jit(solution)/shard_map/ppermute | solution.py:265
  271.7 16.4 %collective-permute-start.72 = (f32[96,128]{1,0:T(8,128)}, f32[96,128]{1,0:T(8,128)S(1)}, u32[]{:S(2)}, u32[]{:S(2)}) collective-permute-start(f32[96,128]{1,0:T(8,128)} %get-tuple-element.134), channel_id=1, source_target_pairs={{0,20},{4,16},{8,28},{12,24},{16,4},{20,0},{24,12},{28,8},{1,21},{... | collective-permute-start | bytes 147464 | tf_op jit(solution)/shard_map/ppermute | solution.py:265
  275.0 13.1 %collective-permute-start.73 = (f32[96,128]{1,0:T(8,128)}, f32[96,128]{1,0:T(8,128)S(1)}, u32[]{:S(2)}, u32[]{:S(2)}) collective-permute-start(f32[96,128]{1,0:T(8,128)} %get-tuple-element.135), channel_id=1, source_target_pairs={{0,24},{4,28},{8,16},{12,20},{16,8},{20,12},{24,0},{28,4},{1,25},{... | collective-permute-start | bytes 147464 | tf_op jit(solution)/shard_map/ppermute | solution.py:265
  291.4 12.0 %collective-permute-start.86 = (f32[96,128]{1,0:T(8,128)}, f32[96,128]{1,0:T(8,128)S(1)}, u32[]{:S(2)}, u32[]{:S(2)}) collective-permute-start(f32[96,128]{1,0:T(8,128)} %get-tuple-element.142), channel_id=1, source_target_pairs={{0,20},{4,16},{8,28},{12,24},{16,4},{20,0},{24,12},{28,8},{1,21},{... | collective-permute-start | bytes 147464 | tf_op jit(solution)/shard_map/ppermute | solution.py:265
  304.2 12.0 %collective-permute-start.78 = (f32[96,128]{1,0:T(8,128)}, f32[96,128]{1,0:T(8,128)S(1)}, u32[]{:S(2)}, u32[]{:S(2)}) collective-permute-start(f32[96,128]{1,0:T(8,128)} %right_sum.6.refs_0_), channel_id=1, source_target_pairs={{0,16},{4,20},{8,24},{12,28},{16,0},{20,4},{24,8},{28,12},{1,17},{... | collective-permute-start | bytes 147464 | tf_op jit(solution)/shard_map/ppermute | solution.py:265
  318.2 17.8 %collective-permute-start.93 = (f32[96,128]{1,0:T(8,128)S(1)}, f32[96,128]{1,0:T(8,128)S(1)}, u32[]{:S(2)}, u32[]{:S(2)}) collective-permute-start(f32[96,128]{1,0:T(8,128)S(1)} %copy-done.18), channel_id=1, source_target_pairs={{0,20},{4,16},{8,28},{12,24},{16,4},{20,0},{24,12},{28,8},{1,21},{... | collective-permute-start | bytes 147464 | tf_op jit(solution)/shard_map/ppermute | solution.py:265
  318.5 17.5 %collective-permute-start.92 = (f32[96,128]{1,0:T(8,128)S(1)}, f32[96,128]{1,0:T(8,128)S(1)}, u32[]{:S(2)}, u32[]{:S(2)}) collective-permute-start(f32[96,128]{1,0:T(8,128)S(1)} %copy-done.18), channel_id=1, source_target_pairs={{0,16},{4,20},{8,24},{12,28},{16,0},{20,4},{24,8},{28,12},{1,17},{... | collective-permute-start | bytes 147464 | tf_op jit(solution)/shard_map/ppermute | solution.py:265
  321.7 14.3 %collective-permute-start.91 = (f32[96,128]{1,0:T(8,128)S(1)}, f32[96,128]{1,0:T(8,128)S(1)}, u32[]{:S(2)}, u32[]{:S(2)}) collective-permute-start(f32[96,128]{1,0:T(8,128)S(1)} %copy-done.18), channel_id=1, source_target_pairs={{0,12},{4,8},{8,4},{12,0},{16,28},{20,24},{24,20},{28,16},{1,13},{... | collective-permute-start | bytes 147464 | tf_op jit(solution)/shard_map/ppermute | solution.py:265
  322.8 13.2 %collective-permute-start.90 = (f32[96,128]{1,0:T(8,128)S(1)}, f32[96,128]{1,0:T(8,128)S(1)}, u32[]{:S(2)}, u32[]{:S(2)}) collective-permute-start(f32[96,128]{1,0:T(8,128)S(1)} %copy-done.18), channel_id=1, source_target_pairs={{0,8},{4,12},{8,0},{12,4},{16,24},{20,28},{24,16},{28,20},{1,9},{5... | collective-permute-start | bytes 147464 | tf_op jit(solution)/shard_map/ppermute | solution.py:265
  324.1 11.9 %collective-permute-start.89 = (f32[96,128]{1,0:T(8,128)S(1)}, f32[96,128]{1,0:T(8,128)S(1)}, u32[]{:S(2)}, u32[]{:S(2)}) collective-permute-start(f32[96,128]{1,0:T(8,128)S(1)} %copy-done.18), channel_id=1, source_target_pairs={{0,4},{4,0},{8,12},{12,8},{16,20},{20,16},{24,28},{28,24},{1,5},{5... | collective-permute-start | bytes 147464 | tf_op jit(solution)/shard_map/ppermute | solution.py:265
  345.8 22.7 %collective-permute-start.97 = (f32[2,32,512]{2,1,0:T(8,128)S(1)}, f32[2,32,512]{2,1,0:T(8,128)S(1)}, u32[]{:S(2)}, u32[]{:S(2)}) collective-permute-start(f32[2,32,512]{2,1,0:T(8,128)S(1)} %constant_dynamic-slice_fusion), channel_id=1, source_target_pairs={{0,2},{1,3},{2,0},{3,1},{4,6},{5,7},{6,4},{7,5},{8,10},{9,11},{10,... | collective-permute-start | bytes 393224 | tf_op jit(solution)/shard_map/ppermute | solution.py:265
  346.9 21.7 %collective-permute-start.96 = (f32[2,32,512]{2,1,0:T(8,128)S(1)}, f32[2,32,512]{2,1,0:T(8,128)S(1)}, u32[]{:S(2)}, u32[]{:S(2)}) collective-permute-start(f32[2,32,512]{2,1,0:T(8,128)S(1)} %constant_dynamic-slice_fusion), channel_id=1, source_target_pairs={{0,1},{1,0},{2,3},{3,2},{4,5},{5,4},{6,7},{7,6},{8,9},{9,8},{10,11... | collective-permute-start | bytes 393224 | tf_op jit(solution)/shard_map/ppermute | solution.py:265
  346.9 21.7 %collective-permute-start.98 = (f32[2,32,512]{2,1,0:T(8,128)S(1)}, f32[2,32,512]{2,1,0:T(8,128)S(1)}, u32[]{:S(2)}, u32[]{:S(2)}) collective-permute-start(f32[2,32,512]{2,1,0:T(8,128)S(1)} %constant_dynamic-slice_fusion), channel_id=1, source_target_pairs={{0,3},{1,2},{2,1},{3,0},{4,7},{5,6},{6,5},{7,4},{8,11},{9,10},{10,... | collective-permute-start | bytes 393224 | tf_op jit(solution)/shard_map/ppermute | solution.py:265
  (163 other events, 1347.9 us)
Sparse Core Ops, SparseCore 0:
  42.5 106.0 all-gather.10
  150.7 96.6 all-gather.8
  345.0 79.0 all-gather.6

commit v2 on v1

--- a/solution.py
+++ b/solution.py
@@ -19,7 +19,6 @@
 LANES = 128
 EARLY = 2
 F32, BF16 = jnp.float32, jnp.bfloat16
-PARAMS = pltpu.CompilerParams(vmem_limit_bytes=60 * 2**20)
 SCALARS = pl.BlockSpec(memory_space=pltpu.SMEM)
 
 
@@ -117,10 +116,14 @@
     put_left(small_by_large(own, high_ref[0], low_ref[0], True), step, left_refs, per_tp)
 
 
-def split_kernel(tps, ids_ref, *refs):
-    scratch = refs[-1]
-    lay_lanes(scratch, sum_of(refs[:tps]))
-    split_parts(scratch, ids_ref[0], refs[tps:-1])
+def split_kernel(tps, *refs):
+    lay_lanes(refs[-1], sum_of(refs[:tps]))
+
+
+def total_kernel(parts_ref, out_ref):
+    summed = sum_of([parts_ref.at[part] for part in range(parts_ref.shape[0])])
+    for part in range(parts_ref.shape[0]):
+        out_ref[part] = summed
 
 
 def sum_kernel(scale, *refs):
@@ -151,11 +154,9 @@
     return mixed
 
 
-def basis_kernel(rank, ids_ref, *refs):
-    basis_ref, scratch = refs[-2:]
-    join_parts(scratch, ids_ref[0], refs[:-2])
+def basis_kernel(rank, left_ref, basis_ref):
     rows = basis_ref.shape[0]
-    left = read_lanes(scratch, rows)
+    left = read_lanes(left_ref, rows)
     padded = jnp.concatenate([left, jnp.zeros((-rows % LANES, left.shape[1]), F32)], axis=0)
     basis_ref[...] = dot3(mixing(padded, rank), padded)[:rows]
 
@@ -174,54 +175,94 @@
         split_parts(scratch, ids_ref[0], part_refs)
 
 
-def factor_kernel(ids_ref, basis_ref, factors_ref):
-    high, low = two_terms(basis_ref[0].T)
-    factors_ref[...] = jnp.concatenate([high, low, high], axis=1)
-
-
-def query_kernel(tps, ids_ref, *refs):
-    query_ref, scratch = refs[-2:]
+def rows_of_update(basis_ref, right_ref, scratch, first_unit, unit, per_tp, rank, tp, first_matrix):
+    per_matrix = basis_ref.shape[1] // unit
+    for u in range(scratch.shape[0] // unit):
+        at = first_unit + u
+        matrix = at // per_matrix
+        slot = ((matrix // per_tp) ^ tp) * per_tp + matrix % per_tp
+        lanes = pl.ds(pl.multiple_of((at % per_matrix) * unit, LANES), unit)
+        factor = basis_ref[part_at(slot, rank), lanes]
+        right = right_ref[part_at(matrix - first_matrix, rank), :]
+        scratch[u * unit : (u + 1) * unit] = product(factor, right)
+
+
+def product(factor, right):
+    high, low = two_terms(factor.T)
+    return dot(jnp.concatenate([high, low, high], axis=1), stacked(right))
+
+
+def late_kernel(tps, early, unit, per_tp, rank, ids_ref, basis_ref, *refs):
+    late = tps - early
+    lanes, approx = refs[-2:]
+    query_ref, weight_refs = refs[-3 - late], refs[-2 - late : -2]
+    base_refs = refs[-3 - 2 * late : -3 - late]
+    part_refs = refs[: -3 - 2 * late]
     halves = tps // 2
-    per_half = (len(refs) - 2) // halves
+    per_half = len(part_refs) // halves
     rows = query_ref.shape[0] // halves
+    tp = ids_ref[1]
     for half in range(halves):
-        join_parts(scratch, ids_ref[0], refs[half * per_half : (half + 1) * per_half])
-        value = read_lanes(scratch, rows)
+        join_parts(lanes, ids_ref[0], part_refs[half * per_half : (half + 1) * per_half])
+        value = read_lanes(lanes, rows)
         for which in range(2):
-            owner = ids_ref[1] ^ (2 * half + which)
+            owner = tp ^ (2 * half + which)
             query_ref[part_at(owner, rows // 2), :] = value[which * (rows // 2) : (which + 1) * (rows // 2)]
-
-
-def weight_kernel(ids_ref, factors_ref, right_ref, base_ref, weights_ref):
-    approx = dot(factors_ref[...], stacked(right_ref[...]))
-    weights = (base_ref[...].reshape(approx.shape) - LEARNING_RATE * approx).astype(BF16)
-    weights_ref[...] = weights.reshape(weights_ref.shape)
+    units = approx.shape[0] // unit
+    rows_of_update(basis_ref, query_ref, approx, ids_ref[0] * units, unit, per_tp, rank, tp, 0)
+    for which in range(late):
+        base = base_refs[which][...]
+        own = approx[part_at(tp ^ (early + which), base.shape[0]), :]
+        weight_refs[which][...] = (base - LEARNING_RATE * own).astype(BF16)
 
 
 def place_kernel(ids_ref, part_ref, _, weights_ref):
     weights_ref[...] = part_ref[...].reshape(weights_ref.shape)
 
 
-def error_kernel(per_half, ids_ref, factors_ref, right_ref, *refs):
-    new_error_ref = refs[-1]
-    approx = dot(factors_ref[...], stacked(right_ref[...]))
-    for half in range(len(refs) // 2):
-        high_ref, low_ref = refs[2 * half : 2 * half + 2]
-
-        @pl.when(pl.program_id(0) // per_half == half)
+def update_kernel(early, per_tp, rank, ids_ref, basis_ref, right_ref, *refs):
+    new_error_ref, weights_ref, approx = refs[-3:]
+    base_refs, term_refs = refs[:early], refs[early:-3]
+    slot, matrix = pl.program_id(0), pl.program_id(1)
+    at = part_at(matrix, rank)
+    own = product(basis_ref[at, :], right_ref[at, :])
+    width = own.shape[0]
+    approx[part_at(matrix, width), :] = own
+    for half in range(len(term_refs) // 2):
+
+        @pl.when(slot // 2 == half)
         def _():
-            new_error_ref[0, 0] = high_ref[0].astype(F32) + low_ref[0].astype(F32) - approx
-
-
-def flat_kernel(ids_ref, factors_ref, right_ref, momentum_ref, master_ref, new_momentum_ref, new_master_ref):
-    approx = dot(factors_ref[...], stacked(right_ref[...].reshape(right_ref.shape[-2:])))
-    new_momentum = MOMENTUM_DECAY * momentum_ref[...] + approx
+            high, low = (ref[0].astype(F32) for ref in term_refs[2 * half : 2 * half + 2])
+            new_error_ref[0, 0] = high + low - own
+
+    @pl.when(matrix == per_tp - 1)
+    def _():
+        replicas, tps, own_rows, _ = weights_ref.shape
+        for replica in range(replicas):
+            for offset, base_ref in enumerate(base_refs):
+                owner = ids_ref[1] ^ offset
+                rows = approx[part_at(replica * tps + owner, own_rows), :]
+                weights_ref[replica, owner] = (base_ref[replica] - LEARNING_RATE * rows).astype(BF16)
+
+
+def flat_kernel(unit, per_tp, rank, matrices, ids_ref, basis_ref, near_ref, momentum_ref, master_ref, new_momentum_ref, new_master_ref, approx):
+    units = approx.shape[0] // unit
+    spans = near_ref.shape[1] // rank
+    first_unit = ids_ref[0] * units
+    first = jnp.minimum(first_unit // (basis_ref.shape[1] // unit), matrices - spans)
+    rows_of_update(basis_ref, near_ref.at[0], approx, first_unit, unit, per_tp, rank, ids_ref[1], first)
+    own = approx[part_at(ids_ref[1], momentum_ref.shape[0]), :]
+    new_momentum = MOMENTUM_DECAY * momentum_ref[...] + own
     new_momentum_ref[...] = new_momentum
     new_master_ref[...] = master_ref[...] - LEARNING_RATE * new_momentum
 
 
 def shape(*dims, dtype=F32):
     return jax.ShapeDtypeStruct(dims, dtype)
+
+
+def grant(mib):
+    return pltpu.CompilerParams(vmem_limit_bytes=mib * 2**20)
 
 
 def whole_call(kernel, name, out_shape, operands, ids=None, scratch=()):
@@ -237,13 +278,13 @@
         out_specs=[out_spec] * len(out_shape) if many else out_spec,
         out_shape=out_shape,
         scratch_shapes=list(scratch),
-        compiler_params=PARAMS,
+        compiler_params=grant(12),
         name=name,
         cost_estimate=pl.CostEstimate(flops=moved, bytes_accessed=2 * moved, transcendentals=0),
     )(*operands)
 
 
-def grid_call(kernel, name, ids, grid, in_specs, out_specs, out_shape, operands, scratch=(), aliases=None, flops=0, moved=0):
+def grid_call(kernel, name, ids, grid, in_specs, out_specs, out_shape, operands, scratch=(), aliases=None, flops=0, moved=0, mib=20):
     return pl.pallas_call(
         kernel,
         grid_spec=pltpu.PrefetchScalarGridSpec(
@@ -255,7 +296,7 @@
         ),
         out_shape=out_shape,
         input_output_aliases=aliases or {},
-        compiler_params=PARAMS,
+        compiler_params=grant(mib),
         name=name,
         cost_estimate=pl.CostEstimate(flops=flops, bytes_accessed=moved, transcendentals=0),
     )(ids, *operands)
@@ -325,38 +366,39 @@
         terms[half] = (high, low)
         lefts[2 * half : 2 * half + 2] = out
 
-    gathered = []
+    def base_at(offset, new_values, old_values):
+        column = (tp ^ offset) * cols
+        piece = lax.dynamic_slice_in_dim(new_values, column, cols, 1)
+        piece = piece - (LEARNING_RATE * MOMENTUM_DECAY) * lax.dynamic_slice_in_dim(old_values, column, cols, 1)
+        return piece if offset == 0 else swap(piece, "tp", tps, offset)
+
+    base = [base_at(0, master, momentum)]
+    gathered = [lax.all_gather(base[0], "rep")]
     for power_pass in range(ROUNDS):
         met = [lefts[0]] + [swap(lefts[offset], "tp", tps, offset) for offset in range(1, tps)]
         parts = whole_call(
-            functools.partial(split_kernel, tps),
-            "left_split",
-            [shape(left_part, LANES)] * replicas,
-            met,
-            ids,
-            [pltpu.VMEM((left_part * replicas, LANES), F32)],
+            functools.partial(split_kernel, tps), "left_split", shape(left_part * replicas, LANES), met
         )
         if power_pass == 0:
-            base = []
-            tied = lax.optimization_barrier((master, momentum, *parts))
-            parts = list(tied[2:])
-            for offset in range(tps):
-                column = (tp ^ offset) * cols
-                piece = lax.dynamic_slice_in_dim(tied[0], column, cols, 1)
-                piece = piece - (LEARNING_RATE * MOMENTUM_DECAY) * lax.dynamic_slice_in_dim(tied[1], column, cols, 1)
-                base.append(piece if offset == 0 else swap(piece, "tp", tps, offset))
-            gathered = [lax.all_gather(base[offset], "rep") for offset in range(EARLY)]
-        met = scattered(parts, replicas)
-        part = whole_call(functools.partial(sum_kernel, 1.0), "left_sum", shape(left_part, LANES), met)
+            parts, new_values, old_values = lax.optimization_barrier((parts, master, momentum))
+            base += [base_at(offset, new_values, old_values) for offset in range(1, tps)]
+            gathered += [lax.all_gather(base[offset], "rep") for offset in range(1, EARLY)]
+        parts = parts.reshape(replicas, left_part, LANES)
+        parts = lax.all_to_all(parts, "rep", split_axis=0, concat_axis=0, tiled=True)
+        parts = whole_call(total_kernel, "left_sum", shape(*parts.shape), [parts])
+        parts = lax.all_to_all(parts, "rep", split_axis=0, concat_axis=0, tiled=True)
         basis = whole_call(
-            functools.partial(basis_kernel, rank),
-            "basis",
-            shape(tp_rows, width),
-            spread(part, "rep", replicas),
-            ids,
-            [pltpu.VMEM((left_part * replicas, LANES), F32)],
+            functools.partial(basis_kernel, rank), "basis", shape(tp_rows, width), [parts.reshape(-1, LANES)]
         )
-        bases = spread(basis, "tp", tps)
+        bases = [basis]
+        for bit in range(tps.bit_length() - 2, 0, -1):
+            bases += [swap(one, "tp", tps, 1 << bit) for one in bases]
+        even = {}
+        for at, one in enumerate(bases):
+            even[sum(1 << bit for place, bit in enumerate(range(tps.bit_length() - 2, 0, -1)) if at >> place & 1)] = one
+        bases = []
+        for offset in range(0, tps, 2):
+            bases += [even[offset], swap(even[offset], "tp", tps, 1)]
         rights = []
         for half in range(halves):
             parts = grid_call(
@@ -391,139 +433,93 @@
                     moved=4 * elements,
                 )
 
-    factors = grid_call(
-        factor_kernel,
-        "factors",
+    all_bases = jnp.concatenate(bases, axis=0)
+    late = tps - EARLY
+    rep_rows = tps * own_rows
+    unit = math.gcd(rep_rows, width)
+    right, *blocks = whole_call(
+        functools.partial(late_kernel, tps, EARLY, unit, per_tp, rank),
+        "late_rows",
+        [shape(matrices * rank, cols)] + [shape(own_rows, cols, dtype=BF16)] * late,
+        [all_bases, *[part for parts in rights for part in parts], *base[EARLY:]],
         ids,
-        (matrices,),
-        [pl.BlockSpec((1, rank, width), lambda k, at: ((at[1] ^ (k // per_tp)) * per_tp + k % per_tp, 0, 0))],
-        pl.BlockSpec((width, 3 * rank), lambda k, at: (k, 0)),
-        shape(matrices * width, 3 * rank, dtype=BF16),
-        (jnp.concatenate(bases, axis=0).reshape(matrices, rank, width),),
+        [pltpu.VMEM((right_part * replicas, LANES), F32), pltpu.VMEM((rep_rows, cols), F32)],
     )
-    right = whole_call(
-        functools.partial(query_kernel, tps),
-        "new_query",
-        shape(matrices * rank, cols),
-        [part for parts in rights for part in parts],
+    late_rows = [lax.all_gather(block, "rep") for block in blocks]
+
+    new_error, weights = grid_call(
+        functools.partial(update_kernel, EARLY, per_tp, rank),
+        "update",
         ids,
-        [pltpu.VMEM((right_part * replicas, LANES), F32)],
-    )
-
-    chunk = math.gcd(own_rows, width)
-    chunks = own_rows // chunk
-
-    def chunk_at(replica, owner, b):
-        return (replica * tps + owner) * chunks + b
-
-    late = tps - EARLY
-    block = grid_call(
-        weight_kernel,
-        "late_weights",
-        ids,
-        (late, chunks),
+        (tps, per_tp),
         [
-            pl.BlockSpec((chunk, 3 * rank), lambda s, b, at: (chunk_at(at[0], at[1] ^ (EARLY + s), b), 0)),
-            pl.BlockSpec((rank, cols), lambda s, b, at: (chunk_at(at[0], at[1] ^ (EARLY + s), b) * chunk // width, 0)),
-            pl.BlockSpec((1, chunk, cols), lambda s, b, at: (s, b, 0)),
-        ],
-        pl.BlockSpec((1, chunk, cols), lambda s, b, at: (s, b, 0)),
-        shape(late, own_rows, cols, dtype=BF16),
-        (factors, right, jnp.stack(base[EARLY:])),
-    )
-    late_rows = lax.all_gather(block, "rep")
-
-    weights_shape = shape(replicas, tps, own_rows, cols, dtype=BF16)
-    weights = None
-    for offset in range(EARLY):
-        kernel = weight_kernel if weights is None else lambda ids_ref, a, b, c, _, out: weight_kernel(ids_ref, a, b, c, out)
-        weights = grid_call(
-            kernel,
-            "early_weights",
-            ids,
-            (replicas, chunks),
-            [
-                pl.BlockSpec((chunk, 3 * rank), lambda q, b, at, offset=offset: (chunk_at(q, at[1] ^ offset, b), 0)),
-                pl.BlockSpec((rank, cols), lambda q, b, at, offset=offset: (chunk_at(q, at[1] ^ offset, b) * chunk // width, 0)),
-                pl.BlockSpec((1, chunk, cols), lambda q, b, at: (q, b, 0)),
-            ]
-            + ([] if weights is None else [pl.BlockSpec(memory_space=pl.ANY)]),
-            pl.BlockSpec((1, 1, chunk, cols), lambda q, b, at, offset=offset: (q, at[1] ^ offset, b, 0)),
-            weights_shape,
-            (factors, right, gathered[offset]) + (() if weights is None else (weights,)),
-            aliases=None if weights is None else {4: 0},
-            flops=2 * 3 * rank * replicas * own_rows * cols,
-            moved=6 * replicas * own_rows * cols,
-        )
-    weights = grid_call(
-        place_kernel,
-        "place_late",
-        ids,
-        (replicas, late),
-        [
-            pl.BlockSpec((1, 1, own_rows, cols), lambda q, s, at: (q, s, 0, 0)),
-            pl.BlockSpec(memory_space=pl.ANY),
-        ],
-        pl.BlockSpec((1, 1, own_rows, cols), lambda q, s, at: (q, at[1] ^ (EARLY + s), 0, 0)),
-        weights_shape,
-        (late_rows, weights),
-        aliases={2: 0},
-    )
-    weights = weights.reshape(matrices, width, cols)
-
-    def picked(k, at):
-        return matrix_of(k // per_half, k % per_half, at)
-
-    new_error = grid_call(
-        functools.partial(error_kernel, per_half),
-        "new_error",
-        ids,
-        (matrices,),
-        [
-            pl.BlockSpec((width, 3 * rank), lambda k, at: (picked(k, at), 0)),
-            pl.BlockSpec((rank, cols), lambda k, at: (picked(k, at), 0)),
+            pl.BlockSpec((tp_rows, width), lambda s, j, at: (s, 0)),
+            pl.BlockSpec((tp_rows, cols), lambda s, j, at: (at[1] ^ s, 0)),
         ]
+        + [pl.BlockSpec((replicas // tps, own_rows, cols), lambda s, j, at: (at[1] ^ s, 0, 0))] * EARLY
         + [
-            pl.BlockSpec((1, width, cols), lambda k, at, half=half: (jnp.clip(k - half * per_half, 0, per_half - 1), 0, 0))
+            pl.BlockSpec(
+                (1, width, cols),
+                lambda s, j, at, half=half: (jnp.clip(s * per_tp + j - half * per_half, 0, per_half - 1), 0, 0),
+            )
             for half in range(halves)
             for _ in range(2)
         ],
-        pl.BlockSpec((1, 1, width, cols), lambda k, at: (0, picked(k, at), 0, 0)),
-        shape(*error.shape),
-        (factors, right, *[term for pair in terms for term in pair]),
+        [
+            pl.BlockSpec((1, 1, width, cols), lambda s, j, at: (0, (at[1] ^ s) * per_tp + j, 0, 0)),
+            pl.BlockSpec((replicas // tps, tps, own_rows, cols), lambda s, j, at: (at[1] ^ s, 0, 0, 0)),
+        ],
+        [shape(*error.shape), shape(replicas, tps, own_rows, cols, dtype=BF16)],
+        (all_bases, right, *gathered, *[term for pair in terms for term in pair]),
+        [pltpu.VMEM((per_tp * width, cols), F32)],
         flops=2 * 3 * rank * error.size,
-        moved=8 * error.size,
+        moved=12 * error.size,
+        mib=36,
     )
 
-    rep_rows = tps * own_rows
-    spans = -(-(width - math.gcd(rep_rows, width) + rep_rows) // width)
-
-    def first_near(at):
-        return jnp.minimum(at[0] * rep_rows // width, matrices - spans)
-
-    near = lax.dynamic_slice_in_dim(right.reshape(matrices, rank, cols), first_near(ids), spans, 0)
+    spans = -(-(width - unit + rep_rows) // width)
+    first = jnp.minimum(rep * rep_rows // width, matrices - spans)
+    near = lax.dynamic_slice_in_dim(right, first * rank, spans * rank, 0)
     near = jnp.stack(spread(near, "tp", tps))
-    wide = pl.BlockSpec((chunk, cols), lambda b, s, at: (b, at[1] ^ s))
+    wide = pl.BlockSpec((own_rows, cols), lambda s, at: (0, at[1] ^ s))
     new_momentum, new_master = grid_call(
-        flat_kernel,
+        functools.partial(flat_kernel, unit, per_tp, rank, matrices),
         "flat_rows",
         ids,
-        (chunks, tps),
+        (tps,),
         [
-            pl.BlockSpec((chunk, 3 * rank), lambda b, s, at: (chunk_at(at[0], at[1], b), 0)),
-            pl.BlockSpec(
-                (1, 1, rank, cols),
-                lambda b, s, at: (s, chunk_at(at[0], at[1], b) * chunk // width - first_near(at), 0, 0),
-            ),
+            whole_spec(matrices * rank, width),
+            pl.BlockSpec((1, spans * rank, cols), lambda s, at: (s, 0, 0)),
             wide,
             wide,
         ],
         [wide, wide],
         [shape(*momentum.shape), shape(*master.shape)],
-        (factors, near, momentum, master),
-        flops=2 * 3 * rank * momentum.size,
+        (all_bases, near, momentum, master),
+        [pltpu.VMEM((rep_rows, cols), F32)],
+        flops=2 * 3 * rank * momentum.size * tps,
         moved=16 * momentum.size,
     )
+
+    for which in range(late):
+        groups = 2
+        weights = grid_call(
+            place_kernel,
+            "place_late",
+            ids,
+            (groups,),
+            [
+                pl.BlockSpec((replicas // groups, own_rows, cols), lambda q, at: (q, 0, 0)),
+                pl.BlockSpec(memory_space=pl.ANY),
+            ],
+            pl.BlockSpec(
+                (replicas // groups, 1, own_rows, cols), lambda q, at, which=which: (q, at[1] ^ (EARLY + which), 0, 0)
+            ),
+            shape(*weights.shape, dtype=BF16),
+            (late_rows[which], weights),
+            aliases={2: 0},
+        )
+    weights = weights.reshape(matrices, width, cols)
     return (new_error, right.reshape(matrices, rank, cols), new_momentum, new_master, weights)
 
 
@@ -568,7 +564,9 @@
 
 def divides(mesh, matrices, rank, width, cols):
     replicas, tps = mesh.shape["rep"], mesh.shape["tp"]
-    if replicas & (replicas - 1) or tps & (tps - 1) or tps < 4 or matrices % tps or cols % (tps * LANES) or width % LANES:
+    if replicas & (replicas - 1) or tps & (tps - 1) or tps < 4 or replicas % tps or matrices % tps or cols % (tps * LANES) or width % LANES:
+        return False
+    if math.gcd(matrices * width // replicas, width) % LANES:
         return False
     tp_rows = matrices // tps * rank
     tiles = 8 * LANES * replicas

time: 445 us -> 429 us (0.964)
  Pallas kernels: 183 us -> 77.4 us
  blocking collectives: 0 us -> 60.4 us
  waiting for transfers between devices: 70.7 us -> 121 us
  starting transfers between devices: 155 us -> 106 us
  local copies, waits for them, and re-layouts: 11.6 us -> 43.7 us
    pallas_call x15 -> x12, Pallas kernels: 160 us -> 69.1 us  [grid_call(): pl.pallas_call(kernel, grid_spec=pltpu.PrefetchScalarGridSpec(num_scalar_...]
    all_to_all x0 -> x3, blocking collectives: none -> 60.4 us  [local(): lax.all_to_all(parts, 'rep', split_axis=0, concat_axis=0, tiled=True)]
    ppermute x102 -> x74, starting transfers between devices: 155 us -> 103 us  [swap(): lax.ppermute(x, axis, [(index, index ^ offset) for index in range(size)])]
    all_gather x3 -> x4, waiting for transfers between devices: 11.7 us -> 52.6 us  [the longest x2 52.6 us: local(): late_rows = [lax.all_gather(block, 'rep') for block in blocks]]
    unnamed x212 -> x62, local copies, waits for them, and re-layouts: 9.79 us -> 41.9 us
    pallas_call x11, Pallas kernels: 22.9 us -> 8.32 us  [whole_call(): pl.pallas_call(kernel, in_specs=specs, out_specs=[out_spec] * len(out_sha...]
    all_to_all x0 -> x1, waiting for transfers between devices: none -> 8.69 us  [local(): lax.all_to_all(parts, 'rep', split_axis=0, concat_axis=0, tiled=True)]
    ppermute x102 -> x74, waiting for transfers between devices: 59 us -> 58.7 us  [swap(): lax.ppermute(x, axis, [(index, index ^ offset) for index in range(size)])]
  transfers between devices with their start and end apart: 105 -> 79, of which waited for: 25 -> 23; matrix products, arithmetic and copies ran while one was open for 1% -> 1% of each run, Pallas kernels for 36% -> 18%
where the time goes in v2:
time: 429 us; the launch traced here: 428 us
  waiting for transfers between devices  121 us (28%)
  starting transfers between devices  106 us (25%)
  Pallas kernels  77.4 us (18%)
  blocking collectives  60.4 us (14%)
  local copies, waits for them, and re-layouts  43.7 us (10%)
  between operations  14.2 us (3%)
  other arithmetic  5.31 us (1%)
    ppermute x74, starting transfers between devices, swap(): lax.ppermute(x, axis, [(index, index ^ offset) for index in range(size)])  103 us
    pallas_call x12, Pallas kernels, grid_call(): pl.pallas_call(kernel, grid_spec=pltpu.PrefetchScalarGridSpec(num_scalar_...  69.1 us
    all_to_all x3, blocking collectives, local(): lax.all_to_all(parts, 'rep', split_axis=0, concat_axis=0, tiled=True)  60.4 us
    ppermute x74, waiting for transfers between devices, swap(): lax.ppermute(x, axis, [(index, index ^ offset) for index in range(size)])  58.7 us
    all_gather x2, waiting for transfers between devices, local(): late_rows = [lax.all_gather(block, 'rep') for block in blocks]  52.6 us
    unnamed x62, local copies, waits for them, and re-layouts  41.9 us
    all_to_all x1, waiting for transfers between devices, local(): lax.all_to_all(parts, 'rep', split_axis=0, concat_axis=0, tiled=True)  8.69 us
  transfers between devices with their start and end apart: 79, of which 23 were waited for; matrix products, arithmetic and copies ran while one was open for 1% of the time, Pallas kernels for 18%

profile of v2, /device:TPU:0, one launch (start us, length us, event | category | flops | bytes accessed | tf_op | source)
XLA Modules:
  0.0 427.9 jit_solution(13226946592902059035)
XLA Ops:
  9.6 3.7 copy-done.11
  13.3 8.4 %first_left.3 = (bf16[6,768,512]{2,1,0:T(8,128)(2,1)S(1)}, bf16[6,768,512]{2,1,0:T(8,128)(2,1)S(1)}, f32[96,768]{1,0:T(8,128)}, f32[96,768]{1,0:T(8,128)}) custom-call(s32[2]{0:T(128)S(1)} %pad_add_fusion.ids_ref, bf16[1,12,768,512]{3,2,1,0:T(8,128)(2,1)S(1)} %copy-done.11, f32[1,12,768,512]{3,2,1,0:T(8,128)} %error_ref.3, f32[12,32,512]{2,1,0:T(8,128)S(1)} %copy-done.16), custom_call_target="tpu_custom_call" | custom-call | flops 452984832 | bytes 23592960 | tf_op jit(solution)/shard_map/first_left/pallas_call | solution.py:288
  26.1 3.1 collective-permute-start.1
  29.2 8.5 %first_left.2 = (bf16[6,768,512]{2,1,0:T(8,128)(2,1)S(1)}, bf16[6,768,512]{2,1,0:T(8,128)(2,1)S(1)}, f32[96,768]{1,0:T(8,128)S(1)}, f32[96,768]{1,0:T(8,128)}) custom-call(s32[2]{0:T(128)S(1)} %pad_add_fusion.ids_ref, bf16[1,12,768,512]{3,2,1,0:T(8,128)(2,1)S(1)} %copy-done.11, f32[1,12,768,512]{3,2,1,0:T(8,128)} %error_ref.3, f32[12,32,512]{2,1,0:T(8,128)S(1)} %copy-done.16), custom_call_target="tpu_custom_call" | custom-call | flops 452984832 | bytes 23592960 | tf_op jit(solution)/shard_map/first_left/pallas_call | solution.py:288
  46.5 2.9 multiply_subtract_fusion
  52.3 25.0 %all_to_all.20.parts_ref = f32[8,72,128]{2,1,0:T(8,128)S(1)} all-to-all(f32[8,72,128]{2,1,0:T(8,128)S(1)} %bitcast.28), channel_id=1, replica_groups=mesh['rep'=8,'tp'=4] {'rep'}, dimensions={0} | all-to-all | bytes 589824 | tf_op jit(solution)/shard_map/all_to_all | solution.py:387
  77.3 20.9 %all_to_all.21 = f32[8,72,128]{2,1,0:T(8,128)S(1)} all-to-all(f32[8,72,128]{2,1,0:T(8,128)S(1)} %left_sum.2), channel_id=1, replica_groups=mesh['rep'=8,'tp'=4] {'rep'}, dimensions={0} | all-to-all | bytes 589824 | tf_op jit(solution)/shard_map/all_to_all | solution.py:389
  101.7 6.7 %collective-permute-done.19.first_ref = f32[96,768]{1,0:T(8,128)S(1)} collective-permute-done((f32[96,768]{1,0:T(8,128)S(1)}, f32[96,768]{1,0:T(8,128)S(1)}, u32[]{:S(2)}, u32[]{:S(2)}) %collective-permute-start.19) | collective-permute-done | bytes 294944 | tf_op jit(solution)/shard_map/ppermute | solution.py:306
  108.4 2.5 copy-done.5
  110.9 2.9 copy-done.9
  113.8 2.9 right.4
  120.7 3.3 collective-permute-start.8
  124.0 2.9 right.5
  127.8 3.1 collective-permute-start.10
  132.2 4.6 %collective-permute-done.8.refs_5_ = f32[96,128]{1,0:T(8,128)S(1)} collective-permute-done((f32[96,128]{1,0:T(8,128)S(1)}, f32[96,128]{1,0:T(8,128)S(1)}, u32[]{:S(2)}, u32[]{:S(2)}) %collective-permute-start.8) | collective-permute-done | bytes 49184 | tf_op jit(solution)/shard_map/ppermute | solution.py:306
  139.1 5.1 %collective-permute-start.25 = (f32[96,128]{1,0:T(8,128)S(1)}, f32[96,128]{1,0:T(8,128)S(1)}, u32[]{:S(2)}, u32[]{:S(2)}) collective-permute-start(f32[96,128]{1,0:T(8,128)S(1)} %get-tuple-element.83), channel_id=1, source_target_pairs={{0,20},{4,16},{8,28},{12,24},{16,4},{20,0},{24,12},{28,8},{1,21},{... | collective-permute-start | bytes 147464 | tf_op jit(solution)/shard_map/ppermute | solution.py:306
  144.2 3.9 collective-permute-start.26
  149.0 3.9 collective-permute-start.17
  153.3 3.4 collective-permute-start.14
  161.1 5.9 %collective-permute-done.15.refs_5_ = f32[96,128]{1,0:T(8,128)S(1)} collective-permute-done((f32[96,128]{1,0:T(8,128)S(1)}, f32[96,128]{1,0:T(8,128)S(1)}, u32[]{:S(2)}, u32[]{:S(2)}) %collective-permute-start.15) | collective-permute-done | bytes 49184 | tf_op jit(solution)/shard_map/ppermute | solution.py:306
  167.8 2.8 collective-permute-done.14.refs_4_
  171.5 3.2 collective-permute-start.31
  179.2 4.2 left.2
  183.4 2.5 collective-permute-done.32.refs_5_
  188.1 4.2 left.3
  193.9 8.4 %collective-permute-done.35.refs_2_ = f32[96,768]{1,0:T(8,128)S(1)} collective-permute-done((f32[96,768]{1,0:T(8,128)S(1)}, f32[96,768]{1,0:T(8,128)S(1)}, u32[]{:S(2)}, u32[]{:S(2)}) %collective-permute-start.35) | collective-permute-done | bytes 294944 | tf_op jit(solution)/shard_map/ppermute | solution.py:306
  202.3 2.4 collective-permute-done.36.refs_3_
  204.8 14.5 %all_to_all.22.parts_ref = f32[8,72,128]{2,1,0:T(8,128)S(1)} all-to-all(f32[8,72,128]{2,1,0:T(8,128)S(1)} %bitcast.29), channel_id=1, replica_groups=mesh['rep'=8,'tp'=4] {'rep'}, dimensions={0} | all-to-all | bytes 589824 | tf_op jit(solution)/shard_map/all_to_all | solution.py:387
  220.1 3.4 all-to-all-start.3
  223.8 8.7 %all-to-all-done.3 = f32[8,72,128]{2,1,0:T(8,128)S(1)} async-done(((f32[8,72,128]{2,1,0:T(8,128)}), f32[8,72,128]{2,1,0:T(8,128)S(1)}, u32[]{:S(2)}, u32[]{:S(2)}) %all-to-all-start.3) | async-done | bytes 294944 | tf_op jit(solution)/shard_map/all_to_all | solution.py:389
  236.6 9.1 %collective-permute-done.38.first_ref = f32[96,768]{1,0:T(8,128)S(1)} collective-permute-done((f32[96,768]{1,0:T(8,128)S(1)}, f32[96,768]{1,0:T(8,128)S(1)}, u32[]{:S(2)}, u32[]{:S(2)}) %collective-permute-start.38) | collective-permute-done | bytes 294944 | tf_op jit(solution)/shard_map/ppermute | solution.py:306
  246.1 2.3 copy-done.6
  250.8 2.8 right.6
  257.8 2.5 collective-permute-start.43
  261.8 3.3 collective-permute-start.45
  267.4 2.9 right.7
  272.5 3.2 collective-permute-start.56
  277.6 2.9 collective-permute-start.58
  282.3 2.9 collective-permute-start.60
  289.3 3.7 collective-permute-start.50
  300.4 3.8 collective-permute-start.64
  310.4 2.4 late_rows.1
  318.9 2.5 collective-permute-done.72
  324.8 6.2 %flat_rows.1 = (f32[288,2048]{1,0:T(8,128)}, f32[288,2048]{1,0:T(8,128)}) custom-call(s32[2]{0:T(128)S(1)} %pad_add_fusion.ids_ref, f32[384,768]{1,0:T(8,128)S(1)} %pad_maximum_fusion.basis_ref, f32[4,64,512]{2,1,0:T(8,128)S(1)} %pad_maximum_fusion.1.near_ref, f32[288,2048]{1,0:T(8,128)S(1)} %copy-done.12, f32[288,2048]{1,0:T(8,128)S(1)} %copy-done.13), custom_call_target="tpu_custom_call" | custom-call | flops 452984832 | bytes 9437184 | tf_op jit(solution)/shard_map/flat_rows/pallas_call | solution.py:288
  331.0 2.4 copy-done.7
  339.2 22.1 %update.1 = (f32[1,12,768,512]{3,2,1,0:T(8,128)}, bf16[8,4,288,512]{3,2,1,0:T(8,128)(2,1)}) custom-call(s32[2]{0:T(128)S(1)} %pad_add_fusion.ids_ref, f32[384,768]{1,0:T(8,128)S(1)} %pad_maximum_fusion.basis_ref, f32[384,512]{1,0:T(8,128)S(1)} %copy-done.19, f32[8,288,512]{2,1,0:T(8,128)S(1)} %bitcast.21, f32[8,288,512]{2,1,0:T(8,128)S(1)} %bitcast.22, ...), custom_call_target="tpu_custom_call" | custom-call | flops 905969664 | bytes 56623104 | tf_op jit(solution)/shard_map/update/pallas_call | solution.py:288
  361.3 3.6 all-gather.15.cloned.1.call-done
  368.6 49.0 %all-gather.13.cloned.1.call-done = bf16[2304,512]{1,0:T(8,128)(2,1)} async-done(((bf16[288,512]{1,0:T(8,128)(2,1)}), bf16[2304,512]{1,0:T(8,128)(2,1)}) %all-gather.13.cloned.1.call-update) | async-done | bytes 2359312 | tf_op jit(solution)/shard_map/all_gather | solution.py:448
  (211 shorter events, 107.9 us)
Async XLA Ops:
  7.2 323.8 %all-gather.9.cloned.1.call-start = ((), (), s32[]{:S(2)}) async-start(), calls=%async_computation.4 | async-start | bytes 5308416 | tf_op jit(solution)/shard_map/all_gather | solution.py:376
  9.5 321.5 %all-gather.11.cloned.1.call-start = ((), (), s32[]{:S(2)}) async-start(), calls=%async_computation.5 | async-start | bytes 5308416 | tf_op jit(solution)/shard_map/all_gather | solution.py:385
  26.1 16.7 %collective-permute-start.1 = (f32[96,768]{1,0:T(8,128)}, f32[96,768]{1,0:T(8,128)S(1)}, u32[]{:S(2)}, u32[]{:S(2)}) collective-permute-start(f32[96,768]{1,0:T(8,128)} %get-tuple-element.63), channel_id=1, source_target_pairs={{0,2},{1,3},{2,0},{3,1},{4,6},{5,7},{6,4},{7,5},{8,10},{9,11},{10,... | collective-permute-start | bytes 884744 | tf_op jit(solution)/shard_map/ppermute | solution.py:306
  29.2 13.7 %collective-permute-start.2 = (f32[96,768]{1,0:T(8,128)}, f32[96,768]{1,0:T(8,128)}, u32[]{:S(2)}, u32[]{:S(2)}) collective-permute-start(f32[96,768]{1,0:T(8,128)} %get-tuple-element.64), channel_id=1, source_target_pairs={{0,3},{1,2},{2,1},{3,0},{4,7},{5,6},{6,5},{7,4},{8,11},{9,10},{10,... | collective-permute-start | bytes 884744 | tf_op jit(solution)/shard_map/ppermute | solution.py:306
  108.4 12.3 %collective-permute-start.20 = (f32[96,768]{1,0:T(8,128)S(1)}, f32[96,768]{1,0:T(8,128)S(1)}, u32[]{:S(2)}, u32[]{:S(2)}) collective-permute-start(f32[96,768]{1,0:T(8,128)S(1)} %collective-permute-done.19.first_ref), channel_id=1, source_target_pairs={{0,1},{1,0},{2,3},{3,2},{4,5},{5,4},{6,7},{7,6},{8,9},{9,8},{10,11... | collective-permute-start | bytes 884744 | tf_op jit(solution)/shard_map/ppermute | solution.py:306
  116.7 10.2 %collective-permute-start.4 = (f32[96,128]{1,0:T(8,128)S(1)}, f32[96,128]{1,0:T(8,128)S(1)}, u32[]{:S(2)}, u32[]{:S(2)}) collective-permute-start(f32[96,128]{1,0:T(8,128)S(1)} %get-tuple-element.67), channel_id=1, source_target_pairs={{0,4},{4,0},{8,12},{12,8},{16,20},{20,16},{24,28},{28,24},{1,5},{5... | collective-permute-start | bytes 147464 | tf_op jit(solution)/shard_map/ppermute | solution.py:306
  118.1 9.7 %collective-permute-start.5 = (f32[96,128]{1,0:T(8,128)S(1)}, f32[96,128]{1,0:T(8,128)S(1)}, u32[]{:S(2)}, u32[]{:S(2)}) collective-permute-start(f32[96,128]{1,0:T(8,128)S(1)} %get-tuple-element.68), channel_id=1, source_target_pairs={{0,8},{4,12},{8,0},{12,4},{16,24},{20,28},{24,16},{28,20},{1,9},{5... | collective-permute-start | bytes 147464 | tf_op jit(solution)/shard_map/ppermute | solution.py:306
  118.1 12.7 %collective-permute-start.6 = (f32[96,128]{1,0:T(8,128)S(1)}, f32[96,128]{1,0:T(8,128)S(1)}, u32[]{:S(2)}, u32[]{:S(2)}) collective-permute-start(f32[96,128]{1,0:T(8,128)S(1)} %get-tuple-element.69), channel_id=1, source_target_pairs={{0,12},{4,8},{8,4},{12,0},{16,28},{20,24},{24,20},{28,16},{1,13},{... | collective-permute-start | bytes 147464 | tf_op jit(solution)/shard_map/ppermute | solution.py:306
  120.2 12.0 %collective-permute-start.7 = (f32[96,128]{1,0:T(8,128)S(1)}, f32[96,128]{1,0:T(8,128)S(1)}, u32[]{:S(2)}, u32[]{:S(2)}) collective-permute-start(f32[96,128]{1,0:T(8,128)S(1)} %get-tuple-element.70), channel_id=1, source_target_pairs={{0,16},{4,20},{8,24},{12,28},{16,0},{20,4},{24,8},{28,12},{1,17},{... | collective-permute-start | bytes 147464 | tf_op jit(solution)/shard_map/ppermute | solution.py:306
  120.7 16.2 %collective-permute-start.8 = (f32[96,128]{1,0:T(8,128)S(1)}, f32[96,128]{1,0:T(8,128)S(1)}, u32[]{:S(2)}, u32[]{:S(2)}) collective-permute-start(f32[96,128]{1,0:T(8,128)S(1)} %get-tuple-element.71), channel_id=1, source_target_pairs={{0,20},{4,16},{8,28},{12,24},{16,4},{20,0},{24,12},{28,8},{1,21},{... | collective-permute-start | bytes 147464 | tf_op jit(solution)/shard_map/ppermute | solution.py:306
  126.9 10.0 %collective-permute-start.9 = (f32[96,128]{1,0:T(8,128)S(1)}, f32[96,128]{1,0:T(8,128)S(1)}, u32[]{:S(2)}, u32[]{:S(2)}) collective-permute-start(f32[96,128]{1,0:T(8,128)S(1)} %get-tuple-element.72), channel_id=1, source_target_pairs={{0,24},{4,28},{8,16},{12,20},{16,8},{20,12},{24,0},{28,4},{1,25},{... | collective-permute-start | bytes 147464 | tf_op jit(solution)/shard_map/ppermute | solution.py:306
  127.8 11.3 %collective-permute-start.10 = (f32[96,128]{1,0:T(8,128)S(1)}, f32[96,128]{1,0:T(8,128)S(1)}, u32[]{:S(2)}, u32[]{:S(2)}) collective-permute-start(f32[96,128]{1,0:T(8,128)S(1)} %get-tuple-element.73), channel_id=1, source_target_pairs={{0,28},{4,24},{8,20},{12,16},{16,12},{20,8},{24,4},{28,0},{1,29},{... | collective-permute-start | bytes 147464 | tf_op jit(solution)/shard_map/ppermute | solution.py:306
  130.8 13.3 %collective-permute-start.21 = (f32[96,128]{1,0:T(8,128)S(1)}, f32[96,128]{1,0:T(8,128)S(1)}, u32[]{:S(2)}, u32[]{:S(2)}) collective-permute-start(f32[96,128]{1,0:T(8,128)S(1)} %get-tuple-element.79), channel_id=1, source_target_pairs={{0,4},{4,0},{8,12},{12,8},{16,20},{20,16},{24,28},{28,24},{1,5},{5... | collective-permute-start | bytes 147464 | tf_op jit(solution)/shard_map/ppermute | solution.py:306
  132.2 15.9 %collective-permute-start.22 = (f32[96,128]{1,0:T(8,128)S(1)}, f32[96,128]{1,0:T(8,128)S(1)}, u32[]{:S(2)}, u32[]{:S(2)}) collective-permute-start(f32[96,128]{1,0:T(8,128)S(1)} %get-tuple-element.80), channel_id=1, source_target_pairs={{0,8},{4,12},{8,0},{12,4},{16,24},{20,28},{24,16},{28,20},{1,9},{5... | collective-permute-start | bytes 147464 | tf_op jit(solution)/shard_map/ppermute | solution.py:306
  136.9 12.1 %collective-permute-start.23 = (f32[96,128]{1,0:T(8,128)S(1)}, f32[96,128]{1,0:T(8,128)S(1)}, u32[]{:S(2)}, u32[]{:S(2)}) collective-permute-start(f32[96,128]{1,0:T(8,128)S(1)} %get-tuple-element.81), channel_id=1, source_target_pairs={{0,12},{4,8},{8,4},{12,0},{16,28},{20,24},{24,20},{28,16},{1,13},{... | collective-permute-start | bytes 147464 | tf_op jit(solution)/shard_map/ppermute | solution.py:306
  136.9 16.1 %collective-permute-start.24 = (f32[96,128]{1,0:T(8,128)S(1)}, f32[96,128]{1,0:T(8,128)S(1)}, u32[]{:S(2)}, u32[]{:S(2)}) collective-permute-start(f32[96,128]{1,0:T(8,128)S(1)} %get-tuple-element.82), channel_id=1, source_target_pairs={{0,16},{4,20},{8,24},{12,28},{16,0},{20,4},{24,8},{28,12},{1,17},{... | collective-permute-start | bytes 147464 | tf_op jit(solution)/shard_map/ppermute | solution.py:306
  139.1 14.2 %collective-permute-start.25 = (f32[96,128]{1,0:T(8,128)S(1)}, f32[96,128]{1,0:T(8,128)S(1)}, u32[]{:S(2)}, u32[]{:S(2)}) collective-permute-start(f32[96,128]{1,0:T(8,128)S(1)} %get-tuple-element.83), channel_id=1, source_target_pairs={{0,20},{4,16},{8,28},{12,24},{16,4},{20,0},{24,12},{28,8},{1,21},{... | collective-permute-start | bytes 147464 | tf_op jit(solution)/shard_map/ppermute | solution.py:306
  144.2 9.1 %collective-permute-start.26 = (f32[96,128]{1,0:T(8,128)S(1)}, f32[96,128]{1,0:T(8,128)S(1)}, u32[]{:S(2)}, u32[]{:S(2)}) collective-permute-start(f32[96,128]{1,0:T(8,128)S(1)} %get-tuple-element.84), channel_id=1, source_target_pairs={{0,24},{4,28},{8,16},{12,20},{16,8},{20,12},{24,0},{28,4},{1,25},{... | collective-permute-start | bytes 147464 | tf_op jit(solution)/shard_map/ppermute | solution.py:306
  149.0 9.3 %collective-permute-start.17 = (f32[96,128]{1,0:T(8,128)S(1)}, f32[96,128]{1,0:T(8,128)S(1)}, u32[]{:S(2)}, u32[]{:S(2)}) collective-permute-start(f32[96,128]{1,0:T(8,128)S(1)} %right_sum.4.refs_0_), channel_id=1, source_target_pairs={{0,28},{4,24},{8,20},{12,16},{16,12},{20,8},{24,4},{28,0},{1,29},{... | collective-permute-start | bytes 147464 | tf_op jit(solution)/shard_map/ppermute | solution.py:306
  153.3 13.7 %collective-permute-start.15 = (f32[96,128]{1,0:T(8,128)S(1)}, f32[96,128]{1,0:T(8,128)S(1)}, u32[]{:S(2)}, u32[]{:S(2)}) collective-permute-start(f32[96,128]{1,0:T(8,128)S(1)} %right_sum.4.refs_0_), channel_id=1, source_target_pairs={{0,20},{4,16},{8,28},{12,24},{16,4},{20,0},{24,12},{28,8},{1,21},{... | collective-permute-start | bytes 147464 | tf_op jit(solution)/shard_map/ppermute | solution.py:306
  153.3 17.3 %collective-permute-start.14 = (f32[96,128]{1,0:T(8,128)S(1)}, f32[96,128]{1,0:T(8,128)S(1)}, u32[]{:S(2)}, u32[]{:S(2)}) collective-permute-start(f32[96,128]{1,0:T(8,128)S(1)} %right_sum.4.refs_0_), channel_id=1, source_target_pairs={{0,16},{4,20},{8,24},{12,28},{16,0},{20,4},{24,8},{28,12},{1,17},{... | collective-permute-start | bytes 147464 | tf_op jit(solution)/shard_map/ppermute | solution.py:306
  156.7 14.8 %collective-permute-start.13 = (f32[96,128]{1,0:T(8,128)S(1)}, f32[96,128]{1,0:T(8,128)S(1)}, u32[]{:S(2)}, u32[]{:S(2)}) collective-permute-start(f32[96,128]{1,0:T(8,128)S(1)} %right_sum.4.refs_0_), channel_id=1, source_target_pairs={{0,12},{4,8},{8,4},{12,0},{16,28},{20,24},{24,20},{28,16},{1,13},{... | collective-permute-start | bytes 147464 | tf_op jit(solution)/shard_map/ppermute | solution.py:306
  158.4 13.1 %collective-permute-start.12 = (f32[96,128]{1,0:T(8,128)S(1)}, f32[96,128]{1,0:T(8,128)S(1)}, u32[]{:S(2)}, u32[]{:S(2)}) collective-permute-start(f32[96,128]{1,0:T(8,128)S(1)} %right_sum.4.refs_0_), channel_id=1, source_target_pairs={{0,8},{4,12},{8,0},{12,4},{16,24},{20,28},{24,16},{28,20},{1,9},{5... | collective-permute-start | bytes 147464 | tf_op jit(solution)/shard_map/ppermute | solution.py:306
  160.1 14.6 %collective-permute-start.11 = (f32[96,128]{1,0:T(8,128)S(1)}, f32[96,128]{1,0:T(8,128)S(1)}, u32[]{:S(2)}, u32[]{:S(2)}) collective-permute-start(f32[96,128]{1,0:T(8,128)S(1)} %right_sum.4.refs_0_), channel_id=1, source_target_pairs={{0,4},{4,0},{8,12},{12,8},{16,20},{20,16},{24,28},{28,24},{1,5},{5... | collective-permute-start | bytes 147464 | tf_op jit(solution)/shard_map/ppermute | solution.py:306
  167.0 8.9 %collective-permute-start.34 = (f32[96,128]{1,0:T(8,128)S(1)}, f32[96,128]{1,0:T(8,128)S(1)}, u32[]{:S(2)}, u32[]{:S(2)}) collective-permute-start(f32[96,128]{1,0:T(8,128)S(1)} %right_sum.5.refs_0_), channel_id=1, source_target_pairs={{0,28},{4,24},{8,20},{12,16},{16,12},{20,8},{24,4},{28,0},{1,29},{... | collective-permute-start | bytes 147464 | tf_op jit(solution)/shard_map/ppermute | solution.py:306
  171.5 14.4 %collective-permute-start.32 = (f32[96,128]{1,0:T(8,128)S(1)}, f32[96,128]{1,0:T(8,128)S(1)}, u32[]{:S(2)}, u32[]{:S(2)}) collective-permute-start(f32[96,128]{1,0:T(8,128)S(1)} %right_sum.5.refs_0_), channel_id=1, source_target_pairs={{0,20},{4,16},{8,28},{12,24},{16,4},{20,0},{24,12},{28,8},{1,21},{... | collective-permute-start | bytes 147464 | tf_op jit(solution)/shard_map/ppermute | solution.py:306
  171.5 16.6 %collective-permute-start.31 = (f32[96,128]{1,0:T(8,128)S(1)}, f32[96,128]{1,0:T(8,128)S(1)}, u32[]{:S(2)}, u32[]{:S(2)}) collective-permute-start(f32[96,128]{1,0:T(8,128)S(1)} %right_sum.5.refs_0_), channel_id=1, source_target_pairs={{0,16},{4,20},{8,24},{12,28},{16,0},{20,4},{24,8},{28,12},{1,17},{... | collective-permute-start | bytes 147464 | tf_op jit(solution)/shard_map/ppermute | solution.py:306
  174.7 13.4 %collective-permute-start.30 = (f32[96,128]{1,0:T(8,128)S(1)}, f32[96,128]{1,0:T(8,128)S(1)}, u32[]{:S(2)}, u32[]{:S(2)}) collective-permute-start(f32[96,128]{1,0:T(8,128)S(1)} %right_sum.5.refs_0_), channel_id=1, source_target_pairs={{0,12},{4,8},{8,4},{12,0},{16,28},{20,24},{24,20},{28,16},{1,13},{... | collective-permute-start | bytes 147464 | tf_op jit(solution)/shard_map/ppermute | solution.py:306
  176.0 12.2 %collective-permute-start.29 = (f32[96,128]{1,0:T(8,128)S(1)}, f32[96,128]{1,0:T(8,128)S(1)}, u32[]{:S(2)}, u32[]{:S(2)}) collective-permute-start(f32[96,128]{1,0:T(8,128)S(1)} %right_sum.5.refs_0_), channel_id=1, source_target_pairs={{0,8},{4,12},{8,0},{12,4},{16,24},{20,28},{24,16},{28,20},{1,9},{5... | collective-permute-start | bytes 147464 | tf_op jit(solution)/shard_map/ppermute | solution.py:306
  178.1 10.0 %collective-permute-start.28 = (f32[96,128]{1,0:T(8,128)S(1)}, f32[96,128]{1,0:T(8,128)S(1)}, u32[]{:S(2)}, u32[]{:S(2)}) collective-permute-start(f32[96,128]{1,0:T(8,128)S(1)} %right_sum.5.refs_0_), channel_id=1, source_target_pairs={{0,4},{4,0},{8,12},{12,8},{16,20},{20,16},{24,28},{28,24},{1,5},{5... | collective-permute-start | bytes 147464 | tf_op jit(solution)/shard_map/ppermute | solution.py:306
  192.3 10.0 %collective-permute-start.35 = (f32[96,768]{1,0:T(8,128)S(1)}, f32[96,768]{1,0:T(8,128)S(1)}, u32[]{:S(2)}, u32[]{:S(2)}) collective-permute-start(f32[96,768]{1,0:T(8,128)S(1)} %get-tuple-element.86), channel_id=1, source_target_pairs={{0,2},{1,3},{2,0},{3,1},{4,6},{5,7},{6,4},{7,5},{8,10},{9,11},{10,... | collective-permute-start | bytes 884744 | tf_op jit(solution)/shard_map/ppermute | solution.py:306
  193.9 10.9 %collective-permute-start.36 = (f32[96,768]{1,0:T(8,128)S(1)}, f32[96,768]{1,0:T(8,128)S(1)}, u32[]{:S(2)}, u32[]{:S(2)}) collective-permute-start(f32[96,768]{1,0:T(8,128)S(1)} %get-tuple-element.87), channel_id=1, source_target_pairs={{0,3},{1,2},{2,1},{3,0},{4,7},{5,6},{6,5},{7,4},{8,11},{9,10},{10,... | collective-permute-start | bytes 884744 | tf_op jit(solution)/shard_map/ppermute | solution.py:306
  220.1 12.4 %all-to-all-start.3 = ((f32[8,72,128]{2,1,0:T(8,128)}), f32[8,72,128]{2,1,0:T(8,128)S(1)}, u32[]{:S(2)}, u32[]{:S(2)}) async-start(f32[8,72,128]{2,1,0:T(8,128)} %left_sum.3), calls=%async_computation.3 | async-start | bytes 589824 | tf_op jit(solution)/shard_map/all_to_all | solution.py:389
  223.5 141.4 %all-gather.15.cloned.1.call-start = ((), (), s32[]{:S(2)}) async-start(), calls=%async_computation.7 | async-start | bytes 2654208 | tf_op jit(solution)/shard_map/all_gather | solution.py:448
  223.8 33.0 %collective-permute-start.69 = (f32[288,512]{1,0:T(8,128)}, f32[288,512]{1,0:T(8,128)S(1)}, u32[]{:S(2)}, u32[]{:S(2)}) collective-permute-start(f32[288,512]{1,0:T(8,128)} %get-tuple-element.114), channel_id=1, source_target_pairs={{0,3},{1,2},{2,1},{3,0},{4,7},{5,6},{6,5},{7,4},{8,11},{9,10},{10,... | collective-permute-start | bytes 1769480 | tf_op jit(solution)/shard_map/ppermute | solution.py:306
  234.5 11.2 %collective-permute-start.38 = (f32[96,768]{1,0:T(8,128)S(1)}, f32[96,768]{1,0:T(8,128)S(1)}, u32[]{:S(2)}, u32[]{:S(2)}) collective-permute-start(f32[96,768]{1,0:T(8,128)S(1)} %basis.3.first_ref), channel_id=1, source_target_pairs={{0,2},{1,3},{2,0},{3,1},{4,6},{5,7},{6,4},{7,5},{8,10},{9,11},{10,... | collective-permute-start | bytes 884744 | tf_op jit(solution)/shard_map/ppermute | solution.py:306
  235.9 57.2 %collective-permute-start.68 = (f32[288,512]{1,0:T(8,128)}, f32[288,512]{1,0:T(8,128)S(1)}, u32[]{:S(2)}, u32[]{:S(2)}) collective-permute-start(f32[288,512]{1,0:T(8,128)} %get-tuple-element.115), channel_id=1, source_target_pairs={{0,2},{1,3},{2,0},{3,1},{4,6},{5,7},{6,4},{7,5},{8,10},{9,11},{10,... | collective-permute-start | bytes 1769480 | tf_op jit(solution)/shard_map/ppermute | solution.py:306
  236.6 9.5 %collective-permute-start.37 = (f32[96,768]{1,0:T(8,128)S(1)}, f32[96,768]{1,0:T(8,128)S(1)}, u32[]{:S(2)}, u32[]{:S(2)}) collective-permute-start(f32[96,768]{1,0:T(8,128)S(1)} %basis.3.first_ref), channel_id=1, source_target_pairs={{0,1},{1,0},{2,3},{3,2},{4,5},{5,4},{6,7},{7,6},{8,9},{9,8},{10,11... | collective-permute-start | bytes 884744 | tf_op jit(solution)/shard_map/ppermute | solution.py:306
  245.7 16.1 %collective-permute-start.39 = (f32[96,768]{1,0:T(8,128)S(1)}, f32[96,768]{1,0:T(8,128)S(1)}, u32[]{:S(2)}, u32[]{:S(2)}) collective-permute-start(f32[96,768]{1,0:T(8,128)S(1)} %collective-permute-done.38.first_ref), channel_id=1, source_target_pairs={{0,1},{1,0},{2,3},{3,2},{4,5},{5,4},{6,7},{7,6},{8,9},{9,8},{10,11... | collective-permute-start | bytes 884744 | tf_op jit(solution)/shard_map/ppermute | solution.py:306
  256.8 13.5 %collective-permute-start.42 = (f32[96,128]{1,0:T(8,128)S(1)}, f32[96,128]{1,0:T(8,128)S(1)}, u32[]{:S(2)}, u32[]{:S(2)}) collective-permute-start(f32[96,128]{1,0:T(8,128)S(1)} %get-tuple-element.91), channel_id=1, source_target_pairs={{0,12},{4,8},{8,4},{12,0},{16,28},{20,24},{24,20},{28,16},{1,13},{... | collective-permute-start | bytes 147464 | tf_op jit(solution)/shard_map/ppermute | solution.py:306
  257.8 14.5 %collective-permute-start.43 = (f32[96,128]{1,0:T(8,128)S(1)}, f32[96,128]{1,0:T(8,128)S(1)}, u32[]{:S(2)}, u32[]{:S(2)}) collective-permute-start(f32[96,128]{1,0:T(8,128)S(1)} %get-tuple-element.92), channel_id=1, source_target_pairs={{0,16},{4,20},{8,24},{12,28},{16,0},{20,4},{24,8},{28,12},{1,17},{... | collective-permute-start | bytes 147464 | tf_op jit(solution)/shard_map/ppermute | solution.py:306
  260.3 12.1 %collective-permute-start.44 = (f32[96,128]{1,0:T(8,128)S(1)}, f32[96,128]{1,0:T(8,128)S(1)}, u32[]{:S(2)}, u32[]{:S(2)}) collective-permute-start(f32[96,128]{1,0:T(8,128)S(1)} %get-tuple-element.93), channel_id=1, source_target_pairs={{0,20},{4,16},{8,28},{12,24},{16,4},{20,0},{24,12},{28,8},{1,21},{... | collective-permute-start | bytes 147464 | tf_op jit(solution)/shard_map/ppermute | solution.py:306
  261.8 10.7 %collective-permute-start.45 = (f32[96,128]{1,0:T(8,128)S(1)}, f32[96,128]{1,0:T(8,128)S(1)}, u32[]{:S(2)}, u32[]{:S(2)}) collective-permute-start(f32[96,128]{1,0:T(8,128)S(1)} %get-tuple-element.94), channel_id=1, source_target_pairs={{0,24},{4,28},{8,16},{12,20},{16,8},{20,12},{24,0},{28,4},{1,25},{... | collective-permute-start | bytes 147464 | tf_op jit(solution)/shard_map/ppermute | solution.py:306
  272.5 9.8 %collective-permute-start.56 = (f32[96,128]{1,0:T(8,128)S(1)}, f32[96,128]{1,0:T(8,128)S(1)}, u32[]{:S(2)}, u32[]{:S(2)}) collective-permute-start(f32[96,128]{1,0:T(8,128)S(1)} %get-tuple-element.99), channel_id=1, source_target_pairs={{0,12},{4,8},{8,4},{12,0},{16,28},{20,24},{24,20},{28,16},{1,13},{... | collective-permute-start | bytes 147464 | tf_op jit(solution)/shard_map/ppermute | solution.py:306
  277.6 9.6 %collective-permute-start.58 = (f32[96,128]{1,0:T(8,128)S(1)}, f32[96,128]{1,0:T(8,128)S(1)}, u32[]{:S(2)}, u32[]{:S(2)}) collective-permute-start(f32[96,128]{1,0:T(8,128)S(1)} %get-tuple-element.101), channel_id=1, source_target_pairs={{0,20},{4,16},{8,28},{12,24},{16,4},{20,0},{24,12},{28,8},{1,21},{... | collective-permute-start | bytes 147464 | tf_op jit(solution)/shard_map/ppermute | solution.py:306
  289.3 9.1 %collective-permute-start.50 = (f32[96,128]{1,0:T(8,128)S(1)}, f32[96,128]{1,0:T(8,128)S(1)}, u32[]{:S(2)}, u32[]{:S(2)}) collective-permute-start(f32[96,128]{1,0:T(8,128)S(1)} %right_sum.6.refs_0_), channel_id=1, source_target_pairs={{0,16},{4,20},{8,24},{12,28},{16,0},{20,4},{24,8},{28,12},{1,17},{... | collective-permute-start | bytes 147464 | tf_op jit(solution)/shard_map/ppermute | solution.py:306
  295.1 9.1 %collective-permute-start.47 = (f32[96,128]{1,0:T(8,128)S(1)}, f32[96,128]{1,0:T(8,128)S(1)}, u32[]{:S(2)}, u32[]{:S(2)}) collective-permute-start(f32[96,128]{1,0:T(8,128)S(1)} %right_sum.6.refs_0_), channel_id=1, source_target_pairs={{0,4},{4,0},{8,12},{12,8},{16,20},{20,16},{24,28},{28,24},{1,5},{5... | collective-permute-start | bytes 147464 | tf_op jit(solution)/shard_map/ppermute | solution.py:306
  314.3 103.4 %all-gather.13.cloned.1.call-start = ((), (), s32[]{:S(2)}) async-start(), calls=%async_computation.6 | async-start | bytes 2654208 | tf_op jit(solution)/shard_map/all_gather | solution.py:448
  (62 other events, 410.7 us)
Sparse Core Ops, SparseCore 0:
  10.8 92.6 all-gather.8
  105.7 102.3 all-gather.10
  314.4 50.4 all-gather.14
  366.9 50.6 all-gather.12

commit v3 on v2

--- a/solution.py
+++ b/solution.py
@@ -87,6 +87,26 @@
     return values[0]
 
 
+def streamed(sources, buffers, sems, picked=lambda k: (k,)):
+    step = pl.program_id(0)
+
+    def copies(k):
+        return [
+            pltpu.make_async_copy(source.at[picked(k)], buffer.at[k], sems.at[which, k])
+            for which, (source, buffer) in enumerate(zip(sources, buffers))
+        ]
+
+    @pl.when(step == 0)
+    def _():
+        for k in range(buffers[0].shape[0]):
+            for copy in copies(k):
+                copy.start()
+
+    for copy in copies(step):
+        copy.wait()
+    return [buffer[step] for buffer in buffers]
+
+
 def put_left(left, step, left_refs, per_tp):
     for which, left_ref in enumerate(left_refs):
 
@@ -95,25 +115,32 @@
             left_ref[...] = left
 
 
-def first_left_kernel(per_tp, ids_ref, grads_ref, error_ref, query_ref, high_ref, low_ref, *left_refs):
-    high, low = two_terms(grads_ref[0, 0].astype(F32) + error_ref[0, 0])
+def first_left_kernel(per_tp, picked, ids_ref, grads_ref, error_ref, query_ref, high_ref, low_ref, *refs):
+    left_refs, (grads_buffer, error_buffer, sems) = refs[:-3], refs[-3:]
+    grads, error = streamed(
+        (grads_ref, error_ref), (grads_buffer, error_buffer), sems, lambda k: (0, picked(k, ids_ref))
+    )
+    high, low = two_terms(grads.astype(F32) + error)
     high_ref[0] = high
     low_ref[0] = low
     put_left(small_by_large(query_ref[0], high, low, True), pl.program_id(0), left_refs, per_tp)
 
 
-def left_kernel(per_tp, ids_ref, high_ref, low_ref, *refs):
-    parts, left_refs, (scratch, current) = refs[:-4], refs[-4:-2], refs[-2:]
+def left_kernel(per_tp, half, ids_ref, high_ref, low_ref, *refs):
+    parts, left_refs, (scratch, current), stream = refs[:-7], refs[-7:-5], refs[-5:-3], refs[-3:]
     step = pl.program_id(0)
     rank = left_refs[0].shape[0]
+    rows = current.shape[0]
+    lanes = rows * (current.shape[1] // LANES)
 
     @pl.when(step == 0)
     def _():
         join_parts(scratch, ids_ref[0], parts)
-        current[...] = read_lanes(scratch, current.shape[0])
-
+        current[...] = read_lanes(scratch.at[half * lanes : (half + 1) * lanes], rows)
+
+    high, low = streamed((high_ref, low_ref), stream[:2], stream[2])
     own = current[part_at(step, rank), :]
-    put_left(small_by_large(own, high_ref[0], low_ref[0], True), step, left_refs, per_tp)
+    put_left(small_by_large(own, high, low, True), step, left_refs, per_tp)
 
 
 def split_kernel(tps, *refs):
@@ -162,16 +189,24 @@
 
 
 def right_kernel(per_tp, ids_ref, first_ref, second_ref, high_ref, low_ref, *refs):
-    part_refs, (scratch, right) = refs[:-2], refs[-2:]
     step = pl.program_id(0)
     rank = first_ref.shape[0] // per_tp
     at = part_at(step % per_tp, rank)
     own = jnp.where(step // per_tp == 0, first_ref[at, :], second_ref[at, :])
-    right[part_at(step, rank), :] = small_by_large(own, high_ref[0], low_ref[0], False)
+    refs, stream = refs[:-3], refs[-3:]
+    high, low = streamed((high_ref, low_ref), stream[:2], stream[2])
+    product_now = small_by_large(own, high, low, False)
+    if len(refs) == 1:
+        refs[0][...] = product_now
+        return
+    before_ref, part_refs, (scratch, right) = refs[0], refs[1:-2], refs[-2:]
+    right[part_at(step, rank), :] = product_now
 
     @pl.when(step == pl.num_programs(0) - 1)
     def _():
-        lay_lanes(scratch, right[...])
+        lanes = scratch.shape[0] // 2
+        lay_lanes(scratch.at[:lanes], before_ref[...])
+        lay_lanes(scratch.at[lanes:], right[...])
         split_parts(scratch, ids_ref[0], part_refs)
 
 
@@ -192,19 +227,16 @@
     return dot(jnp.concatenate([high, low, high], axis=1), stacked(right))
 
 
-def late_kernel(tps, early, unit, per_tp, rank, ids_ref, basis_ref, *refs):
-    late = tps - early
-    lanes, approx = refs[-2:]
-    query_ref, weight_refs = refs[-3 - late], refs[-2 - late : -2]
-    base_refs = refs[-3 - 2 * late : -3 - late]
-    part_refs = refs[: -3 - 2 * late]
-    halves = tps // 2
-    per_half = len(part_refs) // halves
-    rows = query_ref.shape[0] // halves
+def late_kernel(early, unit, per_tp, rank, ids_ref, basis_ref, *refs):
+    query_ref, weights_ref, lanes, approx = refs[-4:]
+    late = weights_ref.shape[0]
+    part_refs, base_refs = refs[: -4 - late], refs[-4 - late : -4]
+    rows = query_ref.shape[0] // 2
     tp = ids_ref[1]
-    for half in range(halves):
-        join_parts(lanes, ids_ref[0], part_refs[half * per_half : (half + 1) * per_half])
-        value = read_lanes(lanes, rows)
+    join_parts(lanes, ids_ref[0], part_refs)
+    for half in range(2):
+        per_half = lanes.shape[0] // 2
+        value = read_lanes(lanes.at[half * per_half : (half + 1) * per_half], rows)
         for which in range(2):
             owner = tp ^ (2 * half + which)
             query_ref[part_at(owner, rows // 2), :] = value[which * (rows // 2) : (which + 1) * (rows // 2)]
@@ -212,28 +244,32 @@
     rows_of_update(basis_ref, query_ref, approx, ids_ref[0] * units, unit, per_tp, rank, tp, 0)
     for which in range(late):
         base = base_refs[which][...]
-        own = approx[part_at(tp ^ (early + which), base.shape[0]), :]
-        weight_refs[which][...] = (base - LEARNING_RATE * own).astype(BF16)
-
-
-def place_kernel(ids_ref, part_ref, _, weights_ref):
-    weights_ref[...] = part_ref[...].reshape(weights_ref.shape)
+        owner = tp ^ (early + which)
+        own = approx[part_at(owner, base.shape[0]), :]
+        weights_ref[owner % late] = (base - LEARNING_RATE * own).astype(BF16)
+
+
+def owner_of(step, rep, replicas):
+    half = replicas // 2
+    return ((rep ^ (step // half)) + 2 * replicas - 2 * (step % half)) % replicas
+
+
+def place_kernel(ids_ref, *refs):
+    for at, part_ref in enumerate(refs[:-2]):
+
+        @pl.when(pl.program_id(0) == at)
+        def _():
+            refs[-1][0] = part_ref[...]
 
 
 def update_kernel(early, per_tp, rank, ids_ref, basis_ref, right_ref, *refs):
     new_error_ref, weights_ref, approx = refs[-3:]
-    base_refs, term_refs = refs[:early], refs[early:-3]
-    slot, matrix = pl.program_id(0), pl.program_id(1)
+    base_refs, (high_ref, low_ref) = refs[:early], refs[early : early + 2]
+    matrix = pl.program_id(1)
     at = part_at(matrix, rank)
     own = product(basis_ref[at, :], right_ref[at, :])
-    width = own.shape[0]
-    approx[part_at(matrix, width), :] = own
-    for half in range(len(term_refs) // 2):
-
-        @pl.when(slot // 2 == half)
-        def _():
-            high, low = (ref[0].astype(F32) for ref in term_refs[2 * half : 2 * half + 2])
-            new_error_ref[0, 0] = high + low - own
+    approx[part_at(matrix, own.shape[0]), :] = own
+    new_error_ref[0, 0] = high_ref[0].astype(F32) + low_ref[0].astype(F32) - own
 
     @pl.when(matrix == per_tp - 1)
     def _():
@@ -284,7 +320,7 @@
     )(*operands)
 
 
-def grid_call(kernel, name, ids, grid, in_specs, out_specs, out_shape, operands, scratch=(), aliases=None, flops=0, moved=0, mib=20):
+def grid_call(kernel, name, ids, grid, in_specs, out_specs, out_shape, operands, scratch=(), aliases=None, flops=0, moved=0):
     return pl.pallas_call(
         kernel,
         grid_spec=pltpu.PrefetchScalarGridSpec(
@@ -296,7 +332,7 @@
         ),
         out_shape=out_shape,
         input_output_aliases=aliases or {},
-        compiler_params=grant(mib),
+        compiler_params=grant(60),
         name=name,
         cost_estimate=pl.CostEstimate(flops=flops, bytes_accessed=moved, transcendentals=0),
     )(ids, *operands)
@@ -325,7 +361,7 @@
     halves = tps // 2
     tp_rows = per_tp * rank
     left_part = tp_rows * width // LANES // replicas
-    right_part = 2 * tp_rows * cols // LANES // replicas
+    right_part = tps * tp_rows * cols // LANES // replicas
     own_rows = momentum.shape[0]
     flops = 2 * 3 * per_half * rank * width * cols
     elements = per_half * width * cols
@@ -334,6 +370,12 @@
         return (at[1] ^ (2 * half + k // per_tp)) * per_tp + k % per_tp
 
     term_spec = pl.BlockSpec((1, width, cols), lambda k, at: (k, 0, 0))
+    read_spec = pl.BlockSpec(memory_space=pl.ANY)
+    streams = [
+        pltpu.VMEM((per_half, width, cols), BF16),
+        pltpu.VMEM((per_half, width, cols), BF16),
+        pltpu.SemaphoreType.DMA((2, per_half)),
+    ]
     term_shape = shape(per_half, width, cols, dtype=BF16)
     left_specs = [
         pl.BlockSpec((rank, width), lambda k, at, which=which: (jnp.clip(k - which * per_tp, 0, per_tp - 1), 0))
@@ -348,18 +390,23 @@
     for half in reversed(range(halves)):
         picked = functools.partial(matrix_of, half)
         high, low, *out = grid_call(
-            functools.partial(first_left_kernel, per_tp),
+            functools.partial(first_left_kernel, per_tp, picked),
             "first_left",
             ids,
             (per_half,),
             [
-                pl.BlockSpec((1, 1, width, cols), lambda k, at, picked=picked: (0, picked(k, at), 0, 0)),
-                pl.BlockSpec((1, 1, width, cols), lambda k, at, picked=picked: (0, picked(k, at), 0, 0)),
+                read_spec,
+                read_spec,
                 pl.BlockSpec((1, rank, cols), lambda k, at, picked=picked: (picked(k, at), 0, 0)),
             ],
             [term_spec, term_spec, *left_specs],
             [term_shape, term_shape, *left_shapes],
             (grads, error, query),
+            [
+                pltpu.VMEM((per_half, width, cols), BF16),
+                pltpu.VMEM((per_half, width, cols), F32),
+                pltpu.SemaphoreType.DMA((2, per_half)),
+            ],
             flops=flops,
             moved=10 * elements,
         )
@@ -390,134 +437,157 @@
         basis = whole_call(
             functools.partial(basis_kernel, rank), "basis", shape(tp_rows, width), [parts.reshape(-1, LANES)]
         )
-        bases = [basis]
-        for bit in range(tps.bit_length() - 2, 0, -1):
-            bases += [swap(one, "tp", tps, 1 << bit) for one in bases]
-        even = {}
-        for at, one in enumerate(bases):
-            even[sum(1 << bit for place, bit in enumerate(range(tps.bit_length() - 2, 0, -1)) if at >> place & 1)] = one
-        bases = []
-        for offset in range(0, tps, 2):
-            bases += [even[offset], swap(even[offset], "tp", tps, 1)]
-        rights = []
-        for half in range(halves):
-            parts = grid_call(
-                functools.partial(right_kernel, per_tp),
-                "right",
-                ids,
-                (per_half,),
-                [whole_spec(tp_rows, width), whole_spec(tp_rows, width), term_spec, term_spec],
-                [whole_spec(right_part, LANES)] * replicas,
-                [shape(right_part, LANES)] * replicas,
-                (*bases[2 * half : 2 * half + 2], *terms[half]),
-                [pltpu.VMEM((right_part * replicas, LANES), F32), pltpu.VMEM((2 * tp_rows, cols), F32)],
-                flops=flops,
-                moved=4 * elements,
-            )
-            met = scattered(parts, replicas)
-            part = whole_call(functools.partial(sum_kernel, 1.0 / replicas), "right_sum", shape(right_part, LANES), met)
-            rights.append(spread(part, "rep", replicas))
+        across = swap(basis, "tp", tps, 2)
+        bases = [basis, swap(basis, "tp", tps, 1)]
+        before = grid_call(
+            functools.partial(right_kernel, per_tp),
+            "right_near",
+            ids,
+            (per_half,),
+            [whole_spec(tp_rows, width), whole_spec(tp_rows, width), read_spec, read_spec],
+            pl.BlockSpec((rank, cols), lambda k, at: (k, 0)),
+            shape(2 * tp_rows, cols),
+            (*bases, *terms[0]),
+            streams,
+            flops=flops,
+            moved=4 * elements,
+        )
+        before, across = lax.optimization_barrier((before, across))
+        bases += [across, swap(across, "tp", tps, 1)]
+        parts = grid_call(
+            functools.partial(right_kernel, per_tp),
+            "right_far",
+            ids,
+            (per_half,),
+            [whole_spec(tp_rows, width), whole_spec(tp_rows, width), read_spec, read_spec, whole_spec(2 * tp_rows, cols)],
+            [whole_spec(right_part, LANES)] * replicas,
+            [shape(right_part, LANES)] * replicas,
+            (*bases[2:], *terms[1], before),
+            [pltpu.VMEM((right_part * replicas, LANES), F32), pltpu.VMEM((2 * tp_rows, cols), F32), *streams],
+            flops=flops,
+            moved=4 * elements,
+        )
+        met = scattered(parts, replicas)
+        part = whole_call(functools.partial(sum_kernel, 1.0 / replicas), "right_sum", shape(right_part, LANES), met)
+        rights = spread(part, "rep", replicas)
         if power_pass < ROUNDS - 1:
-            for half in range(halves):
+            near_parts = rights
+            for half in reversed(range(halves)):
                 lefts[2 * half : 2 * half + 2] = grid_call(
-                    functools.partial(left_kernel, per_tp),
+                    functools.partial(left_kernel, per_tp, half),
                     "left",
                     ids,
                     (per_half,),
-                    [term_spec, term_spec] + [whole_spec(right_part, LANES)] * replicas,
+                    [read_spec, read_spec] + [whole_spec(right_part, LANES)] * replicas,
                     left_specs,
                     left_shapes,
-                    (*terms[half], *rights[half]),
-                    [pltpu.VMEM((right_part * replicas, LANES), F32), pltpu.VMEM((2 * tp_rows, cols), F32)],
+                    (*terms[half], *near_parts),
+                    [pltpu.VMEM((right_part * replicas, LANES), F32), pltpu.VMEM((2 * tp_rows, cols), F32), *streams],
                     flops=flops,
                     moved=4 * elements,
                 )
+                if half:
+                    far, near_parts = lax.optimization_barrier((lefts[2 * half : 2 * half + 2], rights))
+                    lefts[2 * half : 2 * half + 2] = far
 
     all_bases = jnp.concatenate(bases, axis=0)
     late = tps - EARLY
     rep_rows = tps * own_rows
     unit = math.gcd(rep_rows, width)
-    right, *blocks = whole_call(
-        functools.partial(late_kernel, tps, EARLY, unit, per_tp, rank),
+    right, block = whole_call(
+        functools.partial(late_kernel, EARLY, unit, per_tp, rank),
         "late_rows",
-        [shape(matrices * rank, cols)] + [shape(own_rows, cols, dtype=BF16)] * late,
-        [all_bases, *[part for parts in rights for part in parts], *base[EARLY:]],
+        [shape(matrices * rank, cols), shape(late, own_rows, cols, dtype=BF16)],
+        [all_bases, *rights, *base[EARLY:]],
         ids,
         [pltpu.VMEM((right_part * replicas, LANES), F32), pltpu.VMEM((rep_rows, cols), F32)],
     )
-    late_rows = [lax.all_gather(block, "rep") for block in blocks]
-
-    new_error, weights = grid_call(
-        functools.partial(update_kernel, EARLY, per_tp, rank),
-        "update",
-        ids,
-        (tps, per_tp),
-        [
-            pl.BlockSpec((tp_rows, width), lambda s, j, at: (s, 0)),
-            pl.BlockSpec((tp_rows, cols), lambda s, j, at: (at[1] ^ s, 0)),
-        ]
-        + [pl.BlockSpec((replicas // tps, own_rows, cols), lambda s, j, at: (at[1] ^ s, 0, 0))] * EARLY
-        + [
-            pl.BlockSpec(
-                (1, width, cols),
-                lambda s, j, at, half=half: (jnp.clip(s * per_tp + j - half * per_half, 0, per_half - 1), 0, 0),
-            )
-            for half in range(halves)
-            for _ in range(2)
-        ],
-        [
-            pl.BlockSpec((1, 1, width, cols), lambda s, j, at: (0, (at[1] ^ s) * per_tp + j, 0, 0)),
-            pl.BlockSpec((replicas // tps, tps, own_rows, cols), lambda s, j, at: (at[1] ^ s, 0, 0, 0)),
-        ],
-        [shape(*error.shape), shape(replicas, tps, own_rows, cols, dtype=BF16)],
-        (all_bases, right, *gathered, *[term for pair in terms for term in pair]),
-        [pltpu.VMEM((per_tp * width, cols), F32)],
-        flops=2 * 3 * rank * error.size,
-        moved=12 * error.size,
-        mib=36,
-    )
-
     spans = -(-(width - unit + rep_rows) // width)
     first = jnp.minimum(rep * rep_rows // width, matrices - spans)
     near = lax.dynamic_slice_in_dim(right, first * rank, spans * rank, 0)
-    near = jnp.stack(spread(near, "tp", tps))
-    wide = pl.BlockSpec((own_rows, cols), lambda s, at: (0, at[1] ^ s))
-    new_momentum, new_master = grid_call(
-        functools.partial(flat_kernel, unit, per_tp, rank, matrices),
-        "flat_rows",
-        ids,
-        (tps,),
-        [
-            whole_spec(matrices * rank, width),
-            pl.BlockSpec((1, spans * rank, cols), lambda s, at: (s, 0, 0)),
-            wide,
-            wide,
-        ],
-        [wide, wide],
-        [shape(*momentum.shape), shape(*master.shape)],
-        (all_bases, near, momentum, master),
-        [pltpu.VMEM((rep_rows, cols), F32)],
-        flops=2 * 3 * rank * momentum.size * tps,
-        moved=16 * momentum.size,
-    )
-
-    for which in range(late):
-        groups = 2
+
+    def update(half, ids, outs):
+        def owner(s, at):
+            return at[1] ^ (2 * half + s)
+
+        return grid_call(
+            functools.partial(update_kernel, EARLY, per_tp, rank),
+            "update",
+            ids,
+            (2, per_tp),
+            [
+                pl.BlockSpec((tp_rows, width), lambda s, j, at: (2 * half + s, 0)),
+                pl.BlockSpec((tp_rows, cols), lambda s, j, at: (owner(s, at), 0)),
+            ]
+            + [pl.BlockSpec((replicas // tps, own_rows, cols), lambda s, j, at: (owner(s, at), 0, 0))] * EARLY
+            + [pl.BlockSpec((1, width, cols), lambda s, j, at: (s * per_tp + j, 0, 0))] * 2
+            + [pl.BlockSpec(memory_space=pl.ANY)] * len(outs),
+            [
+                pl.BlockSpec((1, 1, width, cols), lambda s, j, at: (0, owner(s, at) * per_tp + j, 0, 0)),
+                pl.BlockSpec((replicas // tps, tps, own_rows, cols), lambda s, j, at: (owner(s, at), 0, 0, 0)),
+            ],
+            [shape(*error.shape), shape(replicas, tps, own_rows, cols, dtype=BF16)],
+            (all_bases, right, *gathered, *terms[half], *outs),
+            [pltpu.VMEM((per_tp * width, cols), F32)],
+            aliases={5 + EARLY + at: at for at in range(len(outs))},
+            flops=2 * 3 * rank * error.size // 2,
+            moved=6 * error.size,
+        )
+
+    def flat_rows(ids, all_bases, near):
+        wide = pl.BlockSpec((own_rows, cols), lambda s, at: (0, at[1] ^ s))
+        return grid_call(
+            functools.partial(flat_kernel, unit, per_tp, rank, matrices),
+            "flat_rows",
+            ids,
+            (tps,),
+            [
+                whole_spec(matrices * rank, width),
+                pl.BlockSpec((1, spans * rank, cols), lambda s, at: (s, 0, 0)),
+                wide,
+                wide,
+            ],
+            [wide, wide],
+            [shape(*momentum.shape), shape(*master.shape)],
+            (all_bases, near, momentum, master),
+            [pltpu.VMEM((rep_rows, cols), F32)],
+            flops=2 * 3 * rank * momentum.size * tps,
+            moved=16 * momentum.size,
+        )
+
+    ring = [(index, (index + 2) % replicas) for index in range(replicas)]
+    held, beside = [block], []
+    stages = replicas // 2
+    outs, flat = (), ()
+    for stage in range(stages):
+        beside.append(swap(held[-1], "rep", replicas, 1))
+        if stage < stages - 1:
+            held.append(lax.ppermute(held[-1], "rep", ring))
+        if stage == 0:
+            near = spread(near, "tp", tps)
+        if stage < 2:
+            outs = tuple(update(stage, ids, outs))
+        elif stage == 2:
+            flat = flat_rows(ids, all_bases, jnp.stack(near))
+        if stage < stages - 1:
+            ids, outs, flat, held, beside, near = lax.optimization_barrier((ids, outs, flat, held, beside, near))
+    new_momentum, new_master = flat
+    new_error, weights = outs
+    pieces = [*held, *beside]
+    for some in (range(len(pieces) - 1), range(len(pieces) - 1, len(pieces))):
         weights = grid_call(
             place_kernel,
             "place_late",
             ids,
-            (groups,),
-            [
-                pl.BlockSpec((replicas // groups, own_rows, cols), lambda q, at: (q, 0, 0)),
-                pl.BlockSpec(memory_space=pl.ANY),
-            ],
+            (len(some),),
+            [pl.BlockSpec((late, own_rows, cols), lambda k, at: (0, 0, 0))] * len(some) + [pl.BlockSpec(memory_space=pl.ANY)],
             pl.BlockSpec(
-                (replicas // groups, 1, own_rows, cols), lambda q, at, which=which: (q, at[1] ^ (EARLY + which), 0, 0)
+                (1, late, own_rows, cols),
+                lambda k, at, some=some: (owner_of(k + some[0], at[0], replicas), (at[1] ^ EARLY) // late, 0, 0),
             ),
             shape(*weights.shape, dtype=BF16),
-            (late_rows[which], weights),
-            aliases={2: 0},
+            (*[pieces[at] for at in some], weights),
+            aliases={1 + len(some): 0},
         )
     weights = weights.reshape(matrices, width, cols)
     return (new_error, right.reshape(matrices, rank, cols), new_momentum, new_master, weights)
@@ -564,13 +634,13 @@
 
 def divides(mesh, matrices, rank, width, cols):
     replicas, tps = mesh.shape["rep"], mesh.shape["tp"]
-    if replicas & (replicas - 1) or tps & (tps - 1) or tps < 4 or replicas % tps or matrices % tps or cols % (tps * LANES) or width % LANES:
+    if replicas & (replicas - 1) or tps != 4 or replicas < 8 or matrices % tps or cols % (tps * LANES) or width % LANES:
         return False
     if math.gcd(matrices * width // replicas, width) % LANES:
         return False
     tp_rows = matrices // tps * rank
     tiles = 8 * LANES * replicas
-    return tp_rows * width % tiles == 0 and 2 * tp_rows * (cols // tps) % tiles == 0
+    return tp_rows * width % tiles == 0 and tps * tp_rows * (cols // tps) % tiles == 0
 
 
 def solution(mesh):

time: 429 us -> 399 us (0.930)
  Pallas kernels: 77.4 us -> 119 us
  local copies, waits for them, and re-layouts: 43.7 us -> 11.4 us
  waiting for transfers between devices: 121 us -> 89 us
  starting transfers between devices: 106 us -> 80.4 us
  blocking collectives: 60.4 us -> 75.4 us
    all_gather x2 -> x0, waiting for transfers between devices: 52.6 us -> none  [local(): late_rows = [lax.all_gather(block, 'rep') for block in blocks]]
    pallas_call x12 -> x13, Pallas kernels: 69.1 us -> 113 us  [grid_call(): pl.pallas_call(kernel, grid_spec=pltpu.PrefetchScalarGridSpec(num_scalar_...]
    unnamed x62 -> x84, local copies, waits for them, and re-layouts: 41.9 us -> 10.5 us
    ppermute x74 -> x50, waiting for transfers between devices: 58.7 us -> 83.9 us  [swap(): lax.ppermute(x, axis, [(index, index ^ offset) for index in range(size)])]
    ppermute x74 -> x50, starting transfers between devices: 103 us -> 78.1 us  [swap(): lax.ppermute(x, axis, [(index, index ^ offset) for index in range(size)])]
    all_to_all x3 -> x4, blocking collectives: 60.4 us -> 75.4 us  [local(): lax.all_to_all(parts, 'rep', split_axis=0, concat_axis=0, tiled=True)]
    all_to_all x1 -> x0, waiting for transfers between devices: 8.69 us -> none  [local(): lax.all_to_all(parts, 'rep', split_axis=0, concat_axis=0, tiled=True)]
    ppermute x0 -> x3, waiting for transfers between devices: none -> 5.07 us  [local(): held.append(lax.ppermute(held[-1], 'rep', ring))]
  transfers between devices with their start and end apart: 79 -> 55, of which waited for: 23 -> 27; matrix products, arithmetic and copies ran while one was open for 1% -> 2% of each run, Pallas kernels for 18% -> 29%
where the time goes in v3:
time: 399 us; the launch traced here: 398 us
  Pallas kernels  119 us (30%)
  waiting for transfers between devices  89 us (22%)
  starting transfers between devices  80.4 us (20%)
  blocking collectives  75.4 us (19%)
  between operations  14.5 us (4%)
  local copies, waits for them, and re-layouts  11.4 us (3%)
  other arithmetic  7.64 us (2%)
    pallas_call x13, Pallas kernels, grid_call(): pl.pallas_call(kernel, grid_spec=pltpu.PrefetchScalarGridSpec(num_scalar_...  113 us
    ppermute x50, waiting for transfers between devices, swap(): lax.ppermute(x, axis, [(index, index ^ offset) for index in range(size)])  83.9 us
    ppermute x50, starting transfers between devices, swap(): lax.ppermute(x, axis, [(index, index ^ offset) for index in range(size)])  78.1 us
    all_to_all x4, blocking collectives, local(): lax.all_to_all(parts, 'rep', split_axis=0, concat_axis=0, tiled=True)  75.4 us
    unnamed x84, local copies, waits for them, and re-layouts  10.5 us
  transfers between devices with their start and end apart: 55, of which 27 were waited for; matrix products, arithmetic and copies ran while one was open for 2% of the time, Pallas kernels for 29%

profile of v3, /device:TPU:0, one launch (start us, length us, event | category | flops | bytes accessed | tf_op | source)
XLA Modules:
  0.0 397.7 jit_solution(2783599560970028439)
XLA Ops:
  7.2 2.2 multiply_subtract_fusion.1
  10.1 12.6 %first_left.3 = (bf16[6,768,512]{2,1,0:T(8,128)(2,1)}, bf16[6,768,512]{2,1,0:T(8,128)(2,1)}, f32[96,768]{1,0:T(8,128)}, f32[96,768]{1,0:T(8,128)}) custom-call(s32[2]{0:T(128)} %pad_add_fusion.ids_ref, bf16[1,12,768,512]{3,2,1,0:T(8,128)(2,1)} %grads_ref.3, f32[1,12,768,512]{3,2,1,0:T(8,128)} %error_ref.3, f32[12,32,512]{2,1,0:T(8,128)} %query_ref.3), custom_call_target="tpu_custom_call" | custom-call | flops 452984832 | bytes 23592960 | tf_op jit(solution)/shard_map/first_left/pallas_call | solution.py:324
  22.7 3.0 collective-permute-start.1
  25.7 12.8 %first_left.2 = (bf16[6,768,512]{2,1,0:T(8,128)(2,1)}, bf16[6,768,512]{2,1,0:T(8,128)(2,1)}, f32[96,768]{1,0:T(8,128)}, f32[96,768]{1,0:T(8,128)}) custom-call(s32[2]{0:T(128)} %pad_add_fusion.ids_ref, bf16[1,12,768,512]{3,2,1,0:T(8,128)(2,1)} %grads_ref.3, f32[1,12,768,512]{3,2,1,0:T(8,128)} %error_ref.3, f32[12,32,512]{2,1,0:T(8,128)} %query_ref.3), custom_call_target="tpu_custom_call" | custom-call | flops 452984832 | bytes 23592960 | tf_op jit(solution)/shard_map/first_left/pallas_call | solution.py:324
  41.4 2.9 multiply_subtract_fusion
  47.1 24.2 %all_to_all.20.parts_ref = f32[8,72,128]{2,1,0:T(8,128)S(1)} all-to-all(f32[8,72,128]{2,1,0:T(8,128)S(1)} %bitcast.16), channel_id=1, replica_groups=mesh['rep'=8,'tp'=4] {'rep'}, dimensions={0} | all-to-all | bytes 589824 | tf_op jit(solution)/shard_map/all_to_all | solution.py:434
  71.3 22.2 %all_to_all.21 = f32[8,72,128]{2,1,0:T(8,128)S(1)} all-to-all(f32[8,72,128]{2,1,0:T(8,128)S(1)} %left_sum.2), channel_id=1, replica_groups=mesh['rep'=8,'tp'=4] {'rep'}, dimensions={0} | all-to-all | bytes 589824 | tf_op jit(solution)/shard_map/all_to_all | solution.py:436
  97.8 6.7 %right_near.2.refs_0_ = f32[192,512]{1,0:T(8,128)} custom-call(s32[2]{0:T(128)} %pad_add_fusion.ids_ref, f32[96,768]{1,0:T(8,128)} %copy-done.3, f32[96,768]{1,0:T(8,128)} %copy-done.35, bf16[6,768,512]{2,1,0:T(8,128)(2,1)} %get-tuple-element.92.high_ref.refs_2_, bf16[6,768,512]{2,1,0:T(8,128)(2,1)} %get-tuple-element.93.low_ref.refs_3_), custom_call_target="tpu_custom_call" | custom-call | flops 452984832 | bytes 9437184 | tf_op jit(solution)/shard_map/right_near/pallas_call | solution.py:324
  107.2 7.1 %right_far.2 = (f32[192,128]{1,0:T(8,128)}, f32[192,128]{1,0:T(8,128)}, f32[192,128]{1,0:T(8,128)}, f32[192,128]{1,0:T(8,128)}, f32[192,128]{1,0:T(8,128)}, /*in...) custom-call(s32[2]{0:T(128)} %pad_add_fusion.ids_ref, f32[96,768]{1,0:T(8,128)} %copy-done.33, ...), custom_call_target="tpu_custom_call" | custom-call | flops 452984832 | bytes 9437184 | tf_op jit(solution)/shard_map/right_far/pallas_call | solution.py:324
  115.6 2.3 collective-permute-start.8
  118.3 3.2 collective-permute-start.10
  122.6 6.2 %collective-permute-done.7.refs_2_ = f32[192,128]{1,0:T(8,128)S(1)} collective-permute-done((f32[192,128]{1,0:T(8,128)}, f32[192,128]{1,0:T(8,128)S(1)}, u32[]{:S(2)}, u32[]{:S(2)}) %collective-permute-start.7) | collective-permute-done | bytes 98336 | tf_op jit(solution)/shard_map/ppermute | solution.py:342
  128.8 2.9 collective-permute-start.12
  131.7 4.0 %collective-permute-done.8.refs_3_ = f32[192,128]{1,0:T(8,128)S(1)} collective-permute-done((f32[192,128]{1,0:T(8,128)}, f32[192,128]{1,0:T(8,128)S(1)}, u32[]{:S(2)}, u32[]{:S(2)}) %collective-permute-start.8) | collective-permute-done | bytes 98336 | tf_op jit(solution)/shard_map/ppermute | solution.py:342
  135.7 9.5 %collective-permute-done.10.refs_5_ = f32[192,128]{1,0:T(8,128)S(1)} collective-permute-done((f32[192,128]{1,0:T(8,128)}, f32[192,128]{1,0:T(8,128)S(1)}, u32[]{:S(2)}, u32[]{:S(2)}) %collective-permute-start.10) | collective-permute-done | bytes 98336 | tf_op jit(solution)/shard_map/ppermute | solution.py:342
  148.1 3.1 collective-permute-start.18
  151.2 11.5 %collective-permute-start.17 = (f32[192,128]{1,0:T(8,128)S(1)}, f32[192,128]{1,0:T(8,128)S(1)}, u32[]{:S(2)}, u32[]{:S(2)}) collective-permute-start(f32[192,128]{1,0:T(8,128)S(1)} %right_sum.2.refs_0_), channel_id=1, source_target_pairs={{0,20},{4,16},{8,28},{12,24},{16,4},{20,0},{24,12},{28,8},{1,21},{... | collective-permute-start | bytes 294920 | tf_op jit(solution)/shard_map/ppermute | solution.py:342
  162.8 3.1 collective-permute-start.15
  165.9 7.0 %collective-permute-start.14 = (f32[192,128]{1,0:T(8,128)S(1)}, f32[192,128]{1,0:T(8,128)S(1)}, u32[]{:S(2)}, u32[]{:S(2)}) collective-permute-start(f32[192,128]{1,0:T(8,128)S(1)} %right_sum.2.refs_0_), channel_id=1, source_target_pairs={{0,8},{4,12},{8,0},{12,4},{16,24},{20,28},{24,16},{28,20},{1,9},{5... | collective-permute-start | bytes 294920 | tf_op jit(solution)/shard_map/ppermute | solution.py:342
  172.9 13.0 %collective-permute-done.17.refs_5_ = f32[192,128]{1,0:T(8,128)S(1)} collective-permute-done((f32[192,128]{1,0:T(8,128)S(1)}, f32[192,128]{1,0:T(8,128)S(1)}, u32[]{:S(2)}, u32[]{:S(2)}) %collective-permute-start.17) | collective-permute-done | bytes 98336 | tf_op jit(solution)/shard_map/ppermute | solution.py:342
  185.9 3.3 collective-permute-done.16.refs_4_
  190.6 7.8 %left.2 = (f32[96,768]{1,0:T(8,128)}, f32[96,768]{1,0:T(8,128)}) custom-call(s32[2]{0:T(128)} %pad_add_fusion.ids_ref, bf16[6,768,512]{2,1,0:T(8,128)(2,1)} %get-tuple-element.94.high_ref.refs_2_, bf16[6,768,512]{2,1,0:T(8,128)(2,1)} %get-tuple-element.95.low_ref.refs_3_, f32[192,128]{1,0:T(8,128)} %copy-done.4, f32[192,128]{1,0:T(8,128)} %copy-done.32, ...), custom_call_target="tpu_custom_call" | custom-call | flops 452984832 | bytes 9437184 | tf_op jit(solution)/shard_map/left/pallas_call | solution.py:324
  198.4 7.9 %left.3 = (f32[96,768]{1,0:T(8,128)}, f32[96,768]{1,0:T(8,128)}) custom-call(s32[2]{0:T(128)} %pad_add_fusion.ids_ref, bf16[6,768,512]{2,1,0:T(8,128)(2,1)} %get-tuple-element.92.high_ref.refs_2_, bf16[6,768,512]{2,1,0:T(8,128)(2,1)} %get-tuple-element.93.low_ref.refs_3_, f32[192,128]{1,0:T(8,128)} %copy-done.4, f32[192,128]{1,0:T(8,128)} %copy-done.32, ...), custom_call_target="tpu_custom_call" | custom-call | flops 452984832 | bytes 9437184 | tf_op jit(solution)/shard_map/left/pallas_call | solution.py:324
  208.2 8.0 %collective-permute-done.21.refs_2_ = f32[96,768]{1,0:T(8,128)S(1)} collective-permute-done((f32[96,768]{1,0:T(8,128)S(1)}, f32[96,768]{1,0:T(8,128)S(1)}, u32[]{:S(2)}, u32[]{:S(2)}) %collective-permute-start.21) | collective-permute-done | bytes 294944 | tf_op jit(solution)/shard_map/ppermute | solution.py:342
  216.3 5.4 %collective-permute-done.22.refs_3_ = f32[96,768]{1,0:T(8,128)S(1)} collective-permute-done((f32[96,768]{1,0:T(8,128)S(1)}, f32[96,768]{1,0:T(8,128)S(1)}, u32[]{:S(2)}, u32[]{:S(2)}) %collective-permute-start.22) | collective-permute-done | bytes 294944 | tf_op jit(solution)/shard_map/ppermute | solution.py:342
  222.7 16.1 %all_to_all.22.parts_ref = f32[8,72,128]{2,1,0:T(8,128)S(1)} all-to-all(f32[8,72,128]{2,1,0:T(8,128)S(1)} %bitcast.17), channel_id=1, replica_groups=mesh['rep'=8,'tp'=4] {'rep'}, dimensions={0} | all-to-all | bytes 589824 | tf_op jit(solution)/shard_map/all_to_all | solution.py:434
  238.8 13.0 %all_to_all.23 = f32[8,72,128]{2,1,0:T(8,128)S(1)} all-to-all(f32[8,72,128]{2,1,0:T(8,128)S(1)} %left_sum.3), channel_id=1, replica_groups=mesh['rep'=8,'tp'=4] {'rep'}, dimensions={0} | all-to-all | bytes 589824 | tf_op jit(solution)/shard_map/all_to_all | solution.py:436
  256.1 6.7 %right_near.3.refs_0_ = f32[192,512]{1,0:T(8,128)} custom-call(s32[2]{0:T(128)} %pad_add_fusion.ids_ref, f32[96,768]{1,0:T(8,128)} %copy-done.1, f32[96,768]{1,0:T(8,128)} %copy-done.12, bf16[6,768,512]{2,1,0:T(8,128)(2,1)} %get-tuple-element.92.high_ref.refs_2_, bf16[6,768,512]{2,1,0:T(8,128)(2,1)} %get-tuple-element.93.low_ref.refs_3_), custom_call_target="tpu_custom_call" | custom-call | flops 452984832 | bytes 9437184 | tf_op jit(solution)/shard_map/right_near/pallas_call | solution.py:324
  266.2 7.0 %right_far.3 = (f32[192,128]{1,0:T(8,128)}, f32[192,128]{1,0:T(8,128)}, f32[192,128]{1,0:T(8,128)}, f32[192,128]{1,0:T(8,128)}, f32[192,128]{1,0:T(8,128)}, /*in...) custom-call(s32[2]{0:T(128)} %pad_add_fusion.ids_ref, f32[96,768]{1,0:T(8,128)} %copy-done.14, ...), custom_call_target="tpu_custom_call" | custom-call | flops 452984832 | bytes 9437184 | tf_op jit(solution)/shard_map/right_far/pallas_call | solution.py:324
  274.4 2.3 collective-permute-start.28
  283.6 5.8 %collective-permute-done.29.refs_4_ = f32[192,128]{1,0:T(8,128)S(1)} collective-permute-done((f32[192,128]{1,0:T(8,128)}, f32[192,128]{1,0:T(8,128)S(1)}, u32[]{:S(2)}, u32[]{:S(2)}) %collective-permute-start.29) | collective-permute-done | bytes 98336 | tf_op jit(solution)/shard_map/ppermute | solution.py:342
  289.4 2.5 collective-permute-start.32
  292.3 4.6 %collective-permute-done.32.refs_7_ = f32[192,128]{1,0:T(8,128)S(1)} collective-permute-done((f32[192,128]{1,0:T(8,128)}, f32[192,128]{1,0:T(8,128)S(1)}, u32[]{:S(2)}, u32[]{:S(2)}) %collective-permute-start.32) | collective-permute-done | bytes 98336 | tf_op jit(solution)/shard_map/ppermute | solution.py:342
  297.9 2.6 collective-permute-start.39
  300.5 2.2 collective-permute-start.38
  302.7 2.9 collective-permute-start.36
  305.9 6.5 %collective-permute-start.34 = (f32[192,128]{1,0:T(8,128)S(1)}, f32[192,128]{1,0:T(8,128)S(1)}, u32[]{:S(2)}, u32[]{:S(2)}) collective-permute-start(f32[192,128]{1,0:T(8,128)S(1)} %right_sum.3.refs_0_), channel_id=1, source_target_pairs={{0,8},{4,12},{8,0},{12,4},{16,24},{20,28},{24,16},{28,20},{1,9},{5... | collective-permute-start | bytes 294920 | tf_op jit(solution)/shard_map/ppermute | solution.py:342
  313.5 3.1 collective-permute-done.37.refs_5_
  317.7 2.2 late_rows.1
  325.2 13.6 %update.2 = (f32[1,12,768,512]{3,2,1,0:T(8,128)}, bf16[8,4,288,512]{3,2,1,0:T(8,128)(2,1)}) custom-call(s32[2]{0:T(128)} %pad_add_fusion.ids_ref, f32[384,768]{1,0:T(8,128)} %copy-done, f32[384,512]{1,0:T(8,128)} %get-tuple-element.137.right_ref, f32[8,288,512]{2,1,0:T(8,128)} %bitcast.19, f32[8,288,512]{2,1,0:T(8,128)} %bitcast.21, ...), custom_call_target="tpu_custom_call" | custom-call | flops 452984832 | bytes 28311552 | tf_op jit(solution)/shard_map/update/pallas_call | solution.py:324
  340.6 13.6 %update.3 = (f32[1,12,768,512]{3,2,1,0:T(8,128)}, bf16[8,4,288,512]{3,2,1,0:T(8,128)(2,1)}) custom-call(s32[2]{0:T(128)} %pad_add_fusion.ids_ref, f32[384,768]{1,0:T(8,128)} %copy-done, f32[384,512]{1,0:T(8,128)} %get-tuple-element.137.right_ref, f32[8,288,512]{2,1,0:T(8,128)} %bitcast.20, ...), custom_call_target="tpu_custom_call", output_to_operand_aliasing={{0}: (7, {}), {1}: (8, {})} | custom-call | flops 452984832 | bytes 28311552 | tf_op jit(solution)/shard_map/update/pallas_call | solution.py:324
  355.0 2.1 collective-permute-done.48.refs_2_
  359.4 8.4 %flat_rows.1 = (f32[288,2048]{1,0:T(8,128)}, f32[288,2048]{1,0:T(8,128)}) custom-call(s32[2]{0:T(128)} %pad_add_fusion.ids_ref, f32[384,768]{1,0:T(8,128)} %copy-done, f32[4,64,512]{2,1,0:T(8,128)} %pad_maximum_fusion.1.near_ref, f32[288,2048]{1,0:T(8,128)} %momentum_ref.1, f32[288,2048]{1,0:T(8,128)} %master_ref.1), custom_call_target="tpu_custom_call" | custom-call | flops 452984832 | bytes 9437184 | tf_op jit(solution)/shard_map/flat_rows/pallas_call | solution.py:324
  367.8 3.6 collective-permute-done.51.refs_6_
  371.4 3.0 collective-permute-done.50.refs_3_
  375.2 6.4 %place_late.2.refs_1_ = bf16[8,4,288,512]{3,2,1,0:T(8,128)(2,1)} custom-call(s32[2]{0:T(128)} %pad_add_fusion.ids_ref, bf16[2,288,512]{2,1,0:T(8,128)(2,1)} %copy-done.5, bf16[2,288,512]{2,1,0:T(8,128)(2,1)} %copy-done.19, bf16[2,288,512]{2,1,0:T(8,128)(2,1)} %copy-done.21, bf16[2,288,512]{2,1,0:T(8,128)(2,1)} %copy-done.23, ...), custom_call_target="tpu_custom_call", output_to_operand_aliasing={{}: (8, {})} | custom-call | tf_op jit(solution)/shard_map/place_late/pallas_call | solution.py:324
  381.6 5.9 %collective-permute-done.52.refs_0_ = bf16[2,288,512]{2,1,0:T(8,128)(2,1)S(1)} collective-permute-done((bf16[2,288,512]{2,1,0:T(8,128)(2,1)S(1)}, bf16[2,288,512]{2,1,0:T(8,128)(2,1)S(1)}, u32[]{:S(2)}, u32[]{:S(2)}) %collective-permute-start.52) | collective-permute-done | bytes 589856 | tf_op jit(solution)/shard_map/ppermute | solution.py:342
  388.3 2.6 place_late.3
  (180 shorter events, 54.8 us)
Async XLA Ops:
  7.2 318.0 %all-gather.5.cloned.1.call-start = ((), (), s32[]{:S(2)}) async-start(), calls=%async_computation.4 | async-start | bytes 5308416 | tf_op jit(solution)/shard_map/all_gather | solution.py:423
  9.4 315.8 %all-gather.7.cloned.1.call-start = ((), (), s32[]{:S(2)}) async-start(), calls=%async_computation.5 | async-start | bytes 5308416 | tf_op jit(solution)/shard_map/all_gather | solution.py:432
  22.7 16.1 %collective-permute-start.1 = (f32[96,768]{1,0:T(8,128)}, f32[96,768]{1,0:T(8,128)S(1)}, u32[]{:S(2)}, u32[]{:S(2)}) collective-permute-start(f32[96,768]{1,0:T(8,128)} %get-tuple-element.98), channel_id=1, source_target_pairs={{0,2},{1,3},{2,0},{3,1},{4,6},{5,7},{6,4},{7,5},{8,10},{9,11},{10,... | collective-permute-start | bytes 884744 | tf_op jit(solution)/shard_map/ppermute | solution.py:342
  25.7 13.1 %collective-permute-start.2 = (f32[96,768]{1,0:T(8,128)}, f32[96,768]{1,0:T(8,128)S(1)}, u32[]{:S(2)}, u32[]{:S(2)}) collective-permute-start(f32[96,768]{1,0:T(8,128)} %get-tuple-element.99), channel_id=1, source_target_pairs={{0,3},{1,2},{2,1},{3,0},{4,7},{5,6},{6,5},{7,4},{8,11},{9,10},{10,... | collective-permute-start | bytes 884744 | tf_op jit(solution)/shard_map/ppermute | solution.py:342
  95.5 9.4 %collective-permute-start.4 = (f32[96,768]{1,0:T(8,128)S(1)}, f32[96,768]{1,0:T(8,128)S(1)}, u32[]{:S(2)}, u32[]{:S(2)}) collective-permute-start(f32[96,768]{1,0:T(8,128)S(1)} %basis.2.first_ref), channel_id=1, source_target_pairs={{0,2},{1,3},{2,0},{3,1},{4,6},{5,7},{6,4},{7,5},{8,10},{9,11},{10,... | collective-permute-start | bytes 884744 | tf_op jit(solution)/shard_map/ppermute | solution.py:342
  114.4 7.6 %collective-permute-start.6 = (f32[192,128]{1,0:T(8,128)}, f32[192,128]{1,0:T(8,128)S(1)}, u32[]{:S(2)}, u32[]{:S(2)}) collective-permute-start(f32[192,128]{1,0:T(8,128)} %get-tuple-element.104), channel_id=1, source_target_pairs={{0,4},{4,0},{8,12},{12,8},{16,20},{20,16},{24,28},{28,24},{1,5},{5... | collective-permute-start | bytes 294920 | tf_op jit(solution)/shard_map/ppermute | solution.py:342
  115.6 13.1 %collective-permute-start.7 = (f32[192,128]{1,0:T(8,128)}, f32[192,128]{1,0:T(8,128)S(1)}, u32[]{:S(2)}, u32[]{:S(2)}) collective-permute-start(f32[192,128]{1,0:T(8,128)} %get-tuple-element.105), channel_id=1, source_target_pairs={{0,8},{4,12},{8,0},{12,4},{16,24},{20,28},{24,16},{28,20},{1,9},{5... | collective-permute-start | bytes 294920 | tf_op jit(solution)/shard_map/ppermute | solution.py:342
  115.6 20.0 %collective-permute-start.8 = (f32[192,128]{1,0:T(8,128)}, f32[192,128]{1,0:T(8,128)S(1)}, u32[]{:S(2)}, u32[]{:S(2)}) collective-permute-start(f32[192,128]{1,0:T(8,128)} %get-tuple-element.106), channel_id=1, source_target_pairs={{0,12},{4,8},{8,4},{12,0},{16,28},{20,24},{24,20},{28,16},{1,13},{... | collective-permute-start | bytes 294920 | tf_op jit(solution)/shard_map/ppermute | solution.py:342
  117.9 17.8 %collective-permute-start.9 = (f32[192,128]{1,0:T(8,128)}, f32[192,128]{1,0:T(8,128)S(1)}, u32[]{:S(2)}, u32[]{:S(2)}) collective-permute-start(f32[192,128]{1,0:T(8,128)} %get-tuple-element.107), channel_id=1, source_target_pairs={{0,16},{4,20},{8,24},{12,28},{16,0},{20,4},{24,8},{28,12},{1,17},{... | collective-permute-start | bytes 294920 | tf_op jit(solution)/shard_map/ppermute | solution.py:342
  118.3 26.9 %collective-permute-start.10 = (f32[192,128]{1,0:T(8,128)}, f32[192,128]{1,0:T(8,128)S(1)}, u32[]{:S(2)}, u32[]{:S(2)}) collective-permute-start(f32[192,128]{1,0:T(8,128)} %get-tuple-element.108), channel_id=1, source_target_pairs={{0,20},{4,16},{8,28},{12,24},{16,4},{20,0},{24,12},{28,8},{1,21},{... | collective-permute-start | bytes 294920 | tf_op jit(solution)/shard_map/ppermute | solution.py:342
  122.0 23.2 %collective-permute-start.11 = (f32[192,128]{1,0:T(8,128)}, f32[192,128]{1,0:T(8,128)S(1)}, u32[]{:S(2)}, u32[]{:S(2)}) collective-permute-start(f32[192,128]{1,0:T(8,128)} %get-tuple-element.109), channel_id=1, source_target_pairs={{0,24},{4,28},{8,16},{12,20},{16,8},{20,12},{24,0},{28,4},{1,25},{... | collective-permute-start | bytes 294920 | tf_op jit(solution)/shard_map/ppermute | solution.py:342
  128.8 16.5 %collective-permute-start.12 = (f32[192,128]{1,0:T(8,128)}, f32[192,128]{1,0:T(8,128)S(1)}, u32[]{:S(2)}, u32[]{:S(2)}) collective-permute-start(f32[192,128]{1,0:T(8,128)} %get-tuple-element.110), channel_id=1, source_target_pairs={{0,28},{4,24},{8,20},{12,16},{16,12},{20,8},{24,4},{28,0},{1,29},{... | collective-permute-start | bytes 294920 | tf_op jit(solution)/shard_map/ppermute | solution.py:342
  146.2 19.7 %collective-permute-start.19 = (f32[192,128]{1,0:T(8,128)S(1)}, f32[192,128]{1,0:T(8,128)S(1)}, u32[]{:S(2)}, u32[]{:S(2)}) collective-permute-start(f32[192,128]{1,0:T(8,128)S(1)} %right_sum.2.refs_0_), channel_id=1, source_target_pairs={{0,28},{4,24},{8,20},{12,16},{16,12},{20,8},{24,4},{28,0},{1,29},{... | collective-permute-start | bytes 294920 | tf_op jit(solution)/shard_map/ppermute | solution.py:342
  148.1 24.8 %collective-permute-start.18 = (f32[192,128]{1,0:T(8,128)S(1)}, f32[192,128]{1,0:T(8,128)S(1)}, u32[]{:S(2)}, u32[]{:S(2)}) collective-permute-start(f32[192,128]{1,0:T(8,128)S(1)} %right_sum.2.refs_0_), channel_id=1, source_target_pairs={{0,24},{4,28},{8,16},{12,20},{16,8},{20,12},{24,0},{28,4},{1,25},{... | collective-permute-start | bytes 294920 | tf_op jit(solution)/shard_map/ppermute | solution.py:342
  151.2 34.6 %collective-permute-start.17 = (f32[192,128]{1,0:T(8,128)S(1)}, f32[192,128]{1,0:T(8,128)S(1)}, u32[]{:S(2)}, u32[]{:S(2)}) collective-permute-start(f32[192,128]{1,0:T(8,128)S(1)} %right_sum.2.refs_0_), channel_id=1, source_target_pairs={{0,20},{4,16},{8,28},{12,24},{16,4},{20,0},{24,12},{28,8},{1,21},{... | collective-permute-start | bytes 294920 | tf_op jit(solution)/shard_map/ppermute | solution.py:342
  162.8 26.5 %collective-permute-start.16 = (f32[192,128]{1,0:T(8,128)S(1)}, f32[192,128]{1,0:T(8,128)S(1)}, u32[]{:S(2)}, u32[]{:S(2)}) collective-permute-start(f32[192,128]{1,0:T(8,128)S(1)} %right_sum.2.refs_0_), channel_id=1, source_target_pairs={{0,16},{4,20},{8,24},{12,28},{16,0},{20,4},{24,8},{28,12},{1,17},{... | collective-permute-start | bytes 294920 | tf_op jit(solution)/shard_map/ppermute | solution.py:342
  162.8 26.5 %collective-permute-start.15 = (f32[192,128]{1,0:T(8,128)S(1)}, f32[192,128]{1,0:T(8,128)S(1)}, u32[]{:S(2)}, u32[]{:S(2)}) collective-permute-start(f32[192,128]{1,0:T(8,128)S(1)} %right_sum.2.refs_0_), channel_id=1, source_target_pairs={{0,12},{4,8},{8,4},{12,0},{16,28},{20,24},{24,20},{28,16},{1,13},{... | collective-permute-start | bytes 294920 | tf_op jit(solution)/shard_map/ppermute | solution.py:342
  165.9 23.3 %collective-permute-start.14 = (f32[192,128]{1,0:T(8,128)S(1)}, f32[192,128]{1,0:T(8,128)S(1)}, u32[]{:S(2)}, u32[]{:S(2)}) collective-permute-start(f32[192,128]{1,0:T(8,128)S(1)} %right_sum.2.refs_0_), channel_id=1, source_target_pairs={{0,8},{4,12},{8,0},{12,4},{16,24},{20,28},{24,16},{28,20},{1,9},{5... | collective-permute-start | bytes 294920 | tf_op jit(solution)/shard_map/ppermute | solution.py:342
  172.9 16.4 %collective-permute-start.13 = (f32[192,128]{1,0:T(8,128)S(1)}, f32[192,128]{1,0:T(8,128)S(1)}, u32[]{:S(2)}, u32[]{:S(2)}) collective-permute-start(f32[192,128]{1,0:T(8,128)S(1)} %right_sum.2.refs_0_), channel_id=1, source_target_pairs={{0,4},{4,0},{8,12},{12,8},{16,20},{20,16},{24,28},{28,24},{1,5},{5... | collective-permute-start | bytes 294920 | tf_op jit(solution)/shard_map/ppermute | solution.py:342
  206.4 9.9 %collective-permute-start.21 = (f32[96,768]{1,0:T(8,128)S(1)}, f32[96,768]{1,0:T(8,128)S(1)}, u32[]{:S(2)}, u32[]{:S(2)}) collective-permute-start(f32[96,768]{1,0:T(8,128)S(1)} %copy-done.41), channel_id=1, source_target_pairs={{0,2},{1,3},{2,0},{3,1},{4,6},{5,7},{6,4},{7,5},{8,10},{9,11},{10,... | collective-permute-start | bytes 884744 | tf_op jit(solution)/shard_map/ppermute | solution.py:342
  207.9 13.7 %collective-permute-start.22 = (f32[96,768]{1,0:T(8,128)S(1)}, f32[96,768]{1,0:T(8,128)S(1)}, u32[]{:S(2)}, u32[]{:S(2)}) collective-permute-start(f32[96,768]{1,0:T(8,128)S(1)} %copy-done.40), channel_id=1, source_target_pairs={{0,3},{1,2},{2,1},{3,0},{4,7},{5,6},{6,5},{7,4},{8,11},{9,10},{10,... | collective-permute-start | bytes 884744 | tf_op jit(solution)/shard_map/ppermute | solution.py:342
  253.9 9.4 %collective-permute-start.24 = (f32[96,768]{1,0:T(8,128)S(1)}, f32[96,768]{1,0:T(8,128)S(1)}, u32[]{:S(2)}, u32[]{:S(2)}) collective-permute-start(f32[96,768]{1,0:T(8,128)S(1)} %basis.3.first_ref), channel_id=1, source_target_pairs={{0,2},{1,3},{2,0},{3,1},{4,6},{5,7},{6,4},{7,5},{8,10},{9,11},{10,... | collective-permute-start | bytes 884744 | tf_op jit(solution)/shard_map/ppermute | solution.py:342
  263.3 39.4 %collective-permute-start.41 = (f32[288,512]{1,0:T(8,128)S(1)}, f32[288,512]{1,0:T(8,128)S(1)}, u32[]{:S(2)}, u32[]{:S(2)}) collective-permute-start(f32[288,512]{1,0:T(8,128)S(1)} %copy-done.17), channel_id=1, source_target_pairs={{0,3},{1,2},{2,1},{3,0},{4,7},{5,6},{6,5},{7,4},{8,11},{9,10},{10,... | collective-permute-start | bytes 1769480 | tf_op jit(solution)/shard_map/ppermute | solution.py:342
  264.9 40.7 %collective-permute-start.40 = (f32[288,512]{1,0:T(8,128)S(1)}, f32[288,512]{1,0:T(8,128)S(1)}, u32[]{:S(2)}, u32[]{:S(2)}) collective-permute-start(f32[288,512]{1,0:T(8,128)S(1)} %copy-done.16), channel_id=1, source_target_pairs={{0,2},{1,3},{2,0},{3,1},{4,6},{5,7},{6,4},{7,5},{8,10},{9,11},{10,... | collective-permute-start | bytes 1769480 | tf_op jit(solution)/shard_map/ppermute | solution.py:342
  273.1 4.9 %collective-permute-start.26 = (f32[192,128]{1,0:T(8,128)}, f32[192,128]{1,0:T(8,128)S(1)}, u32[]{:S(2)}, u32[]{:S(2)}) collective-permute-start(f32[192,128]{1,0:T(8,128)} %get-tuple-element.128), channel_id=1, source_target_pairs={{0,4},{4,0},{8,12},{12,8},{16,20},{20,16},{24,28},{28,24},{1,5},{5... | collective-permute-start | bytes 294920 | tf_op jit(solution)/shard_map/ppermute | solution.py:342
  273.9 5.5 %collective-permute-start.27 = (f32[192,128]{1,0:T(8,128)}, f32[192,128]{1,0:T(8,128)S(1)}, u32[]{:S(2)}, u32[]{:S(2)}) collective-permute-start(f32[192,128]{1,0:T(8,128)} %get-tuple-element.129), channel_id=1, source_target_pairs={{0,8},{4,12},{8,0},{12,4},{16,24},{20,28},{24,16},{28,20},{1,9},{5... | collective-permute-start | bytes 294920 | tf_op jit(solution)/shard_map/ppermute | solution.py:342
  274.4 7.2 %collective-permute-start.28 = (f32[192,128]{1,0:T(8,128)}, f32[192,128]{1,0:T(8,128)S(1)}, u32[]{:S(2)}, u32[]{:S(2)}) collective-permute-start(f32[192,128]{1,0:T(8,128)} %get-tuple-element.130), channel_id=1, source_target_pairs={{0,12},{4,8},{8,4},{12,0},{16,28},{20,24},{24,20},{28,16},{1,13},{... | collective-permute-start | bytes 294920 | tf_op jit(solution)/shard_map/ppermute | solution.py:342
  278.0 11.4 %collective-permute-start.29 = (f32[192,128]{1,0:T(8,128)}, f32[192,128]{1,0:T(8,128)S(1)}, u32[]{:S(2)}, u32[]{:S(2)}) collective-permute-start(f32[192,128]{1,0:T(8,128)} %get-tuple-element.131), channel_id=1, source_target_pairs={{0,16},{4,20},{8,24},{12,28},{16,0},{20,4},{24,8},{28,12},{1,17},{... | collective-permute-start | bytes 294920 | tf_op jit(solution)/shard_map/ppermute | solution.py:342
  279.5 12.8 %collective-permute-start.30 = (f32[192,128]{1,0:T(8,128)}, f32[192,128]{1,0:T(8,128)S(1)}, u32[]{:S(2)}, u32[]{:S(2)}) collective-permute-start(f32[192,128]{1,0:T(8,128)} %get-tuple-element.132), channel_id=1, source_target_pairs={{0,20},{4,16},{8,28},{12,24},{16,4},{20,0},{24,12},{28,8},{1,21},{... | collective-permute-start | bytes 294920 | tf_op jit(solution)/shard_map/ppermute | solution.py:342
  281.6 10.7 %collective-permute-start.31 = (f32[192,128]{1,0:T(8,128)}, f32[192,128]{1,0:T(8,128)S(1)}, u32[]{:S(2)}, u32[]{:S(2)}) collective-permute-start(f32[192,128]{1,0:T(8,128)} %get-tuple-element.133), channel_id=1, source_target_pairs={{0,24},{4,28},{8,16},{12,20},{16,8},{20,12},{24,0},{28,4},{1,25},{... | collective-permute-start | bytes 294920 | tf_op jit(solution)/shard_map/ppermute | solution.py:342
  289.4 7.5 %collective-permute-start.32 = (f32[192,128]{1,0:T(8,128)}, f32[192,128]{1,0:T(8,128)S(1)}, u32[]{:S(2)}, u32[]{:S(2)}) collective-permute-start(f32[192,128]{1,0:T(8,128)} %get-tuple-element.134), channel_id=1, source_target_pairs={{0,28},{4,24},{8,20},{12,16},{16,12},{20,8},{24,4},{28,0},{1,29},{... | collective-permute-start | bytes 294920 | tf_op jit(solution)/shard_map/ppermute | solution.py:342
  297.9 8.0 %collective-permute-start.39 = (f32[192,128]{1,0:T(8,128)S(1)}, f32[192,128]{1,0:T(8,128)S(1)}, u32[]{:S(2)}, u32[]{:S(2)}) collective-permute-start(f32[192,128]{1,0:T(8,128)S(1)} %right_sum.3.refs_0_), channel_id=1, source_target_pairs={{0,28},{4,24},{8,20},{12,16},{16,12},{20,8},{24,4},{28,0},{1,29},{... | collective-permute-start | bytes 294920 | tf_op jit(solution)/shard_map/ppermute | solution.py:342
  300.5 11.9 %collective-permute-start.38 = (f32[192,128]{1,0:T(8,128)S(1)}, f32[192,128]{1,0:T(8,128)S(1)}, u32[]{:S(2)}, u32[]{:S(2)}) collective-permute-start(f32[192,128]{1,0:T(8,128)S(1)} %right_sum.3.refs_0_), channel_id=1, source_target_pairs={{0,24},{4,28},{8,16},{12,20},{16,8},{20,12},{24,0},{28,4},{1,25},{... | collective-permute-start | bytes 294920 | tf_op jit(solution)/shard_map/ppermute | solution.py:342
  302.7 14.0 %collective-permute-start.37 = (f32[192,128]{1,0:T(8,128)S(1)}, f32[192,128]{1,0:T(8,128)S(1)}, u32[]{:S(2)}, u32[]{:S(2)}) collective-permute-start(f32[192,128]{1,0:T(8,128)S(1)} %right_sum.3.refs_0_), channel_id=1, source_target_pairs={{0,20},{4,16},{8,28},{12,24},{16,4},{20,0},{24,12},{28,8},{1,21},{... | collective-permute-start | bytes 294920 | tf_op jit(solution)/shard_map/ppermute | solution.py:342
  302.7 14.1 %collective-permute-start.36 = (f32[192,128]{1,0:T(8,128)S(1)}, f32[192,128]{1,0:T(8,128)S(1)}, u32[]{:S(2)}, u32[]{:S(2)}) collective-permute-start(f32[192,128]{1,0:T(8,128)S(1)} %right_sum.3.refs_0_), channel_id=1, source_target_pairs={{0,16},{4,20},{8,24},{12,28},{16,0},{20,4},{24,8},{28,12},{1,17},{... | collective-permute-start | bytes 294920 | tf_op jit(solution)/shard_map/ppermute | solution.py:342
  305.6 11.2 %collective-permute-start.35 = (f32[192,128]{1,0:T(8,128)S(1)}, f32[192,128]{1,0:T(8,128)S(1)}, u32[]{:S(2)}, u32[]{:S(2)}) collective-permute-start(f32[192,128]{1,0:T(8,128)S(1)} %right_sum.3.refs_0_), channel_id=1, source_target_pairs={{0,12},{4,8},{8,4},{12,0},{16,28},{20,24},{24,20},{28,16},{1,13},{... | collective-permute-start | bytes 294920 | tf_op jit(solution)/shard_map/ppermute | solution.py:342
  305.9 11.9 %collective-permute-start.34 = (f32[192,128]{1,0:T(8,128)S(1)}, f32[192,128]{1,0:T(8,128)S(1)}, u32[]{:S(2)}, u32[]{:S(2)}) collective-permute-start(f32[192,128]{1,0:T(8,128)S(1)} %right_sum.3.refs_0_), channel_id=1, source_target_pairs={{0,8},{4,12},{8,0},{12,4},{16,24},{20,28},{24,16},{28,20},{1,9},{5... | collective-permute-start | bytes 294920 | tf_op jit(solution)/shard_map/ppermute | solution.py:342
  312.4 5.4 %collective-permute-start.33 = (f32[192,128]{1,0:T(8,128)S(1)}, f32[192,128]{1,0:T(8,128)S(1)}, u32[]{:S(2)}, u32[]{:S(2)}) collective-permute-start(f32[192,128]{1,0:T(8,128)S(1)} %right_sum.3.refs_0_), channel_id=1, source_target_pairs={{0,4},{4,0},{8,12},{12,8},{16,20},{20,16},{24,28},{28,24},{1,5},{5... | collective-permute-start | bytes 294920 | tf_op jit(solution)/shard_map/ppermute | solution.py:342
  319.9 18.9 %collective-permute-start.44 = (bf16[2,288,512]{2,1,0:T(8,128)(2,1)S(1)}, bf16[2,288,512]{2,1,0:T(8,128)(2,1)S(1)}, u32[]{:S(2)}, u32[]{:S(2)}) collective-permute-start(bf16[2,288,512]{2,1,0:T(8,128)(2,1)S(1)} %get-tuple-element.172.refs_0_), channel_id=1, source_target_pairs={{0,4},{4,0},{8,12},{12,8},{16,20},{20,16},{24,28},{28,24},{1,5},{5... | collective-permute-start | bytes 1769480 | tf_op jit(solution)/shard_map/ppermute | solution.py:342
  320.7 18.1 %collective-permute-start.43 = (bf16[2,288,512]{2,1,0:T(8,128)(2,1)S(1)}, bf16[2,288,512]{2,1,0:T(8,128)(2,1)S(1)}, u32[]{:S(2)}, u32[]{:S(2)}) collective-permute-start(bf16[2,288,512]{2,1,0:T(8,128)(2,1)S(1)} %get-tuple-element.172.refs_0_), channel_id=1, source_target_pairs={{0,8},{4,12},{8,16},{12,20},{16,24},{20,28},{24,0},{28,4},{1,9},{5... | collective-permute-start | bytes 1769480 | tf_op jit(solution)/shard_map/ppermute | solution.py:565
  323.3 15.5 %collective-permute-start.47 = (f32[64,512]{1,0:T(8,128)S(1)}, f32[64,512]{1,0:T(8,128)S(1)}, u32[]{:S(2)}, u32[]{:S(2)}) collective-permute-start(f32[64,512]{1,0:T(8,128)S(1)} %constant_dynamic-slice_fusion), channel_id=1, source_target_pairs={{0,3},{1,2},{2,1},{3,0},{4,7},{5,6},{6,5},{7,4},{8,11},{9,10},{10,... | collective-permute-start | bytes 393224 | tf_op jit(solution)/shard_map/ppermute | solution.py:342
  323.3 15.4 %collective-permute-start.46 = (f32[64,512]{1,0:T(8,128)S(1)}, f32[64,512]{1,0:T(8,128)S(1)}, u32[]{:S(2)}, u32[]{:S(2)}) collective-permute-start(f32[64,512]{1,0:T(8,128)S(1)} %constant_dynamic-slice_fusion), channel_id=1, source_target_pairs={{0,2},{1,3},{2,0},{3,1},{4,6},{5,7},{6,4},{7,5},{8,10},{9,11},{10,... | collective-permute-start | bytes 393224 | tf_op jit(solution)/shard_map/ppermute | solution.py:342
  324.9 13.9 %collective-permute-start.45 = (f32[64,512]{1,0:T(8,128)S(1)}, f32[64,512]{1,0:T(8,128)S(1)}, u32[]{:S(2)}, u32[]{:S(2)}) collective-permute-start(f32[64,512]{1,0:T(8,128)S(1)} %constant_dynamic-slice_fusion), channel_id=1, source_target_pairs={{0,1},{1,0},{2,3},{3,2},{4,5},{5,4},{6,7},{7,6},{8,9},{9,8},{10,11... | collective-permute-start | bytes 393224 | tf_op jit(solution)/shard_map/ppermute | solution.py:342
  339.5 15.5 %collective-permute-start.49 = (bf16[2,288,512]{2,1,0:T(8,128)(2,1)S(1)}, bf16[2,288,512]{2,1,0:T(8,128)(2,1)S(1)}, u32[]{:S(2)}, u32[]{:S(2)}) collective-permute-start(bf16[2,288,512]{2,1,0:T(8,128)(2,1)S(1)} %collective-permute-done.43.refs_1_), channel_id=1, source_target_pairs={{0,4},{4,0},{8,12},{12,8},{16,20},{20,16},{24,28},{28,24},{1,5},{5... | collective-permute-start | bytes 1769480 | tf_op jit(solution)/shard_map/ppermute | solution.py:342
  340.1 17.0 %collective-permute-start.48 = (bf16[2,288,512]{2,1,0:T(8,128)(2,1)S(1)}, bf16[2,288,512]{2,1,0:T(8,128)(2,1)S(1)}, u32[]{:S(2)}, u32[]{:S(2)}) collective-permute-start(bf16[2,288,512]{2,1,0:T(8,128)(2,1)S(1)} %collective-permute-done.43.refs_1_), channel_id=1, source_target_pairs={{0,8},{4,12},{8,16},{12,20},{16,24},{20,28},{24,0},{28,4},{1,9},{5... | collective-permute-start | bytes 1769480 | tf_op jit(solution)/shard_map/ppermute | solution.py:565
  357.0 14.3 %collective-permute-start.51 = (bf16[2,288,512]{2,1,0:T(8,128)(2,1)S(1)}, bf16[2,288,512]{2,1,0:T(8,128)(2,1)S(1)}, u32[]{:S(2)}, u32[]{:S(2)}) collective-permute-start(bf16[2,288,512]{2,1,0:T(8,128)(2,1)S(1)} %collective-permute-done.48.refs_2_), channel_id=1, source_target_pairs={{0,4},{4,0},{8,12},{12,8},{16,20},{20,16},{24,28},{28,24},{1,5},{5... | collective-permute-start | bytes 1769480 | tf_op jit(solution)/shard_map/ppermute | solution.py:342
  358.5 15.8 %collective-permute-start.50 = (bf16[2,288,512]{2,1,0:T(8,128)(2,1)S(1)}, bf16[2,288,512]{2,1,0:T(8,128)(2,1)S(1)}, u32[]{:S(2)}, u32[]{:S(2)}) collective-permute-start(bf16[2,288,512]{2,1,0:T(8,128)(2,1)S(1)} %collective-permute-done.48.refs_2_), channel_id=1, source_target_pairs={{0,8},{4,12},{8,16},{12,20},{16,24},{20,28},{24,0},{28,4},{1,9},{5... | collective-permute-start | bytes 1769480 | tf_op jit(solution)/shard_map/ppermute | solution.py:565
  374.4 13.1 %collective-permute-start.52 = (bf16[2,288,512]{2,1,0:T(8,128)(2,1)S(1)}, bf16[2,288,512]{2,1,0:T(8,128)(2,1)S(1)}, u32[]{:S(2)}, u32[]{:S(2)}) collective-permute-start(bf16[2,288,512]{2,1,0:T(8,128)(2,1)S(1)} %collective-permute-done.50.refs_3_), channel_id=1, source_target_pairs={{0,4},{4,0},{8,12},{12,8},{16,20},{20,16},{24,28},{28,24},{1,5},{5... | collective-permute-start | bytes 1769480 | tf_op jit(solution)/shard_map/ppermute | solution.py:342
  (49 other events, 439.0 us)
Sparse Core Ops, SparseCore 0:
  10.8 92.6 all-gather.4
  106.2 106.4 all-gather.6

commit v4 on v3

--- a/solution.py
+++ b/solution.py
@@ -17,7 +17,6 @@
 LEARNING_RATE = 0.5
 HIGHEST = lax.Precision.HIGHEST
 LANES = 128
-EARLY = 2
 F32, BF16 = jnp.float32, jnp.bfloat16
 SCALARS = pl.BlockSpec(memory_space=pltpu.SMEM)
 
@@ -87,26 +86,6 @@
     return values[0]
 
 
-def streamed(sources, buffers, sems, picked=lambda k: (k,)):
-    step = pl.program_id(0)
-
-    def copies(k):
-        return [
-            pltpu.make_async_copy(source.at[picked(k)], buffer.at[k], sems.at[which, k])
-            for which, (source, buffer) in enumerate(zip(sources, buffers))
-        ]
-
-    @pl.when(step == 0)
-    def _():
-        for k in range(buffers[0].shape[0]):
-            for copy in copies(k):
-                copy.start()
-
-    for copy in copies(step):
-        copy.wait()
-    return [buffer[step] for buffer in buffers]
-
-
 def put_left(left, step, left_refs, per_tp):
     for which, left_ref in enumerate(left_refs):
 
@@ -115,19 +94,15 @@
             left_ref[...] = left
 
 
-def first_left_kernel(per_tp, picked, ids_ref, grads_ref, error_ref, query_ref, high_ref, low_ref, *refs):
-    left_refs, (grads_buffer, error_buffer, sems) = refs[:-3], refs[-3:]
-    grads, error = streamed(
-        (grads_ref, error_ref), (grads_buffer, error_buffer), sems, lambda k: (0, picked(k, ids_ref))
-    )
-    high, low = two_terms(grads.astype(F32) + error)
+def first_left_kernel(per_tp, ids_ref, grads_ref, error_ref, query_ref, high_ref, low_ref, *left_refs):
+    high, low = two_terms(grads_ref[0, 0].astype(F32) + error_ref[0, 0])
     high_ref[0] = high
     low_ref[0] = low
     put_left(small_by_large(query_ref[0], high, low, True), pl.program_id(0), left_refs, per_tp)
 
 
 def left_kernel(per_tp, half, ids_ref, high_ref, low_ref, *refs):
-    parts, left_refs, (scratch, current), stream = refs[:-7], refs[-7:-5], refs[-5:-3], refs[-3:]
+    parts, left_refs, (scratch, current) = refs[:-4], refs[-4:-2], refs[-2:]
     step = pl.program_id(0)
     rank = left_refs[0].shape[0]
     rows = current.shape[0]
@@ -138,9 +113,8 @@
         join_parts(scratch, ids_ref[0], parts)
         current[...] = read_lanes(scratch.at[half * lanes : (half + 1) * lanes], rows)
 
-    high, low = streamed((high_ref, low_ref), stream[:2], stream[2])
     own = current[part_at(step, rank), :]
-    put_left(small_by_large(own, high, low, True), step, left_refs, per_tp)
+    put_left(small_by_large(own, high_ref[0], low_ref[0], True), step, left_refs, per_tp)
 
 
 def split_kernel(tps, *refs):
@@ -193,9 +167,7 @@
     rank = first_ref.shape[0] // per_tp
     at = part_at(step % per_tp, rank)
     own = jnp.where(step // per_tp == 0, first_ref[at, :], second_ref[at, :])
-    refs, stream = refs[:-3], refs[-3:]
-    high, low = streamed((high_ref, low_ref), stream[:2], stream[2])
-    product_now = small_by_large(own, high, low, False)
+    product_now = small_by_large(own, high_ref[0], low_ref[0], False)
     if len(refs) == 1:
         refs[0][...] = product_now
         return
@@ -227,10 +199,10 @@
     return dot(jnp.concatenate([high, low, high], axis=1), stacked(right))
 
 
-def late_kernel(early, unit, per_tp, rank, ids_ref, basis_ref, *refs):
-    query_ref, weights_ref, lanes, approx = refs[-4:]
-    late = weights_ref.shape[0]
-    part_refs, base_refs = refs[: -4 - late], refs[-4 - late : -4]
+def late_kernel(unit, per_tp, rank, ids_ref, basis_ref, *refs):
+    query_ref, *weight_refs, lanes, approx = refs[-5:]
+    tps = query_ref.shape[0] // (per_tp * rank)
+    part_refs, base_refs = refs[: -5 - tps], refs[-5 - tps : -5]
     rows = query_ref.shape[0] // 2
     tp = ids_ref[1]
     join_parts(lanes, ids_ref[0], part_refs)
@@ -242,11 +214,12 @@
             query_ref[part_at(owner, rows // 2), :] = value[which * (rows // 2) : (which + 1) * (rows // 2)]
     units = approx.shape[0] // unit
     rows_of_update(basis_ref, query_ref, approx, ids_ref[0] * units, unit, per_tp, rank, tp, 0)
-    for which in range(late):
-        base = base_refs[which][...]
-        owner = tp ^ (early + which)
-        own = approx[part_at(owner, base.shape[0]), :]
-        weights_ref[owner % late] = (base - LEARNING_RATE * own).astype(BF16)
+    for offset, base_ref in enumerate(base_refs):
+        at = part_at(tp ^ offset, base_ref.shape[0])
+        approx[at, :] = base_ref[...] - LEARNING_RATE * approx[at, :]
+    for half, weight_ref in enumerate(weight_refs):
+        per_half = weight_ref.shape[0]
+        weight_ref[...] = approx[half * per_half : (half + 1) * per_half].astype(BF16)
 
 
 def owner_of(step, rep, replicas):
@@ -254,31 +227,18 @@
     return ((rep ^ (step // half)) + 2 * replicas - 2 * (step % half)) % replicas
 
 
-def place_kernel(ids_ref, *refs):
-    for at, part_ref in enumerate(refs[:-2]):
+def place_kernel(count, ids_ref, *refs):
+    for at, part_ref in enumerate(refs[:count]):
 
         @pl.when(pl.program_id(0) == at)
         def _():
-            refs[-1][0] = part_ref[...]
-
-
-def update_kernel(early, per_tp, rank, ids_ref, basis_ref, right_ref, *refs):
-    new_error_ref, weights_ref, approx = refs[-3:]
-    base_refs, (high_ref, low_ref) = refs[:early], refs[early : early + 2]
-    matrix = pl.program_id(1)
-    at = part_at(matrix, rank)
-    own = product(basis_ref[at, :], right_ref[at, :])
-    approx[part_at(matrix, own.shape[0]), :] = own
-    new_error_ref[0, 0] = high_ref[0].astype(F32) + low_ref[0].astype(F32) - own
-
-    @pl.when(matrix == per_tp - 1)
-    def _():
-        replicas, tps, own_rows, _ = weights_ref.shape
-        for replica in range(replicas):
-            for offset, base_ref in enumerate(base_refs):
-                owner = ids_ref[1] ^ offset
-                rows = approx[part_at(replica * tps + owner, own_rows), :]
-                weights_ref[replica, owner] = (base_ref[replica] - LEARNING_RATE * rows).astype(BF16)
+            refs[-1][0, 0] = part_ref[...]
+
+
+def update_kernel(rank, ids_ref, basis_ref, right_ref, high_ref, low_ref, *refs):
+    at = part_at(pl.program_id(0), rank)
+    approx = product(basis_ref[at, :], right_ref[at, :])
+    refs[-1][0, 0] = high_ref[0].astype(F32) + low_ref[0].astype(F32) - approx
 
 
 def flat_kernel(unit, per_tp, rank, matrices, ids_ref, basis_ref, near_ref, momentum_ref, master_ref, new_momentum_ref, new_master_ref, approx):
@@ -332,7 +292,7 @@
         ),
         out_shape=out_shape,
         input_output_aliases=aliases or {},
-        compiler_params=grant(60),
+        compiler_params=grant(20),
         name=name,
         cost_estimate=pl.CostEstimate(flops=flops, bytes_accessed=moved, transcendentals=0),
     )(ids, *operands)
@@ -370,12 +330,6 @@
         return (at[1] ^ (2 * half + k // per_tp)) * per_tp + k % per_tp
 
     term_spec = pl.BlockSpec((1, width, cols), lambda k, at: (k, 0, 0))
-    read_spec = pl.BlockSpec(memory_space=pl.ANY)
-    streams = [
-        pltpu.VMEM((per_half, width, cols), BF16),
-        pltpu.VMEM((per_half, width, cols), BF16),
-        pltpu.SemaphoreType.DMA((2, per_half)),
-    ]
     term_shape = shape(per_half, width, cols, dtype=BF16)
     left_specs = [
         pl.BlockSpec((rank, width), lambda k, at, which=which: (jnp.clip(k - which * per_tp, 0, per_tp - 1), 0))
@@ -390,37 +344,24 @@
     for half in reversed(range(halves)):
         picked = functools.partial(matrix_of, half)
         high, low, *out = grid_call(
-            functools.partial(first_left_kernel, per_tp, picked),
+            functools.partial(first_left_kernel, per_tp),
             "first_left",
             ids,
             (per_half,),
             [
-                read_spec,
-                read_spec,
+                pl.BlockSpec((1, 1, width, cols), lambda k, at, picked=picked: (0, picked(k, at), 0, 0)),
+                pl.BlockSpec((1, 1, width, cols), lambda k, at, picked=picked: (0, picked(k, at), 0, 0)),
                 pl.BlockSpec((1, rank, cols), lambda k, at, picked=picked: (picked(k, at), 0, 0)),
             ],
             [term_spec, term_spec, *left_specs],
             [term_shape, term_shape, *left_shapes],
             (grads, error, query),
-            [
-                pltpu.VMEM((per_half, width, cols), BF16),
-                pltpu.VMEM((per_half, width, cols), F32),
-                pltpu.SemaphoreType.DMA((2, per_half)),
-            ],
             flops=flops,
             moved=10 * elements,
         )
         terms[half] = (high, low)
         lefts[2 * half : 2 * half + 2] = out
 
-    def base_at(offset, new_values, old_values):
-        column = (tp ^ offset) * cols
-        piece = lax.dynamic_slice_in_dim(new_values, column, cols, 1)
-        piece = piece - (LEARNING_RATE * MOMENTUM_DECAY) * lax.dynamic_slice_in_dim(old_values, column, cols, 1)
-        return piece if offset == 0 else swap(piece, "tp", tps, offset)
-
-    base = [base_at(0, master, momentum)]
-    gathered = [lax.all_gather(base[0], "rep")]
     for power_pass in range(ROUNDS):
         met = [lefts[0]] + [swap(lefts[offset], "tp", tps, offset) for offset in range(1, tps)]
         parts = whole_call(
@@ -428,8 +369,12 @@
         )
         if power_pass == 0:
             parts, new_values, old_values = lax.optimization_barrier((parts, master, momentum))
-            base += [base_at(offset, new_values, old_values) for offset in range(1, tps)]
-            gathered += [lax.all_gather(base[offset], "rep") for offset in range(1, EARLY)]
+            base = []
+            for offset in range(tps):
+                column = (tp ^ offset) * cols
+                piece = lax.dynamic_slice_in_dim(new_values, column, cols, 1)
+                piece = piece - (LEARNING_RATE * MOMENTUM_DECAY) * lax.dynamic_slice_in_dim(old_values, column, cols, 1)
+                base.append(piece if offset == 0 else swap(piece, "tp", tps, offset))
         parts = parts.reshape(replicas, left_part, LANES)
         parts = lax.all_to_all(parts, "rep", split_axis=0, concat_axis=0, tiled=True)
         parts = whole_call(total_kernel, "left_sum", shape(*parts.shape), [parts])
@@ -444,11 +389,10 @@
             "right_near",
             ids,
             (per_half,),
-            [whole_spec(tp_rows, width), whole_spec(tp_rows, width), read_spec, read_spec],
+            [whole_spec(tp_rows, width), whole_spec(tp_rows, width), term_spec, term_spec],
             pl.BlockSpec((rank, cols), lambda k, at: (k, 0)),
             shape(2 * tp_rows, cols),
             (*bases, *terms[0]),
-            streams,
             flops=flops,
             moved=4 * elements,
         )
@@ -459,11 +403,11 @@
             "right_far",
             ids,
             (per_half,),
-            [whole_spec(tp_rows, width), whole_spec(tp_rows, width), read_spec, read_spec, whole_spec(2 * tp_rows, cols)],
+            [whole_spec(tp_rows, width), whole_spec(tp_rows, width), term_spec, term_spec, whole_spec(2 * tp_rows, cols)],
             [whole_spec(right_part, LANES)] * replicas,
             [shape(right_part, LANES)] * replicas,
             (*bases[2:], *terms[1], before),
-            [pltpu.VMEM((right_part * replicas, LANES), F32), pltpu.VMEM((2 * tp_rows, cols), F32), *streams],
+            [pltpu.VMEM((right_part * replicas, LANES), F32), pltpu.VMEM((2 * tp_rows, cols), F32)],
             flops=flops,
             moved=4 * elements,
         )
@@ -471,34 +415,29 @@
         part = whole_call(functools.partial(sum_kernel, 1.0 / replicas), "right_sum", shape(right_part, LANES), met)
         rights = spread(part, "rep", replicas)
         if power_pass < ROUNDS - 1:
-            near_parts = rights
             for half in reversed(range(halves)):
                 lefts[2 * half : 2 * half + 2] = grid_call(
                     functools.partial(left_kernel, per_tp, half),
                     "left",
                     ids,
                     (per_half,),
-                    [read_spec, read_spec] + [whole_spec(right_part, LANES)] * replicas,
+                    [term_spec, term_spec] + [whole_spec(right_part, LANES)] * replicas,
                     left_specs,
                     left_shapes,
-                    (*terms[half], *near_parts),
-                    [pltpu.VMEM((right_part * replicas, LANES), F32), pltpu.VMEM((2 * tp_rows, cols), F32), *streams],
+                    (*terms[half], *rights),
+                    [pltpu.VMEM((right_part * replicas, LANES), F32), pltpu.VMEM((2 * tp_rows, cols), F32)],
                     flops=flops,
-                    moved=4 * elements,
+                    moved=10 * elements,
                 )
-                if half:
-                    far, near_parts = lax.optimization_barrier((lefts[2 * half : 2 * half + 2], rights))
-                    lefts[2 * half : 2 * half + 2] = far
 
     all_bases = jnp.concatenate(bases, axis=0)
-    late = tps - EARLY
     rep_rows = tps * own_rows
     unit = math.gcd(rep_rows, width)
-    right, block = whole_call(
-        functools.partial(late_kernel, EARLY, unit, per_tp, rank),
+    right, *block = whole_call(
+        functools.partial(late_kernel, unit, per_tp, rank),
         "late_rows",
-        [shape(matrices * rank, cols), shape(late, own_rows, cols, dtype=BF16)],
-        [all_bases, *rights, *base[EARLY:]],
+        [shape(matrices * rank, cols)] + [shape(rep_rows // 2, cols, dtype=BF16)] * 2,
+        [all_bases, *rights, *base],
         ids,
         [pltpu.VMEM((right_part * replicas, LANES), F32), pltpu.VMEM((rep_rows, cols), F32)],
     )
@@ -506,32 +445,50 @@
     first = jnp.minimum(rep * rep_rows // width, matrices - spans)
     near = lax.dynamic_slice_in_dim(right, first * rank, spans * rank, 0)
 
-    def update(half, ids, outs):
-        def owner(s, at):
-            return at[1] ^ (2 * half + s)
-
+    def update(slot, ids, before):
+        half, start = slot // 2, slot % 2 * per_tp
         return grid_call(
-            functools.partial(update_kernel, EARLY, per_tp, rank),
+            functools.partial(update_kernel, rank),
             "update",
             ids,
-            (2, per_tp),
+            (per_tp,),
             [
-                pl.BlockSpec((tp_rows, width), lambda s, j, at: (2 * half + s, 0)),
-                pl.BlockSpec((tp_rows, cols), lambda s, j, at: (owner(s, at), 0)),
+                pl.BlockSpec((tp_rows, width), lambda j, at: (slot, 0)),
+                pl.BlockSpec((tp_rows, cols), lambda j, at: (at[1] ^ slot, 0)),
+                pl.BlockSpec((1, width, cols), lambda j, at: (start + j, 0, 0)),
+                pl.BlockSpec((1, width, cols), lambda j, at: (start + j, 0, 0)),
             ]
-            + [pl.BlockSpec((replicas // tps, own_rows, cols), lambda s, j, at: (owner(s, at), 0, 0))] * EARLY
-            + [pl.BlockSpec((1, width, cols), lambda s, j, at: (s * per_tp + j, 0, 0))] * 2
-            + [pl.BlockSpec(memory_space=pl.ANY)] * len(outs),
-            [
-                pl.BlockSpec((1, 1, width, cols), lambda s, j, at: (0, owner(s, at) * per_tp + j, 0, 0)),
-                pl.BlockSpec((replicas // tps, tps, own_rows, cols), lambda s, j, at: (owner(s, at), 0, 0, 0)),
-            ],
-            [shape(*error.shape), shape(replicas, tps, own_rows, cols, dtype=BF16)],
-            (all_bases, right, *gathered, *terms[half], *outs),
-            [pltpu.VMEM((per_tp * width, cols), F32)],
-            aliases={5 + EARLY + at: at for at in range(len(outs))},
-            flops=2 * 3 * rank * error.size // 2,
-            moved=6 * error.size,
+            + [pl.BlockSpec(memory_space=pl.ANY)] * len(before),
+            pl.BlockSpec((1, 1, width, cols), lambda j, at: (0, (at[1] ^ slot) * per_tp + j, 0, 0)),
+            shape(*error.shape),
+            (all_bases, right, *terms[half], *before),
+            aliases={5: 0} if before else None,
+            flops=2 * 3 * rank * error.size // tps,
+            moved=8 * error.size // tps,
+        )
+
+    def place(pieces, ids, before):
+        count = len(pieces)
+
+        def where(k, at):
+            at_half, step = pieces[-1][1:]
+            for index in range(count - 1):
+                at_half = jnp.where(k == index, pieces[index][1], at_half)
+                step = jnp.where(k == index, pieces[index][2], step)
+            return (owner_of(step, at[0], replicas), at_half, 0, 0)
+
+        return grid_call(
+            functools.partial(place_kernel, count),
+            "place",
+            ids,
+            (count,),
+            [pl.BlockSpec((rep_rows // 2, cols), lambda k, at: (0, 0))] * count
+            + [pl.BlockSpec(memory_space=pl.ANY)] * len(before),
+            pl.BlockSpec((1, 1, rep_rows // 2, cols), where),
+            shape(replicas, 2, rep_rows // 2, cols, dtype=BF16),
+            (*[piece[0] for piece in pieces], *before),
+            aliases={1 + count: 0} if before else None,
+            moved=4 * count * rep_rows * cols,
         )
 
     def flat_rows(ids, all_bases, near):
@@ -556,40 +513,40 @@
         )
 
     ring = [(index, (index + 2) % replicas) for index in range(replicas)]
-    held, beside = [block], []
     stages = replicas // 2
-    outs, flat = (), ()
+    held, beside = block, [None, None]
+    pieces = [(block[half], half, 0) for half in range(2)]
+    errors, flat, weights = (), (), ()
     for stage in range(stages):
-        beside.append(swap(held[-1], "rep", replicas, 1))
         if stage < stages - 1:
-            held.append(lax.ppermute(held[-1], "rep", ring))
+            onward = [lax.ppermute(held[half], "rep", ring) for half in range(2)]
+            beside = [swap(held[half], "rep", replicas, 1) for half in range(2)]
+            arrived = [(onward[half], half, stage + 1) for half in range(2)]
+            arrived += [(beside[half], half, stages + stage) for half in range(2)]
+        else:
+            arrived = [
+                (swap(held[0], "rep", replicas, 1), 0, 2 * stages - 1),
+                (lax.ppermute(beside[1], "rep", ring), 1, 2 * stages - 1),
+            ]
         if stage == 0:
             near = spread(near, "tp", tps)
-        if stage < 2:
-            outs = tuple(update(stage, ids, outs))
-        elif stage == 2:
+            for slot in range(tps):
+                errors = (update(slot, ids, errors),)
+        if stage == 1:
             flat = flat_rows(ids, all_bases, jnp.stack(near))
+        if stage > 0:
+            weights = (place(pieces, ids, weights),)
+        arrays = [piece[0] for piece in arrived]
         if stage < stages - 1:
-            ids, outs, flat, held, beside, near = lax.optimization_barrier((ids, outs, flat, held, beside, near))
+            ids, errors, flat, weights, near, arrays = lax.optimization_barrier((ids, errors, flat, weights, near, arrays))
+            held, beside = arrays[:2], arrays[2:]
+        if stage == 0:
+            arrived = [(block[half], half, 0) for half in range(2)] + arrived
+            arrays = [*block, *arrays]
+        pieces = [(array, *piece[1:]) for array, piece in zip(arrays, arrived)]
+    weights = place(pieces, ids, weights).reshape(matrices, width, cols)
+    (new_error,) = errors
     new_momentum, new_master = flat
-    new_error, weights = outs
-    pieces = [*held, *beside]
-    for some in (range(len(pieces) - 1), range(len(pieces) - 1, len(pieces))):
-        weights = grid_call(
-            place_kernel,
-            "place_late",
-            ids,
-            (len(some),),
-            [pl.BlockSpec((late, own_rows, cols), lambda k, at: (0, 0, 0))] * len(some) + [pl.BlockSpec(memory_space=pl.ANY)],
-            pl.BlockSpec(
-                (1, late, own_rows, cols),
-                lambda k, at, some=some: (owner_of(k + some[0], at[0], replicas), (at[1] ^ EARLY) // late, 0, 0),
-            ),
-            shape(*weights.shape, dtype=BF16),
-            (*[pieces[at] for at in some], weights),
-            aliases={1 + len(some): 0},
-        )
-    weights = weights.reshape(matrices, width, cols)
     return (new_error, right.reshape(matrices, rank, cols), new_momentum, new_master, weights)
 
 

time: 399 us -> 380 us (0.952)
  waiting for transfers between devices: 89 us -> 140 us
  Pallas kernels: 119 us -> 78.4 us
  blocking collectives: 75.4 us -> 60.9 us
  between operations: 14.5 us -> 1.04 us
  local copies, waits for them, and re-layouts: 11.4 us -> 16.3 us
  other arithmetic: 7.64 us -> 3.53 us
    pallas_call x13 -> x17, Pallas kernels: 113 us -> 71.3 us  [grid_call(): pl.pallas_call(kernel, grid_spec=pltpu.PrefetchScalarGridSpec(num_scalar_...]
    ppermute x3 -> x7, waiting for transfers between devices: 5.07 us -> 41.3 us  [the longest x6 38.7 us: local(): onward = [lax.ppermute(held[half], 'rep', ring) for half in range(2)]]
    ppermute x50 -> x53, starting transfers between devices: 78.1 us -> 54.7 us  [swap(): lax.ppermute(x, axis, [(index, index ^ offset) for index in range(size)])]
    ppermute x3 -> x7, starting transfers between devices: 2.16 us -> 24.7 us  [the longest x6 24.4 us: local(): onward = [lax.ppermute(held[half], 'rep', ring) for half in range(2)]]
    ppermute x50 -> x53, waiting for transfers between devices: 83.9 us -> 98.5 us  [swap(): lax.ppermute(x, axis, [(index, index ^ offset) for index in range(size)])]
    all_to_all x4, blocking collectives: 75.4 us -> 60.9 us  [local(): lax.all_to_all(parts, 'rep', split_axis=0, concat_axis=0, tiled=True)]
    unnamed x84 -> x48, local copies, waits for them, and re-layouts: 10.5 us -> 15.4 us
  transfers between devices with their start and end apart: 55 -> 60, of which waited for: 27 -> 29; matrix products, arithmetic and copies ran while one was open for 2% -> 1% of each run, Pallas kernels for 29% -> 14%
where the time goes in v4:
time: 380 us; the launch traced here: 379 us
  waiting for transfers between devices  140 us (37%)
  starting transfers between devices  79.4 us (21%)
  Pallas kernels  78.4 us (21%)
  blocking collectives  60.9 us (16%)
  local copies, waits for them, and re-layouts  16.3 us (4%)
    ppermute x53, waiting for transfers between devices, swap(): lax.ppermute(x, axis, [(index, index ^ offset) for index in range(size)])  98.5 us
    pallas_call x17, Pallas kernels, grid_call(): pl.pallas_call(kernel, grid_spec=pltpu.PrefetchScalarGridSpec(num_scalar_...  71.3 us
    all_to_all x4, blocking collectives, local(): lax.all_to_all(parts, 'rep', split_axis=0, concat_axis=0, tiled=True)  60.9 us
    ppermute x53, starting transfers between devices, swap(): lax.ppermute(x, axis, [(index, index ^ offset) for index in range(size)])  54.7 us
    ppermute x6, waiting for transfers between devices, local(): onward = [lax.ppermute(held[half], 'rep', ring) for half in range(2)]  38.7 us
    ppermute x6, starting transfers between devices, local(): onward = [lax.ppermute(held[half], 'rep', ring) for half in range(2)]  24.4 us
    unnamed x48, local copies, waits for them, and re-layouts  15.4 us
  transfers between devices with their start and end apart: 60, of which 29 were waited for; matrix products, arithmetic and copies ran while one was open for 1% of the time, Pallas kernels for 14%

profile of v4, /device:TPU:0, one launch (start us, length us, event | category | flops | bytes accessed | tf_op | source)
XLA Modules:
  0.0 379.4 jit_solution(713036598593531269)
XLA Ops:
  0.7 3.7 copy-done.8
  5.5 7.6 %first_left.2 = (bf16[6,768,512]{2,1,0:T(8,128)(2,1)S(1)}, bf16[6,768,512]{2,1,0:T(8,128)(2,1)S(1)}, f32[96,768]{1,0:T(8,128)S(1)}, f32[96,768]{1,0:T(8,128)S(1)}) custom-call(s32[2]{0:T(128)S(1)} %pad_add_fusion.ids_ref, bf16[1,12,768,512]{3,2,1,0:T(8,128)(2,1)S(1)} %copy-done.8, f32[1,12,768,512]{3,2,1,0:T(8,128)} %error_ref.3, f32[12,32,512]{2,1,0:T(8,128)S(1)} %copy-done.12), custom_call_target="tpu_custom_call" | custom-call | flops 452984832 | bytes 23592960 | tf_op jit(solution)/shard_map/first_left/pallas_call | solution.py:284
  13.7 9.4 %first_left.3 = (bf16[6,768,512]{2,1,0:T(8,128)(2,1)S(1)}, bf16[6,768,512]{2,1,0:T(8,128)(2,1)S(1)}, f32[96,768]{1,0:T(8,128)S(1)}, f32[96,768]{1,0:T(8,128)S(1)}) custom-call(s32[2]{0:T(128)S(1)} %pad_add_fusion.ids_ref, bf16[1,12,768,512]{3,2,1,0:T(8,128)(2,1)S(1)} %copy-done.8, f32[1,12,768,512]{3,2,1,0:T(8,128)} %error_ref.3, f32[12,32,512]{2,1,0:T(8,128)S(1)} %copy-done.13), custom_call_target="tpu_custom_call" | custom-call | flops 452984832 | bytes 23592960 | tf_op jit(solution)/shard_map/first_left/pallas_call | solution.py:284
  23.1 2.8 collective-permute-start.1
  25.9 7.8 %collective-permute-done.1.refs_2_ = f32[96,768]{1,0:T(8,128)S(1)} collective-permute-done((f32[96,768]{1,0:T(8,128)S(1)}, f32[96,768]{1,0:T(8,128)S(1)}, u32[]{:S(2)}, u32[]{:S(2)}) %collective-permute-start.1) | collective-permute-done | bytes 294944 | tf_op jit(solution)/shard_map/ppermute | solution.py:302
  33.7 5.2 %collective-permute-done.2.refs_3_ = f32[96,768]{1,0:T(8,128)S(1)} collective-permute-done((f32[96,768]{1,0:T(8,128)S(1)}, f32[96,768]{1,0:T(8,128)S(1)}, u32[]{:S(2)}, u32[]{:S(2)}) %collective-permute-start.2) | collective-permute-done | bytes 294944 | tf_op jit(solution)/shard_map/ppermute | solution.py:302
  39.0 16.8 %all_to_all.20.parts_ref = f32[8,72,128]{2,1,0:T(8,128)S(1)} all-to-all(f32[8,72,128]{2,1,0:T(8,128)S(1)} %bitcast.19), channel_id=1, replica_groups=mesh['rep'=8,'tp'=4] {'rep'}, dimensions={0} | all-to-all | bytes 589824 | tf_op jit(solution)/shard_map/all_to_all | solution.py:379
  55.9 13.0 %all_to_all.21 = f32[8,72,128]{2,1,0:T(8,128)S(1)} all-to-all(f32[8,72,128]{2,1,0:T(8,128)S(1)} %left_sum.2), channel_id=1, replica_groups=mesh['rep'=8,'tp'=4] {'rep'}, dimensions={0} | all-to-all | bytes 589824 | tf_op jit(solution)/shard_map/all_to_all | solution.py:381
  72.5 2.8 right_near.2.refs_0_
  75.3 5.1 %collective-permute-done.4.first_ref = f32[96,768]{1,0:T(8,128)S(1)} collective-permute-done((f32[96,768]{1,0:T(8,128)S(1)}, f32[96,768]{1,0:T(8,128)S(1)}, u32[]{:S(2)}, u32[]{:S(2)}) %collective-permute-start.4) | collective-permute-done | bytes 294944 | tf_op jit(solution)/shard_map/ppermute | solution.py:302
  81.9 2.9 right_far.2
  90.8 7.3 %collective-permute-done.10.refs_5_ = f32[192,128]{1,0:T(8,128)S(1)} collective-permute-done((f32[192,128]{1,0:T(8,128)S(1)}, f32[192,128]{1,0:T(8,128)S(1)}, u32[]{:S(2)}, u32[]{:S(2)}) %collective-permute-start.10) | collective-permute-done | bytes 98336 | tf_op jit(solution)/shard_map/ppermute | solution.py:302
  100.1 4.3 %collective-permute-done.8.refs_3_ = f32[192,128]{1,0:T(8,128)S(1)} collective-permute-done((f32[192,128]{1,0:T(8,128)S(1)}, f32[192,128]{1,0:T(8,128)S(1)}, u32[]{:S(2)}, u32[]{:S(2)}) %collective-permute-start.8) | collective-permute-done | bytes 98336 | tf_op jit(solution)/shard_map/ppermute | solution.py:302
  109.8 3.7 collective-permute-start.17
  117.0 6.4 %collective-permute-done.16.refs_4_ = f32[192,128]{1,0:T(8,128)S(1)} collective-permute-done((f32[192,128]{1,0:T(8,128)S(1)}, f32[192,128]{1,0:T(8,128)S(1)}, u32[]{:S(2)}, u32[]{:S(2)}) %collective-permute-start.16) | collective-permute-done | bytes 98336 | tf_op jit(solution)/shard_map/ppermute | solution.py:302
  123.4 3.0 collective-permute-done.17.refs_5_
  126.5 4.2 %left.3 = (f32[96,768]{1,0:T(8,128)S(1)}, f32[96,768]{1,0:T(8,128)S(1)}) custom-call(s32[2]{0:T(128)S(1)} %pad_add_fusion.ids_ref, bf16[6,768,512]{2,1,0:T(8,128)(2,1)S(1)} %get-tuple-element.81.high_ref, bf16[6,768,512]{2,1,0:T(8,128)(2,1)S(1)} %get-tuple-element.82.low_ref, f32[192,128]{1,0:T(8,128)S(1)} %right_sum.2.refs_0_, ...), custom_call_target="tpu_custom_call" | custom-call | flops 452984832 | bytes 23592960 | tf_op jit(solution)/shard_map/left/pallas_call | solution.py:284
  132.2 4.2 %left.2 = (f32[96,768]{1,0:T(8,128)S(1)}, f32[96,768]{1,0:T(8,128)S(1)}) custom-call(s32[2]{0:T(128)S(1)} %pad_add_fusion.ids_ref, bf16[6,768,512]{2,1,0:T(8,128)(2,1)S(1)} %get-tuple-element.73.high_ref, bf16[6,768,512]{2,1,0:T(8,128)(2,1)S(1)} %get-tuple-element.74.low_ref, f32[192,128]{1,0:T(8,128)S(1)} %right_sum.2.refs_0_, ...), custom_call_target="tpu_custom_call" | custom-call | flops 452984832 | bytes 23592960 | tf_op jit(solution)/shard_map/left/pallas_call | solution.py:284
  137.1 3.6 collective-permute-done.21.refs_2_
  140.7 2.7 collective-permute-done.22.refs_3_
  143.4 17.9 %all_to_all.22.parts_ref = f32[8,72,128]{2,1,0:T(8,128)S(1)} all-to-all(f32[8,72,128]{2,1,0:T(8,128)S(1)} %bitcast.20), channel_id=1, replica_groups=mesh['rep'=8,'tp'=4] {'rep'}, dimensions={0} | all-to-all | bytes 589824 | tf_op jit(solution)/shard_map/all_to_all | solution.py:379
  161.3 13.2 %all_to_all.23 = f32[8,72,128]{2,1,0:T(8,128)S(1)} all-to-all(f32[8,72,128]{2,1,0:T(8,128)S(1)} %left_sum.3), channel_id=1, replica_groups=mesh['rep'=8,'tp'=4] {'rep'}, dimensions={0} | all-to-all | bytes 589824 | tf_op jit(solution)/shard_map/all_to_all | solution.py:381
  178.2 2.8 right_near.3.refs_0_
  181.0 5.1 %collective-permute-done.24.first_ref = f32[96,768]{1,0:T(8,128)S(1)} collective-permute-done((f32[96,768]{1,0:T(8,128)S(1)}, f32[96,768]{1,0:T(8,128)S(1)}, u32[]{:S(2)}, u32[]{:S(2)}) %collective-permute-start.24) | collective-permute-done | bytes 294944 | tf_op jit(solution)/shard_map/ppermute | solution.py:302
  195.0 2.9 right_far.3
  199.2 4.2 %collective-permute-done.26.refs_1_ = f32[192,128]{1,0:T(8,128)S(1)} collective-permute-done((f32[192,128]{1,0:T(8,128)S(1)}, f32[192,128]{1,0:T(8,128)S(1)}, u32[]{:S(2)}, u32[]{:S(2)}) %collective-permute-start.26) | collective-permute-done | bytes 98336 | tf_op jit(solution)/shard_map/ppermute | solution.py:302
  205.5 4.4 %collective-permute-done.28.refs_3_ = f32[192,128]{1,0:T(8,128)S(1)} collective-permute-done((f32[192,128]{1,0:T(8,128)S(1)}, f32[192,128]{1,0:T(8,128)S(1)}, u32[]{:S(2)}, u32[]{:S(2)}) %collective-permute-start.28) | collective-permute-done | bytes 98336 | tf_op jit(solution)/shard_map/ppermute | solution.py:302
  214.1 7.0 %collective-permute-done.30.refs_5_ = f32[192,128]{1,0:T(8,128)S(1)} collective-permute-done((f32[192,128]{1,0:T(8,128)S(1)}, f32[192,128]{1,0:T(8,128)S(1)}, u32[]{:S(2)}, u32[]{:S(2)}) %collective-permute-start.30) | collective-permute-done | bytes 98336 | tf_op jit(solution)/shard_map/ppermute | solution.py:302
  221.1 7.9 %collective-permute-done.32.refs_7_ = f32[192,128]{1,0:T(8,128)S(1)} collective-permute-done((f32[192,128]{1,0:T(8,128)S(1)}, f32[192,128]{1,0:T(8,128)S(1)}, u32[]{:S(2)}, u32[]{:S(2)}) %collective-permute-start.32) | collective-permute-done | bytes 98336 | tf_op jit(solution)/shard_map/ppermute | solution.py:302
  229.2 3.4 collective-permute-start.35
  235.1 5.1 %collective-permute-start.39 = (f32[192,128]{1,0:T(8,128)S(1)}, f32[192,128]{1,0:T(8,128)S(1)}, u32[]{:S(2)}, u32[]{:S(2)}) collective-permute-start(f32[192,128]{1,0:T(8,128)S(1)} %right_sum.3.refs_0_), channel_id=1, source_target_pairs={{0,28},{4,24},{8,20},{12,16},{16,12},{20,8},{24,4},{28,0},{1,29},{... | collective-permute-start | bytes 294920 | tf_op jit(solution)/shard_map/ppermute | solution.py:302
  244.0 2.9 late_rows.1
  246.9 20.9 %collective-permute-start.46 = (bf16[576,512]{1,0:T(8,128)(2,1)}, bf16[576,512]{1,0:T(8,128)(2,1)}, u32[]{:S(2)}, u32[]{:S(2)}) collective-permute-start(bf16[576,512]{1,0:T(8,128)(2,1)} %get-tuple-element.109.refs_0_), channel_id=1, source_target_pairs={{0,8},{4,12},{8,16},{12,20},{16,24},{20,28},{24,0},{28,4},{1,9},{5... | collective-permute-start | bytes 1769480 | tf_op jit(solution)/shard_map/ppermute | solution.py:522
  273.4 4.3 %collective-permute-done.44 = f32[64,512]{1,0:T(8,128)S(1)} collective-permute-done((f32[64,512]{1,0:T(8,128)S(1)}, f32[64,512]{1,0:T(8,128)S(1)}, u32[]{:S(2)}, u32[]{:S(2)}) %collective-permute-start.44) | collective-permute-done | bytes 131104 | tf_op jit(solution)/shard_map/ppermute | solution.py:302
  283.8 4.1 %update.4.refs_0_ = f32[1,12,768,512]{3,2,1,0:T(8,128)} custom-call(s32[2]{0:T(128)S(1)} %pad_add_fusion.ids_ref, f32[384,768]{1,0:T(8,128)S(1)} %pad_maximum_fusion.basis_ref, f32[384,512]{1,0:T(8,128)S(1)} %copy-done.9, bf16[6,768,512]{2,1,0:T(8,128)(2,1)S(1)} %copy-done.5, bf16[6,768,512]{2,1,0:T(8,128)(2,1)S(1)} %copy-done.7), custom_call_target="tpu_custom_call" | custom-call | flops 226492416 | bytes 9437184 | tf_op jit(solution)/shard_map/update/pallas_call | solution.py:284
  287.9 4.1 %update.5.refs_0_ = f32[1,12,768,512]{3,2,1,0:T(8,128)} custom-call(s32[2]{0:T(128)S(1)} %pad_add_fusion.ids_ref, f32[384,768]{1,0:T(8,128)S(1)} %pad_maximum_fusion.basis_ref, f32[384,512]{1,0:T(8,128)S(1)} %copy-done.9, bf16[6,768,512]{2,1,0:T(8,128)(2,1)S(1)} %copy-done.5, bf16[6,768,512]{2,1,0:T(8,128)(2,1)S(1)} %copy-done.7, ...), custom_call_target="tpu_custom_call", output_to_operand_aliasing={{}: (5, {})} | custom-call | flops 226492416 | bytes 9437184 | tf_op jit(solution)/shard_map/update/pallas_call | solution.py:284
  292.0 4.1 %update.6.refs_0_ = f32[1,12,768,512]{3,2,1,0:T(8,128)} custom-call(s32[2]{0:T(128)S(1)} %pad_add_fusion.ids_ref, f32[384,768]{1,0:T(8,128)S(1)} %pad_maximum_fusion.basis_ref, f32[384,512]{1,0:T(8,128)S(1)} %copy-done.9, bf16[6,768,512]{2,1,0:T(8,128)(2,1)S(1)} %bitcast.13, bf16[6,768,512]{2,1,0:T(8,128)(2,1)S(1)} %bitcast.15, ...), custom_call_target="tpu_custom_call", output_to_operand_aliasing={{}: (5, {})} | custom-call | flops 226492416 | bytes 9437184 | tf_op jit(solution)/shard_map/update/pallas_call | solution.py:284
  296.1 4.1 %update.7 = f32[1,12,768,512]{3,2,1,0:T(8,128)} custom-call(s32[2]{0:T(128)S(1)} %pad_add_fusion.ids_ref, f32[384,768]{1,0:T(8,128)S(1)} %pad_maximum_fusion.basis_ref, f32[384,512]{1,0:T(8,128)S(1)} %copy-done.9, bf16[6,768,512]{2,1,0:T(8,128)(2,1)S(1)} %bitcast.13, bf16[6,768,512]{2,1,0:T(8,128)(2,1)S(1)} %bitcast.15, ...), custom_call_target="tpu_custom_call", output_to_operand_aliasing={{}: (5, {})} | custom-call | flops 226492416 | bytes 9437184 | tf_op jit(solution)/shard_map/update/pallas_call | solution.py:284
  302.4 5.4 %place.4.refs_4_ = bf16[8,2,576,512]{3,2,1,0:T(8,128)(2,1)} custom-call(s32[2]{0:T(128)S(1)} %pad_add_fusion.ids_ref, bf16[576,512]{1,0:T(8,128)(2,1)} %get-tuple-element.109.refs_0_, bf16[576,512]{1,0:T(8,128)(2,1)} %get-tuple-element.110.refs_1_, bf16[576,512]{1,0:T(8,128)(2,1)} %collective-permute-done.46.refs_2_, ...), custom_call_target="tpu_custom_call" | custom-call | bytes 14155776 | tf_op jit(solution)/shard_map/place/pallas_call | solution.py:284
  307.9 6.1 %flat_rows.1 = (f32[288,2048]{1,0:T(8,128)}, f32[288,2048]{1,0:T(8,128)}) custom-call(s32[2]{0:T(128)S(1)} %pad_add_fusion.ids_ref, f32[384,768]{1,0:T(8,128)S(1)} %pad_maximum_fusion.basis_ref, f32[4,64,512]{2,1,0:T(8,128)S(1)} %pad_maximum_fusion.1.near_ref, f32[288,2048]{1,0:T(8,128)S(1)} %copy-done.10, f32[288,2048]{1,0:T(8,128)S(1)} %copy-done.11), custom_call_target="tpu_custom_call" | custom-call | flops 452984832 | bytes 9437184 | tf_op jit(solution)/shard_map/flat_rows/pallas_call | solution.py:284
  314.0 4.2 %collective-permute-done.50.refs_0_ = bf16[576,512]{1,0:T(8,128)(2,1)S(1)} collective-permute-done((bf16[576,512]{1,0:T(8,128)(2,1)}, bf16[576,512]{1,0:T(8,128)(2,1)S(1)}, u32[]{:S(2)}, u32[]{:S(2)}) %collective-permute-start.50) | collective-permute-done | bytes 589856 | tf_op jit(solution)/shard_map/ppermute | solution.py:522
  318.2 12.6 %collective-permute-done.51.refs_1_ = bf16[576,512]{1,0:T(8,128)(2,1)S(1)} collective-permute-done((bf16[576,512]{1,0:T(8,128)(2,1)}, bf16[576,512]{1,0:T(8,128)(2,1)S(1)}, u32[]{:S(2)}, u32[]{:S(2)}) %collective-permute-start.51) | collective-permute-done | bytes 589856 | tf_op jit(solution)/shard_map/ppermute | solution.py:522
  330.8 3.0 collective-permute-start.54
  336.2 2.5 place.5.refs_4_
  338.7 10.1 %collective-permute-done.54.refs_0_ = bf16[576,512]{1,0:T(8,128)(2,1)S(1)} collective-permute-done((bf16[576,512]{1,0:T(8,128)(2,1)S(1)}, bf16[576,512]{1,0:T(8,128)(2,1)S(1)}, u32[]{:S(2)}, u32[]{:S(2)}) %collective-permute-start.54) | collective-permute-done | bytes 589856 | tf_op jit(solution)/shard_map/ppermute | solution.py:522
  348.8 11.8 %collective-permute-done.55.refs_1_ = bf16[576,512]{1,0:T(8,128)(2,1)S(1)} collective-permute-done((bf16[576,512]{1,0:T(8,128)(2,1)S(1)}, bf16[576,512]{1,0:T(8,128)(2,1)S(1)}, u32[]{:S(2)}, u32[]{:S(2)}) %collective-permute-start.55) | collective-permute-done | bytes 589856 | tf_op jit(solution)/shard_map/ppermute | solution.py:522
  365.3 9.8 %collective-permute-done.58.refs_0_ = bf16[576,512]{1,0:T(8,128)(2,1)S(1)} collective-permute-done((bf16[576,512]{1,0:T(8,128)(2,1)S(1)}, bf16[576,512]{1,0:T(8,128)(2,1)S(1)}, u32[]{:S(2)}, u32[]{:S(2)}) %collective-permute-start.58) | collective-permute-done | bytes 589856 | tf_op jit(solution)/shard_map/ppermute | solution.py:302
  375.1 2.6 collective-permute-done.59.refs_1_
  (157 shorter events, 75.4 us)
Async XLA Ops:
  13.2 12.7 %collective-permute-start = (f32[96,768]{1,0:T(8,128)S(1)}, f32[96,768]{1,0:T(8,128)S(1)}, u32[]{:S(2)}, u32[]{:S(2)}) collective-permute-start(f32[96,768]{1,0:T(8,128)S(1)} %get-tuple-element.76), channel_id=1, source_target_pairs={{0,1},{1,0},{2,3},{3,2},{4,5},{5,4},{6,7},{7,6},{8,9},{9,8},{10,11... | collective-permute-start | bytes 884744 | tf_op jit(solution)/shard_map/ppermute | solution.py:302
  23.1 10.6 %collective-permute-start.1 = (f32[96,768]{1,0:T(8,128)S(1)}, f32[96,768]{1,0:T(8,128)S(1)}, u32[]{:S(2)}, u32[]{:S(2)}) collective-permute-start(f32[96,768]{1,0:T(8,128)S(1)} %get-tuple-element.77), channel_id=1, source_target_pairs={{0,2},{1,3},{2,0},{3,1},{4,6},{5,7},{6,4},{7,5},{8,10},{9,11},{10,... | collective-permute-start | bytes 884744 | tf_op jit(solution)/shard_map/ppermute | solution.py:302
  25.9 13.0 %collective-permute-start.2 = (f32[96,768]{1,0:T(8,128)S(1)}, f32[96,768]{1,0:T(8,128)S(1)}, u32[]{:S(2)}, u32[]{:S(2)}) collective-permute-start(f32[96,768]{1,0:T(8,128)S(1)} %get-tuple-element.78), channel_id=1, source_target_pairs={{0,3},{1,2},{2,1},{3,0},{4,7},{5,6},{6,5},{7,4},{8,11},{9,10},{10,... | collective-permute-start | bytes 884744 | tf_op jit(solution)/shard_map/ppermute | solution.py:302
  70.9 9.4 %collective-permute-start.4 = (f32[96,768]{1,0:T(8,128)S(1)}, f32[96,768]{1,0:T(8,128)S(1)}, u32[]{:S(2)}, u32[]{:S(2)}) collective-permute-start(f32[96,768]{1,0:T(8,128)S(1)} %basis.2.first_ref), channel_id=1, source_target_pairs={{0,2},{1,3},{2,0},{3,1},{4,6},{5,7},{6,4},{7,5},{8,10},{9,11},{10,... | collective-permute-start | bytes 884744 | tf_op jit(solution)/shard_map/ppermute | solution.py:302
  84.8 13.3 %collective-permute-start.10 = (f32[192,128]{1,0:T(8,128)S(1)}, f32[192,128]{1,0:T(8,128)S(1)}, u32[]{:S(2)}, u32[]{:S(2)}) collective-permute-start(f32[192,128]{1,0:T(8,128)S(1)} %get-tuple-element.89), channel_id=1, source_target_pairs={{0,20},{4,16},{8,28},{12,24},{16,4},{20,0},{24,12},{28,8},{1,21},{... | collective-permute-start | bytes 294920 | tf_op jit(solution)/shard_map/ppermute | solution.py:302
  85.5 12.6 %collective-permute-start.11 = (f32[192,128]{1,0:T(8,128)S(1)}, f32[192,128]{1,0:T(8,128)S(1)}, u32[]{:S(2)}, u32[]{:S(2)}) collective-permute-start(f32[192,128]{1,0:T(8,128)S(1)} %get-tuple-element.90), channel_id=1, source_target_pairs={{0,24},{4,28},{8,16},{12,20},{16,8},{20,12},{24,0},{28,4},{1,25},{... | collective-permute-start | bytes 294920 | tf_op jit(solution)/shard_map/ppermute | solution.py:302
  87.8 12.2 %collective-permute-start.12 = (f32[192,128]{1,0:T(8,128)S(1)}, f32[192,128]{1,0:T(8,128)S(1)}, u32[]{:S(2)}, u32[]{:S(2)}) collective-permute-start(f32[192,128]{1,0:T(8,128)S(1)} %get-tuple-element.91), channel_id=1, source_target_pairs={{0,28},{4,24},{8,20},{12,16},{16,12},{20,8},{24,4},{28,0},{1,29},{... | collective-permute-start | bytes 294920 | tf_op jit(solution)/shard_map/ppermute | solution.py:302
  90.2 9.8 %collective-permute-start.6 = (f32[192,128]{1,0:T(8,128)S(1)}, f32[192,128]{1,0:T(8,128)S(1)}, u32[]{:S(2)}, u32[]{:S(2)}) collective-permute-start(f32[192,128]{1,0:T(8,128)S(1)} %get-tuple-element.85), channel_id=1, source_target_pairs={{0,4},{4,0},{8,12},{12,8},{16,20},{20,16},{24,28},{28,24},{1,5},{5... | collective-permute-start | bytes 294920 | tf_op jit(solution)/shard_map/ppermute | solution.py:302
  90.8 9.3 %collective-permute-start.7 = (f32[192,128]{1,0:T(8,128)S(1)}, f32[192,128]{1,0:T(8,128)S(1)}, u32[]{:S(2)}, u32[]{:S(2)}) collective-permute-start(f32[192,128]{1,0:T(8,128)S(1)} %get-tuple-element.86), channel_id=1, source_target_pairs={{0,8},{4,12},{8,0},{12,4},{16,24},{20,28},{24,16},{28,20},{1,9},{5... | collective-permute-start | bytes 294920 | tf_op jit(solution)/shard_map/ppermute | solution.py:302
  98.1 7.6 %collective-permute-start.9 = (f32[192,128]{1,0:T(8,128)S(1)}, f32[192,128]{1,0:T(8,128)S(1)}, u32[]{:S(2)}, u32[]{:S(2)}) collective-permute-start(f32[192,128]{1,0:T(8,128)S(1)} %get-tuple-element.88), channel_id=1, source_target_pairs={{0,16},{4,20},{8,24},{12,28},{16,0},{20,4},{24,8},{28,12},{1,17},{... | collective-permute-start | bytes 294920 | tf_op jit(solution)/shard_map/ppermute | solution.py:302
  105.8 7.8 %collective-permute-start.13 = (f32[192,128]{1,0:T(8,128)S(1)}, f32[192,128]{1,0:T(8,128)S(1)}, u32[]{:S(2)}, u32[]{:S(2)}) collective-permute-start(f32[192,128]{1,0:T(8,128)S(1)} %right_sum.2.refs_0_), channel_id=1, source_target_pairs={{0,4},{4,0},{8,12},{12,8},{16,20},{20,16},{24,28},{28,24},{1,5},{5... | collective-permute-start | bytes 294920 | tf_op jit(solution)/shard_map/ppermute | solution.py:302
  107.7 7.2 %collective-permute-start.14 = (f32[192,128]{1,0:T(8,128)S(1)}, f32[192,128]{1,0:T(8,128)S(1)}, u32[]{:S(2)}, u32[]{:S(2)}) collective-permute-start(f32[192,128]{1,0:T(8,128)S(1)} %right_sum.2.refs_0_), channel_id=1, source_target_pairs={{0,8},{4,12},{8,0},{12,4},{16,24},{20,28},{24,16},{28,20},{1,9},{5... | collective-permute-start | bytes 294920 | tf_op jit(solution)/shard_map/ppermute | solution.py:302
  107.7 9.3 %collective-permute-start.15 = (f32[192,128]{1,0:T(8,128)S(1)}, f32[192,128]{1,0:T(8,128)S(1)}, u32[]{:S(2)}, u32[]{:S(2)}) collective-permute-start(f32[192,128]{1,0:T(8,128)S(1)} %right_sum.2.refs_0_), channel_id=1, source_target_pairs={{0,12},{4,8},{8,4},{12,0},{16,28},{20,24},{24,20},{28,16},{1,13},{... | collective-permute-start | bytes 294920 | tf_op jit(solution)/shard_map/ppermute | solution.py:302
  109.3 14.1 %collective-permute-start.16 = (f32[192,128]{1,0:T(8,128)S(1)}, f32[192,128]{1,0:T(8,128)S(1)}, u32[]{:S(2)}, u32[]{:S(2)}) collective-permute-start(f32[192,128]{1,0:T(8,128)S(1)} %right_sum.2.refs_0_), channel_id=1, source_target_pairs={{0,16},{4,20},{8,24},{12,28},{16,0},{20,4},{24,8},{28,12},{1,17},{... | collective-permute-start | bytes 294920 | tf_op jit(solution)/shard_map/ppermute | solution.py:302
  109.8 16.6 %collective-permute-start.17 = (f32[192,128]{1,0:T(8,128)S(1)}, f32[192,128]{1,0:T(8,128)S(1)}, u32[]{:S(2)}, u32[]{:S(2)}) collective-permute-start(f32[192,128]{1,0:T(8,128)S(1)} %right_sum.2.refs_0_), channel_id=1, source_target_pairs={{0,20},{4,16},{8,28},{12,24},{16,4},{20,0},{24,12},{28,8},{1,21},{... | collective-permute-start | bytes 294920 | tf_op jit(solution)/shard_map/ppermute | solution.py:302
  113.6 12.9 %collective-permute-start.18 = (f32[192,128]{1,0:T(8,128)S(1)}, f32[192,128]{1,0:T(8,128)S(1)}, u32[]{:S(2)}, u32[]{:S(2)}) collective-permute-start(f32[192,128]{1,0:T(8,128)S(1)} %right_sum.2.refs_0_), channel_id=1, source_target_pairs={{0,24},{4,28},{8,16},{12,20},{16,8},{20,12},{24,0},{28,4},{1,25},{... | collective-permute-start | bytes 294920 | tf_op jit(solution)/shard_map/ppermute | solution.py:302
  114.9 11.5 %collective-permute-start.19 = (f32[192,128]{1,0:T(8,128)S(1)}, f32[192,128]{1,0:T(8,128)S(1)}, u32[]{:S(2)}, u32[]{:S(2)}) collective-permute-start(f32[192,128]{1,0:T(8,128)S(1)} %right_sum.2.refs_0_), channel_id=1, source_target_pairs={{0,28},{4,24},{8,20},{12,16},{16,12},{20,8},{24,4},{28,0},{1,29},{... | collective-permute-start | bytes 294920 | tf_op jit(solution)/shard_map/ppermute | solution.py:302
  130.7 10.0 %collective-permute-start.21 = (f32[96,768]{1,0:T(8,128)S(1)}, f32[96,768]{1,0:T(8,128)S(1)}, u32[]{:S(2)}, u32[]{:S(2)}) collective-permute-start(f32[96,768]{1,0:T(8,128)S(1)} %get-tuple-element.94), channel_id=1, source_target_pairs={{0,2},{1,3},{2,0},{3,1},{4,6},{5,7},{6,4},{7,5},{8,10},{9,11},{10,... | collective-permute-start | bytes 884744 | tf_op jit(solution)/shard_map/ppermute | solution.py:302
  132.2 11.1 %collective-permute-start.22 = (f32[96,768]{1,0:T(8,128)S(1)}, f32[96,768]{1,0:T(8,128)S(1)}, u32[]{:S(2)}, u32[]{:S(2)}) collective-permute-start(f32[96,768]{1,0:T(8,128)S(1)} %get-tuple-element.95), channel_id=1, source_target_pairs={{0,3},{1,2},{2,1},{3,0},{4,7},{5,6},{6,5},{7,4},{8,11},{9,10},{10,... | collective-permute-start | bytes 884744 | tf_op jit(solution)/shard_map/ppermute | solution.py:302
  136.4 6.9 %collective-permute-start.20 = (f32[96,768]{1,0:T(8,128)S(1)}, f32[96,768]{1,0:T(8,128)S(1)}, u32[]{:S(2)}, u32[]{:S(2)}) collective-permute-start(f32[96,768]{1,0:T(8,128)S(1)} %get-tuple-element.93), channel_id=1, source_target_pairs={{0,1},{1,0},{2,3},{3,2},{4,5},{5,4},{6,7},{7,6},{8,9},{9,8},{10,11... | collective-permute-start | bytes 884744 | tf_op jit(solution)/shard_map/ppermute | solution.py:302
  176.7 9.4 %collective-permute-start.24 = (f32[96,768]{1,0:T(8,128)S(1)}, f32[96,768]{1,0:T(8,128)S(1)}, u32[]{:S(2)}, u32[]{:S(2)}) collective-permute-start(f32[96,768]{1,0:T(8,128)S(1)} %basis.3.first_ref), channel_id=1, source_target_pairs={{0,2},{1,3},{2,0},{3,1},{4,6},{5,7},{6,4},{7,5},{8,10},{9,11},{10,... | collective-permute-start | bytes 884744 | tf_op jit(solution)/shard_map/ppermute | solution.py:302
  188.4 40.8 %collective-permute-start.40 = (f32[288,512]{1,0:T(8,128)S(1)}, f32[288,512]{1,0:T(8,128)S(1)}, u32[]{:S(2)}, u32[]{:S(2)}) collective-permute-start(f32[288,512]{1,0:T(8,128)S(1)} %get-tuple-element.143), channel_id=1, source_target_pairs={{0,1},{1,0},{2,3},{3,2},{4,5},{5,4},{6,7},{7,6},{8,9},{9,8},{10,11... | collective-permute-start | bytes 1769480 | tf_op jit(solution)/shard_map/ppermute | solution.py:302
  188.8 43.8 %collective-permute-start.41 = (f32[288,512]{1,0:T(8,128)S(1)}, f32[288,512]{1,0:T(8,128)S(1)}, u32[]{:S(2)}, u32[]{:S(2)}) collective-permute-start(f32[288,512]{1,0:T(8,128)S(1)} %get-tuple-element.142), channel_id=1, source_target_pairs={{0,2},{1,3},{2,0},{3,1},{4,6},{5,7},{6,4},{7,5},{8,10},{9,11},{10,... | collective-permute-start | bytes 1769480 | tf_op jit(solution)/shard_map/ppermute | solution.py:302
  190.0 42.6 %collective-permute-start.42 = (f32[288,512]{1,0:T(8,128)S(1)}, f32[288,512]{1,0:T(8,128)S(1)}, u32[]{:S(2)}, u32[]{:S(2)}) collective-permute-start(f32[288,512]{1,0:T(8,128)S(1)} %get-tuple-element.141), channel_id=1, source_target_pairs={{0,3},{1,2},{2,1},{3,0},{4,7},{5,6},{6,5},{7,4},{8,11},{9,10},{10,... | collective-permute-start | bytes 1769480 | tf_op jit(solution)/shard_map/ppermute | solution.py:302
  203.4 6.5 %collective-permute-start.28 = (f32[192,128]{1,0:T(8,128)S(1)}, f32[192,128]{1,0:T(8,128)S(1)}, u32[]{:S(2)}, u32[]{:S(2)}) collective-permute-start(f32[192,128]{1,0:T(8,128)S(1)} %get-tuple-element.101), channel_id=1, source_target_pairs={{0,12},{4,8},{8,4},{12,0},{16,28},{20,24},{24,20},{28,16},{1,13},{... | collective-permute-start | bytes 294920 | tf_op jit(solution)/shard_map/ppermute | solution.py:302
  204.0 8.3 %collective-permute-start.29 = (f32[192,128]{1,0:T(8,128)S(1)}, f32[192,128]{1,0:T(8,128)S(1)}, u32[]{:S(2)}, u32[]{:S(2)}) collective-permute-start(f32[192,128]{1,0:T(8,128)S(1)} %get-tuple-element.102), channel_id=1, source_target_pairs={{0,16},{4,20},{8,24},{12,28},{16,0},{20,4},{24,8},{28,12},{1,17},{... | collective-permute-start | bytes 294920 | tf_op jit(solution)/shard_map/ppermute | solution.py:302
  209.9 11.2 %collective-permute-start.30 = (f32[192,128]{1,0:T(8,128)S(1)}, f32[192,128]{1,0:T(8,128)S(1)}, u32[]{:S(2)}, u32[]{:S(2)}) collective-permute-start(f32[192,128]{1,0:T(8,128)S(1)} %get-tuple-element.103), channel_id=1, source_target_pairs={{0,20},{4,16},{8,28},{12,24},{16,4},{20,0},{24,12},{28,8},{1,21},{... | collective-permute-start | bytes 294920 | tf_op jit(solution)/shard_map/ppermute | solution.py:302
  212.3 8.8 %collective-permute-start.31 = (f32[192,128]{1,0:T(8,128)S(1)}, f32[192,128]{1,0:T(8,128)S(1)}, u32[]{:S(2)}, u32[]{:S(2)}) collective-permute-start(f32[192,128]{1,0:T(8,128)S(1)} %get-tuple-element.104), channel_id=1, source_target_pairs={{0,24},{4,28},{8,16},{12,20},{16,8},{20,12},{24,0},{28,4},{1,25},{... | collective-permute-start | bytes 294920 | tf_op jit(solution)/shard_map/ppermute | solution.py:302
  221.1 7.9 %collective-permute-start.32 = (f32[192,128]{1,0:T(8,128)S(1)}, f32[192,128]{1,0:T(8,128)S(1)}, u32[]{:S(2)}, u32[]{:S(2)}) collective-permute-start(f32[192,128]{1,0:T(8,128)S(1)} %get-tuple-element.105), channel_id=1, source_target_pairs={{0,28},{4,24},{8,20},{12,16},{16,12},{20,8},{24,4},{28,0},{1,29},{... | collective-permute-start | bytes 294920 | tf_op jit(solution)/shard_map/ppermute | solution.py:302
  229.2 12.2 %collective-permute-start.35 = (f32[192,128]{1,0:T(8,128)S(1)}, f32[192,128]{1,0:T(8,128)S(1)}, u32[]{:S(2)}, u32[]{:S(2)}) collective-permute-start(f32[192,128]{1,0:T(8,128)S(1)} %right_sum.3.refs_0_), channel_id=1, source_target_pairs={{0,12},{4,8},{8,4},{12,0},{16,28},{20,24},{24,20},{28,16},{1,13},{... | collective-permute-start | bytes 294920 | tf_op jit(solution)/shard_map/ppermute | solution.py:302
  232.6 8.8 %collective-permute-start.36 = (f32[192,128]{1,0:T(8,128)S(1)}, f32[192,128]{1,0:T(8,128)S(1)}, u32[]{:S(2)}, u32[]{:S(2)}) collective-permute-start(f32[192,128]{1,0:T(8,128)S(1)} %right_sum.3.refs_0_), channel_id=1, source_target_pairs={{0,16},{4,20},{8,24},{12,28},{16,0},{20,4},{24,8},{28,12},{1,17},{... | collective-permute-start | bytes 294920 | tf_op jit(solution)/shard_map/ppermute | solution.py:302
  232.6 8.8 %collective-permute-start.37 = (f32[192,128]{1,0:T(8,128)S(1)}, f32[192,128]{1,0:T(8,128)S(1)}, u32[]{:S(2)}, u32[]{:S(2)}) collective-permute-start(f32[192,128]{1,0:T(8,128)S(1)} %right_sum.3.refs_0_), channel_id=1, source_target_pairs={{0,20},{4,16},{8,28},{12,24},{16,4},{20,0},{24,12},{28,8},{1,21},{... | collective-permute-start | bytes 294920 | tf_op jit(solution)/shard_map/ppermute | solution.py:302
  235.1 8.9 %collective-permute-start.39 = (f32[192,128]{1,0:T(8,128)S(1)}, f32[192,128]{1,0:T(8,128)S(1)}, u32[]{:S(2)}, u32[]{:S(2)}) collective-permute-start(f32[192,128]{1,0:T(8,128)S(1)} %right_sum.3.refs_0_), channel_id=1, source_target_pairs={{0,28},{4,24},{8,20},{12,16},{16,12},{20,8},{24,4},{28,0},{1,29},{... | collective-permute-start | bytes 294920 | tf_op jit(solution)/shard_map/ppermute | solution.py:302
  246.9 53.2 %collective-permute-start.46 = (bf16[576,512]{1,0:T(8,128)(2,1)}, bf16[576,512]{1,0:T(8,128)(2,1)}, u32[]{:S(2)}, u32[]{:S(2)}) collective-permute-start(bf16[576,512]{1,0:T(8,128)(2,1)} %get-tuple-element.109.refs_0_), channel_id=1, source_target_pairs={{0,8},{4,12},{8,16},{12,20},{16,24},{20,28},{24,0},{28,4},{1,9},{5... | collective-permute-start | bytes 1769480 | tf_op jit(solution)/shard_map/ppermute | solution.py:522
  267.8 32.4 %collective-permute-start.47 = (bf16[576,512]{1,0:T(8,128)(2,1)}, bf16[576,512]{1,0:T(8,128)(2,1)}, u32[]{:S(2)}, u32[]{:S(2)}) collective-permute-start(bf16[576,512]{1,0:T(8,128)(2,1)} %get-tuple-element.110.refs_1_), channel_id=1, source_target_pairs={{0,8},{4,12},{8,16},{12,20},{16,24},{20,28},{24,0},{28,4},{1,9},{5... | collective-permute-start | bytes 1769480 | tf_op jit(solution)/shard_map/ppermute | solution.py:522
  267.8 32.3 %collective-permute-start.48 = (bf16[576,512]{1,0:T(8,128)(2,1)}, bf16[576,512]{1,0:T(8,128)(2,1)}, u32[]{:S(2)}, u32[]{:S(2)}) collective-permute-start(bf16[576,512]{1,0:T(8,128)(2,1)} %get-tuple-element.109.refs_0_), channel_id=1, source_target_pairs={{0,4},{4,0},{8,12},{12,8},{16,20},{20,16},{24,28},{28,24},{1,5},{5... | collective-permute-start | bytes 1769480 | tf_op jit(solution)/shard_map/ppermute | solution.py:302
  268.9 31.3 %collective-permute-start.49 = (bf16[576,512]{1,0:T(8,128)(2,1)}, bf16[576,512]{1,0:T(8,128)(2,1)}, u32[]{:S(2)}, u32[]{:S(2)}) collective-permute-start(bf16[576,512]{1,0:T(8,128)(2,1)} %get-tuple-element.110.refs_1_), channel_id=1, source_target_pairs={{0,4},{4,0},{8,12},{12,8},{16,20},{20,16},{24,28},{28,24},{1,5},{5... | collective-permute-start | bytes 1769480 | tf_op jit(solution)/shard_map/ppermute | solution.py:302
  277.8 22.4 %collective-permute-start.45 = (f32[64,512]{1,0:T(8,128)S(1)}, f32[64,512]{1,0:T(8,128)S(1)}, u32[]{:S(2)}, u32[]{:S(2)}) collective-permute-start(f32[64,512]{1,0:T(8,128)S(1)} %constant_dynamic-slice_fusion), channel_id=1, source_target_pairs={{0,3},{1,2},{2,1},{3,0},{4,7},{5,6},{6,5},{7,4},{8,11},{9,10},{10,... | collective-permute-start | bytes 393224 | tf_op jit(solution)/shard_map/ppermute | solution.py:302
  300.2 18.0 %collective-permute-start.50 = (bf16[576,512]{1,0:T(8,128)(2,1)}, bf16[576,512]{1,0:T(8,128)(2,1)S(1)}, u32[]{:S(2)}, u32[]{:S(2)}) collective-permute-start(bf16[576,512]{1,0:T(8,128)(2,1)} %collective-permute-done.46.refs_2_), channel_id=1, source_target_pairs={{0,8},{4,12},{8,16},{12,20},{16,24},{20,28},{24,0},{28,4},{1,9},{5... | collective-permute-start | bytes 1769480 | tf_op jit(solution)/shard_map/ppermute | solution.py:522
  300.3 30.5 %collective-permute-start.51 = (bf16[576,512]{1,0:T(8,128)(2,1)}, bf16[576,512]{1,0:T(8,128)(2,1)S(1)}, u32[]{:S(2)}, u32[]{:S(2)}) collective-permute-start(bf16[576,512]{1,0:T(8,128)(2,1)} %collective-permute-done.47.refs_3_), channel_id=1, source_target_pairs={{0,8},{4,12},{8,16},{12,20},{16,24},{20,28},{24,0},{28,4},{1,9},{5... | collective-permute-start | bytes 1769480 | tf_op jit(solution)/shard_map/ppermute | solution.py:522
  300.4 30.5 %collective-permute-start.52 = (bf16[576,512]{1,0:T(8,128)(2,1)}, bf16[576,512]{1,0:T(8,128)(2,1)S(1)}, u32[]{:S(2)}, u32[]{:S(2)}) collective-permute-start(bf16[576,512]{1,0:T(8,128)(2,1)} %collective-permute-done.46.refs_2_), channel_id=1, source_target_pairs={{0,4},{4,0},{8,12},{12,8},{16,20},{20,16},{24,28},{28,24},{1,5},{5... | collective-permute-start | bytes 1769480 | tf_op jit(solution)/shard_map/ppermute | solution.py:302
  301.5 29.4 %collective-permute-start.53 = (bf16[576,512]{1,0:T(8,128)(2,1)}, bf16[576,512]{1,0:T(8,128)(2,1)S(1)}, u32[]{:S(2)}, u32[]{:S(2)}) collective-permute-start(bf16[576,512]{1,0:T(8,128)(2,1)} %collective-permute-done.47.refs_3_), channel_id=1, source_target_pairs={{0,4},{4,0},{8,12},{12,8},{16,20},{20,16},{24,28},{28,24},{1,5},{5... | collective-permute-start | bytes 1769480 | tf_op jit(solution)/shard_map/ppermute | solution.py:302
  330.8 18.0 %collective-permute-start.54 = (bf16[576,512]{1,0:T(8,128)(2,1)S(1)}, bf16[576,512]{1,0:T(8,128)(2,1)S(1)}, u32[]{:S(2)}, u32[]{:S(2)}) collective-permute-start(bf16[576,512]{1,0:T(8,128)(2,1)S(1)} %collective-permute-done.50.refs_0_), channel_id=1, source_target_pairs={{0,8},{4,12},{8,16},{12,20},{16,24},{20,28},{24,0},{28,4},{1,9},{5... | collective-permute-start | bytes 1769480 | tf_op jit(solution)/shard_map/ppermute | solution.py:522
  333.8 26.8 %collective-permute-start.55 = (bf16[576,512]{1,0:T(8,128)(2,1)S(1)}, bf16[576,512]{1,0:T(8,128)(2,1)S(1)}, u32[]{:S(2)}, u32[]{:S(2)}) collective-permute-start(bf16[576,512]{1,0:T(8,128)(2,1)S(1)} %collective-permute-done.51.refs_1_), channel_id=1, source_target_pairs={{0,8},{4,12},{8,16},{12,20},{16,24},{20,28},{24,0},{28,4},{1,9},{5... | collective-permute-start | bytes 1769480 | tf_op jit(solution)/shard_map/ppermute | solution.py:522
  334.1 26.5 %collective-permute-start.56 = (bf16[576,512]{1,0:T(8,128)(2,1)S(1)}, bf16[576,512]{1,0:T(8,128)(2,1)S(1)}, u32[]{:S(2)}, u32[]{:S(2)}) collective-permute-start(bf16[576,512]{1,0:T(8,128)(2,1)S(1)} %collective-permute-done.50.refs_0_), channel_id=1, source_target_pairs={{0,4},{4,0},{8,12},{12,8},{16,20},{20,16},{24,28},{28,24},{1,5},{5... | collective-permute-start | bytes 1769480 | tf_op jit(solution)/shard_map/ppermute | solution.py:302
  335.2 26.2 %collective-permute-start.57 = (bf16[576,512]{1,0:T(8,128)(2,1)S(1)}, bf16[576,512]{1,0:T(8,128)(2,1)S(1)}, u32[]{:S(2)}, u32[]{:S(2)}) collective-permute-start(bf16[576,512]{1,0:T(8,128)(2,1)S(1)} %collective-permute-done.51.refs_1_), channel_id=1, source_target_pairs={{0,4},{4,0},{8,12},{12,8},{16,20},{20,16},{24,28},{28,24},{1,5},{5... | collective-permute-start | bytes 1769480 | tf_op jit(solution)/shard_map/ppermute | solution.py:302
  361.4 13.7 %collective-permute-start.58 = (bf16[576,512]{1,0:T(8,128)(2,1)S(1)}, bf16[576,512]{1,0:T(8,128)(2,1)S(1)}, u32[]{:S(2)}, u32[]{:S(2)}) collective-permute-start(bf16[576,512]{1,0:T(8,128)(2,1)S(1)} %collective-permute-done.54.refs_0_), channel_id=1, source_target_pairs={{0,4},{4,0},{8,12},{12,8},{16,20},{20,16},{24,28},{28,24},{1,5},{5... | collective-permute-start | bytes 1769480 | tf_op jit(solution)/shard_map/ppermute | solution.py:302
  362.5 15.3 %collective-permute-start.59 = (bf16[576,512]{1,0:T(8,128)(2,1)S(1)}, bf16[576,512]{1,0:T(8,128)(2,1)S(1)}, u32[]{:S(2)}, u32[]{:S(2)}) collective-permute-start(bf16[576,512]{1,0:T(8,128)(2,1)S(1)} %collective-permute-done.57.refs_3_), channel_id=1, source_target_pairs={{0,8},{4,12},{8,16},{12,20},{16,24},{20,28},{24,0},{28,4},{1,9},{5... | collective-permute-start | bytes 1769480 | tf_op jit(solution)/shard_map/ppermute | solution.py:529
  (36 other events, 766.2 us)

commit v5 on v4

--- a/solution.py
+++ b/solution.py
@@ -361,9 +361,10 @@
         )
         terms[half] = (high, low)
         lefts[2 * half : 2 * half + 2] = out
+        ids, _ = lax.optimization_barrier((ids, out[0]))
 
     for power_pass in range(ROUNDS):
-        met = [lefts[0]] + [swap(lefts[offset], "tp", tps, offset) for offset in range(1, tps)]
+        met = [lefts[0]] + [swap(lefts[offset], "tp", tps, offset) for offset in reversed(range(1, tps))]
         parts = whole_call(
             functools.partial(split_kernel, tps), "left_split", shape(left_part * replicas, LANES), met
         )
@@ -379,6 +380,8 @@
         parts = lax.all_to_all(parts, "rep", split_axis=0, concat_axis=0, tiled=True)
         parts = whole_call(total_kernel, "left_sum", shape(*parts.shape), [parts])
         parts = lax.all_to_all(parts, "rep", split_axis=0, concat_axis=0, tiled=True)
+        if power_pass == 0:
+            parts, base = lax.optimization_barrier((parts, base))
         basis = whole_call(
             functools.partial(basis_kernel, rank), "basis", shape(tp_rows, width), [parts.reshape(-1, LANES)]
         )
@@ -514,37 +517,39 @@
 
     ring = [(index, (index + 2) % replicas) for index in range(replicas)]
     stages = replicas // 2
-    held, beside = block, [None, None]
+    last = 2 * stages - 1
+    held, beside = list(block), [None, None]
     pieces = [(block[half], half, 0) for half in range(2)]
     errors, flat, weights = (), (), ()
-    for stage in range(stages):
+    jobs = {1: "update update", 2: "update", 3: "update", 4: "place", 6: "place", 2 * stages - 1: "place flat"}
+    updated = 0
+    for step in range(2 * stages):
+        stage, half = step // 2, step % 2
+        if stage > 0:
+            arrived = (held[half], beside[half])
+            ids, errors, flat, weights, arrived = lax.optimization_barrier((ids, errors, flat, weights, arrived))
+            held[half], beside[half] = arrived
+            pieces += [(held[half], half, stage), (beside[half], half, stages + stage - 1)]
         if stage < stages - 1:
-            onward = [lax.ppermute(held[half], "rep", ring) for half in range(2)]
-            beside = [swap(held[half], "rep", replicas, 1) for half in range(2)]
-            arrived = [(onward[half], half, stage + 1) for half in range(2)]
-            arrived += [(beside[half], half, stages + stage) for half in range(2)]
+            here = held[half]
+            held[half] = lax.ppermute(here, "rep", ring)
+            beside[half] = swap(here, "rep", replicas, 1)
+        elif half == 0:
+            beside[half] = swap(held[half], "rep", replicas, 1)
         else:
-            arrived = [
-                (swap(held[0], "rep", replicas, 1), 0, 2 * stages - 1),
-                (lax.ppermute(beside[1], "rep", ring), 1, 2 * stages - 1),
-            ]
-        if stage == 0:
+            beside[half] = lax.ppermute(beside[half], "rep", ring)
+        if step == 2 * stages - 1:
             near = spread(near, "tp", tps)
-            for slot in range(tps):
-                errors = (update(slot, ids, errors),)
-        if stage == 1:
-            flat = flat_rows(ids, all_bases, jnp.stack(near))
-        if stage > 0:
-            weights = (place(pieces, ids, weights),)
-        arrays = [piece[0] for piece in arrived]
-        if stage < stages - 1:
-            ids, errors, flat, weights, near, arrays = lax.optimization_barrier((ids, errors, flat, weights, near, arrays))
-            held, beside = arrays[:2], arrays[2:]
-        if stage == 0:
-            arrived = [(block[half], half, 0) for half in range(2)] + arrived
-            arrays = [*block, *arrays]
-        pieces = [(array, *piece[1:]) for array, piece in zip(arrays, arrived)]
-    weights = place(pieces, ids, weights).reshape(matrices, width, cols)
+        for job in jobs.get(step, "").split():
+            if job == "update":
+                errors = (update(updated, ids, errors),)
+                updated += 1
+            elif job == "flat":
+                flat = flat_rows(ids, all_bases, jnp.stack(near))
+            else:
+                weights = (place(pieces, ids, weights),)
+                pieces = []
+    weights = place([(beside[half], half, last) for half in range(2)], ids, weights).reshape(matrices, width, cols)
     (new_error,) = errors
     new_momentum, new_master = flat
     return (new_error, right.reshape(matrices, rank, cols), new_momentum, new_master, weights)

time: 380 us -> 356 us (0.937)
  blocking collectives: 60.9 us -> 30 us
  waiting for transfers between devices: 140 us -> 130 us
  local copies, waits for them, and re-layouts: 16.3 us -> 23.9 us
  starting transfers between devices: 79.4 us -> 86.6 us
    all_to_all x4 -> x2, blocking collectives: 60.9 us -> 30 us  [local(): lax.all_to_all(parts, 'rep', split_axis=0, concat_axis=0, tiled=True)]
    ppermute x7, starting transfers between devices: 24.7 us -> 7.6 us  [the longest x6 6.61 us: local(): held[half] = lax.ppermute(here, 'rep', ring)]
    ppermute x53, starting transfers between devices: 54.7 us -> 69.6 us  [swap(): lax.ppermute(x, axis, [(index, index ^ offset) for index in range(size)])]
    ppermute x7, waiting for transfers between devices: 41.3 us -> 29.8 us  [the longest x6 29.8 us: local(): held[half] = lax.ppermute(here, 'rep', ring)]
    all_to_all x0 -> x2, starting transfers between devices: none -> 9.47 us  [local(): lax.all_to_all(parts, 'rep', split_axis=0, concat_axis=0, tiled=True)]
    unnamed x48 -> x38, local copies, waits for them, and re-layouts: 15.4 us -> 22.1 us
    all_to_all x0 -> x2, waiting for transfers between devices: none -> 5 us  [local(): lax.all_to_all(parts, 'rep', split_axis=0, concat_axis=0, tiled=True)]
  transfers between devices with their start and end apart: 60 -> 62, of which waited for: 29 -> 33; matrix products, arithmetic and copies ran while one was open for 1% -> 1% of each run, Pallas kernels for 14% -> 14%
where the time goes in v5:
time: 356 us; the launch traced here: 355 us
  waiting for transfers between devices  130 us (37%)
  starting transfers between devices  86.6 us (24%)
  Pallas kernels  80 us (22%)
  blocking collectives  30 us (8%)
  local copies, waits for them, and re-layouts  23.9 us (7%)
    ppermute x53, waiting for transfers between devices, swap(): lax.ppermute(x, axis, [(index, index ^ offset) for index in range(size)])  95.2 us
    pallas_call x17, Pallas kernels, grid_call(): pl.pallas_call(kernel, grid_spec=pltpu.PrefetchScalarGridSpec(num_scalar_...  71.2 us
    ppermute x53, starting transfers between devices, swap(): lax.ppermute(x, axis, [(index, index ^ offset) for index in range(size)])  69.6 us
    all_to_all x2, blocking collectives, local(): lax.all_to_all(parts, 'rep', split_axis=0, concat_axis=0, tiled=True)  30 us
    ppermute x6, waiting for transfers between devices, local(): held[half] = lax.ppermute(here, 'rep', ring)  29.8 us
    unnamed x38, local copies, waits for them, and re-layouts  22.1 us
    all_to_all x2, starting transfers between devices, local(): lax.all_to_all(parts, 'rep', split_axis=0, concat_axis=0, tiled=True)  9.47 us
    pallas_call x9, Pallas kernels, whole_call(): pl.pallas_call(kernel, in_specs=specs, out_specs=[out_spec] * len(out_sha...  8.89 us
  transfers between devices with their start and end apart: 62, of which 33 were waited for; matrix products, arithmetic and copies ran while one was open for 1% of the time, Pallas kernels for 14%

profile of v5, /device:TPU:0, one launch (start us, length us, event | category | flops | bytes accessed | tf_op | source)
XLA Modules:
  0.0 355.1 jit_solution(7495933454844534533)
XLA Ops:
  0.7 3.7 %copy-done.7 = bf16[1,12,768,512]{3,2,1,0:T(8,128)(2,1)S(1)} copy-done((bf16[1,12,768,512]{3,2,1,0:T(8,128)(2,1)S(1)}, bf16[1,12,768,512]{3,2,1,0:T(8,128)(2,1)}, u32[]{:S(2)}) %copy-start.7) | copy-done | bytes 9437208
  5.5 7.7 %first_left.2 = (bf16[6,768,512]{2,1,0:T(8,128)(2,1)S(1)}, bf16[6,768,512]{2,1,0:T(8,128)(2,1)S(1)}, f32[96,768]{1,0:T(8,128)S(1)}, f32[96,768]{1,0:T(8,128)S(1)}) custom-call(s32[2]{0:T(128)S(1)} %pad_add_fusion.ids_ref, bf16[1,12,768,512]{3,2,1,0:T(8,128)(2,1)S(1)} %copy-done.7, f32[1,12,768,512]{3,2,1,0:T(8,128)} %error_ref.3, f32[12,32,512]{2,1,0:T(8,128)S(1)} %copy-done.11), custom_call_target="tpu_custom_call" | custom-call | flops 452984832 | bytes 23592960 | tf_op jit(solution)/shard_map/first_left/pallas_call | solution.py:284
  17.6 2.9 collective-permute-start.1
  20.5 7.7 %first_left.3 = (bf16[6,768,512]{2,1,0:T(8,128)(2,1)S(1)}, bf16[6,768,512]{2,1,0:T(8,128)(2,1)S(1)}, f32[96,768]{1,0:T(8,128)S(1)}, f32[96,768]{1,0:T(8,128)S(1)}) custom-call(s32[2]{0:T(128)S(1)} %pad_add_fusion.ids_ref, bf16[1,12,768,512]{3,2,1,0:T(8,128)(2,1)S(1)} %copy-done.7, f32[1,12,768,512]{3,2,1,0:T(8,128)} %error_ref.3, f32[12,32,512]{2,1,0:T(8,128)S(1)} %copy-done.11), custom_call_target="tpu_custom_call" | custom-call | flops 452984832 | bytes 23592960 | tf_op jit(solution)/shard_map/first_left/pallas_call | solution.py:284
  34.2 7.1 %collective-permute-done.refs_1_ = f32[96,768]{1,0:T(8,128)S(1)} collective-permute-done((f32[96,768]{1,0:T(8,128)S(1)}, f32[96,768]{1,0:T(8,128)S(1)}, u32[]{:S(2)}, u32[]{:S(2)}) %collective-permute-start) | collective-permute-done | bytes 294944 | tf_op jit(solution)/shard_map/ppermute | solution.py:302
  42.1 5.8 %all-to-all-start = ((f32[8,72,128]{2,1,0:T(8,128)}), f32[8,72,128]{2,1,0:T(8,128)S(1)}, u32[]{:S(2)}, u32[]{:S(2)}) async-start(f32[8,72,128]{2,1,0:T(8,128)} %bitcast.2), calls=%async_computation | async-start | bytes 589824 | tf_op jit(solution)/shard_map/all_to_all | solution.py:380
  47.9 3.3 multiply_subtract_fusion
  53.1 5.0 %all-to-all-done.parts_ref = f32[8,72,128]{2,1,0:T(8,128)S(1)} async-done(((f32[8,72,128]{2,1,0:T(8,128)}), f32[8,72,128]{2,1,0:T(8,128)S(1)}, u32[]{:S(2)}, u32[]{:S(2)}) %all-to-all-start) | async-done | bytes 294944 | tf_op jit(solution)/shard_map/all_to_all | solution.py:380
  58.9 3.6 %all-to-all-start.1 = ((f32[8,72,128]{2,1,0:T(8,128)}), f32[8,72,128]{2,1,0:T(8,128)S(1)}, u32[]{:S(2)}, u32[]{:S(2)}) async-start(f32[8,72,128]{2,1,0:T(8,128)} %left_sum.2), calls=%async_computation.1 | async-start | bytes 589824 | tf_op jit(solution)/shard_map/all_to_all | solution.py:382
  63.3 4.6 %collective-permute-done.4.refs_10_ = f32[288,512]{1,0:T(8,128)} collective-permute-done((f32[288,512]{1,0:T(8,128)}, f32[288,512]{1,0:T(8,128)}, u32[]{:S(2)}, u32[]{:S(2)}) %collective-permute-start.4) | collective-permute-done | bytes 589856 | tf_op jit(solution)/shard_map/ppermute | solution.py:302
  67.9 11.4 %collective-permute-done.5.refs_11_ = f32[288,512]{1,0:T(8,128)} collective-permute-done((f32[288,512]{1,0:T(8,128)}, f32[288,512]{1,0:T(8,128)}, u32[]{:S(2)}, u32[]{:S(2)}) %collective-permute-start.5) | collective-permute-done | bytes 589856 | tf_op jit(solution)/shard_map/ppermute | solution.py:302
  92.4 2.9 right_far.2
  101.5 3.7 %collective-permute-start.14 = (f32[192,128]{1,0:T(8,128)S(1)}, f32[192,128]{1,0:T(8,128)S(1)}, u32[]{:S(2)}, u32[]{:S(2)}) collective-permute-start(f32[192,128]{1,0:T(8,128)S(1)} %get-tuple-element.101), channel_id=1, source_target_pairs={{0,24},{4,28},{8,16},{12,20},{16,8},{20,12},{24,0},{28,4},{1,25},{... | collective-permute-start | bytes 294920 | tf_op jit(solution)/shard_map/ppermute | solution.py:302
  107.4 6.2 %collective-permute-done.12.refs_4_ = f32[192,128]{1,0:T(8,128)S(1)} collective-permute-done((f32[192,128]{1,0:T(8,128)S(1)}, f32[192,128]{1,0:T(8,128)S(1)}, u32[]{:S(2)}, u32[]{:S(2)}) %collective-permute-start.12) | collective-permute-done | bytes 98336 | tf_op jit(solution)/shard_map/ppermute | solution.py:302
  113.7 2.8 collective-permute-done.13.refs_5_
  117.3 4.1 %collective-permute-start.17 = (f32[192,128]{1,0:T(8,128)S(1)}, f32[192,128]{1,0:T(8,128)S(1)}, u32[]{:S(2)}, u32[]{:S(2)}) collective-permute-start(f32[192,128]{1,0:T(8,128)S(1)} %right_sum.2.refs_0_), channel_id=1, source_target_pairs={{0,8},{4,12},{8,0},{12,4},{16,24},{20,28},{24,16},{28,20},{1,9},{5... | collective-permute-start | bytes 294920 | tf_op jit(solution)/shard_map/ppermute | solution.py:302
  121.9 3.1 collective-permute-start.19
  129.8 9.5 %collective-permute-done.20.refs_5_ = f32[192,128]{1,0:T(8,128)S(1)} collective-permute-done((f32[192,128]{1,0:T(8,128)S(1)}, f32[192,128]{1,0:T(8,128)S(1)}, u32[]{:S(2)}, u32[]{:S(2)}) %collective-permute-start.20) | collective-permute-done | bytes 98336 | tf_op jit(solution)/shard_map/ppermute | solution.py:302
  139.3 4.2 %left.3 = (f32[96,768]{1,0:T(8,128)S(1)}, f32[96,768]{1,0:T(8,128)S(1)}) custom-call(s32[2]{0:T(128)S(1)} %pad_add_fusion.ids_ref, bf16[6,768,512]{2,1,0:T(8,128)(2,1)S(1)} %bitcast.14, bf16[6,768,512]{2,1,0:T(8,128)(2,1)S(1)} %copy-done.2, f32[192,128]{1,0:T(8,128)S(1)} %right_sum.2.refs_0_, f32[192,128]{1,0:T(8,128)S(1)} %collective-permute-done.16.refs_1_, ...), custom_call_target="tpu_custom_call" | custom-call | flops 452984832 | bytes 23592960 | tf_op jit(solution)/shard_map/left/pallas_call | solution.py:284
  144.2 4.2 %left.2 = (f32[96,768]{1,0:T(8,128)S(1)}, f32[96,768]{1,0:T(8,128)S(1)}) custom-call(s32[2]{0:T(128)S(1)} %pad_add_fusion.ids_ref, bf16[6,768,512]{2,1,0:T(8,128)(2,1)S(1)} %copy-done.4, bf16[6,768,512]{2,1,0:T(8,128)(2,1)S(1)} %copy-done.6, f32[192,128]{1,0:T(8,128)S(1)} %right_sum.2.refs_0_, f32[192,128]{1,0:T(8,128)S(1)} %collective-permute-done.16.refs_1_, ...), custom_call_target="tpu_custom_call" | custom-call | flops 452984832 | bytes 23592960 | tf_op jit(solution)/shard_map/left/pallas_call | solution.py:284
  149.7 3.2 collective-permute-done.23.refs_1_
  152.9 4.5 %collective-permute-done.24.refs_2_ = f32[96,768]{1,0:T(8,128)S(1)} collective-permute-done((f32[96,768]{1,0:T(8,128)S(1)}, f32[96,768]{1,0:T(8,128)S(1)}, u32[]{:S(2)}, u32[]{:S(2)}) %collective-permute-start.24) | collective-permute-done | bytes 294944 | tf_op jit(solution)/shard_map/ppermute | solution.py:302
  157.5 16.9 %all_to_all.20.parts_ref = f32[8,72,128]{2,1,0:T(8,128)S(1)} all-to-all(f32[8,72,128]{2,1,0:T(8,128)S(1)} %bitcast.18), channel_id=1, replica_groups=mesh['rep'=8,'tp'=4] {'rep'}, dimensions={0} | all-to-all | bytes 589824 | tf_op jit(solution)/shard_map/all_to_all | solution.py:380
  174.4 13.0 %all_to_all.21 = f32[8,72,128]{2,1,0:T(8,128)S(1)} all-to-all(f32[8,72,128]{2,1,0:T(8,128)S(1)} %left_sum.3), channel_id=1, replica_groups=mesh['rep'=8,'tp'=4] {'rep'}, dimensions={0} | all-to-all | bytes 589824 | tf_op jit(solution)/shard_map/all_to_all | solution.py:382
  193.9 5.1 %collective-permute-done.27.first_ref = f32[96,768]{1,0:T(8,128)S(1)} collective-permute-done((f32[96,768]{1,0:T(8,128)S(1)}, f32[96,768]{1,0:T(8,128)S(1)}, u32[]{:S(2)}, u32[]{:S(2)}) %collective-permute-start.27) | collective-permute-done | bytes 294944 | tf_op jit(solution)/shard_map/ppermute | solution.py:302
  200.5 2.9 right_far.3
  211.5 3.1 collective-permute-start.35
  214.6 6.5 %collective-permute-done.32.refs_4_ = f32[192,128]{1,0:T(8,128)S(1)} collective-permute-done((f32[192,128]{1,0:T(8,128)S(1)}, f32[192,128]{1,0:T(8,128)S(1)}, u32[]{:S(2)}, u32[]{:S(2)}) %collective-permute-start.32) | collective-permute-done | bytes 98336 | tf_op jit(solution)/shard_map/ppermute | solution.py:302
  224.8 3.9 %collective-permute-start.37 = (f32[192,128]{1,0:T(8,128)S(1)}, f32[192,128]{1,0:T(8,128)S(1)}, u32[]{:S(2)}, u32[]{:S(2)}) collective-permute-start(f32[192,128]{1,0:T(8,128)S(1)} %right_sum.3.refs_0_), channel_id=1, source_target_pairs={{0,8},{4,12},{8,0},{12,4},{16,24},{20,28},{24,16},{28,20},{1,9},{5... | collective-permute-start | bytes 294920 | tf_op jit(solution)/shard_map/ppermute | solution.py:302
  236.6 6.5 %collective-permute-done.39.refs_4_ = f32[192,128]{1,0:T(8,128)S(1)} collective-permute-done((f32[192,128]{1,0:T(8,128)S(1)}, f32[192,128]{1,0:T(8,128)S(1)}, u32[]{:S(2)}, u32[]{:S(2)}) %collective-permute-start.39) | collective-permute-done | bytes 98336 | tf_op jit(solution)/shard_map/ppermute | solution.py:302
  243.1 3.0 collective-permute-done.40.refs_5_
  246.2 3.3 late_rows.1
  249.5 3.7 %collective-permute-start.43 = (bf16[576,512]{1,0:T(8,128)(2,1)S(1)}, bf16[576,512]{1,0:T(8,128)(2,1)S(1)}, u32[]{:S(2)}, u32[]{:S(2)}) collective-permute-start(bf16[576,512]{1,0:T(8,128)(2,1)S(1)} %get-tuple-element.122.refs_0_), channel_id=1, source_target_pairs={{0,8},{4,12},{8,16},{12,20},{16,24},{20,28},{24,0},{28,4},{1,9},{5... | collective-permute-start | bytes 1769480 | tf_op jit(solution)/shard_map/ppermute | solution.py:535
  256.7 4.1 %update.4.refs_0_ = f32[1,12,768,512]{3,2,1,0:T(8,128)} custom-call(s32[2]{0:T(128)S(1)} %pad_add_fusion.ids_ref, f32[384,768]{1,0:T(8,128)S(1)} %pad_maximum_fusion.basis_ref, f32[384,512]{1,0:T(8,128)S(1)} %copy-done.8, bf16[6,768,512]{2,1,0:T(8,128)(2,1)S(1)} %copy-done.4, bf16[6,768,512]{2,1,0:T(8,128)(2,1)S(1)} %copy-done.6), custom_call_target="tpu_custom_call" | custom-call | flops 226492416 | bytes 9437184 | tf_op jit(solution)/shard_map/update/pallas_call | solution.py:284
  260.7 4.1 %update.5.refs_0_ = f32[1,12,768,512]{3,2,1,0:T(8,128)} custom-call(s32[2]{0:T(128)S(1)} %pad_add_fusion.ids_ref, f32[384,768]{1,0:T(8,128)S(1)} %pad_maximum_fusion.basis_ref, f32[384,512]{1,0:T(8,128)S(1)} %copy-done.8, bf16[6,768,512]{2,1,0:T(8,128)(2,1)S(1)} %copy-done.4, bf16[6,768,512]{2,1,0:T(8,128)(2,1)S(1)} %copy-done.6, ...), custom_call_target="tpu_custom_call", output_to_operand_aliasing={{}: (5, {})} | custom-call | flops 226492416 | bytes 9437184 | tf_op jit(solution)/shard_map/update/pallas_call | solution.py:284
  271.4 4.1 %update.6.refs_0_ = f32[1,12,768,512]{3,2,1,0:T(8,128)} custom-call(s32[2]{0:T(128)S(1)} %pad_add_fusion.ids_ref, f32[384,768]{1,0:T(8,128)S(1)} %pad_maximum_fusion.basis_ref, f32[384,512]{1,0:T(8,128)S(1)} %copy-done.8, bf16[6,768,512]{2,1,0:T(8,128)(2,1)S(1)} %bitcast.14, bf16[6,768,512]{2,1,0:T(8,128)(2,1)S(1)} %copy-done.2, ...), custom_call_target="tpu_custom_call", output_to_operand_aliasing={{}: (5, {})} | custom-call | flops 226492416 | bytes 9437184 | tf_op jit(solution)/shard_map/update/pallas_call | solution.py:284
  275.4 4.7 %collective-permute-done.45.refs_4_ = bf16[576,512]{1,0:T(8,128)(2,1)S(1)} collective-permute-done((bf16[576,512]{1,0:T(8,128)(2,1)S(1)}, bf16[576,512]{1,0:T(8,128)(2,1)S(1)}, u32[]{:S(2)}, u32[]{:S(2)}) %collective-permute-start.45) | collective-permute-done | bytes 589856 | tf_op jit(solution)/shard_map/ppermute | solution.py:535
  284.0 4.1 %update.7 = f32[1,12,768,512]{3,2,1,0:T(8,128)} custom-call(s32[2]{0:T(128)S(1)} %pad_add_fusion.ids_ref, f32[384,768]{1,0:T(8,128)S(1)} %pad_maximum_fusion.basis_ref, f32[384,512]{1,0:T(8,128)S(1)} %copy-done.8, bf16[6,768,512]{2,1,0:T(8,128)(2,1)S(1)} %bitcast.14, bf16[6,768,512]{2,1,0:T(8,128)(2,1)S(1)} %copy-done.2, ...), custom_call_target="tpu_custom_call", output_to_operand_aliasing={{}: (5, {})} | custom-call | flops 226492416 | bytes 9437184 | tf_op jit(solution)/shard_map/update/pallas_call | solution.py:284
  288.1 4.7 %collective-permute-done.47.refs_6_ = bf16[576,512]{1,0:T(8,128)(2,1)S(1)} collective-permute-done((bf16[576,512]{1,0:T(8,128)(2,1)S(1)}, bf16[576,512]{1,0:T(8,128)(2,1)S(1)}, u32[]{:S(2)}, u32[]{:S(2)}) %collective-permute-start.47) | collective-permute-done | bytes 589856 | tf_op jit(solution)/shard_map/ppermute | solution.py:535
  296.6 4.4 %place.4.refs_4_ = bf16[8,2,576,512]{3,2,1,0:T(8,128)(2,1)} custom-call(s32[2]{0:T(128)S(1)} %pad_add_fusion.ids_ref, bf16[576,512]{1,0:T(8,128)(2,1)S(1)} %get-tuple-element.122.refs_0_, bf16[576,512]{1,0:T(8,128)(2,1)S(1)} %get-tuple-element.125.refs_1_, bf16[576,512]{1,0:T(8,128)(2,1)S(1)} %collective-permute-done.43.refs_2_, ...), custom_call_target="tpu_custom_call" | custom-call | bytes 18874368 | tf_op jit(solution)/shard_map/place/pallas_call | solution.py:284
  301.0 4.5 %collective-permute-done.49.refs_0_ = bf16[576,512]{1,0:T(8,128)(2,1)S(1)} collective-permute-done((bf16[576,512]{1,0:T(8,128)(2,1)S(1)}, bf16[576,512]{1,0:T(8,128)(2,1)S(1)}, u32[]{:S(2)}, u32[]{:S(2)}) %collective-permute-start.49) | collective-permute-done | bytes 589856 | tf_op jit(solution)/shard_map/ppermute | solution.py:535
  309.3 8.9 %collective-permute-done.51.refs_2_ = bf16[576,512]{1,0:T(8,128)(2,1)} collective-permute-done((bf16[576,512]{1,0:T(8,128)(2,1)S(1)}, bf16[576,512]{1,0:T(8,128)(2,1)}, u32[]{:S(2)}, u32[]{:S(2)}) %collective-permute-start.51) | collective-permute-done | bytes 589856 | tf_op jit(solution)/shard_map/ppermute | solution.py:535
  320.0 3.6 %place.5.refs_2_ = bf16[8,2,576,512]{3,2,1,0:T(8,128)(2,1)} custom-call(s32[2]{0:T(128)S(1)} %pad_add_fusion.ids_ref, bf16[576,512]{1,0:T(8,128)(2,1)S(1)} %collective-permute-done.49.refs_0_, bf16[576,512]{1,0:T(8,128)(2,1)S(1)} %collective-permute-done.50.refs_1_, ...), custom_call_target="tpu_custom_call", output_to_operand_aliasing={{}: (5, {})} | custom-call | bytes 9437184 | tf_op jit(solution)/shard_map/place/pallas_call | solution.py:284
  323.6 4.3 %collective-permute-done.53.refs_0_ = bf16[576,512]{1,0:T(8,128)(2,1)S(1)} collective-permute-done((bf16[576,512]{1,0:T(8,128)(2,1)S(1)}, bf16[576,512]{1,0:T(8,128)(2,1)S(1)}, u32[]{:S(2)}, u32[]{:S(2)}) %collective-permute-start.53) | collective-permute-done | bytes 589856 | tf_op jit(solution)/shard_map/ppermute | solution.py:535
  339.2 2.9 collective-permute-done.56
  343.2 2.8 place.6.refs_2_
  346.0 6.1 %flat_rows.1 = (f32[288,2048]{1,0:T(8,128)}, f32[288,2048]{1,0:T(8,128)}) custom-call(s32[2]{0:T(128)S(1)} %pad_add_fusion.ids_ref, f32[384,768]{1,0:T(8,128)S(1)} %pad_maximum_fusion.basis_ref, f32[4,64,512]{2,1,0:T(8,128)S(1)} %pad_maximum_fusion.1.near_ref, f32[288,2048]{1,0:T(8,128)S(1)} %copy-done.9, f32[288,2048]{1,0:T(8,128)S(1)} %copy-done.10), custom_call_target="tpu_custom_call" | custom-call | flops 452984832 | bytes 9437184 | tf_op jit(solution)/shard_map/flat_rows/pallas_call | solution.py:284
  352.2 2.9 place.7
  (149 shorter events, 108.7 us)
Async XLA Ops:
  17.6 16.6 %collective-permute-start.1 = (f32[96,768]{1,0:T(8,128)S(1)}, f32[96,768]{1,0:T(8,128)S(1)}, u32[]{:S(2)}, u32[]{:S(2)}) collective-permute-start(f32[96,768]{1,0:T(8,128)S(1)} %get-tuple-element.79), channel_id=1, source_target_pairs={{0,2},{1,3},{2,0},{3,1},{4,6},{5,7},{6,4},{7,5},{8,10},{9,11},{10,... | collective-permute-start | bytes 884744 | tf_op jit(solution)/shard_map/ppermute | solution.py:302
  32.6 8.7 %collective-permute-start = (f32[96,768]{1,0:T(8,128)S(1)}, f32[96,768]{1,0:T(8,128)S(1)}, u32[]{:S(2)}, u32[]{:S(2)}) collective-permute-start(f32[96,768]{1,0:T(8,128)S(1)} %get-tuple-element.85), channel_id=1, source_target_pairs={{0,3},{1,2},{2,1},{3,0},{4,7},{5,6},{6,5},{7,4},{8,11},{9,10},{10,... | collective-permute-start | bytes 884744 | tf_op jit(solution)/shard_map/ppermute | solution.py:302
  42.1 16.0 %all-to-all-start = ((f32[8,72,128]{2,1,0:T(8,128)}), f32[8,72,128]{2,1,0:T(8,128)S(1)}, u32[]{:S(2)}, u32[]{:S(2)}) async-start(f32[8,72,128]{2,1,0:T(8,128)} %bitcast.2), calls=%async_computation | async-start | bytes 589824 | tf_op jit(solution)/shard_map/all_to_all | solution.py:380
  51.3 11.2 %collective-permute-start.3 = (f32[288,512]{1,0:T(8,128)}, f32[288,512]{1,0:T(8,128)S(1)}, u32[]{:S(2)}, u32[]{:S(2)}) collective-permute-start(f32[288,512]{1,0:T(8,128)} %get-tuple-element.155), channel_id=1, source_target_pairs={{0,1},{1,0},{2,3},{3,2},{4,5},{5,4},{6,7},{7,6},{8,9},{9,8},{10,11... | collective-permute-start | bytes 1769480 | tf_op jit(solution)/shard_map/ppermute | solution.py:302
  51.4 16.5 %collective-permute-start.4 = (f32[288,512]{1,0:T(8,128)}, f32[288,512]{1,0:T(8,128)}, u32[]{:S(2)}, u32[]{:S(2)}) collective-permute-start(f32[288,512]{1,0:T(8,128)} %get-tuple-element.154), channel_id=1, source_target_pairs={{0,2},{1,3},{2,0},{3,1},{4,6},{5,7},{6,4},{7,5},{8,10},{9,11},{10,... | collective-permute-start | bytes 1769480 | tf_op jit(solution)/shard_map/ppermute | solution.py:302
  52.0 27.4 %collective-permute-start.5 = (f32[288,512]{1,0:T(8,128)}, f32[288,512]{1,0:T(8,128)}, u32[]{:S(2)}, u32[]{:S(2)}) collective-permute-start(f32[288,512]{1,0:T(8,128)} %get-tuple-element.153), channel_id=1, source_target_pairs={{0,3},{1,2},{2,1},{3,0},{4,7},{5,6},{6,5},{7,4},{8,11},{9,10},{10,... | collective-permute-start | bytes 1769480 | tf_op jit(solution)/shard_map/ppermute | solution.py:302
  58.9 20.5 %all-to-all-start.1 = ((f32[8,72,128]{2,1,0:T(8,128)}), f32[8,72,128]{2,1,0:T(8,128)S(1)}, u32[]{:S(2)}, u32[]{:S(2)}) async-start(f32[8,72,128]{2,1,0:T(8,128)} %left_sum.2), calls=%async_computation.1 | async-start | bytes 589824 | tf_op jit(solution)/shard_map/all_to_all | solution.py:382
  81.8 9.0 %collective-permute-start.7 = (f32[96,768]{1,0:T(8,128)S(1)}, f32[96,768]{1,0:T(8,128)S(1)}, u32[]{:S(2)}, u32[]{:S(2)}) collective-permute-start(f32[96,768]{1,0:T(8,128)S(1)} %basis.2.first_ref), channel_id=1, source_target_pairs={{0,2},{1,3},{2,0},{3,1},{4,6},{5,7},{6,4},{7,5},{8,10},{9,11},{10,... | collective-permute-start | bytes 884744 | tf_op jit(solution)/shard_map/ppermute | solution.py:302
  95.3 9.9 %collective-permute-start.10 = (f32[192,128]{1,0:T(8,128)S(1)}, f32[192,128]{1,0:T(8,128)S(1)}, u32[]{:S(2)}, u32[]{:S(2)}) collective-permute-start(f32[192,128]{1,0:T(8,128)S(1)} %get-tuple-element.97), channel_id=1, source_target_pairs={{0,8},{4,12},{8,0},{12,4},{16,24},{20,28},{24,16},{28,20},{1,9},{5... | collective-permute-start | bytes 294920 | tf_op jit(solution)/shard_map/ppermute | solution.py:302
  97.6 9.8 %collective-permute-start.11 = (f32[192,128]{1,0:T(8,128)S(1)}, f32[192,128]{1,0:T(8,128)S(1)}, u32[]{:S(2)}, u32[]{:S(2)}) collective-permute-start(f32[192,128]{1,0:T(8,128)S(1)} %get-tuple-element.98), channel_id=1, source_target_pairs={{0,12},{4,8},{8,4},{12,0},{16,28},{20,24},{24,20},{28,16},{1,13},{... | collective-permute-start | bytes 294920 | tf_op jit(solution)/shard_map/ppermute | solution.py:302
  99.1 14.6 %collective-permute-start.12 = (f32[192,128]{1,0:T(8,128)S(1)}, f32[192,128]{1,0:T(8,128)S(1)}, u32[]{:S(2)}, u32[]{:S(2)}) collective-permute-start(f32[192,128]{1,0:T(8,128)S(1)} %get-tuple-element.99), channel_id=1, source_target_pairs={{0,16},{4,20},{8,24},{12,28},{16,0},{20,4},{24,8},{28,12},{1,17},{... | collective-permute-start | bytes 294920 | tf_op jit(solution)/shard_map/ppermute | solution.py:302
  101.4 15.0 %collective-permute-start.13 = (f32[192,128]{1,0:T(8,128)S(1)}, f32[192,128]{1,0:T(8,128)S(1)}, u32[]{:S(2)}, u32[]{:S(2)}) collective-permute-start(f32[192,128]{1,0:T(8,128)S(1)} %get-tuple-element.100), channel_id=1, source_target_pairs={{0,20},{4,16},{8,28},{12,24},{16,4},{20,0},{24,12},{28,8},{1,21},{... | collective-permute-start | bytes 294920 | tf_op jit(solution)/shard_map/ppermute | solution.py:302
  101.5 15.0 %collective-permute-start.14 = (f32[192,128]{1,0:T(8,128)S(1)}, f32[192,128]{1,0:T(8,128)S(1)}, u32[]{:S(2)}, u32[]{:S(2)}) collective-permute-start(f32[192,128]{1,0:T(8,128)S(1)} %get-tuple-element.101), channel_id=1, source_target_pairs={{0,24},{4,28},{8,16},{12,20},{16,8},{20,12},{24,0},{28,4},{1,25},{... | collective-permute-start | bytes 294920 | tf_op jit(solution)/shard_map/ppermute | solution.py:302
  105.3 11.2 %collective-permute-start.15 = (f32[192,128]{1,0:T(8,128)S(1)}, f32[192,128]{1,0:T(8,128)S(1)}, u32[]{:S(2)}, u32[]{:S(2)}) collective-permute-start(f32[192,128]{1,0:T(8,128)S(1)} %get-tuple-element.102), channel_id=1, source_target_pairs={{0,28},{4,24},{8,20},{12,16},{16,12},{20,8},{24,4},{28,0},{1,29},{... | collective-permute-start | bytes 294920 | tf_op jit(solution)/shard_map/ppermute | solution.py:302
  107.4 9.1 %collective-permute-start.9 = (f32[192,128]{1,0:T(8,128)S(1)}, f32[192,128]{1,0:T(8,128)S(1)}, u32[]{:S(2)}, u32[]{:S(2)}) collective-permute-start(f32[192,128]{1,0:T(8,128)S(1)} %get-tuple-element.96), channel_id=1, source_target_pairs={{0,4},{4,0},{8,12},{12,8},{16,20},{20,16},{24,28},{28,24},{1,5},{5... | collective-permute-start | bytes 294920 | tf_op jit(solution)/shard_map/ppermute | solution.py:302
  116.5 9.3 %collective-permute-start.16 = (f32[192,128]{1,0:T(8,128)S(1)}, f32[192,128]{1,0:T(8,128)S(1)}, u32[]{:S(2)}, u32[]{:S(2)}) collective-permute-start(f32[192,128]{1,0:T(8,128)S(1)} %right_sum.2.refs_0_), channel_id=1, source_target_pairs={{0,4},{4,0},{8,12},{12,8},{16,20},{20,16},{24,28},{28,24},{1,5},{5... | collective-permute-start | bytes 294920 | tf_op jit(solution)/shard_map/ppermute | solution.py:302
  117.3 10.9 %collective-permute-start.17 = (f32[192,128]{1,0:T(8,128)S(1)}, f32[192,128]{1,0:T(8,128)S(1)}, u32[]{:S(2)}, u32[]{:S(2)}) collective-permute-start(f32[192,128]{1,0:T(8,128)S(1)} %right_sum.2.refs_0_), channel_id=1, source_target_pairs={{0,8},{4,12},{8,0},{12,4},{16,24},{20,28},{24,16},{28,20},{1,9},{5... | collective-permute-start | bytes 294920 | tf_op jit(solution)/shard_map/ppermute | solution.py:302
  125.0 14.3 %collective-permute-start.20 = (f32[192,128]{1,0:T(8,128)S(1)}, f32[192,128]{1,0:T(8,128)S(1)}, u32[]{:S(2)}, u32[]{:S(2)}) collective-permute-start(f32[192,128]{1,0:T(8,128)S(1)} %right_sum.2.refs_0_), channel_id=1, source_target_pairs={{0,20},{4,16},{8,28},{12,24},{16,4},{20,0},{24,12},{28,8},{1,21},{... | collective-permute-start | bytes 294920 | tf_op jit(solution)/shard_map/ppermute | solution.py:302
  125.8 13.5 %collective-permute-start.21 = (f32[192,128]{1,0:T(8,128)S(1)}, f32[192,128]{1,0:T(8,128)S(1)}, u32[]{:S(2)}, u32[]{:S(2)}) collective-permute-start(f32[192,128]{1,0:T(8,128)S(1)} %right_sum.2.refs_0_), channel_id=1, source_target_pairs={{0,24},{4,28},{8,16},{12,20},{16,8},{20,12},{24,0},{28,4},{1,25},{... | collective-permute-start | bytes 294920 | tf_op jit(solution)/shard_map/ppermute | solution.py:302
  128.2 11.1 %collective-permute-start.22 = (f32[192,128]{1,0:T(8,128)S(1)}, f32[192,128]{1,0:T(8,128)S(1)}, u32[]{:S(2)}, u32[]{:S(2)}) collective-permute-start(f32[192,128]{1,0:T(8,128)S(1)} %right_sum.2.refs_0_), channel_id=1, source_target_pairs={{0,28},{4,24},{8,20},{12,16},{16,12},{20,8},{24,4},{28,0},{1,29},{... | collective-permute-start | bytes 294920 | tf_op jit(solution)/shard_map/ppermute | solution.py:302
  143.5 9.4 %collective-permute-start.23 = (f32[96,768]{1,0:T(8,128)S(1)}, f32[96,768]{1,0:T(8,128)S(1)}, u32[]{:S(2)}, u32[]{:S(2)}) collective-permute-start(f32[96,768]{1,0:T(8,128)S(1)} %get-tuple-element.104), channel_id=1, source_target_pairs={{0,3},{1,2},{2,1},{3,0},{4,7},{5,6},{6,5},{7,4},{8,11},{9,10},{10,... | collective-permute-start | bytes 884744 | tf_op jit(solution)/shard_map/ppermute | solution.py:302
  143.6 13.8 %collective-permute-start.24 = (f32[96,768]{1,0:T(8,128)S(1)}, f32[96,768]{1,0:T(8,128)S(1)}, u32[]{:S(2)}, u32[]{:S(2)}) collective-permute-start(f32[96,768]{1,0:T(8,128)S(1)} %get-tuple-element.105), channel_id=1, source_target_pairs={{0,2},{1,3},{2,0},{3,1},{4,6},{5,7},{6,4},{7,5},{8,10},{9,11},{10,... | collective-permute-start | bytes 884744 | tf_op jit(solution)/shard_map/ppermute | solution.py:302
  148.4 9.0 %collective-permute-start.25 = (f32[96,768]{1,0:T(8,128)S(1)}, f32[96,768]{1,0:T(8,128)S(1)}, u32[]{:S(2)}, u32[]{:S(2)}) collective-permute-start(f32[96,768]{1,0:T(8,128)S(1)} %get-tuple-element.106), channel_id=1, source_target_pairs={{0,1},{1,0},{2,3},{3,2},{4,5},{5,4},{6,7},{7,6},{8,9},{9,8},{10,11... | collective-permute-start | bytes 884744 | tf_op jit(solution)/shard_map/ppermute | solution.py:302
  189.5 9.4 %collective-permute-start.27 = (f32[96,768]{1,0:T(8,128)S(1)}, f32[96,768]{1,0:T(8,128)S(1)}, u32[]{:S(2)}, u32[]{:S(2)}) collective-permute-start(f32[96,768]{1,0:T(8,128)S(1)} %basis.3.first_ref), channel_id=1, source_target_pairs={{0,2},{1,3},{2,0},{3,1},{4,6},{5,7},{6,4},{7,5},{8,10},{9,11},{10,... | collective-permute-start | bytes 884744 | tf_op jit(solution)/shard_map/ppermute | solution.py:302
  204.6 10.0 %collective-permute-start.31 = (f32[192,128]{1,0:T(8,128)S(1)}, f32[192,128]{1,0:T(8,128)S(1)}, u32[]{:S(2)}, u32[]{:S(2)}) collective-permute-start(f32[192,128]{1,0:T(8,128)S(1)} %get-tuple-element.112), channel_id=1, source_target_pairs={{0,12},{4,8},{8,4},{12,0},{16,28},{20,24},{24,20},{28,16},{1,13},{... | collective-permute-start | bytes 294920 | tf_op jit(solution)/shard_map/ppermute | solution.py:302
  207.0 14.2 %collective-permute-start.32 = (f32[192,128]{1,0:T(8,128)S(1)}, f32[192,128]{1,0:T(8,128)S(1)}, u32[]{:S(2)}, u32[]{:S(2)}) collective-permute-start(f32[192,128]{1,0:T(8,128)S(1)} %get-tuple-element.113), channel_id=1, source_target_pairs={{0,16},{4,20},{8,24},{12,28},{16,0},{20,4},{24,8},{28,12},{1,17},{... | collective-permute-start | bytes 294920 | tf_op jit(solution)/shard_map/ppermute | solution.py:302
  207.6 16.3 %collective-permute-start.33 = (f32[192,128]{1,0:T(8,128)S(1)}, f32[192,128]{1,0:T(8,128)S(1)}, u32[]{:S(2)}, u32[]{:S(2)}) collective-permute-start(f32[192,128]{1,0:T(8,128)S(1)} %get-tuple-element.114), channel_id=1, source_target_pairs={{0,20},{4,16},{8,28},{12,24},{16,4},{20,0},{24,12},{28,8},{1,21},{... | collective-permute-start | bytes 294920 | tf_op jit(solution)/shard_map/ppermute | solution.py:302
  210.0 13.9 %collective-permute-start.34 = (f32[192,128]{1,0:T(8,128)S(1)}, f32[192,128]{1,0:T(8,128)S(1)}, u32[]{:S(2)}, u32[]{:S(2)}) collective-permute-start(f32[192,128]{1,0:T(8,128)S(1)} %get-tuple-element.115), channel_id=1, source_target_pairs={{0,24},{4,28},{8,16},{12,20},{16,8},{20,12},{24,0},{28,4},{1,25},{... | collective-permute-start | bytes 294920 | tf_op jit(solution)/shard_map/ppermute | solution.py:302
  211.5 12.4 %collective-permute-start.35 = (f32[192,128]{1,0:T(8,128)S(1)}, f32[192,128]{1,0:T(8,128)S(1)}, u32[]{:S(2)}, u32[]{:S(2)}) collective-permute-start(f32[192,128]{1,0:T(8,128)S(1)} %get-tuple-element.116), channel_id=1, source_target_pairs={{0,28},{4,24},{8,20},{12,16},{16,12},{20,8},{24,4},{28,0},{1,29},{... | collective-permute-start | bytes 294920 | tf_op jit(solution)/shard_map/ppermute | solution.py:302
  224.8 9.2 %collective-permute-start.37 = (f32[192,128]{1,0:T(8,128)S(1)}, f32[192,128]{1,0:T(8,128)S(1)}, u32[]{:S(2)}, u32[]{:S(2)}) collective-permute-start(f32[192,128]{1,0:T(8,128)S(1)} %right_sum.3.refs_0_), channel_id=1, source_target_pairs={{0,8},{4,12},{8,0},{12,4},{16,24},{20,28},{24,16},{28,20},{1,9},{5... | collective-permute-start | bytes 294920 | tf_op jit(solution)/shard_map/ppermute | solution.py:302
  228.9 14.3 %collective-permute-start.39 = (f32[192,128]{1,0:T(8,128)S(1)}, f32[192,128]{1,0:T(8,128)S(1)}, u32[]{:S(2)}, u32[]{:S(2)}) collective-permute-start(f32[192,128]{1,0:T(8,128)S(1)} %right_sum.3.refs_0_), channel_id=1, source_target_pairs={{0,16},{4,20},{8,24},{12,28},{16,0},{20,4},{24,8},{28,12},{1,17},{... | collective-permute-start | bytes 294920 | tf_op jit(solution)/shard_map/ppermute | solution.py:302
  231.5 14.7 %collective-permute-start.40 = (f32[192,128]{1,0:T(8,128)S(1)}, f32[192,128]{1,0:T(8,128)S(1)}, u32[]{:S(2)}, u32[]{:S(2)}) collective-permute-start(f32[192,128]{1,0:T(8,128)S(1)} %right_sum.3.refs_0_), channel_id=1, source_target_pairs={{0,20},{4,16},{8,28},{12,24},{16,4},{20,0},{24,12},{28,8},{1,21},{... | collective-permute-start | bytes 294920 | tf_op jit(solution)/shard_map/ppermute | solution.py:302
  232.6 13.6 %collective-permute-start.41 = (f32[192,128]{1,0:T(8,128)S(1)}, f32[192,128]{1,0:T(8,128)S(1)}, u32[]{:S(2)}, u32[]{:S(2)}) collective-permute-start(f32[192,128]{1,0:T(8,128)S(1)} %right_sum.3.refs_0_), channel_id=1, source_target_pairs={{0,24},{4,28},{8,16},{12,20},{16,8},{20,12},{24,0},{28,4},{1,25},{... | collective-permute-start | bytes 294920 | tf_op jit(solution)/shard_map/ppermute | solution.py:302
  234.0 12.1 %collective-permute-start.42 = (f32[192,128]{1,0:T(8,128)S(1)}, f32[192,128]{1,0:T(8,128)S(1)}, u32[]{:S(2)}, u32[]{:S(2)}) collective-permute-start(f32[192,128]{1,0:T(8,128)S(1)} %right_sum.3.refs_0_), channel_id=1, source_target_pairs={{0,28},{4,24},{8,20},{12,16},{16,12},{20,8},{24,4},{28,0},{1,29},{... | collective-permute-start | bytes 294920 | tf_op jit(solution)/shard_map/ppermute | solution.py:302
  249.5 18.1 %collective-permute-start.43 = (bf16[576,512]{1,0:T(8,128)(2,1)S(1)}, bf16[576,512]{1,0:T(8,128)(2,1)S(1)}, u32[]{:S(2)}, u32[]{:S(2)}) collective-permute-start(bf16[576,512]{1,0:T(8,128)(2,1)S(1)} %get-tuple-element.122.refs_0_), channel_id=1, source_target_pairs={{0,8},{4,12},{8,16},{12,20},{16,24},{20,28},{24,0},{28,4},{1,9},{5... | collective-permute-start | bytes 1769480 | tf_op jit(solution)/shard_map/ppermute | solution.py:535
  253.2 16.3 %collective-permute-start.44 = (bf16[576,512]{1,0:T(8,128)(2,1)S(1)}, bf16[576,512]{1,0:T(8,128)(2,1)S(1)}, u32[]{:S(2)}, u32[]{:S(2)}) collective-permute-start(bf16[576,512]{1,0:T(8,128)(2,1)S(1)} %get-tuple-element.122.refs_0_), channel_id=1, source_target_pairs={{0,4},{4,0},{8,12},{12,8},{16,20},{20,16},{24,28},{28,24},{1,5},{5... | collective-permute-start | bytes 1769480 | tf_op jit(solution)/shard_map/ppermute | solution.py:302
  253.5 26.6 %collective-permute-start.45 = (bf16[576,512]{1,0:T(8,128)(2,1)S(1)}, bf16[576,512]{1,0:T(8,128)(2,1)S(1)}, u32[]{:S(2)}, u32[]{:S(2)}) collective-permute-start(bf16[576,512]{1,0:T(8,128)(2,1)S(1)} %get-tuple-element.125.refs_1_), channel_id=1, source_target_pairs={{0,8},{4,12},{8,16},{12,20},{16,24},{20,28},{24,0},{28,4},{1,9},{5... | collective-permute-start | bytes 1769480 | tf_op jit(solution)/shard_map/ppermute | solution.py:535
  255.1 27.0 %collective-permute-start.46 = (bf16[576,512]{1,0:T(8,128)(2,1)S(1)}, bf16[576,512]{1,0:T(8,128)(2,1)S(1)}, u32[]{:S(2)}, u32[]{:S(2)}) collective-permute-start(bf16[576,512]{1,0:T(8,128)(2,1)S(1)} %get-tuple-element.125.refs_1_), channel_id=1, source_target_pairs={{0,4},{4,0},{8,12},{12,8},{16,20},{20,16},{24,28},{28,24},{1,5},{5... | collective-permute-start | bytes 1769480 | tf_op jit(solution)/shard_map/ppermute | solution.py:302
  269.4 23.4 %collective-permute-start.47 = (bf16[576,512]{1,0:T(8,128)(2,1)S(1)}, bf16[576,512]{1,0:T(8,128)(2,1)S(1)}, u32[]{:S(2)}, u32[]{:S(2)}) collective-permute-start(bf16[576,512]{1,0:T(8,128)(2,1)S(1)} %collective-permute-done.43.refs_2_), channel_id=1, source_target_pairs={{0,8},{4,12},{8,16},{12,20},{16,24},{20,28},{24,0},{28,4},{1,9},{5... | collective-permute-start | bytes 1769480 | tf_op jit(solution)/shard_map/ppermute | solution.py:535
  269.8 24.9 %collective-permute-start.48 = (bf16[576,512]{1,0:T(8,128)(2,1)S(1)}, bf16[576,512]{1,0:T(8,128)(2,1)S(1)}, u32[]{:S(2)}, u32[]{:S(2)}) collective-permute-start(bf16[576,512]{1,0:T(8,128)(2,1)S(1)} %collective-permute-done.43.refs_2_), channel_id=1, source_target_pairs={{0,4},{4,0},{8,12},{12,8},{16,20},{20,16},{24,28},{28,24},{1,5},{5... | collective-permute-start | bytes 1769480 | tf_op jit(solution)/shard_map/ppermute | solution.py:302
  282.1 23.4 %collective-permute-start.49 = (bf16[576,512]{1,0:T(8,128)(2,1)S(1)}, bf16[576,512]{1,0:T(8,128)(2,1)S(1)}, u32[]{:S(2)}, u32[]{:S(2)}) collective-permute-start(bf16[576,512]{1,0:T(8,128)(2,1)S(1)} %collective-permute-done.45.refs_4_), channel_id=1, source_target_pairs={{0,8},{4,12},{8,16},{12,20},{16,24},{20,28},{24,0},{28,4},{1,9},{5... | collective-permute-start | bytes 1769480 | tf_op jit(solution)/shard_map/ppermute | solution.py:535
  282.4 24.9 %collective-permute-start.50 = (bf16[576,512]{1,0:T(8,128)(2,1)S(1)}, bf16[576,512]{1,0:T(8,128)(2,1)S(1)}, u32[]{:S(2)}, u32[]{:S(2)}) collective-permute-start(bf16[576,512]{1,0:T(8,128)(2,1)S(1)} %collective-permute-done.45.refs_4_), channel_id=1, source_target_pairs={{0,4},{4,0},{8,12},{12,8},{16,20},{20,16},{24,28},{28,24},{1,5},{5... | collective-permute-start | bytes 1769480 | tf_op jit(solution)/shard_map/ppermute | solution.py:302
  294.7 23.5 %collective-permute-start.51 = (bf16[576,512]{1,0:T(8,128)(2,1)S(1)}, bf16[576,512]{1,0:T(8,128)(2,1)}, u32[]{:S(2)}, u32[]{:S(2)}) collective-permute-start(bf16[576,512]{1,0:T(8,128)(2,1)S(1)} %collective-permute-done.47.refs_6_), channel_id=1, source_target_pairs={{0,8},{4,12},{8,16},{12,20},{16,24},{20,28},{24,0},{28,4},{1,9},{5... | collective-permute-start | bytes 1769480 | tf_op jit(solution)/shard_map/ppermute | solution.py:535
  295.0 24.9 %collective-permute-start.52 = (bf16[576,512]{1,0:T(8,128)(2,1)S(1)}, bf16[576,512]{1,0:T(8,128)(2,1)S(1)}, u32[]{:S(2)}, u32[]{:S(2)}) collective-permute-start(bf16[576,512]{1,0:T(8,128)(2,1)S(1)} %collective-permute-done.47.refs_6_), channel_id=1, source_target_pairs={{0,4},{4,0},{8,12},{12,8},{16,20},{20,16},{24,28},{28,24},{1,5},{5... | collective-permute-start | bytes 1769480 | tf_op jit(solution)/shard_map/ppermute | solution.py:302
  307.3 20.5 %collective-permute-start.53 = (bf16[576,512]{1,0:T(8,128)(2,1)S(1)}, bf16[576,512]{1,0:T(8,128)(2,1)S(1)}, u32[]{:S(2)}, u32[]{:S(2)}) collective-permute-start(bf16[576,512]{1,0:T(8,128)(2,1)S(1)} %collective-permute-done.49.refs_0_), channel_id=1, source_target_pairs={{0,8},{4,12},{8,16},{12,20},{16,24},{20,28},{24,0},{28,4},{1,9},{5... | collective-permute-start | bytes 1769480 | tf_op jit(solution)/shard_map/ppermute | solution.py:535
  307.7 22.5 %collective-permute-start.54 = (bf16[576,512]{1,0:T(8,128)(2,1)S(1)}, bf16[576,512]{1,0:T(8,128)(2,1)}, u32[]{:S(2)}, u32[]{:S(2)}) collective-permute-start(bf16[576,512]{1,0:T(8,128)(2,1)S(1)} %collective-permute-done.49.refs_0_), channel_id=1, source_target_pairs={{0,4},{4,0},{8,12},{12,8},{16,20},{20,16},{24,28},{28,24},{1,5},{5... | collective-permute-start | bytes 1769480 | tf_op jit(solution)/shard_map/ppermute | solution.py:302
  330.2 22.0 %collective-permute-start.59 = (bf16[576,512]{1,0:T(8,128)(2,1)}, bf16[576,512]{1,0:T(8,128)(2,1)}, u32[]{:S(2)}, u32[]{:S(2)}) collective-permute-start(bf16[576,512]{1,0:T(8,128)(2,1)} %collective-permute-done.54.refs_1_), channel_id=1, source_target_pairs={{0,8},{4,12},{8,16},{12,20},{16,24},{20,28},{24,0},{28,4},{1,9},{5... | collective-permute-start | bytes 1769480 | tf_op jit(solution)/shard_map/ppermute | solution.py:540
  331.2 21.0 %collective-permute-start.58 = (bf16[576,512]{1,0:T(8,128)(2,1)}, bf16[576,512]{1,0:T(8,128)(2,1)}, u32[]{:S(2)}, u32[]{:S(2)}) collective-permute-start(bf16[576,512]{1,0:T(8,128)(2,1)} %collective-permute-done.51.refs_2_), channel_id=1, source_target_pairs={{0,4},{4,0},{8,12},{12,8},{16,20},{20,16},{24,28},{28,24},{1,5},{5... | collective-permute-start | bytes 1769480 | tf_op jit(solution)/shard_map/ppermute | solution.py:302
  (33 other events, 255.5 us)

commit v6 on v5

--- a/solution.py
+++ b/solution.py
@@ -94,11 +94,29 @@
             left_ref[...] = left
 
 
-def first_left_kernel(per_tp, ids_ref, grads_ref, error_ref, query_ref, high_ref, low_ref, *left_refs):
-    high, low = two_terms(grads_ref[0, 0].astype(F32) + error_ref[0, 0])
+def first_left_kernel(per_tp, picked, ids_ref, grads_ref, error_ref, query_ref, high_ref, low_ref, *refs):
+    left_refs, (grads_buffer, error_buffer, sems) = refs[:-3], refs[-3:]
+    step = pl.program_id(0)
+
+    def copies(k):
+        matrix = picked(k, ids_ref)
+        return [
+            pltpu.make_async_copy(source.at[0, matrix], buffer.at[k], sems.at[which, k])
+            for which, (source, buffer) in enumerate(((grads_ref, grads_buffer), (error_ref, error_buffer)))
+        ]
+
+    @pl.when(step == 0)
+    def _():
+        for k in range(grads_buffer.shape[0]):
+            for copy in copies(k):
+                copy.start()
+
+    for copy in copies(step):
+        copy.wait()
+    high, low = two_terms(grads_buffer[step].astype(F32) + error_buffer[step])
     high_ref[0] = high
     low_ref[0] = low
-    put_left(small_by_large(query_ref[0], high, low, True), pl.program_id(0), left_refs, per_tp)
+    put_left(small_by_large(query_ref[0], high, low, True), step, left_refs, per_tp)
 
 
 def left_kernel(per_tp, half, ids_ref, high_ref, low_ref, *refs):
@@ -280,7 +298,7 @@
     )(*operands)
 
 
-def grid_call(kernel, name, ids, grid, in_specs, out_specs, out_shape, operands, scratch=(), aliases=None, flops=0, moved=0):
+def grid_call(kernel, name, ids, grid, in_specs, out_specs, out_shape, operands, scratch=(), aliases=None, flops=0, moved=0, mib=14):
     return pl.pallas_call(
         kernel,
         grid_spec=pltpu.PrefetchScalarGridSpec(
@@ -292,7 +310,7 @@
         ),
         out_shape=out_shape,
         input_output_aliases=aliases or {},
-        compiler_params=grant(20),
+        compiler_params=grant(mib),
         name=name,
         cost_estimate=pl.CostEstimate(flops=flops, bytes_accessed=moved, transcendentals=0),
     )(ids, *operands)
@@ -344,18 +362,24 @@
     for half in reversed(range(halves)):
         picked = functools.partial(matrix_of, half)
         high, low, *out = grid_call(
-            functools.partial(first_left_kernel, per_tp),
+            functools.partial(first_left_kernel, per_tp, picked),
             "first_left",
             ids,
             (per_half,),
             [
-                pl.BlockSpec((1, 1, width, cols), lambda k, at, picked=picked: (0, picked(k, at), 0, 0)),
-                pl.BlockSpec((1, 1, width, cols), lambda k, at, picked=picked: (0, picked(k, at), 0, 0)),
+                pl.BlockSpec(memory_space=pltpu.HBM),
+                pl.BlockSpec(memory_space=pltpu.HBM),
                 pl.BlockSpec((1, rank, cols), lambda k, at, picked=picked: (picked(k, at), 0, 0)),
             ],
             [term_spec, term_spec, *left_specs],
             [term_shape, term_shape, *left_shapes],
             (grads, error, query),
+            [
+                pltpu.VMEM((per_half, width, cols), BF16),
+                pltpu.VMEM((per_half, width, cols), F32),
+                pltpu.SemaphoreType.DMA((2, per_half)),
+            ],
+            mib=26,
             flops=flops,
             moved=10 * elements,
         )
@@ -363,25 +387,25 @@
         lefts[2 * half : 2 * half + 2] = out
         ids, _ = lax.optimization_barrier((ids, out[0]))
 
+    base = []
     for power_pass in range(ROUNDS):
         met = [lefts[0]] + [swap(lefts[offset], "tp", tps, offset) for offset in reversed(range(1, tps))]
         parts = whole_call(
             functools.partial(split_kernel, tps), "left_split", shape(left_part * replicas, LANES), met
         )
-        if power_pass == 0:
-            parts, new_values, old_values = lax.optimization_barrier((parts, master, momentum))
-            base = []
-            for offset in range(tps):
-                column = (tp ^ offset) * cols
-                piece = lax.dynamic_slice_in_dim(new_values, column, cols, 1)
-                piece = piece - (LEARNING_RATE * MOMENTUM_DECAY) * lax.dynamic_slice_in_dim(old_values, column, cols, 1)
-                base.append(piece if offset == 0 else swap(piece, "tp", tps, offset))
+        parts, new_values, old_values = lax.optimization_barrier((parts, master, momentum))
+        some = []
+        for offset in range(3 * power_pass, 3 + power_pass):
+            column = (tp ^ offset) * cols
+            piece = lax.dynamic_slice_in_dim(new_values, column, cols, 1)
+            piece = piece - (LEARNING_RATE * MOMENTUM_DECAY) * lax.dynamic_slice_in_dim(old_values, column, cols, 1)
+            some.append(piece if offset == 0 else swap(piece, "tp", tps, offset))
         parts = parts.reshape(replicas, left_part, LANES)
         parts = lax.all_to_all(parts, "rep", split_axis=0, concat_axis=0, tiled=True)
         parts = whole_call(total_kernel, "left_sum", shape(*parts.shape), [parts])
         parts = lax.all_to_all(parts, "rep", split_axis=0, concat_axis=0, tiled=True)
-        if power_pass == 0:
-            parts, base = lax.optimization_barrier((parts, base))
+        parts, some = lax.optimization_barrier((parts, some))
+        base += some
         basis = whole_call(
             functools.partial(basis_kernel, rank), "basis", shape(tp_rows, width), [parts.reshape(-1, LANES)]
         )
@@ -521,13 +545,14 @@
     held, beside = list(block), [None, None]
     pieces = [(block[half], half, 0) for half in range(2)]
     errors, flat, weights = (), (), ()
-    jobs = {1: "update update", 2: "update", 3: "update", 4: "place", 6: "place", 2 * stages - 1: "place flat"}
+    jobs = {1: "update update", 2: "update", 3: "update", 4: "flat", 5: "place", 2 * stages - 2: "place", 2 * stages - 1: "place"}
+    near = spread(near, "tp", tps)
     updated = 0
     for step in range(2 * stages):
         stage, half = step // 2, step % 2
         if stage > 0:
             arrived = (held[half], beside[half])
-            ids, errors, flat, weights, arrived = lax.optimization_barrier((ids, errors, flat, weights, arrived))
+            ids, errors, flat, weights, near, arrived = lax.optimization_barrier((ids, errors, flat, weights, near, arrived))
             held[half], beside[half] = arrived
             pieces += [(held[half], half, stage), (beside[half], half, stages + stage - 1)]
         if stage < stages - 1:
@@ -538,8 +563,6 @@
             beside[half] = swap(held[half], "rep", replicas, 1)
         else:
             beside[half] = lax.ppermute(beside[half], "rep", ring)
-        if step == 2 * stages - 1:
-            near = spread(near, "tp", tps)
         for job in jobs.get(step, "").split():
             if job == "update":
                 errors = (update(updated, ids, errors),)

time: 356 us -> 346 us (0.972)
  blocking collectives: 30 us -> 0 us
  waiting for transfers between devices: 130 us -> 141 us
  local copies, waits for them, and re-layouts: 23.9 us -> 33.3 us
  Pallas kernels: 80 us -> 76.3 us
    all_to_all x2 -> x0, blocking collectives: 30 us -> none  [local(): lax.all_to_all(parts, 'rep', split_axis=0, concat_axis=0, tiled=True)]
    ppermute x53, waiting for transfers between devices: 95.2 us -> 71.2 us  [swap(): lax.ppermute(x, axis, [(index, index ^ offset) for index in range(size)])]
    all_to_all x2 -> x4, waiting for transfers between devices: 5 us -> 25.8 us  [local(): lax.all_to_all(parts, 'rep', split_axis=0, concat_axis=0, tiled=True)]
    ppermute x1, waiting for transfers between devices: 0.01 us -> 14.5 us  [local(): beside[half] = lax.ppermute(beside[half], 'rep', ring)]
    unnamed x38 -> x62, local copies, waits for them, and re-layouts: 22.1 us -> 32.4 us
    all_to_all x2 -> x4, starting transfers between devices: 9.47 us -> 18.9 us  [local(): lax.all_to_all(parts, 'rep', split_axis=0, concat_axis=0, tiled=True)]
    pallas_call x17, Pallas kernels: 71.2 us -> 65.9 us  [grid_call(): pl.pallas_call(kernel, grid_spec=pltpu.PrefetchScalarGridSpec(num_scalar_...]
    ppermute x53, starting transfers between devices: 69.6 us -> 65.1 us  [swap(): lax.ppermute(x, axis, [(index, index ^ offset) for index in range(size)])]
  transfers between devices with their start and end apart: 62 -> 64, of which waited for: 33 -> 30; matrix products, arithmetic and copies ran while one was open for 1% -> 2% of each run, Pallas kernels for 14% -> 14%
where the time goes in v6:
time: 346 us; the launch traced here: 345 us
  waiting for transfers between devices  141 us (41%)
  starting transfers between devices  89 us (26%)
  Pallas kernels  76.3 us (22%)
  local copies, waits for them, and re-layouts  33.3 us (10%)
  other arithmetic  4.97 us (1%)
    ppermute x53, waiting for transfers between devices, swap(): lax.ppermute(x, axis, [(index, index ^ offset) for index in range(size)])  71.2 us
    pallas_call x17, Pallas kernels, grid_call(): pl.pallas_call(kernel, grid_spec=pltpu.PrefetchScalarGridSpec(num_scalar_...  65.9 us
    ppermute x53, starting transfers between devices, swap(): lax.ppermute(x, axis, [(index, index ^ offset) for index in range(size)])  65.1 us
    unnamed x62, local copies, waits for them, and re-layouts  32.4 us
    ppermute x6, waiting for transfers between devices, local(): held[half] = lax.ppermute(here, 'rep', ring)  29 us
    all_to_all x4, waiting for transfers between devices, local(): lax.all_to_all(parts, 'rep', split_axis=0, concat_axis=0, tiled=True)  25.8 us
    all_to_all x4, starting transfers between devices, local(): lax.all_to_all(parts, 'rep', split_axis=0, concat_axis=0, tiled=True)  18.9 us
    ppermute x1, waiting for transfers between devices, local(): beside[half] = lax.ppermute(beside[half], 'rep', ring)  14.5 us
  transfers between devices with their start and end apart: 64, of which 30 were waited for; matrix products, arithmetic and copies ran while one was open for 2% of the time, Pallas kernels for 14%

profile of v6, /device:TPU:0, one launch (start us, length us, event | category | flops | bytes accessed | tf_op | source)
XLA Modules:
  0.0 345.1 jit_solution(5669789058432225974)
XLA Ops:
  0.7 3.7 %copy-done.12 = bf16[1,12,768,512]{3,2,1,0:T(8,128)(2,1)S(1)} copy-done((bf16[1,12,768,512]{3,2,1,0:T(8,128)(2,1)S(1)}, bf16[1,12,768,512]{3,2,1,0:T(8,128)(2,1)}, u32[]{:S(2)}) %copy-start.12) | copy-done | bytes 9437208
  5.5 6.0 %first_left.2 = (bf16[6,768,512]{2,1,0:T(8,128)(2,1)S(1)}, bf16[6,768,512]{2,1,0:T(8,128)(2,1)S(1)}, f32[96,768]{1,0:T(8,128)S(1)}, f32[96,768]{1,0:T(8,128)S(1)}) custom-call(s32[2]{0:T(128)S(1)} %pad_add_fusion.ids_ref, bf16[1,12,768,512]{3,2,1,0:T(8,128)(2,1)S(1)} %copy-done.12, f32[1,12,768,512]{3,2,1,0:T(8,128)} %error_ref.3, f32[12,32,512]{2,1,0:T(8,128)S(1)} %copy-done.16), custom_call_target="tpu_custom_call" | custom-call | flops 452984832 | bytes 23592960 | tf_op jit(solution)/shard_map/first_left/pallas_call | solution.py:302
  16.0 2.9 collective-permute-start.1
  18.9 6.1 %first_left.3 = (bf16[6,768,512]{2,1,0:T(8,128)(2,1)S(1)}, bf16[6,768,512]{2,1,0:T(8,128)(2,1)S(1)}, f32[96,768]{1,0:T(8,128)S(1)}, f32[96,768]{1,0:T(8,128)S(1)}) custom-call(s32[2]{0:T(128)S(1)} %pad_add_fusion.ids_ref, bf16[1,12,768,512]{3,2,1,0:T(8,128)(2,1)S(1)} %copy-done.12, f32[1,12,768,512]{3,2,1,0:T(8,128)} %error_ref.3, f32[12,32,512]{2,1,0:T(8,128)S(1)} %copy-done.17), custom_call_target="tpu_custom_call" | custom-call | flops 452984832 | bytes 23592960 | tf_op jit(solution)/shard_map/first_left/pallas_call | solution.py:302
  31.0 7.1 %collective-permute-done.refs_1_ = f32[96,768]{1,0:T(8,128)S(1)} collective-permute-done((f32[96,768]{1,0:T(8,128)S(1)}, f32[96,768]{1,0:T(8,128)S(1)}, u32[]{:S(2)}, u32[]{:S(2)}) %collective-permute-start) | collective-permute-done | bytes 294944 | tf_op jit(solution)/shard_map/ppermute | solution.py:320
  38.8 5.8 %all-to-all-start = ((f32[8,72,128]{2,1,0:T(8,128)}), f32[8,72,128]{2,1,0:T(8,128)S(1)}, u32[]{:S(2)}, u32[]{:S(2)}) async-start(f32[8,72,128]{2,1,0:T(8,128)} %bitcast.2), calls=%async_computation | async-start | bytes 589824 | tf_op jit(solution)/shard_map/all_to_all | solution.py:404
  44.7 2.8 multiply_subtract_fusion.1
  48.2 6.7 %all-to-all-done.parts_ref = f32[8,72,128]{2,1,0:T(8,128)S(1)} async-done(((f32[8,72,128]{2,1,0:T(8,128)}), f32[8,72,128]{2,1,0:T(8,128)S(1)}, u32[]{:S(2)}, u32[]{:S(2)}) %all-to-all-start) | async-done | bytes 294944 | tf_op jit(solution)/shard_map/all_to_all | solution.py:404
  55.6 3.6 %all-to-all-start.1 = ((f32[8,72,128]{2,1,0:T(8,128)}), f32[8,72,128]{2,1,0:T(8,128)S(1)}, u32[]{:S(2)}, u32[]{:S(2)}) async-start(f32[8,72,128]{2,1,0:T(8,128)} %left_sum.2), calls=%async_computation.1 | async-start | bytes 589824 | tf_op jit(solution)/shard_map/all_to_all | solution.py:406
  59.3 4.3 %collective-permute-done.4.refs_10_ = f32[288,512]{1,0:T(8,128)} collective-permute-done((f32[288,512]{1,0:T(8,128)}, f32[288,512]{1,0:T(8,128)}, u32[]{:S(2)}, u32[]{:S(2)}) %collective-permute-start.4) | collective-permute-done | bytes 589856 | tf_op jit(solution)/shard_map/ppermute | solution.py:320
  63.5 5.5 %all-to-all-done.1 = f32[8,72,128]{2,1,0:T(8,128)S(1)} async-done(((f32[8,72,128]{2,1,0:T(8,128)}), f32[8,72,128]{2,1,0:T(8,128)S(1)}, u32[]{:S(2)}, u32[]{:S(2)}) %all-to-all-start.1) | async-done | bytes 294944 | tf_op jit(solution)/shard_map/all_to_all | solution.py:406
  77.7 2.8 right_near.2.refs_0_
  82.1 2.9 right_far.2
  95.3 5.3 %collective-permute-done.11.refs_4_ = f32[192,128]{1,0:T(8,128)S(1)} collective-permute-done((f32[192,128]{1,0:T(8,128)S(1)}, f32[192,128]{1,0:T(8,128)S(1)}, u32[]{:S(2)}, u32[]{:S(2)}) %collective-permute-start.11) | collective-permute-done | bytes 98336 | tf_op jit(solution)/shard_map/ppermute | solution.py:320
  100.6 3.2 collective-permute-done.12.refs_5_
  114.1 3.0 collective-permute-start.21
  117.1 6.8 %collective-permute-done.18.refs_4_ = f32[192,128]{1,0:T(8,128)S(1)} collective-permute-done((f32[192,128]{1,0:T(8,128)S(1)}, f32[192,128]{1,0:T(8,128)S(1)}, u32[]{:S(2)}, u32[]{:S(2)}) %collective-permute-start.18) | collective-permute-done | bytes 98336 | tf_op jit(solution)/shard_map/ppermute | solution.py:320
  126.6 4.2 %left.3 = (f32[96,768]{1,0:T(8,128)S(1)}, f32[96,768]{1,0:T(8,128)S(1)}) custom-call(s32[2]{0:T(128)S(1)} %pad_add_fusion.ids_ref, bf16[6,768,512]{2,1,0:T(8,128)(2,1)S(1)} %bitcast.13, bf16[6,768,512]{2,1,0:T(8,128)(2,1)S(1)} %copy-done.2, f32[192,128]{1,0:T(8,128)S(1)} %right_sum.2.refs_0_, f32[192,128]{1,0:T(8,128)S(1)} %collective-permute-done.15.refs_1_, ...), custom_call_target="tpu_custom_call" | custom-call | flops 452984832 | bytes 23592960 | tf_op jit(solution)/shard_map/left/pallas_call | solution.py:302
  131.5 4.2 %left.2 = (f32[96,768]{1,0:T(8,128)S(1)}, f32[96,768]{1,0:T(8,128)S(1)}) custom-call(s32[2]{0:T(128)S(1)} %pad_add_fusion.ids_ref, bf16[6,768,512]{2,1,0:T(8,128)(2,1)S(1)} %copy-done.5, bf16[6,768,512]{2,1,0:T(8,128)(2,1)S(1)} %copy-done.9, f32[192,128]{1,0:T(8,128)S(1)} %right_sum.2.refs_0_, f32[192,128]{1,0:T(8,128)S(1)} %collective-permute-done.15.refs_1_, ...), custom_call_target="tpu_custom_call" | custom-call | flops 452984832 | bytes 23592960 | tf_op jit(solution)/shard_map/left/pallas_call | solution.py:302
  137.0 3.2 collective-permute-done.22.refs_1_
  140.2 4.5 %collective-permute-done.23.refs_2_ = f32[96,768]{1,0:T(8,128)S(1)} collective-permute-done((f32[96,768]{1,0:T(8,128)S(1)}, f32[96,768]{1,0:T(8,128)S(1)}, u32[]{:S(2)}, u32[]{:S(2)}) %collective-permute-start.23) | collective-permute-done | bytes 294944 | tf_op jit(solution)/shard_map/ppermute | solution.py:320
  145.5 5.7 %all-to-all-start.2 = ((f32[8,72,128]{2,1,0:T(8,128)}), f32[8,72,128]{2,1,0:T(8,128)S(1)}, u32[]{:S(2)}, u32[]{:S(2)}) async-start(f32[8,72,128]{2,1,0:T(8,128)} %bitcast.4), calls=%async_computation.2 | async-start | bytes 589824 | tf_op jit(solution)/shard_map/all_to_all | solution.py:404
  154.9 6.7 %all-to-all-done.2.parts_ref = f32[8,72,128]{2,1,0:T(8,128)S(1)} async-done(((f32[8,72,128]{2,1,0:T(8,128)}), f32[8,72,128]{2,1,0:T(8,128)S(1)}, u32[]{:S(2)}, u32[]{:S(2)}) %all-to-all-start.2) | async-done | bytes 294944 | tf_op jit(solution)/shard_map/all_to_all | solution.py:404
  162.3 3.8 %all-to-all-start.3 = ((f32[8,72,128]{2,1,0:T(8,128)}), f32[8,72,128]{2,1,0:T(8,128)S(1)}, u32[]{:S(2)}, u32[]{:S(2)}) async-start(f32[8,72,128]{2,1,0:T(8,128)} %left_sum.3), calls=%async_computation.3 | async-start | bytes 589824 | tf_op jit(solution)/shard_map/all_to_all | solution.py:406
  166.1 2.8 collective-permute-done.25.refs_11_
  168.9 7.0 %all-to-all-done.3 = f32[8,72,128]{2,1,0:T(8,128)S(1)} async-done(((f32[8,72,128]{2,1,0:T(8,128)}), f32[8,72,128]{2,1,0:T(8,128)S(1)}, u32[]{:S(2)}, u32[]{:S(2)}) %all-to-all-start.3) | async-done | bytes 294944 | tf_op jit(solution)/shard_map/all_to_all | solution.py:406
  184.2 2.8 right_near.3.refs_0_
  191.3 2.9 right_far.3
  198.8 2.8 collective-permute-start.33
  205.4 6.9 %collective-permute-done.32.refs_4_ = f32[192,128]{1,0:T(8,128)S(1)} collective-permute-done((f32[192,128]{1,0:T(8,128)S(1)}, f32[192,128]{1,0:T(8,128)S(1)}, u32[]{:S(2)}, u32[]{:S(2)}) %collective-permute-start.32) | collective-permute-done | bytes 98336 | tf_op jit(solution)/shard_map/ppermute | solution.py:320
  212.4 2.9 collective-permute-done.33.refs_5_
  216.1 3.5 %collective-permute-start.37 = (f32[192,128]{1,0:T(8,128)S(1)}, f32[192,128]{1,0:T(8,128)S(1)}, u32[]{:S(2)}, u32[]{:S(2)}) collective-permute-start(f32[192,128]{1,0:T(8,128)S(1)} %right_sum.3.refs_0_), channel_id=1, source_target_pairs={{0,8},{4,12},{8,0},{12,4},{16,24},{20,28},{24,16},{28,20},{1,9},{5... | collective-permute-start | bytes 294920 | tf_op jit(solution)/shard_map/ppermute | solution.py:320
  225.4 2.7 collective-permute-start.42
  228.2 6.5 %collective-permute-done.39.refs_4_ = f32[192,128]{1,0:T(8,128)S(1)} collective-permute-done((f32[192,128]{1,0:T(8,128)S(1)}, f32[192,128]{1,0:T(8,128)S(1)}, u32[]{:S(2)}, u32[]{:S(2)}) %collective-permute-start.39) | collective-permute-done | bytes 98336 | tf_op jit(solution)/shard_map/ppermute | solution.py:320
  236.7 3.4 late_rows.1
  241.0 3.8 %collective-permute-start.46 = (bf16[576,512]{1,0:T(8,128)(2,1)}, bf16[576,512]{1,0:T(8,128)(2,1)}, u32[]{:S(2)}, u32[]{:S(2)}) collective-permute-start(bf16[576,512]{1,0:T(8,128)(2,1)} %get-tuple-element.147.refs_0_), channel_id=1, source_target_pairs={{0,8},{4,12},{8,16},{12,20},{16,24},{20,28},{24,0},{28,4},{1,9},{5... | collective-permute-start | bytes 1769480 | tf_op jit(solution)/shard_map/ppermute | solution.py:560
  251.7 4.2 %collective-permute-done.44 = f32[64,512]{1,0:T(8,128)S(1)} collective-permute-done((f32[64,512]{1,0:T(8,128)S(1)}, f32[64,512]{1,0:T(8,128)S(1)}, u32[]{:S(2)}, u32[]{:S(2)}) %collective-permute-start.44) | collective-permute-done | bytes 131104 | tf_op jit(solution)/shard_map/ppermute | solution.py:320
  262.1 4.1 %update.4.refs_0_ = f32[1,12,768,512]{3,2,1,0:T(8,128)} custom-call(s32[2]{0:T(128)S(1)} %pad_add_fusion.ids_ref, f32[384,768]{1,0:T(8,128)S(1)} %pad_maximum_fusion.basis_ref, f32[384,512]{1,0:T(8,128)S(1)} %copy-done.13, bf16[6,768,512]{2,1,0:T(8,128)(2,1)S(1)} %copy-done.7, bf16[6,768,512]{2,1,0:T(8,128)(2,1)S(1)} %copy-done.11), custom_call_target="tpu_custom_call" | custom-call | flops 226492416 | bytes 9437184 | tf_op jit(solution)/shard_map/update/pallas_call | solution.py:302
  266.2 4.1 %update.5.refs_0_ = f32[1,12,768,512]{3,2,1,0:T(8,128)} custom-call(s32[2]{0:T(128)S(1)} %pad_add_fusion.ids_ref, f32[384,768]{1,0:T(8,128)S(1)} %pad_maximum_fusion.basis_ref, f32[384,512]{1,0:T(8,128)S(1)} %copy-done.13, bf16[6,768,512]{2,1,0:T(8,128)(2,1)S(1)} %copy-done.7, bf16[6,768,512]{2,1,0:T(8,128)(2,1)S(1)} %copy-done.11, ...), custom_call_target="tpu_custom_call", output_to_operand_aliasing={{}: (5, {})} | custom-call | flops 226492416 | bytes 9437184 | tf_op jit(solution)/shard_map/update/pallas_call | solution.py:302
  271.4 4.1 %update.6.refs_0_ = f32[1,12,768,512]{3,2,1,0:T(8,128)} custom-call(s32[2]{0:T(128)S(1)} %pad_add_fusion.ids_ref, f32[384,768]{1,0:T(8,128)S(1)} %pad_maximum_fusion.basis_ref, f32[384,512]{1,0:T(8,128)S(1)} %copy-done.13, bf16[6,768,512]{2,1,0:T(8,128)(2,1)S(1)} %bitcast.17, bf16[6,768,512]{2,1,0:T(8,128)(2,1)S(1)} %bitcast.19, ...), custom_call_target="tpu_custom_call", output_to_operand_aliasing={{}: (5, {})} | custom-call | flops 226492416 | bytes 9437184 | tf_op jit(solution)/shard_map/update/pallas_call | solution.py:302
  276.6 4.1 %update.7 = f32[1,12,768,512]{3,2,1,0:T(8,128)} custom-call(s32[2]{0:T(128)S(1)} %pad_add_fusion.ids_ref, f32[384,768]{1,0:T(8,128)S(1)} %pad_maximum_fusion.basis_ref, f32[384,512]{1,0:T(8,128)S(1)} %copy-done.13, bf16[6,768,512]{2,1,0:T(8,128)(2,1)S(1)} %bitcast.17, bf16[6,768,512]{2,1,0:T(8,128)(2,1)S(1)} %bitcast.19, ...), custom_call_target="tpu_custom_call", output_to_operand_aliasing={{}: (5, {})} | custom-call | flops 226492416 | bytes 9437184 | tf_op jit(solution)/shard_map/update/pallas_call | solution.py:302
  280.7 7.7 %collective-permute-done.50.refs_6_ = bf16[576,512]{1,0:T(8,128)(2,1)S(1)} collective-permute-done((bf16[576,512]{1,0:T(8,128)(2,1)}, bf16[576,512]{1,0:T(8,128)(2,1)S(1)}, u32[]{:S(2)}, u32[]{:S(2)}) %collective-permute-start.50) | collective-permute-done | bytes 589856 | tf_op jit(solution)/shard_map/ppermute | solution.py:560
  289.4 6.1 %flat_rows.1 = (f32[288,2048]{1,0:T(8,128)}, f32[288,2048]{1,0:T(8,128)}) custom-call(s32[2]{0:T(128)S(1)} %pad_add_fusion.ids_ref, f32[384,768]{1,0:T(8,128)S(1)} %pad_maximum_fusion.basis_ref, f32[4,64,512]{2,1,0:T(8,128)S(1)} %pad_maximum_fusion.1.near_ref, f32[288,2048]{1,0:T(8,128)S(1)} %copy-done.14, f32[288,2048]{1,0:T(8,128)S(1)} %copy-done.15), custom_call_target="tpu_custom_call" | custom-call | flops 452984832 | bytes 9437184 | tf_op jit(solution)/shard_map/flat_rows/pallas_call | solution.py:302
  295.6 5.4 %collective-permute-done.52.refs_8_ = bf16[576,512]{1,0:T(8,128)(2,1)S(1)} collective-permute-done((bf16[576,512]{1,0:T(8,128)(2,1)S(1)}, bf16[576,512]{1,0:T(8,128)(2,1)S(1)}, u32[]{:S(2)}, u32[]{:S(2)}) %collective-permute-start.52) | collective-permute-done | bytes 589856 | tf_op jit(solution)/shard_map/ppermute | solution.py:560
  302.0 6.7 %place.4.refs_2_ = bf16[8,2,576,512]{3,2,1,0:T(8,128)(2,1)} custom-call(s32[2]{0:T(128)S(1)} %pad_add_fusion.ids_ref, bf16[576,512]{1,0:T(8,128)(2,1)} %get-tuple-element.147.refs_0_, bf16[576,512]{1,0:T(8,128)(2,1)S(1)} %copy-done.22, bf16[576,512]{1,0:T(8,128)(2,1)} %collective-permute-done.46.refs_2_, bf16[576,512]{1,0:T(8,128)(2,1)} %collective-permute-done.47.refs_3_, ...), custom_call_target="tpu_custom_call" | custom-call | bytes 23592960 | tf_op jit(solution)/shard_map/place/pallas_call | solution.py:302
  308.7 4.9 %collective-permute-done.54.refs_0_ = bf16[576,512]{1,0:T(8,128)(2,1)S(1)} collective-permute-done((bf16[576,512]{1,0:T(8,128)(2,1)S(1)}, bf16[576,512]{1,0:T(8,128)(2,1)S(1)}, u32[]{:S(2)}, u32[]{:S(2)}) %collective-permute-start.54) | collective-permute-done | bytes 589856 | tf_op jit(solution)/shard_map/ppermute | solution.py:560
  315.3 11.0 %collective-permute-done.56.refs_0_ = bf16[576,512]{1,0:T(8,128)(2,1)S(1)} collective-permute-done((bf16[576,512]{1,0:T(8,128)(2,1)S(1)}, bf16[576,512]{1,0:T(8,128)(2,1)S(1)}, u32[]{:S(2)}, u32[]{:S(2)}) %collective-permute-start.56) | collective-permute-done | bytes 589856 | tf_op jit(solution)/shard_map/ppermute | solution.py:560
  328.9 14.5 %collective-permute-done.59.refs_1_ = bf16[576,512]{1,0:T(8,128)(2,1)S(1)} collective-permute-done((bf16[576,512]{1,0:T(8,128)(2,1)S(1)}, bf16[576,512]{1,0:T(8,128)(2,1)S(1)}, u32[]{:S(2)}, u32[]{:S(2)}) %collective-permute-start.59) | collective-permute-done | bytes 589856 | tf_op jit(solution)/shard_map/ppermute | solution.py:565
  (178 shorter events, 108.6 us)
Async XLA Ops:
  16.0 15.0 %collective-permute-start.1 = (f32[96,768]{1,0:T(8,128)S(1)}, f32[96,768]{1,0:T(8,128)S(1)}, u32[]{:S(2)}, u32[]{:S(2)}) collective-permute-start(f32[96,768]{1,0:T(8,128)S(1)} %get-tuple-element.100), channel_id=1, source_target_pairs={{0,2},{1,3},{2,0},{3,1},{4,6},{5,7},{6,4},{7,5},{8,10},{9,11},{10,... | collective-permute-start | bytes 884744 | tf_op jit(solution)/shard_map/ppermute | solution.py:320
  38.8 16.0 %all-to-all-start = ((f32[8,72,128]{2,1,0:T(8,128)}), f32[8,72,128]{2,1,0:T(8,128)S(1)}, u32[]{:S(2)}, u32[]{:S(2)}) async-start(f32[8,72,128]{2,1,0:T(8,128)} %bitcast.2), calls=%async_computation | async-start | bytes 589824 | tf_op jit(solution)/shard_map/all_to_all | solution.py:404
  47.5 11.8 %collective-permute-start.3 = (f32[288,512]{1,0:T(8,128)}, f32[288,512]{1,0:T(8,128)S(1)}, u32[]{:S(2)}, u32[]{:S(2)}) collective-permute-start(f32[288,512]{1,0:T(8,128)} %get-tuple-element.196), channel_id=1, source_target_pairs={{0,1},{1,0},{2,3},{3,2},{4,5},{5,4},{6,7},{7,6},{8,9},{9,8},{10,11... | collective-permute-start | bytes 1769480 | tf_op jit(solution)/shard_map/ppermute | solution.py:320
  47.7 15.9 %collective-permute-start.4 = (f32[288,512]{1,0:T(8,128)}, f32[288,512]{1,0:T(8,128)}, u32[]{:S(2)}, u32[]{:S(2)}) collective-permute-start(f32[288,512]{1,0:T(8,128)} %get-tuple-element.195), channel_id=1, source_target_pairs={{0,2},{1,3},{2,0},{3,1},{4,6},{5,7},{6,4},{7,5},{8,10},{9,11},{10,... | collective-permute-start | bytes 1769480 | tf_op jit(solution)/shard_map/ppermute | solution.py:320
  55.6 13.4 %all-to-all-start.1 = ((f32[8,72,128]{2,1,0:T(8,128)}), f32[8,72,128]{2,1,0:T(8,128)S(1)}, u32[]{:S(2)}, u32[]{:S(2)}) async-start(f32[8,72,128]{2,1,0:T(8,128)} %left_sum.2), calls=%async_computation.1 | async-start | bytes 589824 | tf_op jit(solution)/shard_map/all_to_all | solution.py:406
  71.1 9.4 %collective-permute-start.6 = (f32[96,768]{1,0:T(8,128)S(1)}, f32[96,768]{1,0:T(8,128)S(1)}, u32[]{:S(2)}, u32[]{:S(2)}) collective-permute-start(f32[96,768]{1,0:T(8,128)S(1)} %basis.2.first_ref), channel_id=1, source_target_pairs={{0,2},{1,3},{2,0},{3,1},{4,6},{5,7},{6,4},{7,5},{8,10},{9,11},{10,... | collective-permute-start | bytes 884744 | tf_op jit(solution)/shard_map/ppermute | solution.py:320
  85.9 14.7 %collective-permute-start.11 = (f32[192,128]{1,0:T(8,128)S(1)}, f32[192,128]{1,0:T(8,128)S(1)}, u32[]{:S(2)}, u32[]{:S(2)}) collective-permute-start(f32[192,128]{1,0:T(8,128)S(1)} %get-tuple-element.120), channel_id=1, source_target_pairs={{0,16},{4,20},{8,24},{12,28},{16,0},{20,4},{24,8},{28,12},{1,17},{... | collective-permute-start | bytes 294920 | tf_op jit(solution)/shard_map/ppermute | solution.py:320
  88.1 15.8 %collective-permute-start.12 = (f32[192,128]{1,0:T(8,128)S(1)}, f32[192,128]{1,0:T(8,128)S(1)}, u32[]{:S(2)}, u32[]{:S(2)}) collective-permute-start(f32[192,128]{1,0:T(8,128)S(1)} %get-tuple-element.121), channel_id=1, source_target_pairs={{0,20},{4,16},{8,28},{12,24},{16,4},{20,0},{24,12},{28,8},{1,21},{... | collective-permute-start | bytes 294920 | tf_op jit(solution)/shard_map/ppermute | solution.py:320
  90.0 13.8 %collective-permute-start.13 = (f32[192,128]{1,0:T(8,128)S(1)}, f32[192,128]{1,0:T(8,128)S(1)}, u32[]{:S(2)}, u32[]{:S(2)}) collective-permute-start(f32[192,128]{1,0:T(8,128)S(1)} %get-tuple-element.122), channel_id=1, source_target_pairs={{0,24},{4,28},{8,16},{12,20},{16,8},{20,12},{24,0},{28,4},{1,25},{... | collective-permute-start | bytes 294920 | tf_op jit(solution)/shard_map/ppermute | solution.py:320
  91.5 12.4 %collective-permute-start.14 = (f32[192,128]{1,0:T(8,128)S(1)}, f32[192,128]{1,0:T(8,128)S(1)}, u32[]{:S(2)}, u32[]{:S(2)}) collective-permute-start(f32[192,128]{1,0:T(8,128)S(1)} %get-tuple-element.123), channel_id=1, source_target_pairs={{0,28},{4,24},{8,20},{12,16},{16,12},{20,8},{24,4},{28,0},{1,29},{... | collective-permute-start | bytes 294920 | tf_op jit(solution)/shard_map/ppermute | solution.py:320
  93.6 10.3 %collective-permute-start.8 = (f32[192,128]{1,0:T(8,128)S(1)}, f32[192,128]{1,0:T(8,128)S(1)}, u32[]{:S(2)}, u32[]{:S(2)}) collective-permute-start(f32[192,128]{1,0:T(8,128)S(1)} %get-tuple-element.117), channel_id=1, source_target_pairs={{0,4},{4,0},{8,12},{12,8},{16,20},{20,16},{24,28},{28,24},{1,5},{5... | collective-permute-start | bytes 294920 | tf_op jit(solution)/shard_map/ppermute | solution.py:320
  108.4 8.7 %collective-permute-start.17 = (f32[192,128]{1,0:T(8,128)S(1)}, f32[192,128]{1,0:T(8,128)S(1)}, u32[]{:S(2)}, u32[]{:S(2)}) collective-permute-start(f32[192,128]{1,0:T(8,128)S(1)} %right_sum.2.refs_0_), channel_id=1, source_target_pairs={{0,12},{4,8},{8,4},{12,0},{16,28},{20,24},{24,20},{28,16},{1,13},{... | collective-permute-start | bytes 294920 | tf_op jit(solution)/shard_map/ppermute | solution.py:320
  109.4 14.5 %collective-permute-start.18 = (f32[192,128]{1,0:T(8,128)S(1)}, f32[192,128]{1,0:T(8,128)S(1)}, u32[]{:S(2)}, u32[]{:S(2)}) collective-permute-start(f32[192,128]{1,0:T(8,128)S(1)} %right_sum.2.refs_0_), channel_id=1, source_target_pairs={{0,16},{4,20},{8,24},{12,28},{16,0},{20,4},{24,8},{28,12},{1,17},{... | collective-permute-start | bytes 294920 | tf_op jit(solution)/shard_map/ppermute | solution.py:320
  111.6 15.1 %collective-permute-start.19 = (f32[192,128]{1,0:T(8,128)S(1)}, f32[192,128]{1,0:T(8,128)S(1)}, u32[]{:S(2)}, u32[]{:S(2)}) collective-permute-start(f32[192,128]{1,0:T(8,128)S(1)} %right_sum.2.refs_0_), channel_id=1, source_target_pairs={{0,20},{4,16},{8,28},{12,24},{16,4},{20,0},{24,12},{28,8},{1,21},{... | collective-permute-start | bytes 294920 | tf_op jit(solution)/shard_map/ppermute | solution.py:320
  112.9 13.7 %collective-permute-start.20 = (f32[192,128]{1,0:T(8,128)S(1)}, f32[192,128]{1,0:T(8,128)S(1)}, u32[]{:S(2)}, u32[]{:S(2)}) collective-permute-start(f32[192,128]{1,0:T(8,128)S(1)} %right_sum.2.refs_0_), channel_id=1, source_target_pairs={{0,24},{4,28},{8,16},{12,20},{16,8},{20,12},{24,0},{28,4},{1,25},{... | collective-permute-start | bytes 294920 | tf_op jit(solution)/shard_map/ppermute | solution.py:320
  114.1 12.6 %collective-permute-start.21 = (f32[192,128]{1,0:T(8,128)S(1)}, f32[192,128]{1,0:T(8,128)S(1)}, u32[]{:S(2)}, u32[]{:S(2)}) collective-permute-start(f32[192,128]{1,0:T(8,128)S(1)} %right_sum.2.refs_0_), channel_id=1, source_target_pairs={{0,28},{4,24},{8,20},{12,16},{16,12},{20,8},{24,4},{28,0},{1,29},{... | collective-permute-start | bytes 294920 | tf_op jit(solution)/shard_map/ppermute | solution.py:320
  130.8 9.4 %collective-permute-start.22 = (f32[96,768]{1,0:T(8,128)S(1)}, f32[96,768]{1,0:T(8,128)S(1)}, u32[]{:S(2)}, u32[]{:S(2)}) collective-permute-start(f32[96,768]{1,0:T(8,128)S(1)} %get-tuple-element.125), channel_id=1, source_target_pairs={{0,3},{1,2},{2,1},{3,0},{4,7},{5,6},{6,5},{7,4},{8,11},{9,10},{10,... | collective-permute-start | bytes 884744 | tf_op jit(solution)/shard_map/ppermute | solution.py:320
  130.9 13.8 %collective-permute-start.23 = (f32[96,768]{1,0:T(8,128)S(1)}, f32[96,768]{1,0:T(8,128)S(1)}, u32[]{:S(2)}, u32[]{:S(2)}) collective-permute-start(f32[96,768]{1,0:T(8,128)S(1)} %get-tuple-element.126), channel_id=1, source_target_pairs={{0,2},{1,3},{2,0},{3,1},{4,6},{5,7},{6,4},{7,5},{8,10},{9,11},{10,... | collective-permute-start | bytes 884744 | tf_op jit(solution)/shard_map/ppermute | solution.py:320
  135.7 9.0 %collective-permute-start.24 = (f32[96,768]{1,0:T(8,128)S(1)}, f32[96,768]{1,0:T(8,128)S(1)}, u32[]{:S(2)}, u32[]{:S(2)}) collective-permute-start(f32[96,768]{1,0:T(8,128)S(1)} %get-tuple-element.127), channel_id=1, source_target_pairs={{0,1},{1,0},{2,3},{3,2},{4,5},{5,4},{6,7},{7,6},{8,9},{9,8},{10,11... | collective-permute-start | bytes 884744 | tf_op jit(solution)/shard_map/ppermute | solution.py:320
  145.5 16.1 %all-to-all-start.2 = ((f32[8,72,128]{2,1,0:T(8,128)}), f32[8,72,128]{2,1,0:T(8,128)S(1)}, u32[]{:S(2)}, u32[]{:S(2)}) async-start(f32[8,72,128]{2,1,0:T(8,128)} %bitcast.4), calls=%async_computation.2 | async-start | bytes 589824 | tf_op jit(solution)/shard_map/all_to_all | solution.py:404
  153.1 15.8 %collective-permute-start.25 = (f32[288,512]{1,0:T(8,128)}, f32[288,512]{1,0:T(8,128)}, u32[]{:S(2)}, u32[]{:S(2)}) collective-permute-start(f32[288,512]{1,0:T(8,128)} %multiply_subtract_fusion), channel_id=1, source_target_pairs={{0,3},{1,2},{2,1},{3,0},{4,7},{5,6},{6,5},{7,4},{8,11},{9,10},{10,... | collective-permute-start | bytes 1769480 | tf_op jit(solution)/shard_map/ppermute | solution.py:320
  162.3 13.6 %all-to-all-start.3 = ((f32[8,72,128]{2,1,0:T(8,128)}), f32[8,72,128]{2,1,0:T(8,128)S(1)}, u32[]{:S(2)}, u32[]{:S(2)}) async-start(f32[8,72,128]{2,1,0:T(8,128)} %left_sum.3), calls=%async_computation.3 | async-start | bytes 589824 | tf_op jit(solution)/shard_map/all_to_all | solution.py:406
  177.9 9.4 %collective-permute-start.27 = (f32[96,768]{1,0:T(8,128)S(1)}, f32[96,768]{1,0:T(8,128)S(1)}, u32[]{:S(2)}, u32[]{:S(2)}) collective-permute-start(f32[96,768]{1,0:T(8,128)S(1)} %basis.3.first_ref), channel_id=1, source_target_pairs={{0,2},{1,3},{2,0},{3,1},{4,6},{5,7},{6,4},{7,5},{8,10},{9,11},{10,... | collective-permute-start | bytes 884744 | tf_op jit(solution)/shard_map/ppermute | solution.py:320
  195.7 9.7 %collective-permute-start.31 = (f32[192,128]{1,0:T(8,128)S(1)}, f32[192,128]{1,0:T(8,128)S(1)}, u32[]{:S(2)}, u32[]{:S(2)}) collective-permute-start(f32[192,128]{1,0:T(8,128)S(1)} %get-tuple-element.137), channel_id=1, source_target_pairs={{0,12},{4,8},{8,4},{12,0},{16,28},{20,24},{24,20},{28,16},{1,13},{... | collective-permute-start | bytes 294920 | tf_op jit(solution)/shard_map/ppermute | solution.py:320
  197.8 14.6 %collective-permute-start.32 = (f32[192,128]{1,0:T(8,128)S(1)}, f32[192,128]{1,0:T(8,128)S(1)}, u32[]{:S(2)}, u32[]{:S(2)}) collective-permute-start(f32[192,128]{1,0:T(8,128)S(1)} %get-tuple-element.138), channel_id=1, source_target_pairs={{0,16},{4,20},{8,24},{12,28},{16,0},{20,4},{24,8},{28,12},{1,17},{... | collective-permute-start | bytes 294920 | tf_op jit(solution)/shard_map/ppermute | solution.py:320
  198.8 16.5 %collective-permute-start.33 = (f32[192,128]{1,0:T(8,128)S(1)}, f32[192,128]{1,0:T(8,128)S(1)}, u32[]{:S(2)}, u32[]{:S(2)}) collective-permute-start(f32[192,128]{1,0:T(8,128)S(1)} %get-tuple-element.139), channel_id=1, source_target_pairs={{0,20},{4,16},{8,28},{12,24},{16,4},{20,0},{24,12},{28,8},{1,21},{... | collective-permute-start | bytes 294920 | tf_op jit(solution)/shard_map/ppermute | solution.py:320
  201.6 13.7 %collective-permute-start.34 = (f32[192,128]{1,0:T(8,128)S(1)}, f32[192,128]{1,0:T(8,128)S(1)}, u32[]{:S(2)}, u32[]{:S(2)}) collective-permute-start(f32[192,128]{1,0:T(8,128)S(1)} %get-tuple-element.140), channel_id=1, source_target_pairs={{0,24},{4,28},{8,16},{12,20},{16,8},{20,12},{24,0},{28,4},{1,25},{... | collective-permute-start | bytes 294920 | tf_op jit(solution)/shard_map/ppermute | solution.py:320
  203.1 12.3 %collective-permute-start.35 = (f32[192,128]{1,0:T(8,128)S(1)}, f32[192,128]{1,0:T(8,128)S(1)}, u32[]{:S(2)}, u32[]{:S(2)}) collective-permute-start(f32[192,128]{1,0:T(8,128)S(1)} %get-tuple-element.141), channel_id=1, source_target_pairs={{0,28},{4,24},{8,20},{12,16},{16,12},{20,8},{24,4},{28,0},{1,29},{... | collective-permute-start | bytes 294920 | tf_op jit(solution)/shard_map/ppermute | solution.py:320
  216.1 9.3 %collective-permute-start.37 = (f32[192,128]{1,0:T(8,128)S(1)}, f32[192,128]{1,0:T(8,128)S(1)}, u32[]{:S(2)}, u32[]{:S(2)}) collective-permute-start(f32[192,128]{1,0:T(8,128)S(1)} %right_sum.3.refs_0_), channel_id=1, source_target_pairs={{0,8},{4,12},{8,0},{12,4},{16,24},{20,28},{24,16},{28,20},{1,9},{5... | collective-permute-start | bytes 294920 | tf_op jit(solution)/shard_map/ppermute | solution.py:320
  220.5 14.2 %collective-permute-start.39 = (f32[192,128]{1,0:T(8,128)S(1)}, f32[192,128]{1,0:T(8,128)S(1)}, u32[]{:S(2)}, u32[]{:S(2)}) collective-permute-start(f32[192,128]{1,0:T(8,128)S(1)} %right_sum.3.refs_0_), channel_id=1, source_target_pairs={{0,16},{4,20},{8,24},{12,28},{16,0},{20,4},{24,8},{28,12},{1,17},{... | collective-permute-start | bytes 294920 | tf_op jit(solution)/shard_map/ppermute | solution.py:320
  223.0 13.6 %collective-permute-start.40 = (f32[192,128]{1,0:T(8,128)S(1)}, f32[192,128]{1,0:T(8,128)S(1)}, u32[]{:S(2)}, u32[]{:S(2)}) collective-permute-start(f32[192,128]{1,0:T(8,128)S(1)} %right_sum.3.refs_0_), channel_id=1, source_target_pairs={{0,20},{4,16},{8,28},{12,24},{16,4},{20,0},{24,12},{28,8},{1,21},{... | collective-permute-start | bytes 294920 | tf_op jit(solution)/shard_map/ppermute | solution.py:320
  223.4 13.3 %collective-permute-start.41 = (f32[192,128]{1,0:T(8,128)S(1)}, f32[192,128]{1,0:T(8,128)S(1)}, u32[]{:S(2)}, u32[]{:S(2)}) collective-permute-start(f32[192,128]{1,0:T(8,128)S(1)} %right_sum.3.refs_0_), channel_id=1, source_target_pairs={{0,24},{4,28},{8,16},{12,20},{16,8},{20,12},{24,0},{28,4},{1,25},{... | collective-permute-start | bytes 294920 | tf_op jit(solution)/shard_map/ppermute | solution.py:320
  225.4 11.3 %collective-permute-start.42 = (f32[192,128]{1,0:T(8,128)S(1)}, f32[192,128]{1,0:T(8,128)S(1)}, u32[]{:S(2)}, u32[]{:S(2)}) collective-permute-start(f32[192,128]{1,0:T(8,128)S(1)} %right_sum.3.refs_0_), channel_id=1, source_target_pairs={{0,28},{4,24},{8,20},{12,16},{16,12},{20,8},{24,4},{28,0},{1,29},{... | collective-permute-start | bytes 294920 | tf_op jit(solution)/shard_map/ppermute | solution.py:320
  241.0 29.3 %collective-permute-start.46 = (bf16[576,512]{1,0:T(8,128)(2,1)}, bf16[576,512]{1,0:T(8,128)(2,1)}, u32[]{:S(2)}, u32[]{:S(2)}) collective-permute-start(bf16[576,512]{1,0:T(8,128)(2,1)} %get-tuple-element.147.refs_0_), channel_id=1, source_target_pairs={{0,8},{4,12},{8,16},{12,20},{16,24},{20,28},{24,0},{28,4},{1,9},{5... | collective-permute-start | bytes 1769480 | tf_op jit(solution)/shard_map/ppermute | solution.py:560
  244.7 25.5 %collective-permute-start.47 = (bf16[576,512]{1,0:T(8,128)(2,1)}, bf16[576,512]{1,0:T(8,128)(2,1)}, u32[]{:S(2)}, u32[]{:S(2)}) collective-permute-start(bf16[576,512]{1,0:T(8,128)(2,1)} %get-tuple-element.147.refs_0_), channel_id=1, source_target_pairs={{0,4},{4,0},{8,12},{12,8},{16,20},{20,16},{24,28},{28,24},{1,5},{5... | collective-permute-start | bytes 1769480 | tf_op jit(solution)/shard_map/ppermute | solution.py:320
  246.0 29.4 %collective-permute-start.48 = (bf16[576,512]{1,0:T(8,128)(2,1)}, bf16[576,512]{1,0:T(8,128)(2,1)S(1)}, u32[]{:S(2)}, u32[]{:S(2)}) collective-permute-start(bf16[576,512]{1,0:T(8,128)(2,1)} %copy-done.21), channel_id=1, source_target_pairs={{0,8},{4,12},{8,16},{12,20},{16,24},{20,28},{24,0},{28,4},{1,9},{5... | collective-permute-start | bytes 1769480 | tf_op jit(solution)/shard_map/ppermute | solution.py:560
  246.7 28.8 %collective-permute-start.49 = (bf16[576,512]{1,0:T(8,128)(2,1)}, bf16[576,512]{1,0:T(8,128)(2,1)S(1)}, u32[]{:S(2)}, u32[]{:S(2)}) collective-permute-start(bf16[576,512]{1,0:T(8,128)(2,1)} %copy-done.21), channel_id=1, source_target_pairs={{0,4},{4,0},{8,12},{12,8},{16,20},{20,16},{24,28},{28,24},{1,5},{5... | collective-permute-start | bytes 1769480 | tf_op jit(solution)/shard_map/ppermute | solution.py:320
  255.8 14.4 %collective-permute-start.45 = (f32[64,512]{1,0:T(8,128)S(1)}, f32[64,512]{1,0:T(8,128)S(1)}, u32[]{:S(2)}, u32[]{:S(2)}) collective-permute-start(f32[64,512]{1,0:T(8,128)S(1)} %constant_dynamic-slice_fusion), channel_id=1, source_target_pairs={{0,3},{1,2},{2,1},{3,0},{4,7},{5,6},{6,5},{7,4},{8,11},{9,10},{10,... | collective-permute-start | bytes 393224 | tf_op jit(solution)/shard_map/ppermute | solution.py:320
  270.2 18.1 %collective-permute-start.50 = (bf16[576,512]{1,0:T(8,128)(2,1)}, bf16[576,512]{1,0:T(8,128)(2,1)S(1)}, u32[]{:S(2)}, u32[]{:S(2)}) collective-permute-start(bf16[576,512]{1,0:T(8,128)(2,1)} %collective-permute-done.46.refs_2_), channel_id=1, source_target_pairs={{0,8},{4,12},{8,16},{12,20},{16,24},{20,28},{24,0},{28,4},{1,9},{5... | collective-permute-start | bytes 1769480 | tf_op jit(solution)/shard_map/ppermute | solution.py:560
  270.3 18.1 %collective-permute-start.51 = (bf16[576,512]{1,0:T(8,128)(2,1)}, bf16[576,512]{1,0:T(8,128)(2,1)S(1)}, u32[]{:S(2)}, u32[]{:S(2)}) collective-permute-start(bf16[576,512]{1,0:T(8,128)(2,1)} %collective-permute-done.46.refs_2_), channel_id=1, source_target_pairs={{0,4},{4,0},{8,12},{12,8},{16,20},{20,16},{24,28},{28,24},{1,5},{5... | collective-permute-start | bytes 1769480 | tf_op jit(solution)/shard_map/ppermute | solution.py:320
  275.5 25.5 %collective-permute-start.52 = (bf16[576,512]{1,0:T(8,128)(2,1)S(1)}, bf16[576,512]{1,0:T(8,128)(2,1)S(1)}, u32[]{:S(2)}, u32[]{:S(2)}) collective-permute-start(bf16[576,512]{1,0:T(8,128)(2,1)S(1)} %collective-permute-done.48.refs_4_), channel_id=1, source_target_pairs={{0,8},{4,12},{8,16},{12,20},{16,24},{20,28},{24,0},{28,4},{1,9},{5... | collective-permute-start | bytes 1769480 | tf_op jit(solution)/shard_map/ppermute | solution.py:560
  275.9 25.1 %collective-permute-start.53 = (bf16[576,512]{1,0:T(8,128)(2,1)S(1)}, bf16[576,512]{1,0:T(8,128)(2,1)S(1)}, u32[]{:S(2)}, u32[]{:S(2)}) collective-permute-start(bf16[576,512]{1,0:T(8,128)(2,1)S(1)} %collective-permute-done.48.refs_4_), channel_id=1, source_target_pairs={{0,4},{4,0},{8,12},{12,8},{16,20},{20,16},{24,28},{28,24},{1,5},{5... | collective-permute-start | bytes 1769480 | tf_op jit(solution)/shard_map/ppermute | solution.py:320
  288.4 25.3 %collective-permute-start.54 = (bf16[576,512]{1,0:T(8,128)(2,1)S(1)}, bf16[576,512]{1,0:T(8,128)(2,1)S(1)}, u32[]{:S(2)}, u32[]{:S(2)}) collective-permute-start(bf16[576,512]{1,0:T(8,128)(2,1)S(1)} %collective-permute-done.50.refs_6_), channel_id=1, source_target_pairs={{0,8},{4,12},{8,16},{12,20},{16,24},{20,28},{24,0},{28,4},{1,9},{5... | collective-permute-start | bytes 1769480 | tf_op jit(solution)/shard_map/ppermute | solution.py:560
  288.4 25.3 %collective-permute-start.55 = (bf16[576,512]{1,0:T(8,128)(2,1)S(1)}, bf16[576,512]{1,0:T(8,128)(2,1)S(1)}, u32[]{:S(2)}, u32[]{:S(2)}) collective-permute-start(bf16[576,512]{1,0:T(8,128)(2,1)S(1)} %collective-permute-done.50.refs_6_), channel_id=1, source_target_pairs={{0,4},{4,0},{8,12},{12,8},{16,20},{20,16},{24,28},{28,24},{1,5},{5... | collective-permute-start | bytes 1769480 | tf_op jit(solution)/shard_map/ppermute | solution.py:320
  301.0 25.3 %collective-permute-start.56 = (bf16[576,512]{1,0:T(8,128)(2,1)S(1)}, bf16[576,512]{1,0:T(8,128)(2,1)S(1)}, u32[]{:S(2)}, u32[]{:S(2)}) collective-permute-start(bf16[576,512]{1,0:T(8,128)(2,1)S(1)} %collective-permute-done.52.refs_8_), channel_id=1, source_target_pairs={{0,8},{4,12},{8,16},{12,20},{16,24},{20,28},{24,0},{28,4},{1,9},{5... | collective-permute-start | bytes 1769480 | tf_op jit(solution)/shard_map/ppermute | solution.py:560
  301.0 25.3 %collective-permute-start.57 = (bf16[576,512]{1,0:T(8,128)(2,1)S(1)}, bf16[576,512]{1,0:T(8,128)(2,1)S(1)}, u32[]{:S(2)}, u32[]{:S(2)}) collective-permute-start(bf16[576,512]{1,0:T(8,128)(2,1)S(1)} %collective-permute-done.52.refs_8_), channel_id=1, source_target_pairs={{0,4},{4,0},{8,12},{12,8},{16,20},{20,16},{24,28},{28,24},{1,5},{5... | collective-permute-start | bytes 1769480 | tf_op jit(solution)/shard_map/ppermute | solution.py:320
  326.3 17.1 %collective-permute-start.59 = (bf16[576,512]{1,0:T(8,128)(2,1)S(1)}, bf16[576,512]{1,0:T(8,128)(2,1)S(1)}, u32[]{:S(2)}, u32[]{:S(2)}) collective-permute-start(bf16[576,512]{1,0:T(8,128)(2,1)S(1)} %collective-permute-done.57.refs_1_), channel_id=1, source_target_pairs={{0,8},{4,12},{8,16},{12,20},{16,24},{20,28},{24,0},{28,4},{1,9},{5... | collective-permute-start | bytes 1769480 | tf_op jit(solution)/shard_map/ppermute | solution.py:565
  326.3 17.1 %collective-permute-start.58 = (bf16[576,512]{1,0:T(8,128)(2,1)S(1)}, bf16[576,512]{1,0:T(8,128)(2,1)S(1)}, u32[]{:S(2)}, u32[]{:S(2)}) collective-permute-start(bf16[576,512]{1,0:T(8,128)(2,1)S(1)} %collective-permute-done.54.refs_0_), channel_id=1, source_target_pairs={{0,4},{4,0},{8,12},{12,8},{16,20},{20,16},{24,28},{28,24},{1,5},{5... | collective-permute-start | bytes 1769480 | tf_op jit(solution)/shard_map/ppermute | solution.py:320
  (47 other events, 371.0 us)

commit v7 on v6

--- a/solution.py
+++ b/solution.py
@@ -348,7 +348,7 @@
         return (at[1] ^ (2 * half + k // per_tp)) * per_tp + k % per_tp
 
     term_spec = pl.BlockSpec((1, width, cols), lambda k, at: (k, 0, 0))
-    term_shape = shape(per_half, width, cols, dtype=BF16)
+    term_shape = pltpu.VMEM((per_half, width, cols), BF16)
     left_specs = [
         pl.BlockSpec((rank, width), lambda k, at, which=which: (jnp.clip(k - which * per_tp, 0, per_tp - 1), 0))
         for which in range(2)
@@ -373,7 +373,7 @@
             ],
             [term_spec, term_spec, *left_specs],
             [term_shape, term_shape, *left_shapes],
-            (grads, error, query),
+            (*(pltpu.with_memory_space_constraint(x, pltpu.HBM) for x in (grads, error)), query),
             [
                 pltpu.VMEM((per_half, width, cols), BF16),
                 pltpu.VMEM((per_half, width, cols), F32),
@@ -383,7 +383,7 @@
             flops=flops,
             moved=10 * elements,
         )
-        terms[half] = (high, low)
+        terms[half] = tuple(pltpu.with_memory_space_constraint(term, pltpu.VMEM) for term in (high, low))
         lefts[2 * half : 2 * half + 2] = out
         ids, _ = lax.optimization_barrier((ids, out[0]))
 
@@ -545,7 +545,7 @@
     held, beside = list(block), [None, None]
     pieces = [(block[half], half, 0) for half in range(2)]
     errors, flat, weights = (), (), ()
-    jobs = {1: "update update", 2: "update", 3: "update", 4: "flat", 5: "place", 2 * stages - 2: "place", 2 * stages - 1: "place"}
+    jobs = {1: "update", 2: "update", 3: "update", 4: "update", 5: "flat place", 2 * stages - 2: "place", 2 * stages - 1: "place"}
     near = spread(near, "tp", tps)
     updated = 0
     for step in range(2 * stages):

time: 346 us -> 338 us (0.977)
  local copies, waits for them, and re-layouts: 33.3 us -> 28.7 us
    ppermute x6, waiting for transfers between devices: 29 us -> 18.2 us  [local(): held[half] = lax.ppermute(here, 'rep', ring)]
    ppermute x53, waiting for transfers between devices: 71.2 us -> 80.1 us  [swap(): lax.ppermute(x, axis, [(index, index ^ offset) for index in range(size)])]
    ppermute x53, starting transfers between devices: 65.1 us -> 60.3 us  [swap(): lax.ppermute(x, axis, [(index, index ^ offset) for index in range(size)])]
    unnamed x62 -> x56, local copies, waits for them, and re-layouts: 32.4 us -> 27.8 us
  transfers between devices with their start and end apart: 64 -> 64, of which waited for: 30 -> 35; matrix products, arithmetic and copies ran while one was open for 2% -> 2% of each run, Pallas kernels for 14% -> 15%
where the time goes in v7:
time: 338 us; the launch traced here: 337 us
  waiting for transfers between devices  138 us (41%)
  starting transfers between devices  86.3 us (26%)
  Pallas kernels  78 us (23%)
  local copies, waits for them, and re-layouts  28.7 us (8%)
  other arithmetic  4.97 us (1%)
    ppermute x53, waiting for transfers between devices, swap(): lax.ppermute(x, axis, [(index, index ^ offset) for index in range(size)])  80.1 us
    pallas_call x17, Pallas kernels, grid_call(): pl.pallas_call(kernel, grid_spec=pltpu.PrefetchScalarGridSpec(num_scalar_...  67.4 us
    ppermute x53, starting transfers between devices, swap(): lax.ppermute(x, axis, [(index, index ^ offset) for index in range(size)])  60.3 us
    unnamed x56, local copies, waits for them, and re-layouts  27.8 us
    all_to_all x4, waiting for transfers between devices, local(): lax.all_to_all(parts, 'rep', split_axis=0, concat_axis=0, tiled=True)  26 us
    all_to_all x4, starting transfers between devices, local(): lax.all_to_all(parts, 'rep', split_axis=0, concat_axis=0, tiled=True)  18.9 us
    ppermute x6, waiting for transfers between devices, local(): held[half] = lax.ppermute(here, 'rep', ring)  18.2 us
    ppermute x1, waiting for transfers between devices, local(): beside[half] = lax.ppermute(beside[half], 'rep', ring)  14 us
  transfers between devices with their start and end apart: 64, of which 35 were waited for; matrix products, arithmetic and copies ran while one was open for 2% of the time, Pallas kernels for 15%

profile of v7, /device:TPU:0, one launch (start us, length us, event | category | flops | bytes accessed | tf_op | source)
XLA Modules:
  0.0 337.3 jit_solution(13191952685866766055)
XLA Ops:
  1.8 6.4 %first_left.2 = (bf16[6,768,512]{2,1,0:T(8,128)(2,1)S(1)}, bf16[6,768,512]{2,1,0:T(8,128)(2,1)S(1)}, f32[96,768]{1,0:T(8,128)S(1)}, f32[96,768]{1,0:T(8,128)S(1)}) custom-call(s32[2]{0:T(128)S(1)} %pad_add_fusion.ids_ref, bf16[1,12,768,512]{3,2,1,0:T(8,128)(2,1)} %grads_ref.3, f32[1,12,768,512]{3,2,1,0:T(8,128)} %error_ref.3, f32[12,32,512]{2,1,0:T(8,128)S(1)} %copy-done.15), custom_call_target="tpu_custom_call" | custom-call | flops 452984832 | bytes 23592960 | tf_op jit(solution)/shard_map/first_left/pallas_call | solution.py:302
  12.7 3.0 collective-permute-start.1
  15.7 6.5 %first_left.3 = (bf16[6,768,512]{2,1,0:T(8,128)(2,1)S(1)}, bf16[6,768,512]{2,1,0:T(8,128)(2,1)S(1)}, f32[96,768]{1,0:T(8,128)S(1)}, f32[96,768]{1,0:T(8,128)S(1)}) custom-call(s32[2]{0:T(128)S(1)} %pad_add_fusion.ids_ref, bf16[1,12,768,512]{3,2,1,0:T(8,128)(2,1)} %grads_ref.3, f32[1,12,768,512]{3,2,1,0:T(8,128)} %error_ref.3, f32[12,32,512]{2,1,0:T(8,128)S(1)} %copy-done.16), custom_call_target="tpu_custom_call" | custom-call | flops 452984832 | bytes 23592960 | tf_op jit(solution)/shard_map/first_left/pallas_call | solution.py:302
  28.2 7.1 %collective-permute-done.refs_1_ = f32[96,768]{1,0:T(8,128)S(1)} collective-permute-done((f32[96,768]{1,0:T(8,128)S(1)}, f32[96,768]{1,0:T(8,128)S(1)}, u32[]{:S(2)}, u32[]{:S(2)}) %collective-permute-start) | collective-permute-done | bytes 294944 | tf_op jit(solution)/shard_map/ppermute | solution.py:320
  36.1 5.8 %all-to-all-start = ((f32[8,72,128]{2,1,0:T(8,128)}), f32[8,72,128]{2,1,0:T(8,128)S(1)}, u32[]{:S(2)}, u32[]{:S(2)}) async-start(f32[8,72,128]{2,1,0:T(8,128)} %bitcast.2), calls=%async_computation | async-start | bytes 589824 | tf_op jit(solution)/shard_map/all_to_all | solution.py:404
  41.9 2.8 multiply_subtract_fusion.1
  45.4 6.7 %all-to-all-done.parts_ref = f32[8,72,128]{2,1,0:T(8,128)S(1)} async-done(((f32[8,72,128]{2,1,0:T(8,128)}), f32[8,72,128]{2,1,0:T(8,128)S(1)}, u32[]{:S(2)}, u32[]{:S(2)}) %all-to-all-start) | async-done | bytes 294944 | tf_op jit(solution)/shard_map/all_to_all | solution.py:404
  52.8 3.6 %all-to-all-start.1 = ((f32[8,72,128]{2,1,0:T(8,128)}), f32[8,72,128]{2,1,0:T(8,128)S(1)}, u32[]{:S(2)}, u32[]{:S(2)}) async-start(f32[8,72,128]{2,1,0:T(8,128)} %left_sum.2), calls=%async_computation.1 | async-start | bytes 589824 | tf_op jit(solution)/shard_map/all_to_all | solution.py:406
  56.5 4.3 %collective-permute-done.4.refs_10_ = f32[288,512]{1,0:T(8,128)} collective-permute-done((f32[288,512]{1,0:T(8,128)}, f32[288,512]{1,0:T(8,128)}, u32[]{:S(2)}, u32[]{:S(2)}) %collective-permute-start.4) | collective-permute-done | bytes 589856 | tf_op jit(solution)/shard_map/ppermute | solution.py:320
  60.8 5.5 %all-to-all-done.1 = f32[8,72,128]{2,1,0:T(8,128)S(1)} async-done(((f32[8,72,128]{2,1,0:T(8,128)}), f32[8,72,128]{2,1,0:T(8,128)S(1)}, u32[]{:S(2)}, u32[]{:S(2)}) %all-to-all-start.1) | async-done | bytes 294944 | tf_op jit(solution)/shard_map/all_to_all | solution.py:406
  74.9 2.8 right_near.2.refs_0_
  79.4 2.9 right_far.2
  92.5 5.3 %collective-permute-done.11.refs_4_ = f32[192,128]{1,0:T(8,128)S(1)} collective-permute-done((f32[192,128]{1,0:T(8,128)S(1)}, f32[192,128]{1,0:T(8,128)S(1)}, u32[]{:S(2)}, u32[]{:S(2)}) %collective-permute-start.11) | collective-permute-done | bytes 98336 | tf_op jit(solution)/shard_map/ppermute | solution.py:320
  97.9 3.2 collective-permute-done.12.refs_5_
  111.3 3.0 collective-permute-start.21
  114.3 6.8 %collective-permute-done.18.refs_4_ = f32[192,128]{1,0:T(8,128)S(1)} collective-permute-done((f32[192,128]{1,0:T(8,128)S(1)}, f32[192,128]{1,0:T(8,128)S(1)}, u32[]{:S(2)}, u32[]{:S(2)}) %collective-permute-start.18) | collective-permute-done | bytes 98336 | tf_op jit(solution)/shard_map/ppermute | solution.py:320
  121.2 2.7 collective-permute-done.19.refs_5_
  123.9 4.2 %left.3 = (f32[96,768]{1,0:T(8,128)S(1)}, f32[96,768]{1,0:T(8,128)S(1)}) custom-call(s32[2]{0:T(128)S(1)} %pad_add_fusion.ids_ref, bf16[6,768,512]{2,1,0:T(8,128)(2,1)S(1)} %bitcast.13, bf16[6,768,512]{2,1,0:T(8,128)(2,1)S(1)} %copy-done.2, f32[192,128]{1,0:T(8,128)S(1)} %right_sum.2.refs_0_, f32[192,128]{1,0:T(8,128)S(1)} %collective-permute-done.15.refs_1_, ...), custom_call_target="tpu_custom_call" | custom-call | flops 452984832 | bytes 23592960 | tf_op jit(solution)/shard_map/left/pallas_call | solution.py:302
  128.7 4.2 %left.2 = (f32[96,768]{1,0:T(8,128)S(1)}, f32[96,768]{1,0:T(8,128)S(1)}) custom-call(s32[2]{0:T(128)S(1)} %pad_add_fusion.ids_ref, bf16[6,768,512]{2,1,0:T(8,128)(2,1)S(1)} %copy-done.5, bf16[6,768,512]{2,1,0:T(8,128)(2,1)S(1)} %copy-done.9, f32[192,128]{1,0:T(8,128)S(1)} %right_sum.2.refs_0_, f32[192,128]{1,0:T(8,128)S(1)} %collective-permute-done.15.refs_1_, ...), custom_call_target="tpu_custom_call" | custom-call | flops 452984832 | bytes 23592960 | tf_op jit(solution)/shard_map/left/pallas_call | solution.py:302
  134.2 3.2 collective-permute-done.22.refs_1_
  137.4 4.6 %collective-permute-done.23.refs_2_ = f32[96,768]{1,0:T(8,128)S(1)} collective-permute-done((f32[96,768]{1,0:T(8,128)S(1)}, f32[96,768]{1,0:T(8,128)S(1)}, u32[]{:S(2)}, u32[]{:S(2)}) %collective-permute-start.23) | collective-permute-done | bytes 294944 | tf_op jit(solution)/shard_map/ppermute | solution.py:320
  142.8 5.6 %all-to-all-start.2 = ((f32[8,72,128]{2,1,0:T(8,128)}), f32[8,72,128]{2,1,0:T(8,128)S(1)}, u32[]{:S(2)}, u32[]{:S(2)}) async-start(f32[8,72,128]{2,1,0:T(8,128)} %bitcast.4), calls=%async_computation.2 | async-start | bytes 589824 | tf_op jit(solution)/shard_map/all_to_all | solution.py:404
  152.1 6.7 %all-to-all-done.2.parts_ref = f32[8,72,128]{2,1,0:T(8,128)S(1)} async-done(((f32[8,72,128]{2,1,0:T(8,128)}), f32[8,72,128]{2,1,0:T(8,128)S(1)}, u32[]{:S(2)}, u32[]{:S(2)}) %all-to-all-start.2) | async-done | bytes 294944 | tf_op jit(solution)/shard_map/all_to_all | solution.py:404
  159.6 3.8 %all-to-all-start.3 = ((f32[8,72,128]{2,1,0:T(8,128)}), f32[8,72,128]{2,1,0:T(8,128)S(1)}, u32[]{:S(2)}, u32[]{:S(2)}) async-start(f32[8,72,128]{2,1,0:T(8,128)} %left_sum.3), calls=%async_computation.3 | async-start | bytes 589824 | tf_op jit(solution)/shard_map/all_to_all | solution.py:406
  163.3 2.8 collective-permute-done.25.refs_11_
  166.1 7.0 %all-to-all-done.3 = f32[8,72,128]{2,1,0:T(8,128)S(1)} async-done(((f32[8,72,128]{2,1,0:T(8,128)}), f32[8,72,128]{2,1,0:T(8,128)S(1)}, u32[]{:S(2)}, u32[]{:S(2)}) %all-to-all-start.3) | async-done | bytes 294944 | tf_op jit(solution)/shard_map/all_to_all | solution.py:406
  181.4 2.8 right_near.3.refs_0_
  188.6 2.9 right_far.3
  196.1 2.8 collective-permute-start.33
  202.7 6.9 %collective-permute-done.32.refs_4_ = f32[192,128]{1,0:T(8,128)S(1)} collective-permute-done((f32[192,128]{1,0:T(8,128)S(1)}, f32[192,128]{1,0:T(8,128)S(1)}, u32[]{:S(2)}, u32[]{:S(2)}) %collective-permute-start.32) | collective-permute-done | bytes 98336 | tf_op jit(solution)/shard_map/ppermute | solution.py:320
  209.6 3.0 collective-permute-done.33.refs_5_
  213.3 3.5 %collective-permute-start.37 = (f32[192,128]{1,0:T(8,128)S(1)}, f32[192,128]{1,0:T(8,128)S(1)}, u32[]{:S(2)}, u32[]{:S(2)}) collective-permute-start(f32[192,128]{1,0:T(8,128)S(1)} %right_sum.3.refs_0_), channel_id=1, source_target_pairs={{0,8},{4,12},{8,0},{12,4},{16,24},{20,28},{24,16},{28,20},{1,9},{5... | collective-permute-start | bytes 294920 | tf_op jit(solution)/shard_map/ppermute | solution.py:320
  217.7 2.6 collective-permute-start.39
  222.7 2.7 collective-permute-start.42
  225.5 6.4 %collective-permute-done.39.refs_4_ = f32[192,128]{1,0:T(8,128)S(1)} collective-permute-done((f32[192,128]{1,0:T(8,128)S(1)}, f32[192,128]{1,0:T(8,128)S(1)}, u32[]{:S(2)}, u32[]{:S(2)}) %collective-permute-start.39) | collective-permute-done | bytes 98336 | tf_op jit(solution)/shard_map/ppermute | solution.py:320
  234.1 3.6 %late_rows.1 = (f32[384,512]{1,0:T(8,128)}, bf16[576,512]{1,0:T(8,128)(2,1)}, bf16[576,512]{1,0:T(8,128)(2,1)}) custom-call(s32[2]{0:T(128)S(1)} %pad_add_fusion.ids_ref, f32[384,768]{1,0:T(8,128)S(1)} %pad_maximum_fusion.basis_ref, f32[192,128]{1,0:T(8,128)S(1)} %right_sum.3.refs_0_, f32[192,128]{1,0:T(8,128)S(1)} %collective-permute-done.36.refs_1_, ...), custom_call_target="tpu_custom_call" | custom-call | flops 4325376 | bytes 8650752 | tf_op jit(solution)/shard_map/late_rows/pallas_call | solution.py:289
  237.7 3.9 %collective-permute-start.46 = (bf16[576,512]{1,0:T(8,128)(2,1)}, bf16[576,512]{1,0:T(8,128)(2,1)}, u32[]{:S(2)}, u32[]{:S(2)}) collective-permute-start(bf16[576,512]{1,0:T(8,128)(2,1)} %get-tuple-element.149.refs_0_), channel_id=1, source_target_pairs={{0,8},{4,12},{8,16},{12,20},{16,24},{20,28},{24,0},{28,4},{1,9},{5... | collective-permute-start | bytes 1769480 | tf_op jit(solution)/shard_map/ppermute | solution.py:560
  248.0 4.5 %collective-permute-done.44 = f32[64,512]{1,0:T(8,128)S(1)} collective-permute-done((f32[64,512]{1,0:T(8,128)S(1)}, f32[64,512]{1,0:T(8,128)S(1)}, u32[]{:S(2)}, u32[]{:S(2)}) %collective-permute-start.44) | collective-permute-done | bytes 131104 | tf_op jit(solution)/shard_map/ppermute | solution.py:320
  258.4 4.1 %update.4.refs_0_ = f32[1,12,768,512]{3,2,1,0:T(8,128)} custom-call(s32[2]{0:T(128)S(1)} %pad_add_fusion.ids_ref, f32[384,768]{1,0:T(8,128)S(1)} %pad_maximum_fusion.basis_ref, f32[384,512]{1,0:T(8,128)S(1)} %copy-done.12, bf16[6,768,512]{2,1,0:T(8,128)(2,1)S(1)} %copy-done.7, bf16[6,768,512]{2,1,0:T(8,128)(2,1)S(1)} %copy-done.11), custom_call_target="tpu_custom_call" | custom-call | flops 226492416 | bytes 9437184 | tf_op jit(solution)/shard_map/update/pallas_call | solution.py:302
  263.5 4.1 %update.5.refs_0_ = f32[1,12,768,512]{3,2,1,0:T(8,128)} custom-call(s32[2]{0:T(128)S(1)} %pad_add_fusion.ids_ref, f32[384,768]{1,0:T(8,128)S(1)} %pad_maximum_fusion.basis_ref, f32[384,512]{1,0:T(8,128)S(1)} %copy-done.12, bf16[6,768,512]{2,1,0:T(8,128)(2,1)S(1)} %copy-done.7, bf16[6,768,512]{2,1,0:T(8,128)(2,1)S(1)} %copy-done.11, ...), custom_call_target="tpu_custom_call", output_to_operand_aliasing={{}: (5, {})} | custom-call | flops 226492416 | bytes 9437184 | tf_op jit(solution)/shard_map/update/pallas_call | solution.py:302
  271.6 4.1 %update.6.refs_0_ = f32[1,12,768,512]{3,2,1,0:T(8,128)} custom-call(s32[2]{0:T(128)S(1)} %pad_add_fusion.ids_ref, f32[384,768]{1,0:T(8,128)S(1)} %pad_maximum_fusion.basis_ref, f32[384,512]{1,0:T(8,128)S(1)} %copy-done.12, bf16[6,768,512]{2,1,0:T(8,128)(2,1)S(1)} %bitcast.17, bf16[6,768,512]{2,1,0:T(8,128)(2,1)S(1)} %bitcast.19, ...), custom_call_target="tpu_custom_call", output_to_operand_aliasing={{}: (5, {})} | custom-call | flops 226492416 | bytes 9437184 | tf_op jit(solution)/shard_map/update/pallas_call | solution.py:302
  275.7 5.3 %collective-permute-done.50.refs_6_ = bf16[576,512]{1,0:T(8,128)(2,1)S(1)} collective-permute-done((bf16[576,512]{1,0:T(8,128)(2,1)}, bf16[576,512]{1,0:T(8,128)(2,1)S(1)}, u32[]{:S(2)}, u32[]{:S(2)}) %collective-permute-start.50) | collective-permute-done | bytes 589856 | tf_op jit(solution)/shard_map/ppermute | solution.py:560
  284.1 4.1 %update.7 = f32[1,12,768,512]{3,2,1,0:T(8,128)} custom-call(s32[2]{0:T(128)S(1)} %pad_add_fusion.ids_ref, f32[384,768]{1,0:T(8,128)S(1)} %pad_maximum_fusion.basis_ref, f32[384,512]{1,0:T(8,128)S(1)} %copy-done.12, bf16[6,768,512]{2,1,0:T(8,128)(2,1)S(1)} %bitcast.17, bf16[6,768,512]{2,1,0:T(8,128)(2,1)S(1)} %bitcast.19, ...), custom_call_target="tpu_custom_call", output_to_operand_aliasing={{}: (5, {})} | custom-call | flops 226492416 | bytes 9437184 | tf_op jit(solution)/shard_map/update/pallas_call | solution.py:302
  288.1 5.5 %collective-permute-done.52.refs_8_ = bf16[576,512]{1,0:T(8,128)(2,1)S(1)} collective-permute-done((bf16[576,512]{1,0:T(8,128)(2,1)}, bf16[576,512]{1,0:T(8,128)(2,1)S(1)}, u32[]{:S(2)}, u32[]{:S(2)}) %collective-permute-start.52) | collective-permute-done | bytes 589856 | tf_op jit(solution)/shard_map/ppermute | solution.py:560
  296.7 7.3 %place.4.refs_2_ = bf16[8,2,576,512]{3,2,1,0:T(8,128)(2,1)} custom-call(s32[2]{0:T(128)S(1)} %pad_add_fusion.ids_ref, bf16[576,512]{1,0:T(8,128)(2,1)} %get-tuple-element.149.refs_0_, bf16[576,512]{1,0:T(8,128)(2,1)} %get-tuple-element.156.refs_1_, bf16[576,512]{1,0:T(8,128)(2,1)} %collective-permute-done.46.refs_2_, ...), custom_call_target="tpu_custom_call" | custom-call | bytes 23592960 | tf_op jit(solution)/shard_map/place/pallas_call | solution.py:302
  304.1 6.1 %flat_rows.1 = (f32[288,2048]{1,0:T(8,128)}, f32[288,2048]{1,0:T(8,128)}) custom-call(s32[2]{0:T(128)S(1)} %pad_add_fusion.ids_ref, f32[384,768]{1,0:T(8,128)S(1)} %pad_maximum_fusion.basis_ref, f32[4,64,512]{2,1,0:T(8,128)S(1)} %pad_maximum_fusion.1.near_ref, f32[288,2048]{1,0:T(8,128)S(1)} %copy-done.13, f32[288,2048]{1,0:T(8,128)S(1)} %copy-done.14), custom_call_target="tpu_custom_call" | custom-call | flops 452984832 | bytes 9437184 | tf_op jit(solution)/shard_map/flat_rows/pallas_call | solution.py:302
  311.9 6.7 %collective-permute-done.56.refs_0_ = bf16[576,512]{1,0:T(8,128)(2,1)S(1)} collective-permute-done((bf16[576,512]{1,0:T(8,128)(2,1)S(1)}, bf16[576,512]{1,0:T(8,128)(2,1)S(1)}, u32[]{:S(2)}, u32[]{:S(2)}) %collective-permute-start.56) | collective-permute-done | bytes 589856 | tf_op jit(solution)/shard_map/ppermute | solution.py:560
  321.6 14.0 %collective-permute-done.59.refs_1_ = bf16[576,512]{1,0:T(8,128)(2,1)S(1)} collective-permute-done((bf16[576,512]{1,0:T(8,128)(2,1)S(1)}, bf16[576,512]{1,0:T(8,128)(2,1)S(1)}, u32[]{:S(2)}, u32[]{:S(2)}) %collective-permute-start.59) | collective-permute-done | bytes 589856 | tf_op jit(solution)/shard_map/ppermute | solution.py:565
  (172 shorter events, 108.9 us)
Async XLA Ops:
  12.7 15.5 %collective-permute-start.1 = (f32[96,768]{1,0:T(8,128)S(1)}, f32[96,768]{1,0:T(8,128)S(1)}, u32[]{:S(2)}, u32[]{:S(2)}) collective-permute-start(f32[96,768]{1,0:T(8,128)S(1)} %get-tuple-element.102), channel_id=1, source_target_pairs={{0,2},{1,3},{2,0},{3,1},{4,6},{5,7},{6,4},{7,5},{8,10},{9,11},{10,... | collective-permute-start | bytes 884744 | tf_op jit(solution)/shard_map/ppermute | solution.py:320
  36.1 16.0 %all-to-all-start = ((f32[8,72,128]{2,1,0:T(8,128)}), f32[8,72,128]{2,1,0:T(8,128)S(1)}, u32[]{:S(2)}, u32[]{:S(2)}) async-start(f32[8,72,128]{2,1,0:T(8,128)} %bitcast.2), calls=%async_computation | async-start | bytes 589824 | tf_op jit(solution)/shard_map/all_to_all | solution.py:404
  44.7 11.8 %collective-permute-start.3 = (f32[288,512]{1,0:T(8,128)}, f32[288,512]{1,0:T(8,128)S(1)}, u32[]{:S(2)}, u32[]{:S(2)}) collective-permute-start(f32[288,512]{1,0:T(8,128)} %get-tuple-element.200), channel_id=1, source_target_pairs={{0,1},{1,0},{2,3},{3,2},{4,5},{5,4},{6,7},{7,6},{8,9},{9,8},{10,11... | collective-permute-start | bytes 1769480 | tf_op jit(solution)/shard_map/ppermute | solution.py:320
  44.9 15.9 %collective-permute-start.4 = (f32[288,512]{1,0:T(8,128)}, f32[288,512]{1,0:T(8,128)}, u32[]{:S(2)}, u32[]{:S(2)}) collective-permute-start(f32[288,512]{1,0:T(8,128)} %get-tuple-element.199), channel_id=1, source_target_pairs={{0,2},{1,3},{2,0},{3,1},{4,6},{5,7},{6,4},{7,5},{8,10},{9,11},{10,... | collective-permute-start | bytes 1769480 | tf_op jit(solution)/shard_map/ppermute | solution.py:320
  52.8 13.4 %all-to-all-start.1 = ((f32[8,72,128]{2,1,0:T(8,128)}), f32[8,72,128]{2,1,0:T(8,128)S(1)}, u32[]{:S(2)}, u32[]{:S(2)}) async-start(f32[8,72,128]{2,1,0:T(8,128)} %left_sum.2), calls=%async_computation.1 | async-start | bytes 589824 | tf_op jit(solution)/shard_map/all_to_all | solution.py:406
  68.3 9.4 %collective-permute-start.6 = (f32[96,768]{1,0:T(8,128)S(1)}, f32[96,768]{1,0:T(8,128)S(1)}, u32[]{:S(2)}, u32[]{:S(2)}) collective-permute-start(f32[96,768]{1,0:T(8,128)S(1)} %basis.2.first_ref), channel_id=1, source_target_pairs={{0,2},{1,3},{2,0},{3,1},{4,6},{5,7},{6,4},{7,5},{8,10},{9,11},{10,... | collective-permute-start | bytes 884744 | tf_op jit(solution)/shard_map/ppermute | solution.py:320
  83.1 14.7 %collective-permute-start.11 = (f32[192,128]{1,0:T(8,128)S(1)}, f32[192,128]{1,0:T(8,128)S(1)}, u32[]{:S(2)}, u32[]{:S(2)}) collective-permute-start(f32[192,128]{1,0:T(8,128)S(1)} %get-tuple-element.122), channel_id=1, source_target_pairs={{0,16},{4,20},{8,24},{12,28},{16,0},{20,4},{24,8},{28,12},{1,17},{... | collective-permute-start | bytes 294920 | tf_op jit(solution)/shard_map/ppermute | solution.py:320
  85.3 15.8 %collective-permute-start.12 = (f32[192,128]{1,0:T(8,128)S(1)}, f32[192,128]{1,0:T(8,128)S(1)}, u32[]{:S(2)}, u32[]{:S(2)}) collective-permute-start(f32[192,128]{1,0:T(8,128)S(1)} %get-tuple-element.123), channel_id=1, source_target_pairs={{0,20},{4,16},{8,28},{12,24},{16,4},{20,0},{24,12},{28,8},{1,21},{... | collective-permute-start | bytes 294920 | tf_op jit(solution)/shard_map/ppermute | solution.py:320
  87.2 13.8 %collective-permute-start.13 = (f32[192,128]{1,0:T(8,128)S(1)}, f32[192,128]{1,0:T(8,128)S(1)}, u32[]{:S(2)}, u32[]{:S(2)}) collective-permute-start(f32[192,128]{1,0:T(8,128)S(1)} %get-tuple-element.124), channel_id=1, source_target_pairs={{0,24},{4,28},{8,16},{12,20},{16,8},{20,12},{24,0},{28,4},{1,25},{... | collective-permute-start | bytes 294920 | tf_op jit(solution)/shard_map/ppermute | solution.py:320
  88.7 12.4 %collective-permute-start.14 = (f32[192,128]{1,0:T(8,128)S(1)}, f32[192,128]{1,0:T(8,128)S(1)}, u32[]{:S(2)}, u32[]{:S(2)}) collective-permute-start(f32[192,128]{1,0:T(8,128)S(1)} %get-tuple-element.125), channel_id=1, source_target_pairs={{0,28},{4,24},{8,20},{12,16},{16,12},{20,8},{24,4},{28,0},{1,29},{... | collective-permute-start | bytes 294920 | tf_op jit(solution)/shard_map/ppermute | solution.py:320
  90.8 10.3 %collective-permute-start.8 = (f32[192,128]{1,0:T(8,128)S(1)}, f32[192,128]{1,0:T(8,128)S(1)}, u32[]{:S(2)}, u32[]{:S(2)}) collective-permute-start(f32[192,128]{1,0:T(8,128)S(1)} %get-tuple-element.119), channel_id=1, source_target_pairs={{0,4},{4,0},{8,12},{12,8},{16,20},{20,16},{24,28},{28,24},{1,5},{5... | collective-permute-start | bytes 294920 | tf_op jit(solution)/shard_map/ppermute | solution.py:320
  105.6 8.7 %collective-permute-start.17 = (f32[192,128]{1,0:T(8,128)S(1)}, f32[192,128]{1,0:T(8,128)S(1)}, u32[]{:S(2)}, u32[]{:S(2)}) collective-permute-start(f32[192,128]{1,0:T(8,128)S(1)} %right_sum.2.refs_0_), channel_id=1, source_target_pairs={{0,12},{4,8},{8,4},{12,0},{16,28},{20,24},{24,20},{28,16},{1,13},{... | collective-permute-start | bytes 294920 | tf_op jit(solution)/shard_map/ppermute | solution.py:320
  106.7 14.5 %collective-permute-start.18 = (f32[192,128]{1,0:T(8,128)S(1)}, f32[192,128]{1,0:T(8,128)S(1)}, u32[]{:S(2)}, u32[]{:S(2)}) collective-permute-start(f32[192,128]{1,0:T(8,128)S(1)} %right_sum.2.refs_0_), channel_id=1, source_target_pairs={{0,16},{4,20},{8,24},{12,28},{16,0},{20,4},{24,8},{28,12},{1,17},{... | collective-permute-start | bytes 294920 | tf_op jit(solution)/shard_map/ppermute | solution.py:320
  108.8 15.1 %collective-permute-start.19 = (f32[192,128]{1,0:T(8,128)S(1)}, f32[192,128]{1,0:T(8,128)S(1)}, u32[]{:S(2)}, u32[]{:S(2)}) collective-permute-start(f32[192,128]{1,0:T(8,128)S(1)} %right_sum.2.refs_0_), channel_id=1, source_target_pairs={{0,20},{4,16},{8,28},{12,24},{16,4},{20,0},{24,12},{28,8},{1,21},{... | collective-permute-start | bytes 294920 | tf_op jit(solution)/shard_map/ppermute | solution.py:320
  110.1 13.7 %collective-permute-start.20 = (f32[192,128]{1,0:T(8,128)S(1)}, f32[192,128]{1,0:T(8,128)S(1)}, u32[]{:S(2)}, u32[]{:S(2)}) collective-permute-start(f32[192,128]{1,0:T(8,128)S(1)} %right_sum.2.refs_0_), channel_id=1, source_target_pairs={{0,24},{4,28},{8,16},{12,20},{16,8},{20,12},{24,0},{28,4},{1,25},{... | collective-permute-start | bytes 294920 | tf_op jit(solution)/shard_map/ppermute | solution.py:320
  111.3 12.6 %collective-permute-start.21 = (f32[192,128]{1,0:T(8,128)S(1)}, f32[192,128]{1,0:T(8,128)S(1)}, u32[]{:S(2)}, u32[]{:S(2)}) collective-permute-start(f32[192,128]{1,0:T(8,128)S(1)} %right_sum.2.refs_0_), channel_id=1, source_target_pairs={{0,28},{4,24},{8,20},{12,16},{16,12},{20,8},{24,4},{28,0},{1,29},{... | collective-permute-start | bytes 294920 | tf_op jit(solution)/shard_map/ppermute | solution.py:320
  128.0 9.4 %collective-permute-start.22 = (f32[96,768]{1,0:T(8,128)S(1)}, f32[96,768]{1,0:T(8,128)S(1)}, u32[]{:S(2)}, u32[]{:S(2)}) collective-permute-start(f32[96,768]{1,0:T(8,128)S(1)} %get-tuple-element.127), channel_id=1, source_target_pairs={{0,3},{1,2},{2,1},{3,0},{4,7},{5,6},{6,5},{7,4},{8,11},{9,10},{10,... | collective-permute-start | bytes 884744 | tf_op jit(solution)/shard_map/ppermute | solution.py:320
  128.1 13.8 %collective-permute-start.23 = (f32[96,768]{1,0:T(8,128)S(1)}, f32[96,768]{1,0:T(8,128)S(1)}, u32[]{:S(2)}, u32[]{:S(2)}) collective-permute-start(f32[96,768]{1,0:T(8,128)S(1)} %get-tuple-element.128), channel_id=1, source_target_pairs={{0,2},{1,3},{2,0},{3,1},{4,6},{5,7},{6,4},{7,5},{8,10},{9,11},{10,... | collective-permute-start | bytes 884744 | tf_op jit(solution)/shard_map/ppermute | solution.py:320
  132.9 9.0 %collective-permute-start.24 = (f32[96,768]{1,0:T(8,128)S(1)}, f32[96,768]{1,0:T(8,128)S(1)}, u32[]{:S(2)}, u32[]{:S(2)}) collective-permute-start(f32[96,768]{1,0:T(8,128)S(1)} %get-tuple-element.129), channel_id=1, source_target_pairs={{0,1},{1,0},{2,3},{3,2},{4,5},{5,4},{6,7},{7,6},{8,9},{9,8},{10,11... | collective-permute-start | bytes 884744 | tf_op jit(solution)/shard_map/ppermute | solution.py:320
  142.8 16.1 %all-to-all-start.2 = ((f32[8,72,128]{2,1,0:T(8,128)}), f32[8,72,128]{2,1,0:T(8,128)S(1)}, u32[]{:S(2)}, u32[]{:S(2)}) async-start(f32[8,72,128]{2,1,0:T(8,128)} %bitcast.4), calls=%async_computation.2 | async-start | bytes 589824 | tf_op jit(solution)/shard_map/all_to_all | solution.py:404
  150.4 15.8 %collective-permute-start.25 = (f32[288,512]{1,0:T(8,128)}, f32[288,512]{1,0:T(8,128)}, u32[]{:S(2)}, u32[]{:S(2)}) collective-permute-start(f32[288,512]{1,0:T(8,128)} %multiply_subtract_fusion), channel_id=1, source_target_pairs={{0,3},{1,2},{2,1},{3,0},{4,7},{5,6},{6,5},{7,4},{8,11},{9,10},{10,... | collective-permute-start | bytes 1769480 | tf_op jit(solution)/shard_map/ppermute | solution.py:320
  159.6 13.6 %all-to-all-start.3 = ((f32[8,72,128]{2,1,0:T(8,128)}), f32[8,72,128]{2,1,0:T(8,128)S(1)}, u32[]{:S(2)}, u32[]{:S(2)}) async-start(f32[8,72,128]{2,1,0:T(8,128)} %left_sum.3), calls=%async_computation.3 | async-start | bytes 589824 | tf_op jit(solution)/shard_map/all_to_all | solution.py:406
  175.2 9.4 %collective-permute-start.27 = (f32[96,768]{1,0:T(8,128)S(1)}, f32[96,768]{1,0:T(8,128)S(1)}, u32[]{:S(2)}, u32[]{:S(2)}) collective-permute-start(f32[96,768]{1,0:T(8,128)S(1)} %basis.3.first_ref), channel_id=1, source_target_pairs={{0,2},{1,3},{2,0},{3,1},{4,6},{5,7},{6,4},{7,5},{8,10},{9,11},{10,... | collective-permute-start | bytes 884744 | tf_op jit(solution)/shard_map/ppermute | solution.py:320
  193.0 9.7 %collective-permute-start.31 = (f32[192,128]{1,0:T(8,128)S(1)}, f32[192,128]{1,0:T(8,128)S(1)}, u32[]{:S(2)}, u32[]{:S(2)}) collective-permute-start(f32[192,128]{1,0:T(8,128)S(1)} %get-tuple-element.139), channel_id=1, source_target_pairs={{0,12},{4,8},{8,4},{12,0},{16,28},{20,24},{24,20},{28,16},{1,13},{... | collective-permute-start | bytes 294920 | tf_op jit(solution)/shard_map/ppermute | solution.py:320
  195.0 14.6 %collective-permute-start.32 = (f32[192,128]{1,0:T(8,128)S(1)}, f32[192,128]{1,0:T(8,128)S(1)}, u32[]{:S(2)}, u32[]{:S(2)}) collective-permute-start(f32[192,128]{1,0:T(8,128)S(1)} %get-tuple-element.140), channel_id=1, source_target_pairs={{0,16},{4,20},{8,24},{12,28},{16,0},{20,4},{24,8},{28,12},{1,17},{... | collective-permute-start | bytes 294920 | tf_op jit(solution)/shard_map/ppermute | solution.py:320
  196.1 16.5 %collective-permute-start.33 = (f32[192,128]{1,0:T(8,128)S(1)}, f32[192,128]{1,0:T(8,128)S(1)}, u32[]{:S(2)}, u32[]{:S(2)}) collective-permute-start(f32[192,128]{1,0:T(8,128)S(1)} %get-tuple-element.141), channel_id=1, source_target_pairs={{0,20},{4,16},{8,28},{12,24},{16,4},{20,0},{24,12},{28,8},{1,21},{... | collective-permute-start | bytes 294920 | tf_op jit(solution)/shard_map/ppermute | solution.py:320
  198.9 13.7 %collective-permute-start.34 = (f32[192,128]{1,0:T(8,128)S(1)}, f32[192,128]{1,0:T(8,128)S(1)}, u32[]{:S(2)}, u32[]{:S(2)}) collective-permute-start(f32[192,128]{1,0:T(8,128)S(1)} %get-tuple-element.142), channel_id=1, source_target_pairs={{0,24},{4,28},{8,16},{12,20},{16,8},{20,12},{24,0},{28,4},{1,25},{... | collective-permute-start | bytes 294920 | tf_op jit(solution)/shard_map/ppermute | solution.py:320
  200.3 12.3 %collective-permute-start.35 = (f32[192,128]{1,0:T(8,128)S(1)}, f32[192,128]{1,0:T(8,128)S(1)}, u32[]{:S(2)}, u32[]{:S(2)}) collective-permute-start(f32[192,128]{1,0:T(8,128)S(1)} %get-tuple-element.143), channel_id=1, source_target_pairs={{0,28},{4,24},{8,20},{12,16},{16,12},{20,8},{24,4},{28,0},{1,29},{... | collective-permute-start | bytes 294920 | tf_op jit(solution)/shard_map/ppermute | solution.py:320
  213.3 9.3 %collective-permute-start.37 = (f32[192,128]{1,0:T(8,128)S(1)}, f32[192,128]{1,0:T(8,128)S(1)}, u32[]{:S(2)}, u32[]{:S(2)}) collective-permute-start(f32[192,128]{1,0:T(8,128)S(1)} %right_sum.3.refs_0_), channel_id=1, source_target_pairs={{0,8},{4,12},{8,0},{12,4},{16,24},{20,28},{24,16},{28,20},{1,9},{5... | collective-permute-start | bytes 294920 | tf_op jit(solution)/shard_map/ppermute | solution.py:320
  217.7 14.2 %collective-permute-start.39 = (f32[192,128]{1,0:T(8,128)S(1)}, f32[192,128]{1,0:T(8,128)S(1)}, u32[]{:S(2)}, u32[]{:S(2)}) collective-permute-start(f32[192,128]{1,0:T(8,128)S(1)} %right_sum.3.refs_0_), channel_id=1, source_target_pairs={{0,16},{4,20},{8,24},{12,28},{16,0},{20,4},{24,8},{28,12},{1,17},{... | collective-permute-start | bytes 294920 | tf_op jit(solution)/shard_map/ppermute | solution.py:320
  220.3 13.8 %collective-permute-start.40 = (f32[192,128]{1,0:T(8,128)S(1)}, f32[192,128]{1,0:T(8,128)S(1)}, u32[]{:S(2)}, u32[]{:S(2)}) collective-permute-start(f32[192,128]{1,0:T(8,128)S(1)} %right_sum.3.refs_0_), channel_id=1, source_target_pairs={{0,20},{4,16},{8,28},{12,24},{16,4},{20,0},{24,12},{28,8},{1,21},{... | collective-permute-start | bytes 294920 | tf_op jit(solution)/shard_map/ppermute | solution.py:320
  220.7 13.4 %collective-permute-start.41 = (f32[192,128]{1,0:T(8,128)S(1)}, f32[192,128]{1,0:T(8,128)S(1)}, u32[]{:S(2)}, u32[]{:S(2)}) collective-permute-start(f32[192,128]{1,0:T(8,128)S(1)} %right_sum.3.refs_0_), channel_id=1, source_target_pairs={{0,24},{4,28},{8,16},{12,20},{16,8},{20,12},{24,0},{28,4},{1,25},{... | collective-permute-start | bytes 294920 | tf_op jit(solution)/shard_map/ppermute | solution.py:320
  222.7 11.4 %collective-permute-start.42 = (f32[192,128]{1,0:T(8,128)S(1)}, f32[192,128]{1,0:T(8,128)S(1)}, u32[]{:S(2)}, u32[]{:S(2)}) collective-permute-start(f32[192,128]{1,0:T(8,128)S(1)} %right_sum.3.refs_0_), channel_id=1, source_target_pairs={{0,28},{4,24},{8,20},{12,16},{16,12},{20,8},{24,4},{28,0},{1,29},{... | collective-permute-start | bytes 294920 | tf_op jit(solution)/shard_map/ppermute | solution.py:320
  237.7 24.8 %collective-permute-start.46 = (bf16[576,512]{1,0:T(8,128)(2,1)}, bf16[576,512]{1,0:T(8,128)(2,1)}, u32[]{:S(2)}, u32[]{:S(2)}) collective-permute-start(bf16[576,512]{1,0:T(8,128)(2,1)} %get-tuple-element.149.refs_0_), channel_id=1, source_target_pairs={{0,8},{4,12},{8,16},{12,20},{16,24},{20,28},{24,0},{28,4},{1,9},{5... | collective-permute-start | bytes 1769480 | tf_op jit(solution)/shard_map/ppermute | solution.py:560
  241.6 20.8 %collective-permute-start.47 = (bf16[576,512]{1,0:T(8,128)(2,1)}, bf16[576,512]{1,0:T(8,128)(2,1)}, u32[]{:S(2)}, u32[]{:S(2)}) collective-permute-start(bf16[576,512]{1,0:T(8,128)(2,1)} %get-tuple-element.149.refs_0_), channel_id=1, source_target_pairs={{0,4},{4,0},{8,12},{12,8},{16,20},{20,16},{24,28},{28,24},{1,5},{5... | collective-permute-start | bytes 1769480 | tf_op jit(solution)/shard_map/ppermute | solution.py:320
  242.6 25.7 %collective-permute-start.48 = (bf16[576,512]{1,0:T(8,128)(2,1)}, bf16[576,512]{1,0:T(8,128)(2,1)}, u32[]{:S(2)}, u32[]{:S(2)}) collective-permute-start(bf16[576,512]{1,0:T(8,128)(2,1)} %get-tuple-element.156.refs_1_), channel_id=1, source_target_pairs={{0,8},{4,12},{8,16},{12,20},{16,24},{20,28},{24,0},{28,4},{1,9},{5... | collective-permute-start | bytes 1769480 | tf_op jit(solution)/shard_map/ppermute | solution.py:560
  243.5 27.4 %collective-permute-start.49 = (bf16[576,512]{1,0:T(8,128)(2,1)}, bf16[576,512]{1,0:T(8,128)(2,1)}, u32[]{:S(2)}, u32[]{:S(2)}) collective-permute-start(bf16[576,512]{1,0:T(8,128)(2,1)} %get-tuple-element.156.refs_1_), channel_id=1, source_target_pairs={{0,4},{4,0},{8,12},{12,8},{16,20},{20,16},{24,28},{28,24},{1,5},{5... | collective-permute-start | bytes 1769480 | tf_op jit(solution)/shard_map/ppermute | solution.py:320
  252.4 10.0 %collective-permute-start.45 = (f32[64,512]{1,0:T(8,128)S(1)}, f32[64,512]{1,0:T(8,128)S(1)}, u32[]{:S(2)}, u32[]{:S(2)}) collective-permute-start(f32[64,512]{1,0:T(8,128)S(1)} %constant_dynamic-slice_fusion), channel_id=1, source_target_pairs={{0,3},{1,2},{2,1},{3,0},{4,7},{5,6},{6,5},{7,4},{8,11},{9,10},{10,... | collective-permute-start | bytes 393224 | tf_op jit(solution)/shard_map/ppermute | solution.py:320
  262.5 18.5 %collective-permute-start.50 = (bf16[576,512]{1,0:T(8,128)(2,1)}, bf16[576,512]{1,0:T(8,128)(2,1)S(1)}, u32[]{:S(2)}, u32[]{:S(2)}) collective-permute-start(bf16[576,512]{1,0:T(8,128)(2,1)} %collective-permute-done.46.refs_2_), channel_id=1, source_target_pairs={{0,8},{4,12},{8,16},{12,20},{16,24},{20,28},{24,0},{28,4},{1,9},{5... | collective-permute-start | bytes 1769480 | tf_op jit(solution)/shard_map/ppermute | solution.py:560
  262.5 20.8 %collective-permute-start.51 = (bf16[576,512]{1,0:T(8,128)(2,1)}, bf16[576,512]{1,0:T(8,128)(2,1)S(1)}, u32[]{:S(2)}, u32[]{:S(2)}) collective-permute-start(bf16[576,512]{1,0:T(8,128)(2,1)} %collective-permute-done.46.refs_2_), channel_id=1, source_target_pairs={{0,4},{4,0},{8,12},{12,8},{16,20},{20,16},{24,28},{28,24},{1,5},{5... | collective-permute-start | bytes 1769480 | tf_op jit(solution)/shard_map/ppermute | solution.py:320
  270.8 22.8 %collective-permute-start.52 = (bf16[576,512]{1,0:T(8,128)(2,1)}, bf16[576,512]{1,0:T(8,128)(2,1)S(1)}, u32[]{:S(2)}, u32[]{:S(2)}) collective-permute-start(bf16[576,512]{1,0:T(8,128)(2,1)} %collective-permute-done.48.refs_4_), channel_id=1, source_target_pairs={{0,8},{4,12},{8,16},{12,20},{16,24},{20,28},{24,0},{28,4},{1,9},{5... | collective-permute-start | bytes 1769480 | tf_op jit(solution)/shard_map/ppermute | solution.py:560
  271.5 24.5 %collective-permute-start.53 = (bf16[576,512]{1,0:T(8,128)(2,1)}, bf16[576,512]{1,0:T(8,128)(2,1)S(1)}, u32[]{:S(2)}, u32[]{:S(2)}) collective-permute-start(bf16[576,512]{1,0:T(8,128)(2,1)} %collective-permute-done.48.refs_4_), channel_id=1, source_target_pairs={{0,4},{4,0},{8,12},{12,8},{16,20},{20,16},{24,28},{28,24},{1,5},{5... | collective-permute-start | bytes 1769480 | tf_op jit(solution)/shard_map/ppermute | solution.py:320
  283.4 26.8 %collective-permute-start.54 = (bf16[576,512]{1,0:T(8,128)(2,1)S(1)}, bf16[576,512]{1,0:T(8,128)(2,1)S(1)}, u32[]{:S(2)}, u32[]{:S(2)}) collective-permute-start(bf16[576,512]{1,0:T(8,128)(2,1)S(1)} %collective-permute-done.50.refs_6_), channel_id=1, source_target_pairs={{0,8},{4,12},{8,16},{12,20},{16,24},{20,28},{24,0},{28,4},{1,9},{5... | collective-permute-start | bytes 1769480 | tf_op jit(solution)/shard_map/ppermute | solution.py:560
  284.1 26.2 %collective-permute-start.55 = (bf16[576,512]{1,0:T(8,128)(2,1)S(1)}, bf16[576,512]{1,0:T(8,128)(2,1)S(1)}, u32[]{:S(2)}, u32[]{:S(2)}) collective-permute-start(bf16[576,512]{1,0:T(8,128)(2,1)S(1)} %collective-permute-done.50.refs_6_), channel_id=1, source_target_pairs={{0,4},{4,0},{8,12},{12,8},{16,20},{20,16},{24,28},{28,24},{1,5},{5... | collective-permute-start | bytes 1769480 | tf_op jit(solution)/shard_map/ppermute | solution.py:320
  296.0 22.5 %collective-permute-start.56 = (bf16[576,512]{1,0:T(8,128)(2,1)S(1)}, bf16[576,512]{1,0:T(8,128)(2,1)S(1)}, u32[]{:S(2)}, u32[]{:S(2)}) collective-permute-start(bf16[576,512]{1,0:T(8,128)(2,1)S(1)} %collective-permute-done.52.refs_8_), channel_id=1, source_target_pairs={{0,8},{4,12},{8,16},{12,20},{16,24},{20,28},{24,0},{28,4},{1,9},{5... | collective-permute-start | bytes 1769480 | tf_op jit(solution)/shard_map/ppermute | solution.py:560
  296.7 22.6 %collective-permute-start.57 = (bf16[576,512]{1,0:T(8,128)(2,1)S(1)}, bf16[576,512]{1,0:T(8,128)(2,1)S(1)}, u32[]{:S(2)}, u32[]{:S(2)}) collective-permute-start(bf16[576,512]{1,0:T(8,128)(2,1)S(1)} %collective-permute-done.52.refs_8_), channel_id=1, source_target_pairs={{0,4},{4,0},{8,12},{12,8},{16,20},{20,16},{24,28},{28,24},{1,5},{5... | collective-permute-start | bytes 1769480 | tf_op jit(solution)/shard_map/ppermute | solution.py:320
  319.3 16.4 %collective-permute-start.59 = (bf16[576,512]{1,0:T(8,128)(2,1)S(1)}, bf16[576,512]{1,0:T(8,128)(2,1)S(1)}, u32[]{:S(2)}, u32[]{:S(2)}) collective-permute-start(bf16[576,512]{1,0:T(8,128)(2,1)S(1)} %collective-permute-done.57.refs_1_), channel_id=1, source_target_pairs={{0,8},{4,12},{8,16},{12,20},{16,24},{20,28},{24,0},{28,4},{1,9},{5... | collective-permute-start | bytes 1769480 | tf_op jit(solution)/shard_map/ppermute | solution.py:565
  319.6 16.1 %collective-permute-start.58 = (bf16[576,512]{1,0:T(8,128)(2,1)S(1)}, bf16[576,512]{1,0:T(8,128)(2,1)S(1)}, u32[]{:S(2)}, u32[]{:S(2)}) collective-permute-start(bf16[576,512]{1,0:T(8,128)(2,1)S(1)} %collective-permute-done.54.refs_0_), channel_id=1, source_target_pairs={{0,4},{4,0},{8,12},{12,8},{16,20},{20,16},{24,28},{28,24},{1,5},{5... | collective-permute-start | bytes 1769480 | tf_op jit(solution)/shard_map/ppermute | solution.py:320
  (44 other events, 365.1 us)

commit v8 on v7

--- a/solution.py
+++ b/solution.py
@@ -399,7 +399,9 @@
             column = (tp ^ offset) * cols
             piece = lax.dynamic_slice_in_dim(new_values, column, cols, 1)
             piece = piece - (LEARNING_RATE * MOMENTUM_DECAY) * lax.dynamic_slice_in_dim(old_values, column, cols, 1)
-            some.append(piece if offset == 0 else swap(piece, "tp", tps, offset))
+            some.append((piece, offset))
+        parts, pieces = lax.optimization_barrier((parts, [piece for piece, _ in some]))
+        some = [piece if offset == 0 else swap(piece, "tp", tps, offset) for piece, (_, offset) in zip(pieces, some)]
         parts = parts.reshape(replicas, left_part, LANES)
         parts = lax.all_to_all(parts, "rep", split_axis=0, concat_axis=0, tiled=True)
         parts = whole_call(total_kernel, "left_sum", shape(*parts.shape), [parts])

time: 338 us -> 346 us (1.024)
  waiting for transfers between devices: 138 us -> 143 us
    all_to_all x4, waiting for transfers between devices: 26 us -> 35.7 us  [local(): lax.all_to_all(parts, 'rep', split_axis=0, concat_axis=0, tiled=True)]
    ppermute x53, waiting for transfers between devices: 80.1 us -> 74.2 us  [swap(): lax.ppermute(x, axis, [(index, index ^ offset) for index in range(size)])]
  transfers between devices with their start and end apart: 64 -> 64, of which waited for: 35 -> 36; matrix products, arithmetic and copies ran while one was open for 2% -> 0% of each run, Pallas kernels for 15% -> 15%
where the time goes in v8:
time: 346 us; the launch traced here: 345 us
  waiting for transfers between devices  143 us (41%)
  starting transfers between devices  86.5 us (25%)
  Pallas kernels  81.1 us (23%)
  local copies, waits for them, and re-layouts  28.7 us (8%)
  other arithmetic  5.06 us (1%)
    ppermute x53, waiting for transfers between devices, swap(): lax.ppermute(x, axis, [(index, index ^ offset) for index in range(size)])  74.2 us
    pallas_call x17, Pallas kernels, grid_call(): pl.pallas_call(kernel, grid_spec=pltpu.PrefetchScalarGridSpec(num_scalar_...  70.5 us
    ppermute x53, starting transfers between devices, swap(): lax.ppermute(x, axis, [(index, index ^ offset) for index in range(size)])  60.6 us
    all_to_all x4, waiting for transfers between devices, local(): lax.all_to_all(parts, 'rep', split_axis=0, concat_axis=0, tiled=True)  35.7 us
    unnamed x56, local copies, waits for them, and re-layouts  27.8 us
    all_to_all x4, starting transfers between devices, local(): lax.all_to_all(parts, 'rep', split_axis=0, concat_axis=0, tiled=True)  19.1 us
    ppermute x6, waiting for transfers between devices, local(): held[half] = lax.ppermute(here, 'rep', ring)  18.7 us
    ppermute x1, waiting for transfers between devices, local(): beside[half] = lax.ppermute(beside[half], 'rep', ring)  14.2 us
  transfers between devices with their start and end apart: 64, of which 36 were waited for; matrix products, arithmetic and copies ran while one was open for 0% of the time, Pallas kernels for 15%

profile of v8, /device:TPU:0, one launch (start us, length us, event | category | flops | bytes accessed | tf_op | source)
XLA Modules:
  0.0 345.1 jit_solution(2718229162541215023)
XLA Ops:
  1.8 7.3 %first_left.2 = (bf16[6,768,512]{2,1,0:T(8,128)(2,1)S(1)}, bf16[6,768,512]{2,1,0:T(8,128)(2,1)S(1)}, f32[96,768]{1,0:T(8,128)}, f32[96,768]{1,0:T(8,128)}) custom-call(s32[2]{0:T(128)S(1)} %pad_add_fusion.ids_ref, bf16[1,12,768,512]{3,2,1,0:T(8,128)(2,1)} %grads_ref.3, f32[1,12,768,512]{3,2,1,0:T(8,128)} %error_ref.3, f32[12,32,512]{2,1,0:T(8,128)S(1)} %copy-done.15), custom_call_target="tpu_custom_call" | custom-call | flops 452984832 | bytes 23592960 | tf_op jit(solution)/shard_map/first_left/pallas_call | solution.py:302
  13.5 2.9 collective-permute-start.1
  16.5 7.3 %first_left.3 = (bf16[6,768,512]{2,1,0:T(8,128)(2,1)S(1)}, bf16[6,768,512]{2,1,0:T(8,128)(2,1)S(1)}, f32[96,768]{1,0:T(8,128)S(1)}, f32[96,768]{1,0:T(8,128)}) custom-call(s32[2]{0:T(128)S(1)} %pad_add_fusion.ids_ref, bf16[1,12,768,512]{3,2,1,0:T(8,128)(2,1)} %grads_ref.3, f32[1,12,768,512]{3,2,1,0:T(8,128)} %error_ref.3, f32[12,32,512]{2,1,0:T(8,128)S(1)} %copy-done.16), custom_call_target="tpu_custom_call" | custom-call | flops 452984832 | bytes 23592960 | tf_op jit(solution)/shard_map/first_left/pallas_call | solution.py:302
  29.9 7.1 %collective-permute-done.refs_1_ = f32[96,768]{1,0:T(8,128)S(1)} collective-permute-done((f32[96,768]{1,0:T(8,128)}, f32[96,768]{1,0:T(8,128)S(1)}, u32[]{:S(2)}, u32[]{:S(2)}) %collective-permute-start) | collective-permute-done | bytes 294944 | tf_op jit(solution)/shard_map/ppermute | solution.py:320
  37.8 2.9 multiply_subtract_fusion.1
  40.6 5.8 %all-to-all-start = ((f32[8,72,128]{2,1,0:T(8,128)}), f32[8,72,128]{2,1,0:T(8,128)S(1)}, u32[]{:S(2)}, u32[]{:S(2)}) async-start(f32[8,72,128]{2,1,0:T(8,128)} %bitcast.2), calls=%async_computation | async-start | bytes 589824 | tf_op jit(solution)/shard_map/all_to_all | solution.py:406
  47.2 9.5 %all-to-all-done.parts_ref = f32[8,72,128]{2,1,0:T(8,128)S(1)} async-done(((f32[8,72,128]{2,1,0:T(8,128)}), f32[8,72,128]{2,1,0:T(8,128)S(1)}, u32[]{:S(2)}, u32[]{:S(2)}) %all-to-all-start) | async-done | bytes 294944 | tf_op jit(solution)/shard_map/all_to_all | solution.py:406
  57.4 3.6 %all-to-all-start.1 = ((f32[8,72,128]{2,1,0:T(8,128)}), f32[8,72,128]{2,1,0:T(8,128)S(1)}, u32[]{:S(2)}, u32[]{:S(2)}) async-start(f32[8,72,128]{2,1,0:T(8,128)} %left_sum.2), calls=%async_computation.1 | async-start | bytes 589824 | tf_op jit(solution)/shard_map/all_to_all | solution.py:408
  62.5 8.3 %all-to-all-done.1 = f32[8,72,128]{2,1,0:T(8,128)S(1)} async-done(((f32[8,72,128]{2,1,0:T(8,128)}), f32[8,72,128]{2,1,0:T(8,128)S(1)}, u32[]{:S(2)}, u32[]{:S(2)}) %all-to-all-start.1) | async-done | bytes 294944 | tf_op jit(solution)/shard_map/all_to_all | solution.py:408
  74.4 2.5 copy-done.5
  76.9 2.5 copy-done.9
  79.4 2.8 right_near.2.refs_0_
  83.9 2.9 right_far.2
  97.0 5.3 %collective-permute-done.11.refs_4_ = f32[192,128]{1,0:T(8,128)S(1)} collective-permute-done((f32[192,128]{1,0:T(8,128)S(1)}, f32[192,128]{1,0:T(8,128)S(1)}, u32[]{:S(2)}, u32[]{:S(2)}) %collective-permute-start.11) | collective-permute-done | bytes 98336 | tf_op jit(solution)/shard_map/ppermute | solution.py:320
  102.4 3.2 collective-permute-done.12.refs_5_
  115.8 3.0 collective-permute-start.21
  118.8 6.8 %collective-permute-done.18.refs_4_ = f32[192,128]{1,0:T(8,128)S(1)} collective-permute-done((f32[192,128]{1,0:T(8,128)S(1)}, f32[192,128]{1,0:T(8,128)S(1)}, u32[]{:S(2)}, u32[]{:S(2)}) %collective-permute-start.18) | collective-permute-done | bytes 98336 | tf_op jit(solution)/shard_map/ppermute | solution.py:320
  125.7 2.7 collective-permute-done.19.refs_5_
  128.4 5.0 %left.3 = (f32[96,768]{1,0:T(8,128)}, f32[96,768]{1,0:T(8,128)}) custom-call(s32[2]{0:T(128)S(1)} %pad_add_fusion.ids_ref, bf16[6,768,512]{2,1,0:T(8,128)(2,1)S(1)} %bitcast.13, bf16[6,768,512]{2,1,0:T(8,128)(2,1)S(1)} %copy-done.2, f32[192,128]{1,0:T(8,128)S(1)} %right_sum.2.refs_0_, f32[192,128]{1,0:T(8,128)S(1)} %collective-permute-done.15.refs_1_, ...), custom_call_target="tpu_custom_call" | custom-call | flops 452984832 | bytes 23592960 | tf_op jit(solution)/shard_map/left/pallas_call | solution.py:302
  134.0 4.9 %left.2 = (f32[96,768]{1,0:T(8,128)S(1)}, f32[96,768]{1,0:T(8,128)}) custom-call(s32[2]{0:T(128)S(1)} %pad_add_fusion.ids_ref, bf16[6,768,512]{2,1,0:T(8,128)(2,1)S(1)} %copy-done.5, bf16[6,768,512]{2,1,0:T(8,128)(2,1)S(1)} %copy-done.9, f32[192,128]{1,0:T(8,128)S(1)} %right_sum.2.refs_0_, f32[192,128]{1,0:T(8,128)S(1)} %collective-permute-done.15.refs_1_, ...), custom_call_target="tpu_custom_call" | custom-call | flops 452984832 | bytes 23592960 | tf_op jit(solution)/shard_map/left/pallas_call | solution.py:302
  140.1 2.8 collective-permute-done.22.refs_1_
  142.9 4.6 %collective-permute-done.23.refs_2_ = f32[96,768]{1,0:T(8,128)S(1)} collective-permute-done((f32[96,768]{1,0:T(8,128)}, f32[96,768]{1,0:T(8,128)S(1)}, u32[]{:S(2)}, u32[]{:S(2)}) %collective-permute-start.23) | collective-permute-done | bytes 294944 | tf_op jit(solution)/shard_map/ppermute | solution.py:320
  150.3 5.9 %all-to-all-start.2 = ((f32[8,72,128]{2,1,0:T(8,128)}), f32[8,72,128]{2,1,0:T(8,128)S(1)}, u32[]{:S(2)}, u32[]{:S(2)}) async-start(f32[8,72,128]{2,1,0:T(8,128)} %bitcast.4), calls=%async_computation.2 | async-start | bytes 589824 | tf_op jit(solution)/shard_map/all_to_all | solution.py:406
  157.6 8.8 %all-to-all-done.2.parts_ref = f32[8,72,128]{2,1,0:T(8,128)S(1)} async-done(((f32[8,72,128]{2,1,0:T(8,128)}), f32[8,72,128]{2,1,0:T(8,128)S(1)}, u32[]{:S(2)}, u32[]{:S(2)}) %all-to-all-start.2) | async-done | bytes 294944 | tf_op jit(solution)/shard_map/all_to_all | solution.py:406
  167.2 3.8 %all-to-all-start.3 = ((f32[8,72,128]{2,1,0:T(8,128)}), f32[8,72,128]{2,1,0:T(8,128)S(1)}, u32[]{:S(2)}, u32[]{:S(2)}) async-start(f32[8,72,128]{2,1,0:T(8,128)} %left_sum.3), calls=%async_computation.3 | async-start | bytes 589824 | tf_op jit(solution)/shard_map/all_to_all | solution.py:408
  171.6 9.1 %all-to-all-done.3 = f32[8,72,128]{2,1,0:T(8,128)S(1)} async-done(((f32[8,72,128]{2,1,0:T(8,128)}), f32[8,72,128]{2,1,0:T(8,128)S(1)}, u32[]{:S(2)}, u32[]{:S(2)}) %all-to-all-start.3) | async-done | bytes 294944 | tf_op jit(solution)/shard_map/all_to_all | solution.py:408
  189.0 2.8 right_near.3.refs_0_
  196.1 2.9 right_far.3
  203.7 2.8 collective-permute-start.33
  210.3 6.9 %collective-permute-done.32.refs_4_ = f32[192,128]{1,0:T(8,128)S(1)} collective-permute-done((f32[192,128]{1,0:T(8,128)S(1)}, f32[192,128]{1,0:T(8,128)S(1)}, u32[]{:S(2)}, u32[]{:S(2)}) %collective-permute-start.32) | collective-permute-done | bytes 98336 | tf_op jit(solution)/shard_map/ppermute | solution.py:320
  217.2 3.0 collective-permute-done.33.refs_5_
  220.9 3.5 %collective-permute-start.37 = (f32[192,128]{1,0:T(8,128)S(1)}, f32[192,128]{1,0:T(8,128)S(1)}, u32[]{:S(2)}, u32[]{:S(2)}) collective-permute-start(f32[192,128]{1,0:T(8,128)S(1)} %right_sum.3.refs_0_), channel_id=1, source_target_pairs={{0,8},{4,12},{8,0},{12,4},{16,24},{20,28},{24,16},{28,20},{1,9},{5... | collective-permute-start | bytes 294920 | tf_op jit(solution)/shard_map/ppermute | solution.py:320
  225.3 2.6 collective-permute-start.39
  230.3 2.7 collective-permute-start.42
  233.1 6.4 %collective-permute-done.39.refs_4_ = f32[192,128]{1,0:T(8,128)S(1)} collective-permute-done((f32[192,128]{1,0:T(8,128)S(1)}, f32[192,128]{1,0:T(8,128)S(1)}, u32[]{:S(2)}, u32[]{:S(2)}) %collective-permute-start.39) | collective-permute-done | bytes 98336 | tf_op jit(solution)/shard_map/ppermute | solution.py:320
  241.7 3.6 %late_rows.1 = (f32[384,512]{1,0:T(8,128)}, bf16[576,512]{1,0:T(8,128)(2,1)}, bf16[576,512]{1,0:T(8,128)(2,1)}) custom-call(s32[2]{0:T(128)S(1)} %pad_add_fusion.ids_ref, f32[384,768]{1,0:T(8,128)S(1)} %pad_maximum_fusion.basis_ref, f32[192,128]{1,0:T(8,128)S(1)} %right_sum.3.refs_0_, f32[192,128]{1,0:T(8,128)S(1)} %collective-permute-done.36.refs_1_, ...), custom_call_target="tpu_custom_call" | custom-call | flops 4325376 | bytes 8650752 | tf_op jit(solution)/shard_map/late_rows/pallas_call | solution.py:289
  245.3 3.9 %collective-permute-start.46 = (bf16[576,512]{1,0:T(8,128)(2,1)}, bf16[576,512]{1,0:T(8,128)(2,1)}, u32[]{:S(2)}, u32[]{:S(2)}) collective-permute-start(bf16[576,512]{1,0:T(8,128)(2,1)} %get-tuple-element.161.refs_0_), channel_id=1, source_target_pairs={{0,8},{4,12},{8,16},{12,20},{16,24},{20,28},{24,0},{28,4},{1,9},{5... | collective-permute-start | bytes 1769480 | tf_op jit(solution)/shard_map/ppermute | solution.py:562
  255.7 4.3 %collective-permute-done.44 = f32[64,512]{1,0:T(8,128)S(1)} collective-permute-done((f32[64,512]{1,0:T(8,128)S(1)}, f32[64,512]{1,0:T(8,128)S(1)}, u32[]{:S(2)}, u32[]{:S(2)}) %collective-permute-start.44) | collective-permute-done | bytes 131104 | tf_op jit(solution)/shard_map/ppermute | solution.py:320
  266.1 4.1 %update.4.refs_0_ = f32[1,12,768,512]{3,2,1,0:T(8,128)} custom-call(s32[2]{0:T(128)S(1)} %pad_add_fusion.ids_ref, f32[384,768]{1,0:T(8,128)S(1)} %pad_maximum_fusion.basis_ref, f32[384,512]{1,0:T(8,128)S(1)} %copy-done.12, bf16[6,768,512]{2,1,0:T(8,128)(2,1)S(1)} %copy-done.7, bf16[6,768,512]{2,1,0:T(8,128)(2,1)S(1)} %copy-done.11), custom_call_target="tpu_custom_call" | custom-call | flops 226492416 | bytes 9437184 | tf_op jit(solution)/shard_map/update/pallas_call | solution.py:302
  271.4 4.1 %update.5.refs_0_ = f32[1,12,768,512]{3,2,1,0:T(8,128)} custom-call(s32[2]{0:T(128)S(1)} %pad_add_fusion.ids_ref, f32[384,768]{1,0:T(8,128)S(1)} %pad_maximum_fusion.basis_ref, f32[384,512]{1,0:T(8,128)S(1)} %copy-done.12, bf16[6,768,512]{2,1,0:T(8,128)(2,1)S(1)} %copy-done.7, bf16[6,768,512]{2,1,0:T(8,128)(2,1)S(1)} %copy-done.11, ...), custom_call_target="tpu_custom_call", output_to_operand_aliasing={{}: (5, {})} | custom-call | flops 226492416 | bytes 9437184 | tf_op jit(solution)/shard_map/update/pallas_call | solution.py:302
  279.0 4.1 %update.6.refs_0_ = f32[1,12,768,512]{3,2,1,0:T(8,128)} custom-call(s32[2]{0:T(128)S(1)} %pad_add_fusion.ids_ref, f32[384,768]{1,0:T(8,128)S(1)} %pad_maximum_fusion.basis_ref, f32[384,512]{1,0:T(8,128)S(1)} %copy-done.12, bf16[6,768,512]{2,1,0:T(8,128)(2,1)S(1)} %bitcast.17, bf16[6,768,512]{2,1,0:T(8,128)(2,1)S(1)} %bitcast.19, ...), custom_call_target="tpu_custom_call", output_to_operand_aliasing={{}: (5, {})} | custom-call | flops 226492416 | bytes 9437184 | tf_op jit(solution)/shard_map/update/pallas_call | solution.py:302
  283.1 5.5 %collective-permute-done.50.refs_6_ = bf16[576,512]{1,0:T(8,128)(2,1)S(1)} collective-permute-done((bf16[576,512]{1,0:T(8,128)(2,1)}, bf16[576,512]{1,0:T(8,128)(2,1)S(1)}, u32[]{:S(2)}, u32[]{:S(2)}) %collective-permute-start.50) | collective-permute-done | bytes 589856 | tf_op jit(solution)/shard_map/ppermute | solution.py:562
  291.5 4.1 %update.7 = f32[1,12,768,512]{3,2,1,0:T(8,128)} custom-call(s32[2]{0:T(128)S(1)} %pad_add_fusion.ids_ref, f32[384,768]{1,0:T(8,128)S(1)} %pad_maximum_fusion.basis_ref, f32[384,512]{1,0:T(8,128)S(1)} %copy-done.12, bf16[6,768,512]{2,1,0:T(8,128)(2,1)S(1)} %bitcast.17, bf16[6,768,512]{2,1,0:T(8,128)(2,1)S(1)} %bitcast.19, ...), custom_call_target="tpu_custom_call", output_to_operand_aliasing={{}: (5, {})} | custom-call | flops 226492416 | bytes 9437184 | tf_op jit(solution)/shard_map/update/pallas_call | solution.py:302
  295.6 5.7 %collective-permute-done.52.refs_8_ = bf16[576,512]{1,0:T(8,128)(2,1)S(1)} collective-permute-done((bf16[576,512]{1,0:T(8,128)(2,1)}, bf16[576,512]{1,0:T(8,128)(2,1)S(1)}, u32[]{:S(2)}, u32[]{:S(2)}) %collective-permute-start.52) | collective-permute-done | bytes 589856 | tf_op jit(solution)/shard_map/ppermute | solution.py:562
  304.1 7.3 %place.4.refs_2_ = bf16[8,2,576,512]{3,2,1,0:T(8,128)(2,1)} custom-call(s32[2]{0:T(128)S(1)} %pad_add_fusion.ids_ref, bf16[576,512]{1,0:T(8,128)(2,1)} %get-tuple-element.161.refs_0_, bf16[576,512]{1,0:T(8,128)(2,1)} %get-tuple-element.168.refs_1_, bf16[576,512]{1,0:T(8,128)(2,1)} %collective-permute-done.46.refs_2_, ...), custom_call_target="tpu_custom_call" | custom-call | bytes 23592960 | tf_op jit(solution)/shard_map/place/pallas_call | solution.py:302
  311.5 6.2 %flat_rows.1 = (f32[288,2048]{1,0:T(8,128)}, f32[288,2048]{1,0:T(8,128)}) custom-call(s32[2]{0:T(128)S(1)} %pad_add_fusion.ids_ref, f32[384,768]{1,0:T(8,128)S(1)} %pad_maximum_fusion.basis_ref, f32[4,64,512]{2,1,0:T(8,128)S(1)} %pad_maximum_fusion.1.near_ref, f32[288,2048]{1,0:T(8,128)S(1)} %copy-done.13, f32[288,2048]{1,0:T(8,128)S(1)} %copy-done.14), custom_call_target="tpu_custom_call" | custom-call | flops 452984832 | bytes 9437184 | tf_op jit(solution)/shard_map/flat_rows/pallas_call | solution.py:302
  319.3 7.0 %collective-permute-done.56.refs_0_ = bf16[576,512]{1,0:T(8,128)(2,1)S(1)} collective-permute-done((bf16[576,512]{1,0:T(8,128)(2,1)S(1)}, bf16[576,512]{1,0:T(8,128)(2,1)S(1)}, u32[]{:S(2)}, u32[]{:S(2)}) %collective-permute-start.56) | collective-permute-done | bytes 589856 | tf_op jit(solution)/shard_map/ppermute | solution.py:562
  329.2 14.2 %collective-permute-done.59.refs_1_ = bf16[576,512]{1,0:T(8,128)(2,1)S(1)} collective-permute-done((bf16[576,512]{1,0:T(8,128)(2,1)S(1)}, bf16[576,512]{1,0:T(8,128)(2,1)S(1)}, u32[]{:S(2)}, u32[]{:S(2)}) %collective-permute-start.59) | collective-permute-done | bytes 589856 | tf_op jit(solution)/shard_map/ppermute | solution.py:567
  (172 shorter events, 105.4 us)
Async XLA Ops:
  13.5 16.4 %collective-permute-start.1 = (f32[96,768]{1,0:T(8,128)}, f32[96,768]{1,0:T(8,128)S(1)}, u32[]{:S(2)}, u32[]{:S(2)}) collective-permute-start(f32[96,768]{1,0:T(8,128)} %get-tuple-element.108), channel_id=1, source_target_pairs={{0,2},{1,3},{2,0},{3,1},{4,6},{5,7},{6,4},{7,5},{8,10},{9,11},{10,... | collective-permute-start | bytes 884744 | tf_op jit(solution)/shard_map/ppermute | solution.py:320
  28.1 8.9 %collective-permute-start = (f32[96,768]{1,0:T(8,128)}, f32[96,768]{1,0:T(8,128)S(1)}, u32[]{:S(2)}, u32[]{:S(2)}) collective-permute-start(f32[96,768]{1,0:T(8,128)} %get-tuple-element.114), channel_id=1, source_target_pairs={{0,3},{1,2},{2,1},{3,0},{4,7},{5,6},{6,5},{7,4},{8,11},{9,10},{10,... | collective-permute-start | bytes 884744 | tf_op jit(solution)/shard_map/ppermute | solution.py:320
  40.6 16.0 %all-to-all-start = ((f32[8,72,128]{2,1,0:T(8,128)}), f32[8,72,128]{2,1,0:T(8,128)S(1)}, u32[]{:S(2)}, u32[]{:S(2)}) async-start(f32[8,72,128]{2,1,0:T(8,128)} %bitcast.2), calls=%async_computation | async-start | bytes 589824 | tf_op jit(solution)/shard_map/all_to_all | solution.py:406
  46.4 14.6 %collective-permute-start.3 = (f32[288,512]{1,0:T(8,128)}, f32[288,512]{1,0:T(8,128)S(1)}, u32[]{:S(2)}, u32[]{:S(2)}) collective-permute-start(f32[288,512]{1,0:T(8,128)} %get-tuple-element.121), channel_id=1, source_target_pairs={{0,1},{1,0},{2,3},{3,2},{4,5},{5,4},{6,7},{7,6},{8,9},{9,8},{10,11... | collective-permute-start | bytes 1769480 | tf_op jit(solution)/shard_map/ppermute | solution.py:320
  46.6 15.9 %collective-permute-start.4 = (f32[288,512]{1,0:T(8,128)}, f32[288,512]{1,0:T(8,128)}, u32[]{:S(2)}, u32[]{:S(2)}) collective-permute-start(f32[288,512]{1,0:T(8,128)} %get-tuple-element.122), channel_id=1, source_target_pairs={{0,2},{1,3},{2,0},{3,1},{4,6},{5,7},{6,4},{7,5},{8,10},{9,11},{10,... | collective-permute-start | bytes 1769480 | tf_op jit(solution)/shard_map/ppermute | solution.py:320
  57.4 13.4 %all-to-all-start.1 = ((f32[8,72,128]{2,1,0:T(8,128)}), f32[8,72,128]{2,1,0:T(8,128)S(1)}, u32[]{:S(2)}, u32[]{:S(2)}) async-start(f32[8,72,128]{2,1,0:T(8,128)} %left_sum.2), calls=%async_computation.1 | async-start | bytes 589824 | tf_op jit(solution)/shard_map/all_to_all | solution.py:408
  72.8 9.4 %collective-permute-start.6 = (f32[96,768]{1,0:T(8,128)S(1)}, f32[96,768]{1,0:T(8,128)S(1)}, u32[]{:S(2)}, u32[]{:S(2)}) collective-permute-start(f32[96,768]{1,0:T(8,128)S(1)} %basis.2.first_ref), channel_id=1, source_target_pairs={{0,2},{1,3},{2,0},{3,1},{4,6},{5,7},{6,4},{7,5},{8,10},{9,11},{10,... | collective-permute-start | bytes 884744 | tf_op jit(solution)/shard_map/ppermute | solution.py:320
  87.6 14.7 %collective-permute-start.11 = (f32[192,128]{1,0:T(8,128)S(1)}, f32[192,128]{1,0:T(8,128)S(1)}, u32[]{:S(2)}, u32[]{:S(2)}) collective-permute-start(f32[192,128]{1,0:T(8,128)S(1)} %get-tuple-element.132), channel_id=1, source_target_pairs={{0,16},{4,20},{8,24},{12,28},{16,0},{20,4},{24,8},{28,12},{1,17},{... | collective-permute-start | bytes 294920 | tf_op jit(solution)/shard_map/ppermute | solution.py:320
  89.8 15.8 %collective-permute-start.12 = (f32[192,128]{1,0:T(8,128)S(1)}, f32[192,128]{1,0:T(8,128)S(1)}, u32[]{:S(2)}, u32[]{:S(2)}) collective-permute-start(f32[192,128]{1,0:T(8,128)S(1)} %get-tuple-element.133), channel_id=1, source_target_pairs={{0,20},{4,16},{8,28},{12,24},{16,4},{20,0},{24,12},{28,8},{1,21},{... | collective-permute-start | bytes 294920 | tf_op jit(solution)/shard_map/ppermute | solution.py:320
  91.7 13.8 %collective-permute-start.13 = (f32[192,128]{1,0:T(8,128)S(1)}, f32[192,128]{1,0:T(8,128)S(1)}, u32[]{:S(2)}, u32[]{:S(2)}) collective-permute-start(f32[192,128]{1,0:T(8,128)S(1)} %get-tuple-element.134), channel_id=1, source_target_pairs={{0,24},{4,28},{8,16},{12,20},{16,8},{20,12},{24,0},{28,4},{1,25},{... | collective-permute-start | bytes 294920 | tf_op jit(solution)/shard_map/ppermute | solution.py:320
  93.2 12.4 %collective-permute-start.14 = (f32[192,128]{1,0:T(8,128)S(1)}, f32[192,128]{1,0:T(8,128)S(1)}, u32[]{:S(2)}, u32[]{:S(2)}) collective-permute-start(f32[192,128]{1,0:T(8,128)S(1)} %get-tuple-element.135), channel_id=1, source_target_pairs={{0,28},{4,24},{8,20},{12,16},{16,12},{20,8},{24,4},{28,0},{1,29},{... | collective-permute-start | bytes 294920 | tf_op jit(solution)/shard_map/ppermute | solution.py:320
  95.3 10.3 %collective-permute-start.8 = (f32[192,128]{1,0:T(8,128)S(1)}, f32[192,128]{1,0:T(8,128)S(1)}, u32[]{:S(2)}, u32[]{:S(2)}) collective-permute-start(f32[192,128]{1,0:T(8,128)S(1)} %get-tuple-element.129), channel_id=1, source_target_pairs={{0,4},{4,0},{8,12},{12,8},{16,20},{20,16},{24,28},{28,24},{1,5},{5... | collective-permute-start | bytes 294920 | tf_op jit(solution)/shard_map/ppermute | solution.py:320
  110.1 8.7 %collective-permute-start.17 = (f32[192,128]{1,0:T(8,128)S(1)}, f32[192,128]{1,0:T(8,128)S(1)}, u32[]{:S(2)}, u32[]{:S(2)}) collective-permute-start(f32[192,128]{1,0:T(8,128)S(1)} %right_sum.2.refs_0_), channel_id=1, source_target_pairs={{0,12},{4,8},{8,4},{12,0},{16,28},{20,24},{24,20},{28,16},{1,13},{... | collective-permute-start | bytes 294920 | tf_op jit(solution)/shard_map/ppermute | solution.py:320
  111.2 14.5 %collective-permute-start.18 = (f32[192,128]{1,0:T(8,128)S(1)}, f32[192,128]{1,0:T(8,128)S(1)}, u32[]{:S(2)}, u32[]{:S(2)}) collective-permute-start(f32[192,128]{1,0:T(8,128)S(1)} %right_sum.2.refs_0_), channel_id=1, source_target_pairs={{0,16},{4,20},{8,24},{12,28},{16,0},{20,4},{24,8},{28,12},{1,17},{... | collective-permute-start | bytes 294920 | tf_op jit(solution)/shard_map/ppermute | solution.py:320
  113.3 15.1 %collective-permute-start.19 = (f32[192,128]{1,0:T(8,128)S(1)}, f32[192,128]{1,0:T(8,128)S(1)}, u32[]{:S(2)}, u32[]{:S(2)}) collective-permute-start(f32[192,128]{1,0:T(8,128)S(1)} %right_sum.2.refs_0_), channel_id=1, source_target_pairs={{0,20},{4,16},{8,28},{12,24},{16,4},{20,0},{24,12},{28,8},{1,21},{... | collective-permute-start | bytes 294920 | tf_op jit(solution)/shard_map/ppermute | solution.py:320
  114.6 13.7 %collective-permute-start.20 = (f32[192,128]{1,0:T(8,128)S(1)}, f32[192,128]{1,0:T(8,128)S(1)}, u32[]{:S(2)}, u32[]{:S(2)}) collective-permute-start(f32[192,128]{1,0:T(8,128)S(1)} %right_sum.2.refs_0_), channel_id=1, source_target_pairs={{0,24},{4,28},{8,16},{12,20},{16,8},{20,12},{24,0},{28,4},{1,25},{... | collective-permute-start | bytes 294920 | tf_op jit(solution)/shard_map/ppermute | solution.py:320
  115.8 12.6 %collective-permute-start.21 = (f32[192,128]{1,0:T(8,128)S(1)}, f32[192,128]{1,0:T(8,128)S(1)}, u32[]{:S(2)}, u32[]{:S(2)}) collective-permute-start(f32[192,128]{1,0:T(8,128)S(1)} %right_sum.2.refs_0_), channel_id=1, source_target_pairs={{0,28},{4,24},{8,20},{12,16},{16,12},{20,8},{24,4},{28,0},{1,29},{... | collective-permute-start | bytes 294920 | tf_op jit(solution)/shard_map/ppermute | solution.py:320
  133.4 9.5 %collective-permute-start.22 = (f32[96,768]{1,0:T(8,128)}, f32[96,768]{1,0:T(8,128)S(1)}, u32[]{:S(2)}, u32[]{:S(2)}) collective-permute-start(f32[96,768]{1,0:T(8,128)} %get-tuple-element.137), channel_id=1, source_target_pairs={{0,3},{1,2},{2,1},{3,0},{4,7},{5,6},{6,5},{7,4},{8,11},{9,10},{10,... | collective-permute-start | bytes 884744 | tf_op jit(solution)/shard_map/ppermute | solution.py:320
  133.4 14.1 %collective-permute-start.23 = (f32[96,768]{1,0:T(8,128)}, f32[96,768]{1,0:T(8,128)S(1)}, u32[]{:S(2)}, u32[]{:S(2)}) collective-permute-start(f32[96,768]{1,0:T(8,128)} %get-tuple-element.138), channel_id=1, source_target_pairs={{0,2},{1,3},{2,0},{3,1},{4,6},{5,7},{6,4},{7,5},{8,10},{9,11},{10,... | collective-permute-start | bytes 884744 | tf_op jit(solution)/shard_map/ppermute | solution.py:320
  150.3 16.2 %all-to-all-start.2 = ((f32[8,72,128]{2,1,0:T(8,128)}), f32[8,72,128]{2,1,0:T(8,128)S(1)}, u32[]{:S(2)}, u32[]{:S(2)}) async-start(f32[8,72,128]{2,1,0:T(8,128)} %bitcast.4), calls=%async_computation.2 | async-start | bytes 589824 | tf_op jit(solution)/shard_map/all_to_all | solution.py:406
  156.2 15.5 %collective-permute-start.25 = (f32[288,512]{1,0:T(8,128)}, f32[288,512]{1,0:T(8,128)}, u32[]{:S(2)}, u32[]{:S(2)}) collective-permute-start(f32[288,512]{1,0:T(8,128)} %multiply_subtract_fusion), channel_id=1, source_target_pairs={{0,3},{1,2},{2,1},{3,0},{4,7},{5,6},{6,5},{7,4},{8,11},{9,10},{10,... | collective-permute-start | bytes 1769480 | tf_op jit(solution)/shard_map/ppermute | solution.py:320
  167.2 13.6 %all-to-all-start.3 = ((f32[8,72,128]{2,1,0:T(8,128)}), f32[8,72,128]{2,1,0:T(8,128)S(1)}, u32[]{:S(2)}, u32[]{:S(2)}) async-start(f32[8,72,128]{2,1,0:T(8,128)} %left_sum.3), calls=%async_computation.3 | async-start | bytes 589824 | tf_op jit(solution)/shard_map/all_to_all | solution.py:408
  182.8 9.4 %collective-permute-start.27 = (f32[96,768]{1,0:T(8,128)S(1)}, f32[96,768]{1,0:T(8,128)S(1)}, u32[]{:S(2)}, u32[]{:S(2)}) collective-permute-start(f32[96,768]{1,0:T(8,128)S(1)} %basis.3.first_ref), channel_id=1, source_target_pairs={{0,2},{1,3},{2,0},{3,1},{4,6},{5,7},{6,4},{7,5},{8,10},{9,11},{10,... | collective-permute-start | bytes 884744 | tf_op jit(solution)/shard_map/ppermute | solution.py:320
  200.6 9.7 %collective-permute-start.31 = (f32[192,128]{1,0:T(8,128)S(1)}, f32[192,128]{1,0:T(8,128)S(1)}, u32[]{:S(2)}, u32[]{:S(2)}) collective-permute-start(f32[192,128]{1,0:T(8,128)S(1)} %get-tuple-element.151), channel_id=1, source_target_pairs={{0,12},{4,8},{8,4},{12,0},{16,28},{20,24},{24,20},{28,16},{1,13},{... | collective-permute-start | bytes 294920 | tf_op jit(solution)/shard_map/ppermute | solution.py:320
  202.6 14.6 %collective-permute-start.32 = (f32[192,128]{1,0:T(8,128)S(1)}, f32[192,128]{1,0:T(8,128)S(1)}, u32[]{:S(2)}, u32[]{:S(2)}) collective-permute-start(f32[192,128]{1,0:T(8,128)S(1)} %get-tuple-element.152), channel_id=1, source_target_pairs={{0,16},{4,20},{8,24},{12,28},{16,0},{20,4},{24,8},{28,12},{1,17},{... | collective-permute-start | bytes 294920 | tf_op jit(solution)/shard_map/ppermute | solution.py:320
  203.7 16.5 %collective-permute-start.33 = (f32[192,128]{1,0:T(8,128)S(1)}, f32[192,128]{1,0:T(8,128)S(1)}, u32[]{:S(2)}, u32[]{:S(2)}) collective-permute-start(f32[192,128]{1,0:T(8,128)S(1)} %get-tuple-element.153), channel_id=1, source_target_pairs={{0,20},{4,16},{8,28},{12,24},{16,4},{20,0},{24,12},{28,8},{1,21},{... | collective-permute-start | bytes 294920 | tf_op jit(solution)/shard_map/ppermute | solution.py:320
  206.5 13.7 %collective-permute-start.34 = (f32[192,128]{1,0:T(8,128)S(1)}, f32[192,128]{1,0:T(8,128)S(1)}, u32[]{:S(2)}, u32[]{:S(2)}) collective-permute-start(f32[192,128]{1,0:T(8,128)S(1)} %get-tuple-element.154), channel_id=1, source_target_pairs={{0,24},{4,28},{8,16},{12,20},{16,8},{20,12},{24,0},{28,4},{1,25},{... | collective-permute-start | bytes 294920 | tf_op jit(solution)/shard_map/ppermute | solution.py:320
  207.9 12.3 %collective-permute-start.35 = (f32[192,128]{1,0:T(8,128)S(1)}, f32[192,128]{1,0:T(8,128)S(1)}, u32[]{:S(2)}, u32[]{:S(2)}) collective-permute-start(f32[192,128]{1,0:T(8,128)S(1)} %get-tuple-element.155), channel_id=1, source_target_pairs={{0,28},{4,24},{8,20},{12,16},{16,12},{20,8},{24,4},{28,0},{1,29},{... | collective-permute-start | bytes 294920 | tf_op jit(solution)/shard_map/ppermute | solution.py:320
  220.9 9.3 %collective-permute-start.37 = (f32[192,128]{1,0:T(8,128)S(1)}, f32[192,128]{1,0:T(8,128)S(1)}, u32[]{:S(2)}, u32[]{:S(2)}) collective-permute-start(f32[192,128]{1,0:T(8,128)S(1)} %right_sum.3.refs_0_), channel_id=1, source_target_pairs={{0,8},{4,12},{8,0},{12,4},{16,24},{20,28},{24,16},{28,20},{1,9},{5... | collective-permute-start | bytes 294920 | tf_op jit(solution)/shard_map/ppermute | solution.py:320
  225.3 14.2 %collective-permute-start.39 = (f32[192,128]{1,0:T(8,128)S(1)}, f32[192,128]{1,0:T(8,128)S(1)}, u32[]{:S(2)}, u32[]{:S(2)}) collective-permute-start(f32[192,128]{1,0:T(8,128)S(1)} %right_sum.3.refs_0_), channel_id=1, source_target_pairs={{0,16},{4,20},{8,24},{12,28},{16,0},{20,4},{24,8},{28,12},{1,17},{... | collective-permute-start | bytes 294920 | tf_op jit(solution)/shard_map/ppermute | solution.py:320
  227.9 13.8 %collective-permute-start.40 = (f32[192,128]{1,0:T(8,128)S(1)}, f32[192,128]{1,0:T(8,128)S(1)}, u32[]{:S(2)}, u32[]{:S(2)}) collective-permute-start(f32[192,128]{1,0:T(8,128)S(1)} %right_sum.3.refs_0_), channel_id=1, source_target_pairs={{0,20},{4,16},{8,28},{12,24},{16,4},{20,0},{24,12},{28,8},{1,21},{... | collective-permute-start | bytes 294920 | tf_op jit(solution)/shard_map/ppermute | solution.py:320
  228.2 13.4 %collective-permute-start.41 = (f32[192,128]{1,0:T(8,128)S(1)}, f32[192,128]{1,0:T(8,128)S(1)}, u32[]{:S(2)}, u32[]{:S(2)}) collective-permute-start(f32[192,128]{1,0:T(8,128)S(1)} %right_sum.3.refs_0_), channel_id=1, source_target_pairs={{0,24},{4,28},{8,16},{12,20},{16,8},{20,12},{24,0},{28,4},{1,25},{... | collective-permute-start | bytes 294920 | tf_op jit(solution)/shard_map/ppermute | solution.py:320
  230.3 11.4 %collective-permute-start.42 = (f32[192,128]{1,0:T(8,128)S(1)}, f32[192,128]{1,0:T(8,128)S(1)}, u32[]{:S(2)}, u32[]{:S(2)}) collective-permute-start(f32[192,128]{1,0:T(8,128)S(1)} %right_sum.3.refs_0_), channel_id=1, source_target_pairs={{0,28},{4,24},{8,20},{12,16},{16,12},{20,8},{24,4},{28,0},{1,29},{... | collective-permute-start | bytes 294920 | tf_op jit(solution)/shard_map/ppermute | solution.py:320
  245.3 24.9 %collective-permute-start.46 = (bf16[576,512]{1,0:T(8,128)(2,1)}, bf16[576,512]{1,0:T(8,128)(2,1)}, u32[]{:S(2)}, u32[]{:S(2)}) collective-permute-start(bf16[576,512]{1,0:T(8,128)(2,1)} %get-tuple-element.161.refs_0_), channel_id=1, source_target_pairs={{0,8},{4,12},{8,16},{12,20},{16,24},{20,28},{24,0},{28,4},{1,9},{5... | collective-permute-start | bytes 1769480 | tf_op jit(solution)/shard_map/ppermute | solution.py:562
  249.2 21.0 %collective-permute-start.47 = (bf16[576,512]{1,0:T(8,128)(2,1)}, bf16[576,512]{1,0:T(8,128)(2,1)}, u32[]{:S(2)}, u32[]{:S(2)}) collective-permute-start(bf16[576,512]{1,0:T(8,128)(2,1)} %get-tuple-element.161.refs_0_), channel_id=1, source_target_pairs={{0,4},{4,0},{8,12},{12,8},{16,20},{20,16},{24,28},{28,24},{1,5},{5... | collective-permute-start | bytes 1769480 | tf_op jit(solution)/shard_map/ppermute | solution.py:320
  250.2 25.8 %collective-permute-start.48 = (bf16[576,512]{1,0:T(8,128)(2,1)}, bf16[576,512]{1,0:T(8,128)(2,1)}, u32[]{:S(2)}, u32[]{:S(2)}) collective-permute-start(bf16[576,512]{1,0:T(8,128)(2,1)} %get-tuple-element.168.refs_1_), channel_id=1, source_target_pairs={{0,8},{4,12},{8,16},{12,20},{16,24},{20,28},{24,0},{28,4},{1,9},{5... | collective-permute-start | bytes 1769480 | tf_op jit(solution)/shard_map/ppermute | solution.py:562
  251.1 27.3 %collective-permute-start.49 = (bf16[576,512]{1,0:T(8,128)(2,1)}, bf16[576,512]{1,0:T(8,128)(2,1)}, u32[]{:S(2)}, u32[]{:S(2)}) collective-permute-start(bf16[576,512]{1,0:T(8,128)(2,1)} %get-tuple-element.168.refs_1_), channel_id=1, source_target_pairs={{0,4},{4,0},{8,12},{12,8},{16,20},{20,16},{24,28},{28,24},{1,5},{5... | collective-permute-start | bytes 1769480 | tf_op jit(solution)/shard_map/ppermute | solution.py:320
  260.0 10.2 %collective-permute-start.45 = (f32[64,512]{1,0:T(8,128)S(1)}, f32[64,512]{1,0:T(8,128)S(1)}, u32[]{:S(2)}, u32[]{:S(2)}) collective-permute-start(f32[64,512]{1,0:T(8,128)S(1)} %constant_dynamic-slice_fusion), channel_id=1, source_target_pairs={{0,3},{1,2},{2,1},{3,0},{4,7},{5,6},{6,5},{7,4},{8,11},{9,10},{10,... | collective-permute-start | bytes 393224 | tf_op jit(solution)/shard_map/ppermute | solution.py:320
  270.2 18.4 %collective-permute-start.50 = (bf16[576,512]{1,0:T(8,128)(2,1)}, bf16[576,512]{1,0:T(8,128)(2,1)S(1)}, u32[]{:S(2)}, u32[]{:S(2)}) collective-permute-start(bf16[576,512]{1,0:T(8,128)(2,1)} %collective-permute-done.46.refs_2_), channel_id=1, source_target_pairs={{0,8},{4,12},{8,16},{12,20},{16,24},{20,28},{24,0},{28,4},{1,9},{5... | collective-permute-start | bytes 1769480 | tf_op jit(solution)/shard_map/ppermute | solution.py:562
  270.3 20.6 %collective-permute-start.51 = (bf16[576,512]{1,0:T(8,128)(2,1)}, bf16[576,512]{1,0:T(8,128)(2,1)S(1)}, u32[]{:S(2)}, u32[]{:S(2)}) collective-permute-start(bf16[576,512]{1,0:T(8,128)(2,1)} %collective-permute-done.46.refs_2_), channel_id=1, source_target_pairs={{0,4},{4,0},{8,12},{12,8},{16,20},{20,16},{24,28},{28,24},{1,5},{5... | collective-permute-start | bytes 1769480 | tf_op jit(solution)/shard_map/ppermute | solution.py:320
  278.4 22.9 %collective-permute-start.52 = (bf16[576,512]{1,0:T(8,128)(2,1)}, bf16[576,512]{1,0:T(8,128)(2,1)S(1)}, u32[]{:S(2)}, u32[]{:S(2)}) collective-permute-start(bf16[576,512]{1,0:T(8,128)(2,1)} %collective-permute-done.48.refs_4_), channel_id=1, source_target_pairs={{0,8},{4,12},{8,16},{12,20},{16,24},{20,28},{24,0},{28,4},{1,9},{5... | collective-permute-start | bytes 1769480 | tf_op jit(solution)/shard_map/ppermute | solution.py:562
  279.0 24.6 %collective-permute-start.53 = (bf16[576,512]{1,0:T(8,128)(2,1)}, bf16[576,512]{1,0:T(8,128)(2,1)S(1)}, u32[]{:S(2)}, u32[]{:S(2)}) collective-permute-start(bf16[576,512]{1,0:T(8,128)(2,1)} %collective-permute-done.48.refs_4_), channel_id=1, source_target_pairs={{0,4},{4,0},{8,12},{12,8},{16,20},{20,16},{24,28},{28,24},{1,5},{5... | collective-permute-start | bytes 1769480 | tf_op jit(solution)/shard_map/ppermute | solution.py:320
  290.9 26.8 %collective-permute-start.54 = (bf16[576,512]{1,0:T(8,128)(2,1)S(1)}, bf16[576,512]{1,0:T(8,128)(2,1)S(1)}, u32[]{:S(2)}, u32[]{:S(2)}) collective-permute-start(bf16[576,512]{1,0:T(8,128)(2,1)S(1)} %collective-permute-done.50.refs_6_), channel_id=1, source_target_pairs={{0,8},{4,12},{8,16},{12,20},{16,24},{20,28},{24,0},{28,4},{1,9},{5... | collective-permute-start | bytes 1769480 | tf_op jit(solution)/shard_map/ppermute | solution.py:562
  291.5 26.2 %collective-permute-start.55 = (bf16[576,512]{1,0:T(8,128)(2,1)S(1)}, bf16[576,512]{1,0:T(8,128)(2,1)S(1)}, u32[]{:S(2)}, u32[]{:S(2)}) collective-permute-start(bf16[576,512]{1,0:T(8,128)(2,1)S(1)} %collective-permute-done.50.refs_6_), channel_id=1, source_target_pairs={{0,4},{4,0},{8,12},{12,8},{16,20},{20,16},{24,28},{28,24},{1,5},{5... | collective-permute-start | bytes 1769480 | tf_op jit(solution)/shard_map/ppermute | solution.py:320
  303.6 22.7 %collective-permute-start.56 = (bf16[576,512]{1,0:T(8,128)(2,1)S(1)}, bf16[576,512]{1,0:T(8,128)(2,1)S(1)}, u32[]{:S(2)}, u32[]{:S(2)}) collective-permute-start(bf16[576,512]{1,0:T(8,128)(2,1)S(1)} %collective-permute-done.52.refs_8_), channel_id=1, source_target_pairs={{0,8},{4,12},{8,16},{12,20},{16,24},{20,28},{24,0},{28,4},{1,9},{5... | collective-permute-start | bytes 1769480 | tf_op jit(solution)/shard_map/ppermute | solution.py:562
  304.1 22.7 %collective-permute-start.57 = (bf16[576,512]{1,0:T(8,128)(2,1)S(1)}, bf16[576,512]{1,0:T(8,128)(2,1)S(1)}, u32[]{:S(2)}, u32[]{:S(2)}) collective-permute-start(bf16[576,512]{1,0:T(8,128)(2,1)S(1)} %collective-permute-done.52.refs_8_), channel_id=1, source_target_pairs={{0,4},{4,0},{8,12},{12,8},{16,20},{20,16},{24,28},{28,24},{1,5},{5... | collective-permute-start | bytes 1769480 | tf_op jit(solution)/shard_map/ppermute | solution.py:320
  326.9 16.6 %collective-permute-start.59 = (bf16[576,512]{1,0:T(8,128)(2,1)S(1)}, bf16[576,512]{1,0:T(8,128)(2,1)S(1)}, u32[]{:S(2)}, u32[]{:S(2)}) collective-permute-start(bf16[576,512]{1,0:T(8,128)(2,1)S(1)} %collective-permute-done.57.refs_1_), channel_id=1, source_target_pairs={{0,8},{4,12},{8,16},{12,20},{16,24},{20,28},{24,0},{28,4},{1,9},{5... | collective-permute-start | bytes 1769480 | tf_op jit(solution)/shard_map/ppermute | solution.py:567
  327.2 16.3 %collective-permute-start.58 = (bf16[576,512]{1,0:T(8,128)(2,1)S(1)}, bf16[576,512]{1,0:T(8,128)(2,1)S(1)}, u32[]{:S(2)}, u32[]{:S(2)}) collective-permute-start(bf16[576,512]{1,0:T(8,128)(2,1)S(1)} %collective-permute-done.54.refs_0_), channel_id=1, source_target_pairs={{0,4},{4,0},{8,12},{12,8},{16,20},{20,16},{24,28},{28,24},{1,5},{5... | collective-permute-start | bytes 1769480 | tf_op jit(solution)/shard_map/ppermute | solution.py:320
  (44 other events, 359.6 us)

commit v9 on v7

--- a/solution.py
+++ b/solution.py
@@ -357,6 +357,12 @@
 
     def whole_spec(*dims):
         return pl.BlockSpec(dims, lambda k, at: (0,) * len(dims))
+
+    pieces = []
+    for offset in range(tps):
+        column = (tp ^ offset) * cols
+        piece = lax.dynamic_slice_in_dim(master, column, cols, 1)
+        pieces.append(piece - (LEARNING_RATE * MOMENTUM_DECAY) * lax.dynamic_slice_in_dim(momentum, column, cols, 1))
 
     terms, lefts = [None] * halves, [None] * tps
     for half in reversed(range(halves)):
@@ -387,25 +393,18 @@
         lefts[2 * half : 2 * half + 2] = out
         ids, _ = lax.optimization_barrier((ids, out[0]))
 
-    base = []
     for power_pass in range(ROUNDS):
         met = [lefts[0]] + [swap(lefts[offset], "tp", tps, offset) for offset in reversed(range(1, tps))]
         parts = whole_call(
             functools.partial(split_kernel, tps), "left_split", shape(left_part * replicas, LANES), met
         )
-        parts, new_values, old_values = lax.optimization_barrier((parts, master, momentum))
-        some = []
-        for offset in range(3 * power_pass, 3 + power_pass):
-            column = (tp ^ offset) * cols
-            piece = lax.dynamic_slice_in_dim(new_values, column, cols, 1)
-            piece = piece - (LEARNING_RATE * MOMENTUM_DECAY) * lax.dynamic_slice_in_dim(old_values, column, cols, 1)
-            some.append(piece if offset == 0 else swap(piece, "tp", tps, offset))
+        if power_pass == 0:
+            parts, pieces = lax.optimization_barrier((parts, pieces))
+            base = [pieces[0]]
         parts = parts.reshape(replicas, left_part, LANES)
         parts = lax.all_to_all(parts, "rep", split_axis=0, concat_axis=0, tiled=True)
         parts = whole_call(total_kernel, "left_sum", shape(*parts.shape), [parts])
         parts = lax.all_to_all(parts, "rep", split_axis=0, concat_axis=0, tiled=True)
-        parts, some = lax.optimization_barrier((parts, some))
-        base += some
         basis = whole_call(
             functools.partial(basis_kernel, rank), "basis", shape(tp_rows, width), [parts.reshape(-1, LANES)]
         )
@@ -439,6 +438,9 @@
             moved=4 * elements,
         )
         met = scattered(parts, replicas)
+        arrived = [swap(pieces[offset], "tp", tps, offset) for offset in ((1, 2) if power_pass == 0 else range(3, tps))]
+        met, pieces, arrived = lax.optimization_barrier((met, pieces, arrived))
+        base += arrived
         part = whole_call(functools.partial(sum_kernel, 1.0 / replicas), "right_sum", shape(right_part, LANES), met)
         rights = spread(part, "rep", replicas)
         if power_pass < ROUNDS - 1:

time: 338 us -> 337 us (level)
  blocking collectives: 0 us -> 59.9 us
  waiting for transfers between devices: 138 us -> 110 us
  starting transfers between devices: 86.3 us -> 69.5 us
  local copies, waits for them, and re-layouts: 28.7 us -> 16.6 us
    all_to_all x0 -> x4, blocking collectives: none -> 59.9 us  [local(): lax.all_to_all(parts, 'rep', split_axis=0, concat_axis=0, tiled=True)]
    all_to_all x4 -> x0, waiting for transfers between devices: 26 us -> none  [local(): lax.all_to_all(parts, 'rep', split_axis=0, concat_axis=0, tiled=True)]
    all_to_all x4 -> x0, starting transfers between devices: 18.9 us -> none  [local(): lax.all_to_all(parts, 'rep', split_axis=0, concat_axis=0, tiled=True)]
    unnamed x56 -> x42, local copies, waits for them, and re-layouts: 27.8 us -> 15.7 us
  transfers between devices with their start and end apart: 64 -> 60, of which waited for: 35 -> 28; matrix products, arithmetic and copies ran while one was open for 2% -> 1% of each run, Pallas kernels for 15% -> 17%
where the time goes in v9:
time: 337 us
  waiting for transfers between devices  110 us (33%)
  Pallas kernels  76.9 us (23%)
  starting transfers between devices  69.5 us (21%)
  blocking collectives  59.9 us (18%)
  local copies, waits for them, and re-layouts  16.6 us (5%)
    ppermute x53, waiting for transfers between devices, swap(): lax.ppermute(x, axis, [(index, index ^ offset) for index in range(size)])  82.3 us
    pallas_call x17, Pallas kernels, grid_call(): pl.pallas_call(kernel, grid_spec=pltpu.PrefetchScalarGridSpec(num_scalar_...  68.8 us
    ppermute x53, starting transfers between devices, swap(): lax.ppermute(x, axis, [(index, index ^ offset) for index in range(size)])  61.6 us
    all_to_all x4, blocking collectives, local(): lax.all_to_all(parts, 'rep', split_axis=0, concat_axis=0, tiled=True)  59.9 us
    unnamed x42, local copies, waits for them, and re-layouts  15.7 us
    ppermute x6, waiting for transfers between devices, local(): held[half] = lax.ppermute(here, 'rep', ring)  14.8 us
    ppermute x1, waiting for transfers between devices, local(): beside[half] = lax.ppermute(beside[half], 'rep', ring)  13.2 us
    pallas_call x9, Pallas kernels, whole_call(): pl.pallas_call(kernel, in_specs=specs, out_specs=[out_spec] * len(out_sha...  8.17 us
  transfers between devices with their start and end apart: 60, of which 28 were waited for; matrix products, arithmetic and copies ran while one was open for 1% of the time, Pallas kernels for 17%

profile of v9, /device:TPU:0, one launch (start us, length us, event | category | flops | bytes accessed | tf_op | source)
XLA Modules:
  0.0 336.9 jit_solution(16056984875376024999)
XLA Ops:
  1.8 7.2 %first_left.2 = (bf16[6,768,512]{2,1,0:T(8,128)(2,1)S(1)}, bf16[6,768,512]{2,1,0:T(8,128)(2,1)S(1)}, f32[96,768]{1,0:T(8,128)}, f32[96,768]{1,0:T(8,128)}) custom-call(s32[2]{0:T(128)S(1)} %pad_add_fusion.ids_ref, bf16[1,12,768,512]{3,2,1,0:T(8,128)(2,1)} %grads_ref.3, f32[1,12,768,512]{3,2,1,0:T(8,128)} %error_ref.3, f32[12,32,512]{2,1,0:T(8,128)S(1)} %copy-done.11), custom_call_target="tpu_custom_call" | custom-call | flops 452984832 | bytes 23592960 | tf_op jit(solution)/shard_map/first_left/pallas_call | solution.py:302
  13.5 2.9 collective-permute-start.1
  16.4 7.1 %first_left.3 = (bf16[6,768,512]{2,1,0:T(8,128)(2,1)S(1)}, bf16[6,768,512]{2,1,0:T(8,128)(2,1)S(1)}, f32[96,768]{1,0:T(8,128)S(1)}, f32[96,768]{1,0:T(8,128)}) custom-call(s32[2]{0:T(128)S(1)} %pad_add_fusion.ids_ref, bf16[1,12,768,512]{3,2,1,0:T(8,128)(2,1)} %grads_ref.3, f32[1,12,768,512]{3,2,1,0:T(8,128)} %error_ref.3, f32[12,32,512]{2,1,0:T(8,128)S(1)} %copy-done.12), custom_call_target="tpu_custom_call" | custom-call | flops 452984832 | bytes 23592960 | tf_op jit(solution)/shard_map/first_left/pallas_call | solution.py:302
  28.1 2.4 multiply_subtract_fusion
  30.5 6.4 %collective-permute-done.refs_1_ = f32[96,768]{1,0:T(8,128)} collective-permute-done((f32[96,768]{1,0:T(8,128)}, f32[96,768]{1,0:T(8,128)}, u32[]{:S(2)}, u32[]{:S(2)}) %collective-permute-start) | collective-permute-done | bytes 294944 | tf_op jit(solution)/shard_map/ppermute | solution.py:320
  38.0 16.6 %all_to_all.20.parts_ref = f32[8,72,128]{2,1,0:T(8,128)S(1)} all-to-all(f32[8,72,128]{2,1,0:T(8,128)S(1)} %bitcast.23), channel_id=1, replica_groups=mesh['rep'=8,'tp'=4] {'rep'}, dimensions={0} | all-to-all | bytes 589824 | tf_op jit(solution)/shard_map/all_to_all | solution.py:405
  54.7 13.0 %all_to_all.21 = f32[8,72,128]{2,1,0:T(8,128)S(1)} all-to-all(f32[8,72,128]{2,1,0:T(8,128)S(1)} %left_sum.2), channel_id=1, replica_groups=mesh['rep'=8,'tp'=4] {'rep'}, dimensions={0} | all-to-all | bytes 589824 | tf_op jit(solution)/shard_map/all_to_all | solution.py:407
  72.0 2.8 right_near.2.refs_0_
  74.8 4.8 %collective-permute-done.4.first_ref = f32[96,768]{1,0:T(8,128)S(1)} collective-permute-done((f32[96,768]{1,0:T(8,128)S(1)}, f32[96,768]{1,0:T(8,128)S(1)}, u32[]{:S(2)}, u32[]{:S(2)}) %collective-permute-start.4) | collective-permute-done | bytes 294944 | tf_op jit(solution)/shard_map/ppermute | solution.py:320
  81.2 2.9 right_far.2
  84.8 2.4 collective-permute-start.11
  87.1 2.4 collective-permute-start.12
  92.4 4.9 %collective-permute-done.10.refs_5_ = f32[192,128]{1,0:T(8,128)S(1)} collective-permute-done((f32[192,128]{1,0:T(8,128)S(1)}, f32[192,128]{1,0:T(8,128)S(1)}, u32[]{:S(2)}, u32[]{:S(2)}) %collective-permute-start.10) | collective-permute-done | bytes 98336 | tf_op jit(solution)/shard_map/ppermute | solution.py:320
  99.4 4.4 %collective-permute-done.8.refs_3_ = f32[192,128]{1,0:T(8,128)S(1)} collective-permute-done((f32[192,128]{1,0:T(8,128)S(1)}, f32[192,128]{1,0:T(8,128)S(1)}, u32[]{:S(2)}, u32[]{:S(2)}) %collective-permute-start.8) | collective-permute-done | bytes 98336 | tf_op jit(solution)/shard_map/ppermute | solution.py:320
  109.1 3.6 %collective-permute-start.19 = (f32[192,128]{1,0:T(8,128)S(1)}, f32[192,128]{1,0:T(8,128)S(1)}, u32[]{:S(2)}, u32[]{:S(2)}) collective-permute-start(f32[192,128]{1,0:T(8,128)S(1)} %right_sum.2.refs_0_), channel_id=1, source_target_pairs={{0,20},{4,16},{8,28},{12,24},{16,4},{20,0},{24,12},{28,8},{1,21},{... | collective-permute-start | bytes 294920 | tf_op jit(solution)/shard_map/ppermute | solution.py:320
  116.2 6.2 %collective-permute-done.18.refs_4_ = f32[192,128]{1,0:T(8,128)S(1)} collective-permute-done((f32[192,128]{1,0:T(8,128)S(1)}, f32[192,128]{1,0:T(8,128)S(1)}, u32[]{:S(2)}, u32[]{:S(2)}) %collective-permute-start.18) | collective-permute-done | bytes 98336 | tf_op jit(solution)/shard_map/ppermute | solution.py:320
  122.5 3.0 collective-permute-done.19.refs_5_
  125.5 4.2 %left.3 = (f32[96,768]{1,0:T(8,128)S(1)}, f32[96,768]{1,0:T(8,128)S(1)}) custom-call(s32[2]{0:T(128)S(1)} %pad_add_fusion.ids_ref, bf16[6,768,512]{2,1,0:T(8,128)(2,1)S(1)} %bitcast.13, bf16[6,768,512]{2,1,0:T(8,128)(2,1)S(1)} %copy-done.2, f32[192,128]{1,0:T(8,128)S(1)} %right_sum.2.refs_0_, f32[192,128]{1,0:T(8,128)S(1)} %collective-permute-done.15.refs_1_, ...), custom_call_target="tpu_custom_call" | custom-call | flops 452984832 | bytes 23592960 | tf_op jit(solution)/shard_map/left/pallas_call | solution.py:302
  130.4 4.2 %left.2 = (f32[96,768]{1,0:T(8,128)S(1)}, f32[96,768]{1,0:T(8,128)S(1)}) custom-call(s32[2]{0:T(128)S(1)} %pad_add_fusion.ids_ref, bf16[6,768,512]{2,1,0:T(8,128)(2,1)S(1)} %bitcast.19, bf16[6,768,512]{2,1,0:T(8,128)(2,1)S(1)} %copy-done.6, f32[192,128]{1,0:T(8,128)S(1)} %right_sum.2.refs_0_, f32[192,128]{1,0:T(8,128)S(1)} %collective-permute-done.15.refs_1_, ...), custom_call_target="tpu_custom_call" | custom-call | flops 452984832 | bytes 23592960 | tf_op jit(solution)/shard_map/left/pallas_call | solution.py:302
  135.9 3.2 collective-permute-done.22.refs_1_
  139.0 4.6 %collective-permute-done.23.refs_2_ = f32[96,768]{1,0:T(8,128)S(1)} collective-permute-done((f32[96,768]{1,0:T(8,128)S(1)}, f32[96,768]{1,0:T(8,128)S(1)}, u32[]{:S(2)}, u32[]{:S(2)}) %collective-permute-start.23) | collective-permute-done | bytes 294944 | tf_op jit(solution)/shard_map/ppermute | solution.py:320
  143.8 17.3 %all_to_all.22.parts_ref = f32[8,72,128]{2,1,0:T(8,128)S(1)} all-to-all(f32[8,72,128]{2,1,0:T(8,128)S(1)} %bitcast.24), channel_id=1, replica_groups=mesh['rep'=8,'tp'=4] {'rep'}, dimensions={0} | all-to-all | bytes 589824 | tf_op jit(solution)/shard_map/all_to_all | solution.py:405
  161.0 13.0 %all_to_all.23 = f32[8,72,128]{2,1,0:T(8,128)S(1)} all-to-all(f32[8,72,128]{2,1,0:T(8,128)S(1)} %left_sum.3), channel_id=1, replica_groups=mesh['rep'=8,'tp'=4] {'rep'}, dimensions={0} | all-to-all | bytes 589824 | tf_op jit(solution)/shard_map/all_to_all | solution.py:407
  177.9 2.8 right_near.3.refs_0_
  180.7 5.2 %collective-permute-done.26.first_ref = f32[96,768]{1,0:T(8,128)S(1)} collective-permute-done((f32[96,768]{1,0:T(8,128)S(1)}, f32[96,768]{1,0:T(8,128)S(1)}, u32[]{:S(2)}, u32[]{:S(2)}) %collective-permute-start.26) | collective-permute-done | bytes 294944 | tf_op jit(solution)/shard_map/ppermute | solution.py:320
  187.5 2.9 right_far.3
  194.7 3.0 collective-permute-done.35.refs_11_
  198.3 2.4 collective-permute-start.33
  200.7 2.4 collective-permute-start.34
  203.1 8.1 %collective-permute-done.32.refs_5_ = f32[192,128]{1,0:T(8,128)S(1)} collective-permute-done((f32[192,128]{1,0:T(8,128)S(1)}, f32[192,128]{1,0:T(8,128)S(1)}, u32[]{:S(2)}, u32[]{:S(2)}) %collective-permute-start.32) | collective-permute-done | bytes 98336 | tf_op jit(solution)/shard_map/ppermute | solution.py:320
  211.8 4.7 %collective-permute-start.37 = (f32[192,128]{1,0:T(8,128)S(1)}, f32[192,128]{1,0:T(8,128)S(1)}, u32[]{:S(2)}, u32[]{:S(2)}) collective-permute-start(f32[192,128]{1,0:T(8,128)S(1)} %right_sum.3.refs_0_), channel_id=1, source_target_pairs={{0,8},{4,12},{8,0},{12,4},{16,24},{20,28},{24,16},{28,20},{1,9},{5... | collective-permute-start | bytes 294920 | tf_op jit(solution)/shard_map/ppermute | solution.py:320
  221.9 2.9 collective-permute-start.42
  224.9 7.0 %collective-permute-done.39.refs_4_ = f32[192,128]{1,0:T(8,128)S(1)} collective-permute-done((f32[192,128]{1,0:T(8,128)S(1)}, f32[192,128]{1,0:T(8,128)S(1)}, u32[]{:S(2)}, u32[]{:S(2)}) %collective-permute-start.39) | collective-permute-done | bytes 98336 | tf_op jit(solution)/shard_map/ppermute | solution.py:320
  231.9 2.5 collective-permute-done.40.refs_5_
  234.4 2.9 late_rows.1
  237.3 3.8 %collective-permute-start.46 = (bf16[576,512]{1,0:T(8,128)(2,1)}, bf16[576,512]{1,0:T(8,128)(2,1)}, u32[]{:S(2)}, u32[]{:S(2)}) collective-permute-start(bf16[576,512]{1,0:T(8,128)(2,1)} %get-tuple-element.175.refs_0_), channel_id=1, source_target_pairs={{0,8},{4,12},{8,16},{12,20},{16,24},{20,28},{24,0},{28,4},{1,9},{5... | collective-permute-start | bytes 1769480 | tf_op jit(solution)/shard_map/ppermute | solution.py:562
  247.5 4.2 %collective-permute-done.44 = f32[64,512]{1,0:T(8,128)S(1)} collective-permute-done((f32[64,512]{1,0:T(8,128)S(1)}, f32[64,512]{1,0:T(8,128)S(1)}, u32[]{:S(2)}, u32[]{:S(2)}) %collective-permute-start.44) | collective-permute-done | bytes 131104 | tf_op jit(solution)/shard_map/ppermute | solution.py:320
  252.1 2.3 copy-done.4
  257.9 4.1 %update.4.refs_0_ = f32[1,12,768,512]{3,2,1,0:T(8,128)} custom-call(s32[2]{0:T(128)S(1)} %pad_add_fusion.ids_ref, f32[384,768]{1,0:T(8,128)S(1)} %pad_maximum_fusion.basis_ref, f32[384,512]{1,0:T(8,128)S(1)} %copy-done.8, bf16[6,768,512]{2,1,0:T(8,128)(2,1)S(1)} %copy-done.4, bf16[6,768,512]{2,1,0:T(8,128)(2,1)S(1)} %copy-done.7), custom_call_target="tpu_custom_call" | custom-call | flops 226492416 | bytes 9437184 | tf_op jit(solution)/shard_map/update/pallas_call | solution.py:302
  263.3 4.1 %update.5.refs_0_ = f32[1,12,768,512]{3,2,1,0:T(8,128)} custom-call(s32[2]{0:T(128)S(1)} %pad_add_fusion.ids_ref, f32[384,768]{1,0:T(8,128)S(1)} %pad_maximum_fusion.basis_ref, f32[384,512]{1,0:T(8,128)S(1)} %copy-done.8, bf16[6,768,512]{2,1,0:T(8,128)(2,1)S(1)} %copy-done.4, bf16[6,768,512]{2,1,0:T(8,128)(2,1)S(1)} %copy-done.7, ...), custom_call_target="tpu_custom_call", output_to_operand_aliasing={{}: (5, {})} | custom-call | flops 226492416 | bytes 9437184 | tf_op jit(solution)/shard_map/update/pallas_call | solution.py:302
  272.2 4.1 %update.6.refs_0_ = f32[1,12,768,512]{3,2,1,0:T(8,128)} custom-call(s32[2]{0:T(128)S(1)} %pad_add_fusion.ids_ref, f32[384,768]{1,0:T(8,128)S(1)} %pad_maximum_fusion.basis_ref, f32[384,512]{1,0:T(8,128)S(1)} %copy-done.8, bf16[6,768,512]{2,1,0:T(8,128)(2,1)S(1)} %bitcast.15, bf16[6,768,512]{2,1,0:T(8,128)(2,1)S(1)} %bitcast.17, ...), custom_call_target="tpu_custom_call", output_to_operand_aliasing={{}: (5, {})} | custom-call | flops 226492416 | bytes 9437184 | tf_op jit(solution)/shard_map/update/pallas_call | solution.py:302
  276.3 4.3 %collective-permute-done.50.refs_6_ = bf16[576,512]{1,0:T(8,128)(2,1)S(1)} collective-permute-done((bf16[576,512]{1,0:T(8,128)(2,1)}, bf16[576,512]{1,0:T(8,128)(2,1)S(1)}, u32[]{:S(2)}, u32[]{:S(2)}) %collective-permute-start.50) | collective-permute-done | bytes 589856 | tf_op jit(solution)/shard_map/ppermute | solution.py:562
  284.7 4.1 %update.7 = f32[1,12,768,512]{3,2,1,0:T(8,128)} custom-call(s32[2]{0:T(128)S(1)} %pad_add_fusion.ids_ref, f32[384,768]{1,0:T(8,128)S(1)} %pad_maximum_fusion.basis_ref, f32[384,512]{1,0:T(8,128)S(1)} %copy-done.8, bf16[6,768,512]{2,1,0:T(8,128)(2,1)S(1)} %bitcast.15, bf16[6,768,512]{2,1,0:T(8,128)(2,1)S(1)} %bitcast.17, ...), custom_call_target="tpu_custom_call", output_to_operand_aliasing={{}: (5, {})} | custom-call | flops 226492416 | bytes 9437184 | tf_op jit(solution)/shard_map/update/pallas_call | solution.py:302
  288.8 4.4 %collective-permute-done.52.refs_8_ = bf16[576,512]{1,0:T(8,128)(2,1)S(1)} collective-permute-done((bf16[576,512]{1,0:T(8,128)(2,1)}, bf16[576,512]{1,0:T(8,128)(2,1)S(1)}, u32[]{:S(2)}, u32[]{:S(2)}) %collective-permute-start.52) | collective-permute-done | bytes 589856 | tf_op jit(solution)/shard_map/ppermute | solution.py:562
  297.3 7.2 %place.4.refs_2_ = bf16[8,2,576,512]{3,2,1,0:T(8,128)(2,1)} custom-call(s32[2]{0:T(128)S(1)} %pad_add_fusion.ids_ref, bf16[576,512]{1,0:T(8,128)(2,1)} %get-tuple-element.175.refs_0_, bf16[576,512]{1,0:T(8,128)(2,1)} %get-tuple-element.182.refs_1_, bf16[576,512]{1,0:T(8,128)(2,1)} %collective-permute-done.46.refs_2_, ...), custom_call_target="tpu_custom_call" | custom-call | bytes 23592960 | tf_op jit(solution)/shard_map/place/pallas_call | solution.py:302
  304.6 6.1 %flat_rows.1 = (f32[288,2048]{1,0:T(8,128)}, f32[288,2048]{1,0:T(8,128)}) custom-call(s32[2]{0:T(128)S(1)} %pad_add_fusion.ids_ref, f32[384,768]{1,0:T(8,128)S(1)} %pad_maximum_fusion.basis_ref, f32[4,64,512]{2,1,0:T(8,128)S(1)} %pad_maximum_fusion.1.near_ref, f32[288,2048]{1,0:T(8,128)S(1)} %copy-done.9, f32[288,2048]{1,0:T(8,128)S(1)} %copy-done.10), custom_call_target="tpu_custom_call" | custom-call | flops 452984832 | bytes 9437184 | tf_op jit(solution)/shard_map/flat_rows/pallas_call | solution.py:302
  312.4 5.7 %collective-permute-done.56.refs_0_ = bf16[576,512]{1,0:T(8,128)(2,1)S(1)} collective-permute-done((bf16[576,512]{1,0:T(8,128)(2,1)S(1)}, bf16[576,512]{1,0:T(8,128)(2,1)S(1)}, u32[]{:S(2)}, u32[]{:S(2)}) %collective-permute-start.56) | collective-permute-done | bytes 589856 | tf_op jit(solution)/shard_map/ppermute | solution.py:562
  322.0 13.2 %collective-permute-done.59.refs_1_ = bf16[576,512]{1,0:T(8,128)(2,1)S(1)} collective-permute-done((bf16[576,512]{1,0:T(8,128)(2,1)S(1)}, bf16[576,512]{1,0:T(8,128)(2,1)S(1)}, u32[]{:S(2)}, u32[]{:S(2)}) %collective-permute-start.59) | collective-permute-done | bytes 589856 | tf_op jit(solution)/shard_map/ppermute | solution.py:567
  (153 shorter events, 81.9 us)
Async XLA Ops:
  13.5 17.0 %collective-permute-start.1 = (f32[96,768]{1,0:T(8,128)}, f32[96,768]{1,0:T(8,128)S(1)}, u32[]{:S(2)}, u32[]{:S(2)}) collective-permute-start(f32[96,768]{1,0:T(8,128)} %get-tuple-element.115), channel_id=1, source_target_pairs={{0,2},{1,3},{2,0},{3,1},{4,6},{5,7},{6,4},{7,5},{8,10},{9,11},{10,... | collective-permute-start | bytes 884744 | tf_op jit(solution)/shard_map/ppermute | solution.py:320
  27.9 9.0 %collective-permute-start = (f32[96,768]{1,0:T(8,128)}, f32[96,768]{1,0:T(8,128)}, u32[]{:S(2)}, u32[]{:S(2)}) collective-permute-start(f32[96,768]{1,0:T(8,128)} %get-tuple-element.121), channel_id=1, source_target_pairs={{0,3},{1,2},{2,1},{3,0},{4,7},{5,6},{6,5},{7,4},{8,11},{9,10},{10,... | collective-permute-start | bytes 884744 | tf_op jit(solution)/shard_map/ppermute | solution.py:320
  69.7 9.9 %collective-permute-start.4 = (f32[96,768]{1,0:T(8,128)S(1)}, f32[96,768]{1,0:T(8,128)S(1)}, u32[]{:S(2)}, u32[]{:S(2)}) collective-permute-start(f32[96,768]{1,0:T(8,128)S(1)} %basis.2.first_ref), channel_id=1, source_target_pairs={{0,2},{1,3},{2,0},{3,1},{4,6},{5,7},{6,4},{7,5},{8,10},{9,11},{10,... | collective-permute-start | bytes 884744 | tf_op jit(solution)/shard_map/ppermute | solution.py:320
  70.3 19.3 %collective-permute-start.13 = (f32[288,512]{1,0:T(8,128)S(1)}, f32[288,512]{1,0:T(8,128)S(1)}, u32[]{:S(2)}, u32[]{:S(2)}) collective-permute-start(f32[288,512]{1,0:T(8,128)S(1)} %get-tuple-element.137), channel_id=1, source_target_pairs={{0,1},{1,0},{2,3},{3,2},{4,5},{5,4},{6,7},{7,6},{8,9},{9,8},{10,11... | collective-permute-start | bytes 1769480 | tf_op jit(solution)/shard_map/ppermute | solution.py:320
  70.4 21.3 %collective-permute-start.14 = (f32[288,512]{1,0:T(8,128)S(1)}, f32[288,512]{1,0:T(8,128)S(1)}, u32[]{:S(2)}, u32[]{:S(2)}) collective-permute-start(f32[288,512]{1,0:T(8,128)S(1)} %get-tuple-element.138), channel_id=1, source_target_pairs={{0,2},{1,3},{2,0},{3,1},{4,6},{5,7},{6,4},{7,5},{8,10},{9,11},{10,... | collective-permute-start | bytes 1769480 | tf_op jit(solution)/shard_map/ppermute | solution.py:320
  84.1 13.2 %collective-permute-start.10 = (f32[192,128]{1,0:T(8,128)S(1)}, f32[192,128]{1,0:T(8,128)S(1)}, u32[]{:S(2)}, u32[]{:S(2)}) collective-permute-start(f32[192,128]{1,0:T(8,128)S(1)} %get-tuple-element.133), channel_id=1, source_target_pairs={{0,20},{4,16},{8,28},{12,24},{16,4},{20,0},{24,12},{28,8},{1,21},{... | collective-permute-start | bytes 294920 | tf_op jit(solution)/shard_map/ppermute | solution.py:320
  84.8 12.6 %collective-permute-start.11 = (f32[192,128]{1,0:T(8,128)S(1)}, f32[192,128]{1,0:T(8,128)S(1)}, u32[]{:S(2)}, u32[]{:S(2)}) collective-permute-start(f32[192,128]{1,0:T(8,128)S(1)} %get-tuple-element.134), channel_id=1, source_target_pairs={{0,24},{4,28},{8,16},{12,20},{16,8},{20,12},{24,0},{28,4},{1,25},{... | collective-permute-start | bytes 294920 | tf_op jit(solution)/shard_map/ppermute | solution.py:320
  87.1 12.2 %collective-permute-start.12 = (f32[192,128]{1,0:T(8,128)S(1)}, f32[192,128]{1,0:T(8,128)S(1)}, u32[]{:S(2)}, u32[]{:S(2)}) collective-permute-start(f32[192,128]{1,0:T(8,128)S(1)} %get-tuple-element.135), channel_id=1, source_target_pairs={{0,28},{4,24},{8,20},{12,16},{16,12},{20,8},{24,4},{28,0},{1,29},{... | collective-permute-start | bytes 294920 | tf_op jit(solution)/shard_map/ppermute | solution.py:320
  89.5 9.8 %collective-permute-start.6 = (f32[192,128]{1,0:T(8,128)S(1)}, f32[192,128]{1,0:T(8,128)S(1)}, u32[]{:S(2)}, u32[]{:S(2)}) collective-permute-start(f32[192,128]{1,0:T(8,128)S(1)} %get-tuple-element.129), channel_id=1, source_target_pairs={{0,4},{4,0},{8,12},{12,8},{16,20},{20,16},{24,28},{28,24},{1,5},{5... | collective-permute-start | bytes 294920 | tf_op jit(solution)/shard_map/ppermute | solution.py:320
  106.8 9.4 %collective-permute-start.17 = (f32[192,128]{1,0:T(8,128)S(1)}, f32[192,128]{1,0:T(8,128)S(1)}, u32[]{:S(2)}, u32[]{:S(2)}) collective-permute-start(f32[192,128]{1,0:T(8,128)S(1)} %right_sum.2.refs_0_), channel_id=1, source_target_pairs={{0,12},{4,8},{8,4},{12,0},{16,28},{20,24},{24,20},{28,16},{1,13},{... | collective-permute-start | bytes 294920 | tf_op jit(solution)/shard_map/ppermute | solution.py:320
  108.6 13.9 %collective-permute-start.18 = (f32[192,128]{1,0:T(8,128)S(1)}, f32[192,128]{1,0:T(8,128)S(1)}, u32[]{:S(2)}, u32[]{:S(2)}) collective-permute-start(f32[192,128]{1,0:T(8,128)S(1)} %right_sum.2.refs_0_), channel_id=1, source_target_pairs={{0,16},{4,20},{8,24},{12,28},{16,0},{20,4},{24,8},{28,12},{1,17},{... | collective-permute-start | bytes 294920 | tf_op jit(solution)/shard_map/ppermute | solution.py:320
  109.1 16.4 %collective-permute-start.19 = (f32[192,128]{1,0:T(8,128)S(1)}, f32[192,128]{1,0:T(8,128)S(1)}, u32[]{:S(2)}, u32[]{:S(2)}) collective-permute-start(f32[192,128]{1,0:T(8,128)S(1)} %right_sum.2.refs_0_), channel_id=1, source_target_pairs={{0,20},{4,16},{8,28},{12,24},{16,4},{20,0},{24,12},{28,8},{1,21},{... | collective-permute-start | bytes 294920 | tf_op jit(solution)/shard_map/ppermute | solution.py:320
  112.7 12.8 %collective-permute-start.20 = (f32[192,128]{1,0:T(8,128)S(1)}, f32[192,128]{1,0:T(8,128)S(1)}, u32[]{:S(2)}, u32[]{:S(2)}) collective-permute-start(f32[192,128]{1,0:T(8,128)S(1)} %right_sum.2.refs_0_), channel_id=1, source_target_pairs={{0,24},{4,28},{8,16},{12,20},{16,8},{20,12},{24,0},{28,4},{1,25},{... | collective-permute-start | bytes 294920 | tf_op jit(solution)/shard_map/ppermute | solution.py:320
  114.2 11.3 %collective-permute-start.21 = (f32[192,128]{1,0:T(8,128)S(1)}, f32[192,128]{1,0:T(8,128)S(1)}, u32[]{:S(2)}, u32[]{:S(2)}) collective-permute-start(f32[192,128]{1,0:T(8,128)S(1)} %right_sum.2.refs_0_), channel_id=1, source_target_pairs={{0,28},{4,24},{8,20},{12,16},{16,12},{20,8},{24,4},{28,0},{1,29},{... | collective-permute-start | bytes 294920 | tf_op jit(solution)/shard_map/ppermute | solution.py:320
  129.7 9.4 %collective-permute-start.22 = (f32[96,768]{1,0:T(8,128)S(1)}, f32[96,768]{1,0:T(8,128)S(1)}, u32[]{:S(2)}, u32[]{:S(2)}) collective-permute-start(f32[96,768]{1,0:T(8,128)S(1)} %get-tuple-element.149), channel_id=1, source_target_pairs={{0,3},{1,2},{2,1},{3,0},{4,7},{5,6},{6,5},{7,4},{8,11},{9,10},{10,... | collective-permute-start | bytes 884744 | tf_op jit(solution)/shard_map/ppermute | solution.py:320
  129.8 13.9 %collective-permute-start.23 = (f32[96,768]{1,0:T(8,128)S(1)}, f32[96,768]{1,0:T(8,128)S(1)}, u32[]{:S(2)}, u32[]{:S(2)}) collective-permute-start(f32[96,768]{1,0:T(8,128)S(1)} %get-tuple-element.150), channel_id=1, source_target_pairs={{0,2},{1,3},{2,0},{3,1},{4,6},{5,7},{6,4},{7,5},{8,10},{9,11},{10,... | collective-permute-start | bytes 884744 | tf_op jit(solution)/shard_map/ppermute | solution.py:320
  134.6 9.1 %collective-permute-start.24 = (f32[96,768]{1,0:T(8,128)S(1)}, f32[96,768]{1,0:T(8,128)S(1)}, u32[]{:S(2)}, u32[]{:S(2)}) collective-permute-start(f32[96,768]{1,0:T(8,128)S(1)} %get-tuple-element.151), channel_id=1, source_target_pairs={{0,1},{1,0},{2,3},{3,2},{4,5},{5,4},{6,7},{7,6},{8,9},{9,8},{10,11... | collective-permute-start | bytes 884744 | tf_op jit(solution)/shard_map/ppermute | solution.py:320
  176.1 9.9 %collective-permute-start.26 = (f32[96,768]{1,0:T(8,128)S(1)}, f32[96,768]{1,0:T(8,128)S(1)}, u32[]{:S(2)}, u32[]{:S(2)}) collective-permute-start(f32[96,768]{1,0:T(8,128)S(1)} %basis.3.first_ref), channel_id=1, source_target_pairs={{0,2},{1,3},{2,0},{3,1},{4,6},{5,7},{6,4},{7,5},{8,10},{9,11},{10,... | collective-permute-start | bytes 884744 | tf_op jit(solution)/shard_map/ppermute | solution.py:320
  177.5 20.2 %collective-permute-start.35 = (f32[288,512]{1,0:T(8,128)S(1)}, f32[288,512]{1,0:T(8,128)S(1)}, u32[]{:S(2)}, u32[]{:S(2)}) collective-permute-start(f32[288,512]{1,0:T(8,128)S(1)} %get-tuple-element.162), channel_id=1, source_target_pairs={{0,3},{1,2},{2,1},{3,0},{4,7},{5,6},{6,5},{7,4},{8,11},{9,10},{10,... | collective-permute-start | bytes 1769480 | tf_op jit(solution)/shard_map/ppermute | solution.py:320
  190.4 7.9 %collective-permute-start.28 = (f32[192,128]{1,0:T(8,128)S(1)}, f32[192,128]{1,0:T(8,128)S(1)}, u32[]{:S(2)}, u32[]{:S(2)}) collective-permute-start(f32[192,128]{1,0:T(8,128)S(1)} %get-tuple-element.155), channel_id=1, source_target_pairs={{0,4},{4,0},{8,12},{12,8},{16,20},{20,16},{24,28},{28,24},{1,5},{5... | collective-permute-start | bytes 294920 | tf_op jit(solution)/shard_map/ppermute | solution.py:320
  191.2 9.5 %collective-permute-start.29 = (f32[192,128]{1,0:T(8,128)S(1)}, f32[192,128]{1,0:T(8,128)S(1)}, u32[]{:S(2)}, u32[]{:S(2)}) collective-permute-start(f32[192,128]{1,0:T(8,128)S(1)} %get-tuple-element.156), channel_id=1, source_target_pairs={{0,8},{4,12},{8,0},{12,4},{16,24},{20,28},{24,16},{28,20},{1,9},{5... | collective-permute-start | bytes 294920 | tf_op jit(solution)/shard_map/ppermute | solution.py:320
  191.7 11.4 %collective-permute-start.30 = (f32[192,128]{1,0:T(8,128)S(1)}, f32[192,128]{1,0:T(8,128)S(1)}, u32[]{:S(2)}, u32[]{:S(2)}) collective-permute-start(f32[192,128]{1,0:T(8,128)S(1)} %get-tuple-element.157), channel_id=1, source_target_pairs={{0,12},{4,8},{8,4},{12,0},{16,28},{20,24},{24,20},{28,16},{1,13},{... | collective-permute-start | bytes 294920 | tf_op jit(solution)/shard_map/ppermute | solution.py:320
  194.0 9.1 %collective-permute-start.31 = (f32[192,128]{1,0:T(8,128)S(1)}, f32[192,128]{1,0:T(8,128)S(1)}, u32[]{:S(2)}, u32[]{:S(2)}) collective-permute-start(f32[192,128]{1,0:T(8,128)S(1)} %get-tuple-element.158), channel_id=1, source_target_pairs={{0,16},{4,20},{8,24},{12,28},{16,0},{20,4},{24,8},{28,12},{1,17},{... | collective-permute-start | bytes 294920 | tf_op jit(solution)/shard_map/ppermute | solution.py:320
  197.7 13.5 %collective-permute-start.32 = (f32[192,128]{1,0:T(8,128)S(1)}, f32[192,128]{1,0:T(8,128)S(1)}, u32[]{:S(2)}, u32[]{:S(2)}) collective-permute-start(f32[192,128]{1,0:T(8,128)S(1)} %get-tuple-element.159), channel_id=1, source_target_pairs={{0,20},{4,16},{8,28},{12,24},{16,4},{20,0},{24,12},{28,8},{1,21},{... | collective-permute-start | bytes 294920 | tf_op jit(solution)/shard_map/ppermute | solution.py:320
  198.3 12.9 %collective-permute-start.33 = (f32[192,128]{1,0:T(8,128)S(1)}, f32[192,128]{1,0:T(8,128)S(1)}, u32[]{:S(2)}, u32[]{:S(2)}) collective-permute-start(f32[192,128]{1,0:T(8,128)S(1)} %get-tuple-element.160), channel_id=1, source_target_pairs={{0,24},{4,28},{8,16},{12,20},{16,8},{20,12},{24,0},{28,4},{1,25},{... | collective-permute-start | bytes 294920 | tf_op jit(solution)/shard_map/ppermute | solution.py:320
  200.7 10.5 %collective-permute-start.34 = (f32[192,128]{1,0:T(8,128)S(1)}, f32[192,128]{1,0:T(8,128)S(1)}, u32[]{:S(2)}, u32[]{:S(2)}) collective-permute-start(f32[192,128]{1,0:T(8,128)S(1)} %get-tuple-element.161), channel_id=1, source_target_pairs={{0,28},{4,24},{8,20},{12,16},{16,12},{20,8},{24,4},{28,0},{1,29},{... | collective-permute-start | bytes 294920 | tf_op jit(solution)/shard_map/ppermute | solution.py:320
  211.3 9.1 %collective-permute-start.36 = (f32[192,128]{1,0:T(8,128)S(1)}, f32[192,128]{1,0:T(8,128)S(1)}, u32[]{:S(2)}, u32[]{:S(2)}) collective-permute-start(f32[192,128]{1,0:T(8,128)S(1)} %right_sum.3.refs_0_), channel_id=1, source_target_pairs={{0,4},{4,0},{8,12},{12,8},{16,20},{20,16},{24,28},{28,24},{1,5},{5... | collective-permute-start | bytes 294920 | tf_op jit(solution)/shard_map/ppermute | solution.py:320
  211.8 10.0 %collective-permute-start.37 = (f32[192,128]{1,0:T(8,128)S(1)}, f32[192,128]{1,0:T(8,128)S(1)}, u32[]{:S(2)}, u32[]{:S(2)}) collective-permute-start(f32[192,128]{1,0:T(8,128)S(1)} %right_sum.3.refs_0_), channel_id=1, source_target_pairs={{0,8},{4,12},{8,0},{12,4},{16,24},{20,28},{24,16},{28,20},{1,9},{5... | collective-permute-start | bytes 294920 | tf_op jit(solution)/shard_map/ppermute | solution.py:320
  216.6 8.3 %collective-permute-start.38 = (f32[192,128]{1,0:T(8,128)S(1)}, f32[192,128]{1,0:T(8,128)S(1)}, u32[]{:S(2)}, u32[]{:S(2)}) collective-permute-start(f32[192,128]{1,0:T(8,128)S(1)} %right_sum.3.refs_0_), channel_id=1, source_target_pairs={{0,12},{4,8},{8,4},{12,0},{16,28},{20,24},{24,20},{28,16},{1,13},{... | collective-permute-start | bytes 294920 | tf_op jit(solution)/shard_map/ppermute | solution.py:320
  217.1 14.7 %collective-permute-start.39 = (f32[192,128]{1,0:T(8,128)S(1)}, f32[192,128]{1,0:T(8,128)S(1)}, u32[]{:S(2)}, u32[]{:S(2)}) collective-permute-start(f32[192,128]{1,0:T(8,128)S(1)} %right_sum.3.refs_0_), channel_id=1, source_target_pairs={{0,16},{4,20},{8,24},{12,28},{16,0},{20,4},{24,8},{28,12},{1,17},{... | collective-permute-start | bytes 294920 | tf_op jit(solution)/shard_map/ppermute | solution.py:320
  219.2 15.2 %collective-permute-start.40 = (f32[192,128]{1,0:T(8,128)S(1)}, f32[192,128]{1,0:T(8,128)S(1)}, u32[]{:S(2)}, u32[]{:S(2)}) collective-permute-start(f32[192,128]{1,0:T(8,128)S(1)} %right_sum.3.refs_0_), channel_id=1, source_target_pairs={{0,20},{4,16},{8,28},{12,24},{16,4},{20,0},{24,12},{28,8},{1,21},{... | collective-permute-start | bytes 294920 | tf_op jit(solution)/shard_map/ppermute | solution.py:320
  220.4 14.0 %collective-permute-start.41 = (f32[192,128]{1,0:T(8,128)S(1)}, f32[192,128]{1,0:T(8,128)S(1)}, u32[]{:S(2)}, u32[]{:S(2)}) collective-permute-start(f32[192,128]{1,0:T(8,128)S(1)} %right_sum.3.refs_0_), channel_id=1, source_target_pairs={{0,24},{4,28},{8,16},{12,20},{16,8},{20,12},{24,0},{28,4},{1,25},{... | collective-permute-start | bytes 294920 | tf_op jit(solution)/shard_map/ppermute | solution.py:320
  221.9 12.5 %collective-permute-start.42 = (f32[192,128]{1,0:T(8,128)S(1)}, f32[192,128]{1,0:T(8,128)S(1)}, u32[]{:S(2)}, u32[]{:S(2)}) collective-permute-start(f32[192,128]{1,0:T(8,128)S(1)} %right_sum.3.refs_0_), channel_id=1, source_target_pairs={{0,28},{4,24},{8,20},{12,16},{16,12},{20,8},{24,4},{28,0},{1,29},{... | collective-permute-start | bytes 294920 | tf_op jit(solution)/shard_map/ppermute | solution.py:320
  237.3 24.7 %collective-permute-start.46 = (bf16[576,512]{1,0:T(8,128)(2,1)}, bf16[576,512]{1,0:T(8,128)(2,1)}, u32[]{:S(2)}, u32[]{:S(2)}) collective-permute-start(bf16[576,512]{1,0:T(8,128)(2,1)} %get-tuple-element.175.refs_0_), channel_id=1, source_target_pairs={{0,8},{4,12},{8,16},{12,20},{16,24},{20,28},{24,0},{28,4},{1,9},{5... | collective-permute-start | bytes 1769480 | tf_op jit(solution)/shard_map/ppermute | solution.py:562
  241.1 20.9 %collective-permute-start.47 = (bf16[576,512]{1,0:T(8,128)(2,1)}, bf16[576,512]{1,0:T(8,128)(2,1)}, u32[]{:S(2)}, u32[]{:S(2)}) collective-permute-start(bf16[576,512]{1,0:T(8,128)(2,1)} %get-tuple-element.175.refs_0_), channel_id=1, source_target_pairs={{0,4},{4,0},{8,12},{12,8},{16,20},{20,16},{24,28},{28,24},{1,5},{5... | collective-permute-start | bytes 1769480 | tf_op jit(solution)/shard_map/ppermute | solution.py:320
  242.3 25.6 %collective-permute-start.48 = (bf16[576,512]{1,0:T(8,128)(2,1)}, bf16[576,512]{1,0:T(8,128)(2,1)}, u32[]{:S(2)}, u32[]{:S(2)}) collective-permute-start(bf16[576,512]{1,0:T(8,128)(2,1)} %get-tuple-element.182.refs_1_), channel_id=1, source_target_pairs={{0,8},{4,12},{8,16},{12,20},{16,24},{20,28},{24,0},{28,4},{1,9},{5... | collective-permute-start | bytes 1769480 | tf_op jit(solution)/shard_map/ppermute | solution.py:562
  242.9 27.2 %collective-permute-start.49 = (bf16[576,512]{1,0:T(8,128)(2,1)}, bf16[576,512]{1,0:T(8,128)(2,1)}, u32[]{:S(2)}, u32[]{:S(2)}) collective-permute-start(bf16[576,512]{1,0:T(8,128)(2,1)} %get-tuple-element.182.refs_1_), channel_id=1, source_target_pairs={{0,4},{4,0},{8,12},{12,8},{16,20},{20,16},{24,28},{28,24},{1,5},{5... | collective-permute-start | bytes 1769480 | tf_op jit(solution)/shard_map/ppermute | solution.py:320
  251.7 10.3 %collective-permute-start.45 = (f32[64,512]{1,0:T(8,128)S(1)}, f32[64,512]{1,0:T(8,128)S(1)}, u32[]{:S(2)}, u32[]{:S(2)}) collective-permute-start(f32[64,512]{1,0:T(8,128)S(1)} %constant_dynamic-slice_fusion), channel_id=1, source_target_pairs={{0,3},{1,2},{2,1},{3,0},{4,7},{5,6},{6,5},{7,4},{8,11},{9,10},{10,... | collective-permute-start | bytes 393224 | tf_op jit(solution)/shard_map/ppermute | solution.py:320
  262.0 18.5 %collective-permute-start.50 = (bf16[576,512]{1,0:T(8,128)(2,1)}, bf16[576,512]{1,0:T(8,128)(2,1)S(1)}, u32[]{:S(2)}, u32[]{:S(2)}) collective-permute-start(bf16[576,512]{1,0:T(8,128)(2,1)} %collective-permute-done.46.refs_2_), channel_id=1, source_target_pairs={{0,8},{4,12},{8,16},{12,20},{16,24},{20,28},{24,0},{28,4},{1,9},{5... | collective-permute-start | bytes 1769480 | tf_op jit(solution)/shard_map/ppermute | solution.py:562
  262.1 20.6 %collective-permute-start.51 = (bf16[576,512]{1,0:T(8,128)(2,1)}, bf16[576,512]{1,0:T(8,128)(2,1)S(1)}, u32[]{:S(2)}, u32[]{:S(2)}) collective-permute-start(bf16[576,512]{1,0:T(8,128)(2,1)} %collective-permute-done.46.refs_2_), channel_id=1, source_target_pairs={{0,4},{4,0},{8,12},{12,8},{16,20},{20,16},{24,28},{28,24},{1,5},{5... | collective-permute-start | bytes 1769480 | tf_op jit(solution)/shard_map/ppermute | solution.py:320
  270.2 23.0 %collective-permute-start.52 = (bf16[576,512]{1,0:T(8,128)(2,1)}, bf16[576,512]{1,0:T(8,128)(2,1)S(1)}, u32[]{:S(2)}, u32[]{:S(2)}) collective-permute-start(bf16[576,512]{1,0:T(8,128)(2,1)} %collective-permute-done.48.refs_4_), channel_id=1, source_target_pairs={{0,8},{4,12},{8,16},{12,20},{16,24},{20,28},{24,0},{28,4},{1,9},{5... | collective-permute-start | bytes 1769480 | tf_op jit(solution)/shard_map/ppermute | solution.py:562
  271.0 24.3 %collective-permute-start.53 = (bf16[576,512]{1,0:T(8,128)(2,1)}, bf16[576,512]{1,0:T(8,128)(2,1)S(1)}, u32[]{:S(2)}, u32[]{:S(2)}) collective-permute-start(bf16[576,512]{1,0:T(8,128)(2,1)} %collective-permute-done.48.refs_4_), channel_id=1, source_target_pairs={{0,4},{4,0},{8,12},{12,8},{16,20},{20,16},{24,28},{28,24},{1,5},{5... | collective-permute-start | bytes 1769480 | tf_op jit(solution)/shard_map/ppermute | solution.py:320
  282.7 28.1 %collective-permute-start.54 = (bf16[576,512]{1,0:T(8,128)(2,1)S(1)}, bf16[576,512]{1,0:T(8,128)(2,1)S(1)}, u32[]{:S(2)}, u32[]{:S(2)}) collective-permute-start(bf16[576,512]{1,0:T(8,128)(2,1)S(1)} %collective-permute-done.50.refs_6_), channel_id=1, source_target_pairs={{0,8},{4,12},{8,16},{12,20},{16,24},{20,28},{24,0},{28,4},{1,9},{5... | collective-permute-start | bytes 1769480 | tf_op jit(solution)/shard_map/ppermute | solution.py:562
  283.6 27.2 %collective-permute-start.55 = (bf16[576,512]{1,0:T(8,128)(2,1)S(1)}, bf16[576,512]{1,0:T(8,128)(2,1)S(1)}, u32[]{:S(2)}, u32[]{:S(2)}) collective-permute-start(bf16[576,512]{1,0:T(8,128)(2,1)S(1)} %collective-permute-done.50.refs_6_), channel_id=1, source_target_pairs={{0,4},{4,0},{8,12},{12,8},{16,20},{20,16},{24,28},{28,24},{1,5},{5... | collective-permute-start | bytes 1769480 | tf_op jit(solution)/shard_map/ppermute | solution.py:320
  295.3 22.7 %collective-permute-start.56 = (bf16[576,512]{1,0:T(8,128)(2,1)S(1)}, bf16[576,512]{1,0:T(8,128)(2,1)S(1)}, u32[]{:S(2)}, u32[]{:S(2)}) collective-permute-start(bf16[576,512]{1,0:T(8,128)(2,1)S(1)} %collective-permute-done.52.refs_8_), channel_id=1, source_target_pairs={{0,8},{4,12},{8,16},{12,20},{16,24},{20,28},{24,0},{28,4},{1,9},{5... | collective-permute-start | bytes 1769480 | tf_op jit(solution)/shard_map/ppermute | solution.py:562
  296.2 22.4 %collective-permute-start.57 = (bf16[576,512]{1,0:T(8,128)(2,1)S(1)}, bf16[576,512]{1,0:T(8,128)(2,1)S(1)}, u32[]{:S(2)}, u32[]{:S(2)}) collective-permute-start(bf16[576,512]{1,0:T(8,128)(2,1)S(1)} %collective-permute-done.52.refs_8_), channel_id=1, source_target_pairs={{0,4},{4,0},{8,12},{12,8},{16,20},{20,16},{24,28},{28,24},{1,5},{5... | collective-permute-start | bytes 1769480 | tf_op jit(solution)/shard_map/ppermute | solution.py:320
  318.6 16.6 %collective-permute-start.59 = (bf16[576,512]{1,0:T(8,128)(2,1)S(1)}, bf16[576,512]{1,0:T(8,128)(2,1)S(1)}, u32[]{:S(2)}, u32[]{:S(2)}) collective-permute-start(bf16[576,512]{1,0:T(8,128)(2,1)S(1)} %collective-permute-done.57.refs_1_), channel_id=1, source_target_pairs={{0,8},{4,12},{8,16},{12,20},{16,24},{20,28},{24,0},{28,4},{1,9},{5... | collective-permute-start | bytes 1769480 | tf_op jit(solution)/shard_map/ppermute | solution.py:567
  319.5 15.8 %collective-permute-start.58 = (bf16[576,512]{1,0:T(8,128)(2,1)S(1)}, bf16[576,512]{1,0:T(8,128)(2,1)S(1)}, u32[]{:S(2)}, u32[]{:S(2)}) collective-permute-start(bf16[576,512]{1,0:T(8,128)(2,1)S(1)} %collective-permute-done.54.refs_0_), channel_id=1, source_target_pairs={{0,4},{4,0},{8,12},{12,8},{16,20},{20,16},{24,28},{28,24},{1,5},{5... | collective-permute-start | bytes 1769480 | tf_op jit(solution)/shard_map/ppermute | solution.py:320
  (33 other events, 326.6 us)

commit v10 on v9

--- a/solution.py
+++ b/solution.py
@@ -253,10 +253,10 @@
             refs[-1][0, 0] = part_ref[...]
 
 
-def update_kernel(rank, ids_ref, basis_ref, right_ref, high_ref, low_ref, *refs):
+def update_kernel(rank, ids_ref, basis_ref, right_ref, grads_ref, error_ref, *refs):
     at = part_at(pl.program_id(0), rank)
     approx = product(basis_ref[at, :], right_ref[at, :])
-    refs[-1][0, 0] = high_ref[0].astype(F32) + low_ref[0].astype(F32) - approx
+    refs[-1][0, 0] = grads_ref[0, 0].astype(F32) + error_ref[0, 0] - approx
 
 
 def flat_kernel(unit, per_tp, rank, matrices, ids_ref, basis_ref, near_ref, momentum_ref, master_ref, new_momentum_ref, new_master_ref, approx):
@@ -332,6 +332,7 @@
     replicas, tps = lax.axis_size("rep"), lax.axis_size("tp")
     rep, tp = lax.axis_index("rep"), lax.axis_index("tp")
     ids = jnp.stack([rep, tp]).astype(jnp.int32)
+    grads, error, query = (pltpu.with_memory_space_constraint(x, pltpu.HBM) for x in (grads, error, query))
     _, matrices, width, cols = grads.shape
     rank = query.shape[1]
     per_tp = matrices // tps
@@ -379,7 +380,7 @@
             ],
             [term_spec, term_spec, *left_specs],
             [term_shape, term_shape, *left_shapes],
-            (*(pltpu.with_memory_space_constraint(x, pltpu.HBM) for x in (grads, error)), query),
+            (grads, error, query),
             [
                 pltpu.VMEM((per_half, width, cols), BF16),
                 pltpu.VMEM((per_half, width, cols), F32),
@@ -475,7 +476,7 @@
     near = lax.dynamic_slice_in_dim(right, first * rank, spans * rank, 0)
 
     def update(slot, ids, before):
-        half, start = slot // 2, slot % 2 * per_tp
+        own = pl.BlockSpec((1, 1, width, cols), lambda j, at: (0, (at[1] ^ slot) * per_tp + j, 0, 0))
         return grid_call(
             functools.partial(update_kernel, rank),
             "update",
@@ -484,13 +485,13 @@
             [
                 pl.BlockSpec((tp_rows, width), lambda j, at: (slot, 0)),
                 pl.BlockSpec((tp_rows, cols), lambda j, at: (at[1] ^ slot, 0)),
-                pl.BlockSpec((1, width, cols), lambda j, at: (start + j, 0, 0)),
-                pl.BlockSpec((1, width, cols), lambda j, at: (start + j, 0, 0)),
+                own,
+                own,
             ]
             + [pl.BlockSpec(memory_space=pl.ANY)] * len(before),
-            pl.BlockSpec((1, 1, width, cols), lambda j, at: (0, (at[1] ^ slot) * per_tp + j, 0, 0)),
+            own,
             shape(*error.shape),
-            (all_bases, right, *terms[half], *before),
+            (all_bases, right, grads, error, *before),
             aliases={5: 0} if before else None,
             flops=2 * 3 * rank * error.size // tps,
             moved=8 * error.size // tps,

time: 337 us -> 341 us (1.012)
  Pallas kernels: 76.9 us -> 96.3 us
  waiting for transfers between devices: 110 us -> 101 us
  local copies, waits for them, and re-layouts: 16.6 us -> 10.8 us
    pallas_call x17, Pallas kernels: 68.8 us -> 88.1 us  [grid_call(): pl.pallas_call(kernel, grid_spec=pltpu.PrefetchScalarGridSpec(num_scalar_...]
    ppermute x6, waiting for transfers between devices: 14.8 us -> 6.32 us  [local(): held[half] = lax.ppermute(here, 'rep', ring)]
    unnamed x42 -> x26, local copies, waits for them, and re-layouts: 15.7 us -> 9.92 us
  transfers between devices with their start and end apart: 60 -> 60, of which waited for: 28 -> 27; matrix products, arithmetic and copies ran while one was open for 1% -> 1% of each run, Pallas kernels for 17% -> 21%
where the time goes in v10:
time: 341 us; the launch traced here: 340 us
  waiting for transfers between devices  101 us (30%)
  Pallas kernels  96.3 us (28%)
  starting transfers between devices  69 us (20%)
  blocking collectives  60.1 us (18%)
  local copies, waits for them, and re-layouts  10.8 us (3%)
    pallas_call x17, Pallas kernels, grid_call(): pl.pallas_call(kernel, grid_spec=pltpu.PrefetchScalarGridSpec(num_scalar_...  88.1 us
    ppermute x53, waiting for transfers between devices, swap(): lax.ppermute(x, axis, [(index, index ^ offset) for index in range(size)])  82.7 us
    ppermute x53, starting transfers between devices, swap(): lax.ppermute(x, axis, [(index, index ^ offset) for index in range(size)])  61.7 us
    all_to_all x4, blocking collectives, local(): lax.all_to_all(parts, 'rep', split_axis=0, concat_axis=0, tiled=True)  60.1 us
    ppermute x1, waiting for transfers between devices, local(): beside[half] = lax.ppermute(beside[half], 'rep', ring)  11.8 us
    unnamed x26, local copies, waits for them, and re-layouts  9.92 us
    pallas_call x9, Pallas kernels, whole_call(): pl.pallas_call(kernel, in_specs=specs, out_specs=[out_spec] * len(out_sha...  8.18 us
  transfers between devices with their start and end apart: 60, of which 27 were waited for; matrix products, arithmetic and copies ran while one was open for 1% of the time, Pallas kernels for 21%

profile of v10, /device:TPU:0, one launch (start us, length us, event | category | flops | bytes accessed | tf_op | source)
XLA Modules:
  0.0 340.4 jit_solution(7152548666180818864)
XLA Ops:
  0.7 10.3 %first_left.2 = (bf16[6,768,512]{2,1,0:T(8,128)(2,1)S(1)}, bf16[6,768,512]{2,1,0:T(8,128)(2,1)S(1)}, f32[96,768]{1,0:T(8,128)}, f32[96,768]{1,0:T(8,128)}) custom-call(s32[2]{0:T(128)S(1)} %pad_add_fusion.ids_ref, bf16[1,12,768,512]{3,2,1,0:T(8,128)(2,1)} %grads_ref.11, f32[1,12,768,512]{3,2,1,0:T(8,128)} %error_ref.11, f32[12,32,512]{2,1,0:T(8,128)} %query_ref.3), custom_call_target="tpu_custom_call" | custom-call | flops 452984832 | bytes 23592960 | tf_op jit(solution)/shard_map/first_left/pallas_call | solution.py:302
  15.4 2.9 collective-permute-start.1
  18.3 10.2 %first_left.3 = (bf16[6,768,512]{2,1,0:T(8,128)(2,1)S(1)}, bf16[6,768,512]{2,1,0:T(8,128)(2,1)S(1)}, f32[96,768]{1,0:T(8,128)S(1)}, f32[96,768]{1,0:T(8,128)}) custom-call(s32[2]{0:T(128)S(1)} %pad_add_fusion.ids_ref, bf16[1,12,768,512]{3,2,1,0:T(8,128)(2,1)} %grads_ref.11, f32[1,12,768,512]{3,2,1,0:T(8,128)} %error_ref.11, f32[12,32,512]{2,1,0:T(8,128)} %query_ref.3), custom_call_target="tpu_custom_call" | custom-call | flops 452984832 | bytes 23592960 | tf_op jit(solution)/shard_map/first_left/pallas_call | solution.py:302
  33.1 2.4 multiply_subtract_fusion
  35.5 6.3 %collective-permute-done.refs_1_ = f32[96,768]{1,0:T(8,128)} collective-permute-done((f32[96,768]{1,0:T(8,128)}, f32[96,768]{1,0:T(8,128)}, u32[]{:S(2)}, u32[]{:S(2)}) %collective-permute-start) | collective-permute-done | bytes 294944 | tf_op jit(solution)/shard_map/ppermute | solution.py:320
  43.0 16.6 %all_to_all.20.parts_ref = f32[8,72,128]{2,1,0:T(8,128)S(1)} all-to-all(f32[8,72,128]{2,1,0:T(8,128)S(1)} %bitcast.19), channel_id=1, replica_groups=mesh['rep'=8,'tp'=4] {'rep'}, dimensions={0} | all-to-all | bytes 589824 | tf_op jit(solution)/shard_map/all_to_all | solution.py:406
  59.6 13.0 %all_to_all.21 = f32[8,72,128]{2,1,0:T(8,128)S(1)} all-to-all(f32[8,72,128]{2,1,0:T(8,128)S(1)} %left_sum.2), channel_id=1, replica_groups=mesh['rep'=8,'tp'=4] {'rep'}, dimensions={0} | all-to-all | bytes 589824 | tf_op jit(solution)/shard_map/all_to_all | solution.py:408
  77.0 2.8 right_near.2.refs_0_
  79.8 4.8 %collective-permute-done.4.first_ref = f32[96,768]{1,0:T(8,128)S(1)} collective-permute-done((f32[96,768]{1,0:T(8,128)S(1)}, f32[96,768]{1,0:T(8,128)S(1)}, u32[]{:S(2)}, u32[]{:S(2)}) %collective-permute-start.4) | collective-permute-done | bytes 294944 | tf_op jit(solution)/shard_map/ppermute | solution.py:320
  86.1 2.9 right_far.2
  89.7 2.4 collective-permute-start.11
  92.1 2.4 collective-permute-start.12
  97.4 4.9 %collective-permute-done.10.refs_5_ = f32[192,128]{1,0:T(8,128)S(1)} collective-permute-done((f32[192,128]{1,0:T(8,128)S(1)}, f32[192,128]{1,0:T(8,128)S(1)}, u32[]{:S(2)}, u32[]{:S(2)}) %collective-permute-start.10) | collective-permute-done | bytes 98336 | tf_op jit(solution)/shard_map/ppermute | solution.py:320
  104.4 4.4 %collective-permute-done.8.refs_3_ = f32[192,128]{1,0:T(8,128)S(1)} collective-permute-done((f32[192,128]{1,0:T(8,128)S(1)}, f32[192,128]{1,0:T(8,128)S(1)}, u32[]{:S(2)}, u32[]{:S(2)}) %collective-permute-start.8) | collective-permute-done | bytes 98336 | tf_op jit(solution)/shard_map/ppermute | solution.py:320
  114.1 3.6 %collective-permute-start.19 = (f32[192,128]{1,0:T(8,128)S(1)}, f32[192,128]{1,0:T(8,128)S(1)}, u32[]{:S(2)}, u32[]{:S(2)}) collective-permute-start(f32[192,128]{1,0:T(8,128)S(1)} %right_sum.2.refs_0_), channel_id=1, source_target_pairs={{0,20},{4,16},{8,28},{12,24},{16,4},{20,0},{24,12},{28,8},{1,21},{... | collective-permute-start | bytes 294920 | tf_op jit(solution)/shard_map/ppermute | solution.py:320
  121.2 6.3 %collective-permute-done.18.refs_4_ = f32[192,128]{1,0:T(8,128)S(1)} collective-permute-done((f32[192,128]{1,0:T(8,128)S(1)}, f32[192,128]{1,0:T(8,128)S(1)}, u32[]{:S(2)}, u32[]{:S(2)}) %collective-permute-start.18) | collective-permute-done | bytes 98336 | tf_op jit(solution)/shard_map/ppermute | solution.py:320
  127.4 3.0 collective-permute-done.19.refs_5_
  130.5 4.2 %left.3 = (f32[96,768]{1,0:T(8,128)S(1)}, f32[96,768]{1,0:T(8,128)S(1)}) custom-call(s32[2]{0:T(128)S(1)} %pad_add_fusion.ids_ref, bf16[6,768,512]{2,1,0:T(8,128)(2,1)S(1)} %bitcast.13, bf16[6,768,512]{2,1,0:T(8,128)(2,1)S(1)} %copy-done.2, f32[192,128]{1,0:T(8,128)S(1)} %right_sum.2.refs_0_, f32[192,128]{1,0:T(8,128)S(1)} %collective-permute-done.15.refs_1_, ...), custom_call_target="tpu_custom_call" | custom-call | flops 452984832 | bytes 23592960 | tf_op jit(solution)/shard_map/left/pallas_call | solution.py:302
  135.3 4.2 %left.2 = (f32[96,768]{1,0:T(8,128)S(1)}, f32[96,768]{1,0:T(8,128)S(1)}) custom-call(s32[2]{0:T(128)S(1)} %pad_add_fusion.ids_ref, bf16[6,768,512]{2,1,0:T(8,128)(2,1)S(1)} %bitcast.15, bf16[6,768,512]{2,1,0:T(8,128)(2,1)S(1)} %copy-done.5, f32[192,128]{1,0:T(8,128)S(1)} %right_sum.2.refs_0_, f32[192,128]{1,0:T(8,128)S(1)} %collective-permute-done.15.refs_1_, ...), custom_call_target="tpu_custom_call" | custom-call | flops 452984832 | bytes 23592960 | tf_op jit(solution)/shard_map/left/pallas_call | solution.py:302
  140.9 3.2 collective-permute-done.22.refs_1_
  144.1 4.4 %collective-permute-done.23.refs_2_ = f32[96,768]{1,0:T(8,128)S(1)} collective-permute-done((f32[96,768]{1,0:T(8,128)S(1)}, f32[96,768]{1,0:T(8,128)S(1)}, u32[]{:S(2)}, u32[]{:S(2)}) %collective-permute-start.23) | collective-permute-done | bytes 294944 | tf_op jit(solution)/shard_map/ppermute | solution.py:320
  148.5 17.4 %all_to_all.22.parts_ref = f32[8,72,128]{2,1,0:T(8,128)S(1)} all-to-all(f32[8,72,128]{2,1,0:T(8,128)S(1)} %bitcast.20), channel_id=1, replica_groups=mesh['rep'=8,'tp'=4] {'rep'}, dimensions={0} | all-to-all | bytes 589824 | tf_op jit(solution)/shard_map/all_to_all | solution.py:406
  166.0 13.0 %all_to_all.23 = f32[8,72,128]{2,1,0:T(8,128)S(1)} all-to-all(f32[8,72,128]{2,1,0:T(8,128)S(1)} %left_sum.3), channel_id=1, replica_groups=mesh['rep'=8,'tp'=4] {'rep'}, dimensions={0} | all-to-all | bytes 589824 | tf_op jit(solution)/shard_map/all_to_all | solution.py:408
  182.9 2.8 right_near.3.refs_0_
  185.7 5.2 %collective-permute-done.26.first_ref = f32[96,768]{1,0:T(8,128)S(1)} collective-permute-done((f32[96,768]{1,0:T(8,128)S(1)}, f32[96,768]{1,0:T(8,128)S(1)}, u32[]{:S(2)}, u32[]{:S(2)}) %collective-permute-start.26) | collective-permute-done | bytes 294944 | tf_op jit(solution)/shard_map/ppermute | solution.py:320
  192.5 2.9 right_far.3
  196.7 2.3 collective-permute-start.30
  199.6 3.0 collective-permute-done.35.refs_11_
  203.3 2.4 collective-permute-start.33
  205.6 2.4 collective-permute-start.34
  208.1 8.1 %collective-permute-done.32.refs_5_ = f32[192,128]{1,0:T(8,128)S(1)} collective-permute-done((f32[192,128]{1,0:T(8,128)S(1)}, f32[192,128]{1,0:T(8,128)S(1)}, u32[]{:S(2)}, u32[]{:S(2)}) %collective-permute-start.32) | collective-permute-done | bytes 98336 | tf_op jit(solution)/shard_map/ppermute | solution.py:320
  216.8 4.7 %collective-permute-start.37 = (f32[192,128]{1,0:T(8,128)S(1)}, f32[192,128]{1,0:T(8,128)S(1)}, u32[]{:S(2)}, u32[]{:S(2)}) collective-permute-start(f32[192,128]{1,0:T(8,128)S(1)} %right_sum.3.refs_0_), channel_id=1, source_target_pairs={{0,8},{4,12},{8,0},{12,4},{16,24},{20,28},{24,16},{28,20},{1,9},{5... | collective-permute-start | bytes 294920 | tf_op jit(solution)/shard_map/ppermute | solution.py:320
  226.8 2.9 collective-permute-start.42
  229.9 7.0 %collective-permute-done.39.refs_4_ = f32[192,128]{1,0:T(8,128)S(1)} collective-permute-done((f32[192,128]{1,0:T(8,128)S(1)}, f32[192,128]{1,0:T(8,128)S(1)}, u32[]{:S(2)}, u32[]{:S(2)}) %collective-permute-start.39) | collective-permute-done | bytes 98336 | tf_op jit(solution)/shard_map/ppermute | solution.py:320
  236.8 2.5 collective-permute-done.40.refs_5_
  239.4 2.9 late_rows.1
  242.3 3.8 %collective-permute-start.46 = (bf16[576,512]{1,0:T(8,128)(2,1)}, bf16[576,512]{1,0:T(8,128)(2,1)}, u32[]{:S(2)}, u32[]{:S(2)}) collective-permute-start(bf16[576,512]{1,0:T(8,128)(2,1)} %get-tuple-element.175.refs_0_), channel_id=1, source_target_pairs={{0,8},{4,12},{8,16},{12,20},{16,24},{20,28},{24,0},{28,4},{1,9},{5... | collective-permute-start | bytes 1769480 | tf_op jit(solution)/shard_map/ppermute | solution.py:563
  252.5 4.2 %collective-permute-done.44 = f32[64,512]{1,0:T(8,128)S(1)} collective-permute-done((f32[64,512]{1,0:T(8,128)S(1)}, f32[64,512]{1,0:T(8,128)S(1)}, u32[]{:S(2)}, u32[]{:S(2)}) %collective-permute-start.44) | collective-permute-done | bytes 131104 | tf_op jit(solution)/shard_map/ppermute | solution.py:320
  258.2 7.4 %update.4.refs_0_ = f32[1,12,768,512]{3,2,1,0:T(8,128)} custom-call(s32[2]{0:T(128)S(1)} %pad_add_fusion.ids_ref, f32[384,768]{1,0:T(8,128)S(1)} %pad_maximum_fusion.basis_ref, f32[384,512]{1,0:T(8,128)S(1)} %copy-done.6, bf16[1,12,768,512]{3,2,1,0:T(8,128)(2,1)} %grads_ref.11, f32[1,12,768,512]{3,2,1,0:T(8,128)} %error_ref.11), custom_call_target="tpu_custom_call" | custom-call | flops 226492416 | bytes 9437184 | tf_op jit(solution)/shard_map/update/pallas_call | solution.py:302
  266.9 7.4 %update.5.refs_0_ = f32[1,12,768,512]{3,2,1,0:T(8,128)} custom-call(s32[2]{0:T(128)S(1)} %pad_add_fusion.ids_ref, f32[384,768]{1,0:T(8,128)S(1)} %pad_maximum_fusion.basis_ref, f32[384,512]{1,0:T(8,128)S(1)} %copy-done.6, bf16[1,12,768,512]{3,2,1,0:T(8,128)(2,1)} %grads_ref.11, f32[1,12,768,512]{3,2,1,0:T(8,128)} %error_ref.11, ...), custom_call_target="tpu_custom_call", output_to_operand_aliasing={{}: (5, {})} | custom-call | flops 226492416 | bytes 9437184 | tf_op jit(solution)/shard_map/update/pallas_call | solution.py:302
  277.1 7.4 %update.6.refs_0_ = f32[1,12,768,512]{3,2,1,0:T(8,128)} custom-call(s32[2]{0:T(128)S(1)} %pad_add_fusion.ids_ref, f32[384,768]{1,0:T(8,128)S(1)} %pad_maximum_fusion.basis_ref, f32[384,512]{1,0:T(8,128)S(1)} %copy-done.6, bf16[1,12,768,512]{3,2,1,0:T(8,128)(2,1)} %grads_ref.11, f32[1,12,768,512]{3,2,1,0:T(8,128)} %error_ref.11, ...), custom_call_target="tpu_custom_call", output_to_operand_aliasing={{}: (5, {})} | custom-call | flops 226492416 | bytes 9437184 | tf_op jit(solution)/shard_map/update/pallas_call | solution.py:302
  285.5 2.4 collective-permute-done.51.refs_7_
  289.7 7.4 %update.7 = f32[1,12,768,512]{3,2,1,0:T(8,128)} custom-call(s32[2]{0:T(128)S(1)} %pad_add_fusion.ids_ref, f32[384,768]{1,0:T(8,128)S(1)} %pad_maximum_fusion.basis_ref, f32[384,512]{1,0:T(8,128)S(1)} %copy-done.6, bf16[1,12,768,512]{3,2,1,0:T(8,128)(2,1)} %grads_ref.11, f32[1,12,768,512]{3,2,1,0:T(8,128)} %error_ref.11, ...), custom_call_target="tpu_custom_call", output_to_operand_aliasing={{}: (5, {})} | custom-call | flops 226492416 | bytes 9437184 | tf_op jit(solution)/shard_map/update/pallas_call | solution.py:302
  298.1 2.4 collective-permute-done.53.refs_9_
  302.3 7.2 %place.4.refs_2_ = bf16[8,2,576,512]{3,2,1,0:T(8,128)(2,1)} custom-call(s32[2]{0:T(128)S(1)} %pad_add_fusion.ids_ref, bf16[576,512]{1,0:T(8,128)(2,1)} %get-tuple-element.175.refs_0_, bf16[576,512]{1,0:T(8,128)(2,1)} %get-tuple-element.182.refs_1_, bf16[576,512]{1,0:T(8,128)(2,1)} %collective-permute-done.46.refs_2_, ...), custom_call_target="tpu_custom_call" | custom-call | bytes 23592960 | tf_op jit(solution)/shard_map/place/pallas_call | solution.py:302
  309.6 6.1 %flat_rows.1 = (f32[288,2048]{1,0:T(8,128)}, f32[288,2048]{1,0:T(8,128)}) custom-call(s32[2]{0:T(128)S(1)} %pad_add_fusion.ids_ref, f32[384,768]{1,0:T(8,128)S(1)} %pad_maximum_fusion.basis_ref, f32[4,64,512]{2,1,0:T(8,128)S(1)} %pad_maximum_fusion.1.near_ref, f32[288,2048]{1,0:T(8,128)S(1)} %copy-done.7, f32[288,2048]{1,0:T(8,128)S(1)} %copy-done.8), custom_call_target="tpu_custom_call" | custom-call | flops 452984832 | bytes 9437184 | tf_op jit(solution)/shard_map/flat_rows/pallas_call | solution.py:302
  317.4 4.3 %collective-permute-done.56.refs_0_ = bf16[576,512]{1,0:T(8,128)(2,1)S(1)} collective-permute-done((bf16[576,512]{1,0:T(8,128)(2,1)S(1)}, bf16[576,512]{1,0:T(8,128)(2,1)S(1)}, u32[]{:S(2)}, u32[]{:S(2)}) %collective-permute-start.56) | collective-permute-done | bytes 589856 | tf_op jit(solution)/shard_map/ppermute | solution.py:563
  327.0 11.8 %collective-permute-done.59.refs_1_ = bf16[576,512]{1,0:T(8,128)(2,1)S(1)} collective-permute-done((bf16[576,512]{1,0:T(8,128)(2,1)S(1)}, bf16[576,512]{1,0:T(8,128)(2,1)S(1)}, u32[]{:S(2)}, u32[]{:S(2)}) %collective-permute-start.59) | collective-permute-done | bytes 589856 | tf_op jit(solution)/shard_map/ppermute | solution.py:568
  (135 shorter events, 72.9 us)
Async XLA Ops:
  15.4 20.1 %collective-permute-start.1 = (f32[96,768]{1,0:T(8,128)}, f32[96,768]{1,0:T(8,128)S(1)}, u32[]{:S(2)}, u32[]{:S(2)}) collective-permute-start(f32[96,768]{1,0:T(8,128)} %get-tuple-element.115), channel_id=1, source_target_pairs={{0,2},{1,3},{2,0},{3,1},{4,6},{5,7},{6,4},{7,5},{8,10},{9,11},{10,... | collective-permute-start | bytes 884744 | tf_op jit(solution)/shard_map/ppermute | solution.py:320
  32.9 9.0 %collective-permute-start = (f32[96,768]{1,0:T(8,128)}, f32[96,768]{1,0:T(8,128)}, u32[]{:S(2)}, u32[]{:S(2)}) collective-permute-start(f32[96,768]{1,0:T(8,128)} %get-tuple-element.121), channel_id=1, source_target_pairs={{0,3},{1,2},{2,1},{3,0},{4,7},{5,6},{6,5},{7,4},{8,11},{9,10},{10,... | collective-permute-start | bytes 884744 | tf_op jit(solution)/shard_map/ppermute | solution.py:320
  74.7 9.9 %collective-permute-start.4 = (f32[96,768]{1,0:T(8,128)S(1)}, f32[96,768]{1,0:T(8,128)S(1)}, u32[]{:S(2)}, u32[]{:S(2)}) collective-permute-start(f32[96,768]{1,0:T(8,128)S(1)} %basis.2.first_ref), channel_id=1, source_target_pairs={{0,2},{1,3},{2,0},{3,1},{4,6},{5,7},{6,4},{7,5},{8,10},{9,11},{10,... | collective-permute-start | bytes 884744 | tf_op jit(solution)/shard_map/ppermute | solution.py:320
  75.2 19.2 %collective-permute-start.13 = (f32[288,512]{1,0:T(8,128)S(1)}, f32[288,512]{1,0:T(8,128)S(1)}, u32[]{:S(2)}, u32[]{:S(2)}) collective-permute-start(f32[288,512]{1,0:T(8,128)S(1)} %get-tuple-element.137), channel_id=1, source_target_pairs={{0,1},{1,0},{2,3},{3,2},{4,5},{5,4},{6,7},{7,6},{8,9},{9,8},{10,11... | collective-permute-start | bytes 1769480 | tf_op jit(solution)/shard_map/ppermute | solution.py:320
  75.4 21.3 %collective-permute-start.14 = (f32[288,512]{1,0:T(8,128)S(1)}, f32[288,512]{1,0:T(8,128)S(1)}, u32[]{:S(2)}, u32[]{:S(2)}) collective-permute-start(f32[288,512]{1,0:T(8,128)S(1)} %get-tuple-element.138), channel_id=1, source_target_pairs={{0,2},{1,3},{2,0},{3,1},{4,6},{5,7},{6,4},{7,5},{8,10},{9,11},{10,... | collective-permute-start | bytes 1769480 | tf_op jit(solution)/shard_map/ppermute | solution.py:320
  89.0 13.2 %collective-permute-start.10 = (f32[192,128]{1,0:T(8,128)S(1)}, f32[192,128]{1,0:T(8,128)S(1)}, u32[]{:S(2)}, u32[]{:S(2)}) collective-permute-start(f32[192,128]{1,0:T(8,128)S(1)} %get-tuple-element.133), channel_id=1, source_target_pairs={{0,20},{4,16},{8,28},{12,24},{16,4},{20,0},{24,12},{28,8},{1,21},{... | collective-permute-start | bytes 294920 | tf_op jit(solution)/shard_map/ppermute | solution.py:320
  89.7 12.6 %collective-permute-start.11 = (f32[192,128]{1,0:T(8,128)S(1)}, f32[192,128]{1,0:T(8,128)S(1)}, u32[]{:S(2)}, u32[]{:S(2)}) collective-permute-start(f32[192,128]{1,0:T(8,128)S(1)} %get-tuple-element.134), channel_id=1, source_target_pairs={{0,24},{4,28},{8,16},{12,20},{16,8},{20,12},{24,0},{28,4},{1,25},{... | collective-permute-start | bytes 294920 | tf_op jit(solution)/shard_map/ppermute | solution.py:320
  92.1 12.3 %collective-permute-start.12 = (f32[192,128]{1,0:T(8,128)S(1)}, f32[192,128]{1,0:T(8,128)S(1)}, u32[]{:S(2)}, u32[]{:S(2)}) collective-permute-start(f32[192,128]{1,0:T(8,128)S(1)} %get-tuple-element.135), channel_id=1, source_target_pairs={{0,28},{4,24},{8,20},{12,16},{16,12},{20,8},{24,4},{28,0},{1,29},{... | collective-permute-start | bytes 294920 | tf_op jit(solution)/shard_map/ppermute | solution.py:320
  94.5 9.9 %collective-permute-start.6 = (f32[192,128]{1,0:T(8,128)S(1)}, f32[192,128]{1,0:T(8,128)S(1)}, u32[]{:S(2)}, u32[]{:S(2)}) collective-permute-start(f32[192,128]{1,0:T(8,128)S(1)} %get-tuple-element.129), channel_id=1, source_target_pairs={{0,4},{4,0},{8,12},{12,8},{16,20},{20,16},{24,28},{28,24},{1,5},{5... | collective-permute-start | bytes 294920 | tf_op jit(solution)/shard_map/ppermute | solution.py:320
  111.8 9.4 %collective-permute-start.17 = (f32[192,128]{1,0:T(8,128)S(1)}, f32[192,128]{1,0:T(8,128)S(1)}, u32[]{:S(2)}, u32[]{:S(2)}) collective-permute-start(f32[192,128]{1,0:T(8,128)S(1)} %right_sum.2.refs_0_), channel_id=1, source_target_pairs={{0,12},{4,8},{8,4},{12,0},{16,28},{20,24},{24,20},{28,16},{1,13},{... | collective-permute-start | bytes 294920 | tf_op jit(solution)/shard_map/ppermute | solution.py:320
  113.5 13.9 %collective-permute-start.18 = (f32[192,128]{1,0:T(8,128)S(1)}, f32[192,128]{1,0:T(8,128)S(1)}, u32[]{:S(2)}, u32[]{:S(2)}) collective-permute-start(f32[192,128]{1,0:T(8,128)S(1)} %right_sum.2.refs_0_), channel_id=1, source_target_pairs={{0,16},{4,20},{8,24},{12,28},{16,0},{20,4},{24,8},{28,12},{1,17},{... | collective-permute-start | bytes 294920 | tf_op jit(solution)/shard_map/ppermute | solution.py:320
  114.1 16.4 %collective-permute-start.19 = (f32[192,128]{1,0:T(8,128)S(1)}, f32[192,128]{1,0:T(8,128)S(1)}, u32[]{:S(2)}, u32[]{:S(2)}) collective-permute-start(f32[192,128]{1,0:T(8,128)S(1)} %right_sum.2.refs_0_), channel_id=1, source_target_pairs={{0,20},{4,16},{8,28},{12,24},{16,4},{20,0},{24,12},{28,8},{1,21},{... | collective-permute-start | bytes 294920 | tf_op jit(solution)/shard_map/ppermute | solution.py:320
  117.7 12.8 %collective-permute-start.20 = (f32[192,128]{1,0:T(8,128)S(1)}, f32[192,128]{1,0:T(8,128)S(1)}, u32[]{:S(2)}, u32[]{:S(2)}) collective-permute-start(f32[192,128]{1,0:T(8,128)S(1)} %right_sum.2.refs_0_), channel_id=1, source_target_pairs={{0,24},{4,28},{8,16},{12,20},{16,8},{20,12},{24,0},{28,4},{1,25},{... | collective-permute-start | bytes 294920 | tf_op jit(solution)/shard_map/ppermute | solution.py:320
  119.1 11.4 %collective-permute-start.21 = (f32[192,128]{1,0:T(8,128)S(1)}, f32[192,128]{1,0:T(8,128)S(1)}, u32[]{:S(2)}, u32[]{:S(2)}) collective-permute-start(f32[192,128]{1,0:T(8,128)S(1)} %right_sum.2.refs_0_), channel_id=1, source_target_pairs={{0,28},{4,24},{8,20},{12,16},{16,12},{20,8},{24,4},{28,0},{1,29},{... | collective-permute-start | bytes 294920 | tf_op jit(solution)/shard_map/ppermute | solution.py:320
  134.7 9.4 %collective-permute-start.22 = (f32[96,768]{1,0:T(8,128)S(1)}, f32[96,768]{1,0:T(8,128)S(1)}, u32[]{:S(2)}, u32[]{:S(2)}) collective-permute-start(f32[96,768]{1,0:T(8,128)S(1)} %get-tuple-element.149), channel_id=1, source_target_pairs={{0,3},{1,2},{2,1},{3,0},{4,7},{5,6},{6,5},{7,4},{8,11},{9,10},{10,... | collective-permute-start | bytes 884744 | tf_op jit(solution)/shard_map/ppermute | solution.py:320
  134.8 13.7 %collective-permute-start.23 = (f32[96,768]{1,0:T(8,128)S(1)}, f32[96,768]{1,0:T(8,128)S(1)}, u32[]{:S(2)}, u32[]{:S(2)}) collective-permute-start(f32[96,768]{1,0:T(8,128)S(1)} %get-tuple-element.150), channel_id=1, source_target_pairs={{0,2},{1,3},{2,0},{3,1},{4,6},{5,7},{6,4},{7,5},{8,10},{9,11},{10,... | collective-permute-start | bytes 884744 | tf_op jit(solution)/shard_map/ppermute | solution.py:320
  139.5 9.0 %collective-permute-start.24 = (f32[96,768]{1,0:T(8,128)S(1)}, f32[96,768]{1,0:T(8,128)S(1)}, u32[]{:S(2)}, u32[]{:S(2)}) collective-permute-start(f32[96,768]{1,0:T(8,128)S(1)} %get-tuple-element.151), channel_id=1, source_target_pairs={{0,1},{1,0},{2,3},{3,2},{4,5},{5,4},{6,7},{7,6},{8,9},{9,8},{10,11... | collective-permute-start | bytes 884744 | tf_op jit(solution)/shard_map/ppermute | solution.py:320
  181.1 9.9 %collective-permute-start.26 = (f32[96,768]{1,0:T(8,128)S(1)}, f32[96,768]{1,0:T(8,128)S(1)}, u32[]{:S(2)}, u32[]{:S(2)}) collective-permute-start(f32[96,768]{1,0:T(8,128)S(1)} %basis.3.first_ref), channel_id=1, source_target_pairs={{0,2},{1,3},{2,0},{3,1},{4,6},{5,7},{6,4},{7,5},{8,10},{9,11},{10,... | collective-permute-start | bytes 884744 | tf_op jit(solution)/shard_map/ppermute | solution.py:320
  182.5 20.2 %collective-permute-start.35 = (f32[288,512]{1,0:T(8,128)S(1)}, f32[288,512]{1,0:T(8,128)S(1)}, u32[]{:S(2)}, u32[]{:S(2)}) collective-permute-start(f32[288,512]{1,0:T(8,128)S(1)} %get-tuple-element.162), channel_id=1, source_target_pairs={{0,3},{1,2},{2,1},{3,0},{4,7},{5,6},{6,5},{7,4},{8,11},{9,10},{10,... | collective-permute-start | bytes 1769480 | tf_op jit(solution)/shard_map/ppermute | solution.py:320
  195.4 7.8 %collective-permute-start.28 = (f32[192,128]{1,0:T(8,128)S(1)}, f32[192,128]{1,0:T(8,128)S(1)}, u32[]{:S(2)}, u32[]{:S(2)}) collective-permute-start(f32[192,128]{1,0:T(8,128)S(1)} %get-tuple-element.155), channel_id=1, source_target_pairs={{0,4},{4,0},{8,12},{12,8},{16,20},{20,16},{24,28},{28,24},{1,5},{5... | collective-permute-start | bytes 294920 | tf_op jit(solution)/shard_map/ppermute | solution.py:320
  196.2 9.5 %collective-permute-start.29 = (f32[192,128]{1,0:T(8,128)S(1)}, f32[192,128]{1,0:T(8,128)S(1)}, u32[]{:S(2)}, u32[]{:S(2)}) collective-permute-start(f32[192,128]{1,0:T(8,128)S(1)} %get-tuple-element.156), channel_id=1, source_target_pairs={{0,8},{4,12},{8,0},{12,4},{16,24},{20,28},{24,16},{28,20},{1,9},{5... | collective-permute-start | bytes 294920 | tf_op jit(solution)/shard_map/ppermute | solution.py:320
  196.7 11.4 %collective-permute-start.30 = (f32[192,128]{1,0:T(8,128)S(1)}, f32[192,128]{1,0:T(8,128)S(1)}, u32[]{:S(2)}, u32[]{:S(2)}) collective-permute-start(f32[192,128]{1,0:T(8,128)S(1)} %get-tuple-element.157), channel_id=1, source_target_pairs={{0,12},{4,8},{8,4},{12,0},{16,28},{20,24},{24,20},{28,16},{1,13},{... | collective-permute-start | bytes 294920 | tf_op jit(solution)/shard_map/ppermute | solution.py:320
  199.0 9.1 %collective-permute-start.31 = (f32[192,128]{1,0:T(8,128)S(1)}, f32[192,128]{1,0:T(8,128)S(1)}, u32[]{:S(2)}, u32[]{:S(2)}) collective-permute-start(f32[192,128]{1,0:T(8,128)S(1)} %get-tuple-element.158), channel_id=1, source_target_pairs={{0,16},{4,20},{8,24},{12,28},{16,0},{20,4},{24,8},{28,12},{1,17},{... | collective-permute-start | bytes 294920 | tf_op jit(solution)/shard_map/ppermute | solution.py:320
  202.7 13.5 %collective-permute-start.32 = (f32[192,128]{1,0:T(8,128)S(1)}, f32[192,128]{1,0:T(8,128)S(1)}, u32[]{:S(2)}, u32[]{:S(2)}) collective-permute-start(f32[192,128]{1,0:T(8,128)S(1)} %get-tuple-element.159), channel_id=1, source_target_pairs={{0,20},{4,16},{8,28},{12,24},{16,4},{20,0},{24,12},{28,8},{1,21},{... | collective-permute-start | bytes 294920 | tf_op jit(solution)/shard_map/ppermute | solution.py:320
  203.3 12.9 %collective-permute-start.33 = (f32[192,128]{1,0:T(8,128)S(1)}, f32[192,128]{1,0:T(8,128)S(1)}, u32[]{:S(2)}, u32[]{:S(2)}) collective-permute-start(f32[192,128]{1,0:T(8,128)S(1)} %get-tuple-element.160), channel_id=1, source_target_pairs={{0,24},{4,28},{8,16},{12,20},{16,8},{20,12},{24,0},{28,4},{1,25},{... | collective-permute-start | bytes 294920 | tf_op jit(solution)/shard_map/ppermute | solution.py:320
  205.6 10.6 %collective-permute-start.34 = (f32[192,128]{1,0:T(8,128)S(1)}, f32[192,128]{1,0:T(8,128)S(1)}, u32[]{:S(2)}, u32[]{:S(2)}) collective-permute-start(f32[192,128]{1,0:T(8,128)S(1)} %get-tuple-element.161), channel_id=1, source_target_pairs={{0,28},{4,24},{8,20},{12,16},{16,12},{20,8},{24,4},{28,0},{1,29},{... | collective-permute-start | bytes 294920 | tf_op jit(solution)/shard_map/ppermute | solution.py:320
  216.3 9.1 %collective-permute-start.36 = (f32[192,128]{1,0:T(8,128)S(1)}, f32[192,128]{1,0:T(8,128)S(1)}, u32[]{:S(2)}, u32[]{:S(2)}) collective-permute-start(f32[192,128]{1,0:T(8,128)S(1)} %right_sum.3.refs_0_), channel_id=1, source_target_pairs={{0,4},{4,0},{8,12},{12,8},{16,20},{20,16},{24,28},{28,24},{1,5},{5... | collective-permute-start | bytes 294920 | tf_op jit(solution)/shard_map/ppermute | solution.py:320
  216.8 10.0 %collective-permute-start.37 = (f32[192,128]{1,0:T(8,128)S(1)}, f32[192,128]{1,0:T(8,128)S(1)}, u32[]{:S(2)}, u32[]{:S(2)}) collective-permute-start(f32[192,128]{1,0:T(8,128)S(1)} %right_sum.3.refs_0_), channel_id=1, source_target_pairs={{0,8},{4,12},{8,0},{12,4},{16,24},{20,28},{24,16},{28,20},{1,9},{5... | collective-permute-start | bytes 294920 | tf_op jit(solution)/shard_map/ppermute | solution.py:320
  221.6 8.3 %collective-permute-start.38 = (f32[192,128]{1,0:T(8,128)S(1)}, f32[192,128]{1,0:T(8,128)S(1)}, u32[]{:S(2)}, u32[]{:S(2)}) collective-permute-start(f32[192,128]{1,0:T(8,128)S(1)} %right_sum.3.refs_0_), channel_id=1, source_target_pairs={{0,12},{4,8},{8,4},{12,0},{16,28},{20,24},{24,20},{28,16},{1,13},{... | collective-permute-start | bytes 294920 | tf_op jit(solution)/shard_map/ppermute | solution.py:320
  222.1 14.7 %collective-permute-start.39 = (f32[192,128]{1,0:T(8,128)S(1)}, f32[192,128]{1,0:T(8,128)S(1)}, u32[]{:S(2)}, u32[]{:S(2)}) collective-permute-start(f32[192,128]{1,0:T(8,128)S(1)} %right_sum.3.refs_0_), channel_id=1, source_target_pairs={{0,16},{4,20},{8,24},{12,28},{16,0},{20,4},{24,8},{28,12},{1,17},{... | collective-permute-start | bytes 294920 | tf_op jit(solution)/shard_map/ppermute | solution.py:320
  224.1 15.2 %collective-permute-start.40 = (f32[192,128]{1,0:T(8,128)S(1)}, f32[192,128]{1,0:T(8,128)S(1)}, u32[]{:S(2)}, u32[]{:S(2)}) collective-permute-start(f32[192,128]{1,0:T(8,128)S(1)} %right_sum.3.refs_0_), channel_id=1, source_target_pairs={{0,20},{4,16},{8,28},{12,24},{16,4},{20,0},{24,12},{28,8},{1,21},{... | collective-permute-start | bytes 294920 | tf_op jit(solution)/shard_map/ppermute | solution.py:320
  225.4 14.0 %collective-permute-start.41 = (f32[192,128]{1,0:T(8,128)S(1)}, f32[192,128]{1,0:T(8,128)S(1)}, u32[]{:S(2)}, u32[]{:S(2)}) collective-permute-start(f32[192,128]{1,0:T(8,128)S(1)} %right_sum.3.refs_0_), channel_id=1, source_target_pairs={{0,24},{4,28},{8,16},{12,20},{16,8},{20,12},{24,0},{28,4},{1,25},{... | collective-permute-start | bytes 294920 | tf_op jit(solution)/shard_map/ppermute | solution.py:320
  226.8 12.5 %collective-permute-start.42 = (f32[192,128]{1,0:T(8,128)S(1)}, f32[192,128]{1,0:T(8,128)S(1)}, u32[]{:S(2)}, u32[]{:S(2)}) collective-permute-start(f32[192,128]{1,0:T(8,128)S(1)} %right_sum.3.refs_0_), channel_id=1, source_target_pairs={{0,28},{4,24},{8,20},{12,16},{16,12},{20,8},{24,4},{28,0},{1,29},{... | collective-permute-start | bytes 294920 | tf_op jit(solution)/shard_map/ppermute | solution.py:320
  242.3 23.3 %collective-permute-start.46 = (bf16[576,512]{1,0:T(8,128)(2,1)}, bf16[576,512]{1,0:T(8,128)(2,1)}, u32[]{:S(2)}, u32[]{:S(2)}) collective-permute-start(bf16[576,512]{1,0:T(8,128)(2,1)} %get-tuple-element.175.refs_0_), channel_id=1, source_target_pairs={{0,8},{4,12},{8,16},{12,20},{16,24},{20,28},{24,0},{28,4},{1,9},{5... | collective-permute-start | bytes 1769480 | tf_op jit(solution)/shard_map/ppermute | solution.py:563
  246.1 19.5 %collective-permute-start.47 = (bf16[576,512]{1,0:T(8,128)(2,1)}, bf16[576,512]{1,0:T(8,128)(2,1)}, u32[]{:S(2)}, u32[]{:S(2)}) collective-permute-start(bf16[576,512]{1,0:T(8,128)(2,1)} %get-tuple-element.175.refs_0_), channel_id=1, source_target_pairs={{0,4},{4,0},{8,12},{12,8},{16,20},{20,16},{24,28},{28,24},{1,5},{5... | collective-permute-start | bytes 1769480 | tf_op jit(solution)/shard_map/ppermute | solution.py:320
  247.3 27.0 %collective-permute-start.48 = (bf16[576,512]{1,0:T(8,128)(2,1)}, bf16[576,512]{1,0:T(8,128)(2,1)}, u32[]{:S(2)}, u32[]{:S(2)}) collective-permute-start(bf16[576,512]{1,0:T(8,128)(2,1)} %get-tuple-element.182.refs_1_), channel_id=1, source_target_pairs={{0,8},{4,12},{8,16},{12,20},{16,24},{20,28},{24,0},{28,4},{1,9},{5... | collective-permute-start | bytes 1769480 | tf_op jit(solution)/shard_map/ppermute | solution.py:563
  247.9 27.4 %collective-permute-start.49 = (bf16[576,512]{1,0:T(8,128)(2,1)}, bf16[576,512]{1,0:T(8,128)(2,1)}, u32[]{:S(2)}, u32[]{:S(2)}) collective-permute-start(bf16[576,512]{1,0:T(8,128)(2,1)} %get-tuple-element.182.refs_1_), channel_id=1, source_target_pairs={{0,4},{4,0},{8,12},{12,8},{16,20},{20,16},{24,28},{28,24},{1,5},{5... | collective-permute-start | bytes 1769480 | tf_op jit(solution)/shard_map/ppermute | solution.py:320
  256.7 8.9 %collective-permute-start.45 = (f32[64,512]{1,0:T(8,128)S(1)}, f32[64,512]{1,0:T(8,128)S(1)}, u32[]{:S(2)}, u32[]{:S(2)}) collective-permute-start(f32[64,512]{1,0:T(8,128)S(1)} %constant_dynamic-slice_fusion), channel_id=1, source_target_pairs={{0,3},{1,2},{2,1},{3,0},{4,7},{5,6},{6,5},{7,4},{8,11},{9,10},{10,... | collective-permute-start | bytes 393224 | tf_op jit(solution)/shard_map/ppermute | solution.py:320
  265.6 19.9 %collective-permute-start.50 = (bf16[576,512]{1,0:T(8,128)(2,1)}, bf16[576,512]{1,0:T(8,128)(2,1)S(1)}, u32[]{:S(2)}, u32[]{:S(2)}) collective-permute-start(bf16[576,512]{1,0:T(8,128)(2,1)} %collective-permute-done.46.refs_2_), channel_id=1, source_target_pairs={{0,8},{4,12},{8,16},{12,20},{16,24},{20,28},{24,0},{28,4},{1,9},{5... | collective-permute-start | bytes 1769480 | tf_op jit(solution)/shard_map/ppermute | solution.py:563
  265.7 22.2 %collective-permute-start.51 = (bf16[576,512]{1,0:T(8,128)(2,1)}, bf16[576,512]{1,0:T(8,128)(2,1)S(1)}, u32[]{:S(2)}, u32[]{:S(2)}) collective-permute-start(bf16[576,512]{1,0:T(8,128)(2,1)} %collective-permute-done.46.refs_2_), channel_id=1, source_target_pairs={{0,4},{4,0},{8,12},{12,8},{16,20},{20,16},{24,28},{28,24},{1,5},{5... | collective-permute-start | bytes 1769480 | tf_op jit(solution)/shard_map/ppermute | solution.py:320
  275.3 22.8 %collective-permute-start.52 = (bf16[576,512]{1,0:T(8,128)(2,1)}, bf16[576,512]{1,0:T(8,128)(2,1)S(1)}, u32[]{:S(2)}, u32[]{:S(2)}) collective-permute-start(bf16[576,512]{1,0:T(8,128)(2,1)} %collective-permute-done.48.refs_4_), channel_id=1, source_target_pairs={{0,8},{4,12},{8,16},{12,20},{16,24},{20,28},{24,0},{28,4},{1,9},{5... | collective-permute-start | bytes 1769480 | tf_op jit(solution)/shard_map/ppermute | solution.py:563
  276.0 24.5 %collective-permute-start.53 = (bf16[576,512]{1,0:T(8,128)(2,1)}, bf16[576,512]{1,0:T(8,128)(2,1)S(1)}, u32[]{:S(2)}, u32[]{:S(2)}) collective-permute-start(bf16[576,512]{1,0:T(8,128)(2,1)} %collective-permute-done.48.refs_4_), channel_id=1, source_target_pairs={{0,4},{4,0},{8,12},{12,8},{16,20},{20,16},{24,28},{28,24},{1,5},{5... | collective-permute-start | bytes 1769480 | tf_op jit(solution)/shard_map/ppermute | solution.py:320
  287.9 27.9 %collective-permute-start.54 = (bf16[576,512]{1,0:T(8,128)(2,1)S(1)}, bf16[576,512]{1,0:T(8,128)(2,1)S(1)}, u32[]{:S(2)}, u32[]{:S(2)}) collective-permute-start(bf16[576,512]{1,0:T(8,128)(2,1)S(1)} %collective-permute-done.50.refs_6_), channel_id=1, source_target_pairs={{0,8},{4,12},{8,16},{12,20},{16,24},{20,28},{24,0},{28,4},{1,9},{5... | collective-permute-start | bytes 1769480 | tf_op jit(solution)/shard_map/ppermute | solution.py:563
  288.5 27.2 %collective-permute-start.55 = (bf16[576,512]{1,0:T(8,128)(2,1)S(1)}, bf16[576,512]{1,0:T(8,128)(2,1)S(1)}, u32[]{:S(2)}, u32[]{:S(2)}) collective-permute-start(bf16[576,512]{1,0:T(8,128)(2,1)S(1)} %collective-permute-done.50.refs_6_), channel_id=1, source_target_pairs={{0,4},{4,0},{8,12},{12,8},{16,20},{20,16},{24,28},{28,24},{1,5},{5... | collective-permute-start | bytes 1769480 | tf_op jit(solution)/shard_map/ppermute | solution.py:320
  300.5 21.1 %collective-permute-start.56 = (bf16[576,512]{1,0:T(8,128)(2,1)S(1)}, bf16[576,512]{1,0:T(8,128)(2,1)S(1)}, u32[]{:S(2)}, u32[]{:S(2)}) collective-permute-start(bf16[576,512]{1,0:T(8,128)(2,1)S(1)} %collective-permute-done.52.refs_8_), channel_id=1, source_target_pairs={{0,8},{4,12},{8,16},{12,20},{16,24},{20,28},{24,0},{28,4},{1,9},{5... | collective-permute-start | bytes 1769480 | tf_op jit(solution)/shard_map/ppermute | solution.py:563
  301.2 22.4 %collective-permute-start.57 = (bf16[576,512]{1,0:T(8,128)(2,1)S(1)}, bf16[576,512]{1,0:T(8,128)(2,1)S(1)}, u32[]{:S(2)}, u32[]{:S(2)}) collective-permute-start(bf16[576,512]{1,0:T(8,128)(2,1)S(1)} %collective-permute-done.52.refs_8_), channel_id=1, source_target_pairs={{0,4},{4,0},{8,12},{12,8},{16,20},{20,16},{24,28},{28,24},{1,5},{5... | collective-permute-start | bytes 1769480 | tf_op jit(solution)/shard_map/ppermute | solution.py:320
  323.6 15.2 %collective-permute-start.59 = (bf16[576,512]{1,0:T(8,128)(2,1)S(1)}, bf16[576,512]{1,0:T(8,128)(2,1)S(1)}, u32[]{:S(2)}, u32[]{:S(2)}) collective-permute-start(bf16[576,512]{1,0:T(8,128)(2,1)S(1)} %collective-permute-done.57.refs_1_), channel_id=1, source_target_pairs={{0,8},{4,12},{8,16},{12,20},{16,24},{20,28},{24,0},{28,4},{1,9},{5... | collective-permute-start | bytes 1769480 | tf_op jit(solution)/shard_map/ppermute | solution.py:568
  324.4 14.4 %collective-permute-start.58 = (bf16[576,512]{1,0:T(8,128)(2,1)S(1)}, bf16[576,512]{1,0:T(8,128)(2,1)S(1)}, u32[]{:S(2)}, u32[]{:S(2)}) collective-permute-start(bf16[576,512]{1,0:T(8,128)(2,1)S(1)} %collective-permute-done.54.refs_0_), channel_id=1, source_target_pairs={{0,4},{4,0},{8,12},{12,8},{16,20},{20,16},{24,28},{28,24},{1,5},{5... | collective-permute-start | bytes 1769480 | tf_op jit(solution)/shard_map/ppermute | solution.py:320
  (25 other events, 257.1 us)

commit v11 on v9

--- a/solution.py
+++ b/solution.py
@@ -547,7 +547,7 @@
     held, beside = list(block), [None, None]
     pieces = [(block[half], half, 0) for half in range(2)]
     errors, flat, weights = (), (), ()
-    jobs = {1: "update", 2: "update", 3: "update", 4: "update", 5: "flat place", 2 * stages - 2: "place", 2 * stages - 1: "place"}
+    jobs = {2: "update", 3: "update update", 4: "update", 5: "flat place", 2 * stages - 2: "place", 2 * stages - 1: "place"}
     near = spread(near, "tp", tps)
     updated = 0
     for step in range(2 * stages):

time: 337 us -> 336 us (level)
    ppermute x53, waiting for transfers between devices: 82.3 us -> 87.8 us  [swap(): lax.ppermute(x, axis, [(index, index ^ offset) for index in range(size)])]
    ppermute x6, waiting for transfers between devices: 14.8 us -> 9.36 us  [local(): held[half] = lax.ppermute(here, 'rep', ring)]
  transfers between devices with their start and end apart: 60 -> 60, of which waited for: 28 -> 29; matrix products, arithmetic and copies ran while one was open for 1% -> 1% of each run, Pallas kernels for 17% -> 17%
where the time goes in v11:
time: 336 us; the launch traced here: 335 us
  waiting for transfers between devices  109 us (32%)
  Pallas kernels  76.9 us (23%)
  starting transfers between devices  69.5 us (21%)
  blocking collectives  59.9 us (18%)
  local copies, waits for them, and re-layouts  16.6 us (5%)
    ppermute x53, waiting for transfers between devices, swap(): lax.ppermute(x, axis, [(index, index ^ offset) for index in range(size)])  87.8 us
    pallas_call x17, Pallas kernels, grid_call(): pl.pallas_call(kernel, grid_spec=pltpu.PrefetchScalarGridSpec(num_scalar_...  68.8 us
    ppermute x53, starting transfers between devices, swap(): lax.ppermute(x, axis, [(index, index ^ offset) for index in range(size)])  61.5 us
    all_to_all x4, blocking collectives, local(): lax.all_to_all(parts, 'rep', split_axis=0, concat_axis=0, tiled=True)  59.9 us
    unnamed x42, local copies, waits for them, and re-layouts  15.7 us
    ppermute x1, waiting for transfers between devices, local(): beside[half] = lax.ppermute(beside[half], 'rep', ring)  11.6 us
    ppermute x6, waiting for transfers between devices, local(): held[half] = lax.ppermute(here, 'rep', ring)  9.36 us
    pallas_call x9, Pallas kernels, whole_call(): pl.pallas_call(kernel, in_specs=specs, out_specs=[out_spec] * len(out_sha...  8.17 us
  transfers between devices with their start and end apart: 60, of which 29 were waited for; matrix products, arithmetic and copies ran while one was open for 1% of the time, Pallas kernels for 17%

profile of v11, /device:TPU:0, one launch (start us, length us, event | category | flops | bytes accessed | tf_op | source)
XLA Modules:
  0.0 335.3 jit_solution(9628127395674454168)
XLA Ops:
  1.8 7.2 %first_left.2 = (bf16[6,768,512]{2,1,0:T(8,128)(2,1)S(1)}, bf16[6,768,512]{2,1,0:T(8,128)(2,1)S(1)}, f32[96,768]{1,0:T(8,128)}, f32[96,768]{1,0:T(8,128)}) custom-call(s32[2]{0:T(128)S(1)} %pad_add_fusion.ids_ref, bf16[1,12,768,512]{3,2,1,0:T(8,128)(2,1)} %grads_ref.3, f32[1,12,768,512]{3,2,1,0:T(8,128)} %error_ref.3, f32[12,32,512]{2,1,0:T(8,128)S(1)} %copy-done.11), custom_call_target="tpu_custom_call" | custom-call | flops 452984832 | bytes 23592960 | tf_op jit(solution)/shard_map/first_left/pallas_call | solution.py:302
  13.5 2.9 collective-permute-start.1
  16.4 7.1 %first_left.3 = (bf16[6,768,512]{2,1,0:T(8,128)(2,1)S(1)}, bf16[6,768,512]{2,1,0:T(8,128)(2,1)S(1)}, f32[96,768]{1,0:T(8,128)S(1)}, f32[96,768]{1,0:T(8,128)}) custom-call(s32[2]{0:T(128)S(1)} %pad_add_fusion.ids_ref, bf16[1,12,768,512]{3,2,1,0:T(8,128)(2,1)} %grads_ref.3, f32[1,12,768,512]{3,2,1,0:T(8,128)} %error_ref.3, f32[12,32,512]{2,1,0:T(8,128)S(1)} %copy-done.12), custom_call_target="tpu_custom_call" | custom-call | flops 452984832 | bytes 23592960 | tf_op jit(solution)/shard_map/first_left/pallas_call | solution.py:302
  28.1 2.4 multiply_subtract_fusion
  30.5 6.4 %collective-permute-done.refs_1_ = f32[96,768]{1,0:T(8,128)} collective-permute-done((f32[96,768]{1,0:T(8,128)}, f32[96,768]{1,0:T(8,128)}, u32[]{:S(2)}, u32[]{:S(2)}) %collective-permute-start) | collective-permute-done | bytes 294944 | tf_op jit(solution)/shard_map/ppermute | solution.py:320
  38.0 16.6 %all_to_all.20.parts_ref = f32[8,72,128]{2,1,0:T(8,128)S(1)} all-to-all(f32[8,72,128]{2,1,0:T(8,128)S(1)} %bitcast.23), channel_id=1, replica_groups=mesh['rep'=8,'tp'=4] {'rep'}, dimensions={0} | all-to-all | bytes 589824 | tf_op jit(solution)/shard_map/all_to_all | solution.py:405
  54.7 13.0 %all_to_all.21 = f32[8,72,128]{2,1,0:T(8,128)S(1)} all-to-all(f32[8,72,128]{2,1,0:T(8,128)S(1)} %left_sum.2), channel_id=1, replica_groups=mesh['rep'=8,'tp'=4] {'rep'}, dimensions={0} | all-to-all | bytes 589824 | tf_op jit(solution)/shard_map/all_to_all | solution.py:407
  72.0 2.8 right_near.2.refs_0_
  74.8 4.8 %collective-permute-done.4.first_ref = f32[96,768]{1,0:T(8,128)S(1)} collective-permute-done((f32[96,768]{1,0:T(8,128)S(1)}, f32[96,768]{1,0:T(8,128)S(1)}, u32[]{:S(2)}, u32[]{:S(2)}) %collective-permute-start.4) | collective-permute-done | bytes 294944 | tf_op jit(solution)/shard_map/ppermute | solution.py:320
  81.2 2.9 right_far.2
  84.8 2.4 collective-permute-start.11
  87.1 2.4 collective-permute-start.12
  92.4 4.9 %collective-permute-done.10.refs_5_ = f32[192,128]{1,0:T(8,128)S(1)} collective-permute-done((f32[192,128]{1,0:T(8,128)S(1)}, f32[192,128]{1,0:T(8,128)S(1)}, u32[]{:S(2)}, u32[]{:S(2)}) %collective-permute-start.10) | collective-permute-done | bytes 98336 | tf_op jit(solution)/shard_map/ppermute | solution.py:320
  99.4 4.4 %collective-permute-done.8.refs_3_ = f32[192,128]{1,0:T(8,128)S(1)} collective-permute-done((f32[192,128]{1,0:T(8,128)S(1)}, f32[192,128]{1,0:T(8,128)S(1)}, u32[]{:S(2)}, u32[]{:S(2)}) %collective-permute-start.8) | collective-permute-done | bytes 98336 | tf_op jit(solution)/shard_map/ppermute | solution.py:320
  109.1 3.6 %collective-permute-start.19 = (f32[192,128]{1,0:T(8,128)S(1)}, f32[192,128]{1,0:T(8,128)S(1)}, u32[]{:S(2)}, u32[]{:S(2)}) collective-permute-start(f32[192,128]{1,0:T(8,128)S(1)} %right_sum.2.refs_0_), channel_id=1, source_target_pairs={{0,20},{4,16},{8,28},{12,24},{16,4},{20,0},{24,12},{28,8},{1,21},{... | collective-permute-start | bytes 294920 | tf_op jit(solution)/shard_map/ppermute | solution.py:320
  116.2 6.2 %collective-permute-done.18.refs_4_ = f32[192,128]{1,0:T(8,128)S(1)} collective-permute-done((f32[192,128]{1,0:T(8,128)S(1)}, f32[192,128]{1,0:T(8,128)S(1)}, u32[]{:S(2)}, u32[]{:S(2)}) %collective-permute-start.18) | collective-permute-done | bytes 98336 | tf_op jit(solution)/shard_map/ppermute | solution.py:320
  122.5 3.0 collective-permute-done.19.refs_5_
  125.5 4.2 %left.3 = (f32[96,768]{1,0:T(8,128)S(1)}, f32[96,768]{1,0:T(8,128)S(1)}) custom-call(s32[2]{0:T(128)S(1)} %pad_add_fusion.ids_ref, bf16[6,768,512]{2,1,0:T(8,128)(2,1)S(1)} %bitcast.13, bf16[6,768,512]{2,1,0:T(8,128)(2,1)S(1)} %copy-done.2, f32[192,128]{1,0:T(8,128)S(1)} %right_sum.2.refs_0_, f32[192,128]{1,0:T(8,128)S(1)} %collective-permute-done.15.refs_1_, ...), custom_call_target="tpu_custom_call" | custom-call | flops 452984832 | bytes 23592960 | tf_op jit(solution)/shard_map/left/pallas_call | solution.py:302
  130.4 4.2 %left.2 = (f32[96,768]{1,0:T(8,128)S(1)}, f32[96,768]{1,0:T(8,128)S(1)}) custom-call(s32[2]{0:T(128)S(1)} %pad_add_fusion.ids_ref, bf16[6,768,512]{2,1,0:T(8,128)(2,1)S(1)} %bitcast.19, bf16[6,768,512]{2,1,0:T(8,128)(2,1)S(1)} %copy-done.6, f32[192,128]{1,0:T(8,128)S(1)} %right_sum.2.refs_0_, f32[192,128]{1,0:T(8,128)S(1)} %collective-permute-done.15.refs_1_, ...), custom_call_target="tpu_custom_call" | custom-call | flops 452984832 | bytes 23592960 | tf_op jit(solution)/shard_map/left/pallas_call | solution.py:302
  135.9 3.2 collective-permute-done.22.refs_1_
  139.0 4.6 %collective-permute-done.23.refs_2_ = f32[96,768]{1,0:T(8,128)S(1)} collective-permute-done((f32[96,768]{1,0:T(8,128)S(1)}, f32[96,768]{1,0:T(8,128)S(1)}, u32[]{:S(2)}, u32[]{:S(2)}) %collective-permute-start.23) | collective-permute-done | bytes 294944 | tf_op jit(solution)/shard_map/ppermute | solution.py:320
  143.8 17.3 %all_to_all.22.parts_ref = f32[8,72,128]{2,1,0:T(8,128)S(1)} all-to-all(f32[8,72,128]{2,1,0:T(8,128)S(1)} %bitcast.24), channel_id=1, replica_groups=mesh['rep'=8,'tp'=4] {'rep'}, dimensions={0} | all-to-all | bytes 589824 | tf_op jit(solution)/shard_map/all_to_all | solution.py:405
  161.0 13.0 %all_to_all.23 = f32[8,72,128]{2,1,0:T(8,128)S(1)} all-to-all(f32[8,72,128]{2,1,0:T(8,128)S(1)} %left_sum.3), channel_id=1, replica_groups=mesh['rep'=8,'tp'=4] {'rep'}, dimensions={0} | all-to-all | bytes 589824 | tf_op jit(solution)/shard_map/all_to_all | solution.py:407
  177.9 2.8 right_near.3.refs_0_
  180.7 5.2 %collective-permute-done.26.first_ref = f32[96,768]{1,0:T(8,128)S(1)} collective-permute-done((f32[96,768]{1,0:T(8,128)S(1)}, f32[96,768]{1,0:T(8,128)S(1)}, u32[]{:S(2)}, u32[]{:S(2)}) %collective-permute-start.26) | collective-permute-done | bytes 294944 | tf_op jit(solution)/shard_map/ppermute | solution.py:320
  187.5 2.9 right_far.3
  194.7 3.0 collective-permute-done.35.refs_11_
  198.3 2.4 collective-permute-start.33
  200.7 2.4 collective-permute-start.34
  203.1 8.1 %collective-permute-done.32.refs_5_ = f32[192,128]{1,0:T(8,128)S(1)} collective-permute-done((f32[192,128]{1,0:T(8,128)S(1)}, f32[192,128]{1,0:T(8,128)S(1)}, u32[]{:S(2)}, u32[]{:S(2)}) %collective-permute-start.32) | collective-permute-done | bytes 98336 | tf_op jit(solution)/shard_map/ppermute | solution.py:320
  211.8 4.7 %collective-permute-start.37 = (f32[192,128]{1,0:T(8,128)S(1)}, f32[192,128]{1,0:T(8,128)S(1)}, u32[]{:S(2)}, u32[]{:S(2)}) collective-permute-start(f32[192,128]{1,0:T(8,128)S(1)} %right_sum.3.refs_0_), channel_id=1, source_target_pairs={{0,8},{4,12},{8,0},{12,4},{16,24},{20,28},{24,16},{28,20},{1,9},{5... | collective-permute-start | bytes 294920 | tf_op jit(solution)/shard_map/ppermute | solution.py:320
  221.9 2.9 collective-permute-start.42
  224.9 7.0 %collective-permute-done.39.refs_4_ = f32[192,128]{1,0:T(8,128)S(1)} collective-permute-done((f32[192,128]{1,0:T(8,128)S(1)}, f32[192,128]{1,0:T(8,128)S(1)}, u32[]{:S(2)}, u32[]{:S(2)}) %collective-permute-start.39) | collective-permute-done | bytes 98336 | tf_op jit(solution)/shard_map/ppermute | solution.py:320
  231.9 2.5 collective-permute-done.40.refs_5_
  234.4 2.9 late_rows.1
  237.3 3.8 %collective-permute-start.46 = (bf16[576,512]{1,0:T(8,128)(2,1)}, bf16[576,512]{1,0:T(8,128)(2,1)}, u32[]{:S(2)}, u32[]{:S(2)}) collective-permute-start(bf16[576,512]{1,0:T(8,128)(2,1)} %get-tuple-element.174.refs_0_), channel_id=1, source_target_pairs={{0,8},{4,12},{8,16},{12,20},{16,24},{20,28},{24,0},{28,4},{1,9},{5... | collective-permute-start | bytes 1769480 | tf_op jit(solution)/shard_map/ppermute | solution.py:562
  247.5 4.2 %collective-permute-done.44 = f32[64,512]{1,0:T(8,128)S(1)} collective-permute-done((f32[64,512]{1,0:T(8,128)S(1)}, f32[64,512]{1,0:T(8,128)S(1)}, u32[]{:S(2)}, u32[]{:S(2)}) %collective-permute-start.44) | collective-permute-done | bytes 131104 | tf_op jit(solution)/shard_map/ppermute | solution.py:320
  252.1 5.3 %collective-permute-done.45 = f32[64,512]{1,0:T(8,128)S(1)} collective-permute-done((f32[64,512]{1,0:T(8,128)S(1)}, f32[64,512]{1,0:T(8,128)S(1)}, u32[]{:S(2)}, u32[]{:S(2)}) %collective-permute-start.45) | collective-permute-done | bytes 131104 | tf_op jit(solution)/shard_map/ppermute | solution.py:320
  259.5 2.3 copy-done.4
  265.3 4.1 %update.4.refs_0_ = f32[1,12,768,512]{3,2,1,0:T(8,128)} custom-call(s32[2]{0:T(128)S(1)} %pad_add_fusion.ids_ref, f32[384,768]{1,0:T(8,128)S(1)} %pad_maximum_fusion.basis_ref, f32[384,512]{1,0:T(8,128)S(1)} %copy-done.8, bf16[6,768,512]{2,1,0:T(8,128)(2,1)S(1)} %copy-done.4, bf16[6,768,512]{2,1,0:T(8,128)(2,1)S(1)} %copy-done.7), custom_call_target="tpu_custom_call" | custom-call | flops 226492416 | bytes 9437184 | tf_op jit(solution)/shard_map/update/pallas_call | solution.py:302
  272.1 4.1 %update.5.refs_0_ = f32[1,12,768,512]{3,2,1,0:T(8,128)} custom-call(s32[2]{0:T(128)S(1)} %pad_add_fusion.ids_ref, f32[384,768]{1,0:T(8,128)S(1)} %pad_maximum_fusion.basis_ref, f32[384,512]{1,0:T(8,128)S(1)} %copy-done.8, bf16[6,768,512]{2,1,0:T(8,128)(2,1)S(1)} %copy-done.4, bf16[6,768,512]{2,1,0:T(8,128)(2,1)S(1)} %copy-done.7, ...), custom_call_target="tpu_custom_call", output_to_operand_aliasing={{}: (5, {})} | custom-call | flops 226492416 | bytes 9437184 | tf_op jit(solution)/shard_map/update/pallas_call | solution.py:302
  276.3 4.1 %update.6.refs_0_ = f32[1,12,768,512]{3,2,1,0:T(8,128)} custom-call(s32[2]{0:T(128)S(1)} %pad_add_fusion.ids_ref, f32[384,768]{1,0:T(8,128)S(1)} %pad_maximum_fusion.basis_ref, f32[384,512]{1,0:T(8,128)S(1)} %copy-done.8, bf16[6,768,512]{2,1,0:T(8,128)(2,1)S(1)} %bitcast.15, bf16[6,768,512]{2,1,0:T(8,128)(2,1)S(1)} %bitcast.17, ...), custom_call_target="tpu_custom_call", output_to_operand_aliasing={{}: (5, {})} | custom-call | flops 226492416 | bytes 9437184 | tf_op jit(solution)/shard_map/update/pallas_call | solution.py:302
  284.7 4.1 %update.7 = f32[1,12,768,512]{3,2,1,0:T(8,128)} custom-call(s32[2]{0:T(128)S(1)} %pad_add_fusion.ids_ref, f32[384,768]{1,0:T(8,128)S(1)} %pad_maximum_fusion.basis_ref, f32[384,512]{1,0:T(8,128)S(1)} %copy-done.8, bf16[6,768,512]{2,1,0:T(8,128)(2,1)S(1)} %bitcast.15, bf16[6,768,512]{2,1,0:T(8,128)(2,1)S(1)} %bitcast.17, ...), custom_call_target="tpu_custom_call", output_to_operand_aliasing={{}: (5, {})} | custom-call | flops 226492416 | bytes 9437184 | tf_op jit(solution)/shard_map/update/pallas_call | solution.py:302
  288.8 4.8 %collective-permute-done.52.refs_8_ = bf16[576,512]{1,0:T(8,128)(2,1)S(1)} collective-permute-done((bf16[576,512]{1,0:T(8,128)(2,1)}, bf16[576,512]{1,0:T(8,128)(2,1)S(1)}, u32[]{:S(2)}, u32[]{:S(2)}) %collective-permute-start.52) | collective-permute-done | bytes 589856 | tf_op jit(solution)/shard_map/ppermute | solution.py:562
  297.3 7.2 %place.4.refs_2_ = bf16[8,2,576,512]{3,2,1,0:T(8,128)(2,1)} custom-call(s32[2]{0:T(128)S(1)} %pad_add_fusion.ids_ref, bf16[576,512]{1,0:T(8,128)(2,1)} %get-tuple-element.174.refs_0_, bf16[576,512]{1,0:T(8,128)(2,1)} %get-tuple-element.180.refs_1_, bf16[576,512]{1,0:T(8,128)(2,1)} %collective-permute-done.46.refs_2_, ...), custom_call_target="tpu_custom_call" | custom-call | bytes 23592960 | tf_op jit(solution)/shard_map/place/pallas_call | solution.py:302
  304.6 6.1 %flat_rows.1 = (f32[288,2048]{1,0:T(8,128)}, f32[288,2048]{1,0:T(8,128)}) custom-call(s32[2]{0:T(128)S(1)} %pad_add_fusion.ids_ref, f32[384,768]{1,0:T(8,128)S(1)} %pad_maximum_fusion.basis_ref, f32[4,64,512]{2,1,0:T(8,128)S(1)} %pad_maximum_fusion.1.near_ref, f32[288,2048]{1,0:T(8,128)S(1)} %copy-done.9, f32[288,2048]{1,0:T(8,128)S(1)} %copy-done.10), custom_call_target="tpu_custom_call" | custom-call | flops 452984832 | bytes 9437184 | tf_op jit(solution)/shard_map/flat_rows/pallas_call | solution.py:302
  312.4 4.0 %collective-permute-done.56.refs_0_ = bf16[576,512]{1,0:T(8,128)(2,1)S(1)} collective-permute-done((bf16[576,512]{1,0:T(8,128)(2,1)S(1)}, bf16[576,512]{1,0:T(8,128)(2,1)S(1)}, u32[]{:S(2)}, u32[]{:S(2)}) %collective-permute-start.56) | collective-permute-done | bytes 589856 | tf_op jit(solution)/shard_map/ppermute | solution.py:562
  322.0 11.6 %collective-permute-done.59.refs_1_ = bf16[576,512]{1,0:T(8,128)(2,1)S(1)} collective-permute-done((bf16[576,512]{1,0:T(8,128)(2,1)S(1)}, bf16[576,512]{1,0:T(8,128)(2,1)S(1)}, u32[]{:S(2)}, u32[]{:S(2)}) %collective-permute-start.59) | collective-permute-done | bytes 589856 | tf_op jit(solution)/shard_map/ppermute | solution.py:567
  (153 shorter events, 82.2 us)
Async XLA Ops:
  13.5 17.0 %collective-permute-start.1 = (f32[96,768]{1,0:T(8,128)}, f32[96,768]{1,0:T(8,128)S(1)}, u32[]{:S(2)}, u32[]{:S(2)}) collective-permute-start(f32[96,768]{1,0:T(8,128)} %get-tuple-element.114), channel_id=1, source_target_pairs={{0,2},{1,3},{2,0},{3,1},{4,6},{5,7},{6,4},{7,5},{8,10},{9,11},{10,... | collective-permute-start | bytes 884744 | tf_op jit(solution)/shard_map/ppermute | solution.py:320
  27.9 9.0 %collective-permute-start = (f32[96,768]{1,0:T(8,128)}, f32[96,768]{1,0:T(8,128)}, u32[]{:S(2)}, u32[]{:S(2)}) collective-permute-start(f32[96,768]{1,0:T(8,128)} %get-tuple-element.120), channel_id=1, source_target_pairs={{0,3},{1,2},{2,1},{3,0},{4,7},{5,6},{6,5},{7,4},{8,11},{9,10},{10,... | collective-permute-start | bytes 884744 | tf_op jit(solution)/shard_map/ppermute | solution.py:320
  69.7 9.9 %collective-permute-start.4 = (f32[96,768]{1,0:T(8,128)S(1)}, f32[96,768]{1,0:T(8,128)S(1)}, u32[]{:S(2)}, u32[]{:S(2)}) collective-permute-start(f32[96,768]{1,0:T(8,128)S(1)} %basis.2.first_ref), channel_id=1, source_target_pairs={{0,2},{1,3},{2,0},{3,1},{4,6},{5,7},{6,4},{7,5},{8,10},{9,11},{10,... | collective-permute-start | bytes 884744 | tf_op jit(solution)/shard_map/ppermute | solution.py:320
  70.3 19.3 %collective-permute-start.13 = (f32[288,512]{1,0:T(8,128)S(1)}, f32[288,512]{1,0:T(8,128)S(1)}, u32[]{:S(2)}, u32[]{:S(2)}) collective-permute-start(f32[288,512]{1,0:T(8,128)S(1)} %get-tuple-element.136), channel_id=1, source_target_pairs={{0,1},{1,0},{2,3},{3,2},{4,5},{5,4},{6,7},{7,6},{8,9},{9,8},{10,11... | collective-permute-start | bytes 1769480 | tf_op jit(solution)/shard_map/ppermute | solution.py:320
  70.4 21.3 %collective-permute-start.14 = (f32[288,512]{1,0:T(8,128)S(1)}, f32[288,512]{1,0:T(8,128)S(1)}, u32[]{:S(2)}, u32[]{:S(2)}) collective-permute-start(f32[288,512]{1,0:T(8,128)S(1)} %get-tuple-element.137), channel_id=1, source_target_pairs={{0,2},{1,3},{2,0},{3,1},{4,6},{5,7},{6,4},{7,5},{8,10},{9,11},{10,... | collective-permute-start | bytes 1769480 | tf_op jit(solution)/shard_map/ppermute | solution.py:320
  84.1 13.2 %collective-permute-start.10 = (f32[192,128]{1,0:T(8,128)S(1)}, f32[192,128]{1,0:T(8,128)S(1)}, u32[]{:S(2)}, u32[]{:S(2)}) collective-permute-start(f32[192,128]{1,0:T(8,128)S(1)} %get-tuple-element.132), channel_id=1, source_target_pairs={{0,20},{4,16},{8,28},{12,24},{16,4},{20,0},{24,12},{28,8},{1,21},{... | collective-permute-start | bytes 294920 | tf_op jit(solution)/shard_map/ppermute | solution.py:320
  84.8 12.6 %collective-permute-start.11 = (f32[192,128]{1,0:T(8,128)S(1)}, f32[192,128]{1,0:T(8,128)S(1)}, u32[]{:S(2)}, u32[]{:S(2)}) collective-permute-start(f32[192,128]{1,0:T(8,128)S(1)} %get-tuple-element.133), channel_id=1, source_target_pairs={{0,24},{4,28},{8,16},{12,20},{16,8},{20,12},{24,0},{28,4},{1,25},{... | collective-permute-start | bytes 294920 | tf_op jit(solution)/shard_map/ppermute | solution.py:320
  87.1 12.2 %collective-permute-start.12 = (f32[192,128]{1,0:T(8,128)S(1)}, f32[192,128]{1,0:T(8,128)S(1)}, u32[]{:S(2)}, u32[]{:S(2)}) collective-permute-start(f32[192,128]{1,0:T(8,128)S(1)} %get-tuple-element.134), channel_id=1, source_target_pairs={{0,28},{4,24},{8,20},{12,16},{16,12},{20,8},{24,4},{28,0},{1,29},{... | collective-permute-start | bytes 294920 | tf_op jit(solution)/shard_map/ppermute | solution.py:320
  89.5 9.8 %collective-permute-start.6 = (f32[192,128]{1,0:T(8,128)S(1)}, f32[192,128]{1,0:T(8,128)S(1)}, u32[]{:S(2)}, u32[]{:S(2)}) collective-permute-start(f32[192,128]{1,0:T(8,128)S(1)} %get-tuple-element.128), channel_id=1, source_target_pairs={{0,4},{4,0},{8,12},{12,8},{16,20},{20,16},{24,28},{28,24},{1,5},{5... | collective-permute-start | bytes 294920 | tf_op jit(solution)/shard_map/ppermute | solution.py:320
  105.0 7.7 %collective-permute-start.15 = (f32[192,128]{1,0:T(8,128)S(1)}, f32[192,128]{1,0:T(8,128)S(1)}, u32[]{:S(2)}, u32[]{:S(2)}) collective-permute-start(f32[192,128]{1,0:T(8,128)S(1)} %right_sum.2.refs_0_), channel_id=1, source_target_pairs={{0,4},{4,0},{8,12},{12,8},{16,20},{20,16},{24,28},{28,24},{1,5},{5... | collective-permute-start | bytes 294920 | tf_op jit(solution)/shard_map/ppermute | solution.py:320
  106.8 9.4 %collective-permute-start.17 = (f32[192,128]{1,0:T(8,128)S(1)}, f32[192,128]{1,0:T(8,128)S(1)}, u32[]{:S(2)}, u32[]{:S(2)}) collective-permute-start(f32[192,128]{1,0:T(8,128)S(1)} %right_sum.2.refs_0_), channel_id=1, source_target_pairs={{0,12},{4,8},{8,4},{12,0},{16,28},{20,24},{24,20},{28,16},{1,13},{... | collective-permute-start | bytes 294920 | tf_op jit(solution)/shard_map/ppermute | solution.py:320
  108.6 13.9 %collective-permute-start.18 = (f32[192,128]{1,0:T(8,128)S(1)}, f32[192,128]{1,0:T(8,128)S(1)}, u32[]{:S(2)}, u32[]{:S(2)}) collective-permute-start(f32[192,128]{1,0:T(8,128)S(1)} %right_sum.2.refs_0_), channel_id=1, source_target_pairs={{0,16},{4,20},{8,24},{12,28},{16,0},{20,4},{24,8},{28,12},{1,17},{... | collective-permute-start | bytes 294920 | tf_op jit(solution)/shard_map/ppermute | solution.py:320
  109.1 16.4 %collective-permute-start.19 = (f32[192,128]{1,0:T(8,128)S(1)}, f32[192,128]{1,0:T(8,128)S(1)}, u32[]{:S(2)}, u32[]{:S(2)}) collective-permute-start(f32[192,128]{1,0:T(8,128)S(1)} %right_sum.2.refs_0_), channel_id=1, source_target_pairs={{0,20},{4,16},{8,28},{12,24},{16,4},{20,0},{24,12},{28,8},{1,21},{... | collective-permute-start | bytes 294920 | tf_op jit(solution)/shard_map/ppermute | solution.py:320
  112.7 12.8 %collective-permute-start.20 = (f32[192,128]{1,0:T(8,128)S(1)}, f32[192,128]{1,0:T(8,128)S(1)}, u32[]{:S(2)}, u32[]{:S(2)}) collective-permute-start(f32[192,128]{1,0:T(8,128)S(1)} %right_sum.2.refs_0_), channel_id=1, source_target_pairs={{0,24},{4,28},{8,16},{12,20},{16,8},{20,12},{24,0},{28,4},{1,25},{... | collective-permute-start | bytes 294920 | tf_op jit(solution)/shard_map/ppermute | solution.py:320
  114.2 11.3 %collective-permute-start.21 = (f32[192,128]{1,0:T(8,128)S(1)}, f32[192,128]{1,0:T(8,128)S(1)}, u32[]{:S(2)}, u32[]{:S(2)}) collective-permute-start(f32[192,128]{1,0:T(8,128)S(1)} %right_sum.2.refs_0_), channel_id=1, source_target_pairs={{0,28},{4,24},{8,20},{12,16},{16,12},{20,8},{24,4},{28,0},{1,29},{... | collective-permute-start | bytes 294920 | tf_op jit(solution)/shard_map/ppermute | solution.py:320
  129.7 9.4 %collective-permute-start.22 = (f32[96,768]{1,0:T(8,128)S(1)}, f32[96,768]{1,0:T(8,128)S(1)}, u32[]{:S(2)}, u32[]{:S(2)}) collective-permute-start(f32[96,768]{1,0:T(8,128)S(1)} %get-tuple-element.148), channel_id=1, source_target_pairs={{0,3},{1,2},{2,1},{3,0},{4,7},{5,6},{6,5},{7,4},{8,11},{9,10},{10,... | collective-permute-start | bytes 884744 | tf_op jit(solution)/shard_map/ppermute | solution.py:320
  129.8 13.9 %collective-permute-start.23 = (f32[96,768]{1,0:T(8,128)S(1)}, f32[96,768]{1,0:T(8,128)S(1)}, u32[]{:S(2)}, u32[]{:S(2)}) collective-permute-start(f32[96,768]{1,0:T(8,128)S(1)} %get-tuple-element.149), channel_id=1, source_target_pairs={{0,2},{1,3},{2,0},{3,1},{4,6},{5,7},{6,4},{7,5},{8,10},{9,11},{10,... | collective-permute-start | bytes 884744 | tf_op jit(solution)/shard_map/ppermute | solution.py:320
  134.6 9.1 %collective-permute-start.24 = (f32[96,768]{1,0:T(8,128)S(1)}, f32[96,768]{1,0:T(8,128)S(1)}, u32[]{:S(2)}, u32[]{:S(2)}) collective-permute-start(f32[96,768]{1,0:T(8,128)S(1)} %get-tuple-element.150), channel_id=1, source_target_pairs={{0,1},{1,0},{2,3},{3,2},{4,5},{5,4},{6,7},{7,6},{8,9},{9,8},{10,11... | collective-permute-start | bytes 884744 | tf_op jit(solution)/shard_map/ppermute | solution.py:320
  176.1 9.9 %collective-permute-start.26 = (f32[96,768]{1,0:T(8,128)S(1)}, f32[96,768]{1,0:T(8,128)S(1)}, u32[]{:S(2)}, u32[]{:S(2)}) collective-permute-start(f32[96,768]{1,0:T(8,128)S(1)} %basis.3.first_ref), channel_id=1, source_target_pairs={{0,2},{1,3},{2,0},{3,1},{4,6},{5,7},{6,4},{7,5},{8,10},{9,11},{10,... | collective-permute-start | bytes 884744 | tf_op jit(solution)/shard_map/ppermute | solution.py:320
  177.5 20.2 %collective-permute-start.35 = (f32[288,512]{1,0:T(8,128)S(1)}, f32[288,512]{1,0:T(8,128)S(1)}, u32[]{:S(2)}, u32[]{:S(2)}) collective-permute-start(f32[288,512]{1,0:T(8,128)S(1)} %get-tuple-element.161), channel_id=1, source_target_pairs={{0,3},{1,2},{2,1},{3,0},{4,7},{5,6},{6,5},{7,4},{8,11},{9,10},{10,... | collective-permute-start | bytes 1769480 | tf_op jit(solution)/shard_map/ppermute | solution.py:320
  190.4 7.9 %collective-permute-start.28 = (f32[192,128]{1,0:T(8,128)S(1)}, f32[192,128]{1,0:T(8,128)S(1)}, u32[]{:S(2)}, u32[]{:S(2)}) collective-permute-start(f32[192,128]{1,0:T(8,128)S(1)} %get-tuple-element.154), channel_id=1, source_target_pairs={{0,4},{4,0},{8,12},{12,8},{16,20},{20,16},{24,28},{28,24},{1,5},{5... | collective-permute-start | bytes 294920 | tf_op jit(solution)/shard_map/ppermute | solution.py:320
  191.2 9.5 %collective-permute-start.29 = (f32[192,128]{1,0:T(8,128)S(1)}, f32[192,128]{1,0:T(8,128)S(1)}, u32[]{:S(2)}, u32[]{:S(2)}) collective-permute-start(f32[192,128]{1,0:T(8,128)S(1)} %get-tuple-element.155), channel_id=1, source_target_pairs={{0,8},{4,12},{8,0},{12,4},{16,24},{20,28},{24,16},{28,20},{1,9},{5... | collective-permute-start | bytes 294920 | tf_op jit(solution)/shard_map/ppermute | solution.py:320
  191.7 11.4 %collective-permute-start.30 = (f32[192,128]{1,0:T(8,128)S(1)}, f32[192,128]{1,0:T(8,128)S(1)}, u32[]{:S(2)}, u32[]{:S(2)}) collective-permute-start(f32[192,128]{1,0:T(8,128)S(1)} %get-tuple-element.156), channel_id=1, source_target_pairs={{0,12},{4,8},{8,4},{12,0},{16,28},{20,24},{24,20},{28,16},{1,13},{... | collective-permute-start | bytes 294920 | tf_op jit(solution)/shard_map/ppermute | solution.py:320
  194.0 9.1 %collective-permute-start.31 = (f32[192,128]{1,0:T(8,128)S(1)}, f32[192,128]{1,0:T(8,128)S(1)}, u32[]{:S(2)}, u32[]{:S(2)}) collective-permute-start(f32[192,128]{1,0:T(8,128)S(1)} %get-tuple-element.157), channel_id=1, source_target_pairs={{0,16},{4,20},{8,24},{12,28},{16,0},{20,4},{24,8},{28,12},{1,17},{... | collective-permute-start | bytes 294920 | tf_op jit(solution)/shard_map/ppermute | solution.py:320
  197.7 13.5 %collective-permute-start.32 = (f32[192,128]{1,0:T(8,128)S(1)}, f32[192,128]{1,0:T(8,128)S(1)}, u32[]{:S(2)}, u32[]{:S(2)}) collective-permute-start(f32[192,128]{1,0:T(8,128)S(1)} %get-tuple-element.158), channel_id=1, source_target_pairs={{0,20},{4,16},{8,28},{12,24},{16,4},{20,0},{24,12},{28,8},{1,21},{... | collective-permute-start | bytes 294920 | tf_op jit(solution)/shard_map/ppermute | solution.py:320
  198.3 12.9 %collective-permute-start.33 = (f32[192,128]{1,0:T(8,128)S(1)}, f32[192,128]{1,0:T(8,128)S(1)}, u32[]{:S(2)}, u32[]{:S(2)}) collective-permute-start(f32[192,128]{1,0:T(8,128)S(1)} %get-tuple-element.159), channel_id=1, source_target_pairs={{0,24},{4,28},{8,16},{12,20},{16,8},{20,12},{24,0},{28,4},{1,25},{... | collective-permute-start | bytes 294920 | tf_op jit(solution)/shard_map/ppermute | solution.py:320
  200.7 10.5 %collective-permute-start.34 = (f32[192,128]{1,0:T(8,128)S(1)}, f32[192,128]{1,0:T(8,128)S(1)}, u32[]{:S(2)}, u32[]{:S(2)}) collective-permute-start(f32[192,128]{1,0:T(8,128)S(1)} %get-tuple-element.160), channel_id=1, source_target_pairs={{0,28},{4,24},{8,20},{12,16},{16,12},{20,8},{24,4},{28,0},{1,29},{... | collective-permute-start | bytes 294920 | tf_op jit(solution)/shard_map/ppermute | solution.py:320
  211.3 9.1 %collective-permute-start.36 = (f32[192,128]{1,0:T(8,128)S(1)}, f32[192,128]{1,0:T(8,128)S(1)}, u32[]{:S(2)}, u32[]{:S(2)}) collective-permute-start(f32[192,128]{1,0:T(8,128)S(1)} %right_sum.3.refs_0_), channel_id=1, source_target_pairs={{0,4},{4,0},{8,12},{12,8},{16,20},{20,16},{24,28},{28,24},{1,5},{5... | collective-permute-start | bytes 294920 | tf_op jit(solution)/shard_map/ppermute | solution.py:320
  211.8 10.0 %collective-permute-start.37 = (f32[192,128]{1,0:T(8,128)S(1)}, f32[192,128]{1,0:T(8,128)S(1)}, u32[]{:S(2)}, u32[]{:S(2)}) collective-permute-start(f32[192,128]{1,0:T(8,128)S(1)} %right_sum.3.refs_0_), channel_id=1, source_target_pairs={{0,8},{4,12},{8,0},{12,4},{16,24},{20,28},{24,16},{28,20},{1,9},{5... | collective-permute-start | bytes 294920 | tf_op jit(solution)/shard_map/ppermute | solution.py:320
  216.6 8.3 %collective-permute-start.38 = (f32[192,128]{1,0:T(8,128)S(1)}, f32[192,128]{1,0:T(8,128)S(1)}, u32[]{:S(2)}, u32[]{:S(2)}) collective-permute-start(f32[192,128]{1,0:T(8,128)S(1)} %right_sum.3.refs_0_), channel_id=1, source_target_pairs={{0,12},{4,8},{8,4},{12,0},{16,28},{20,24},{24,20},{28,16},{1,13},{... | collective-permute-start | bytes 294920 | tf_op jit(solution)/shard_map/ppermute | solution.py:320
  217.1 14.7 %collective-permute-start.39 = (f32[192,128]{1,0:T(8,128)S(1)}, f32[192,128]{1,0:T(8,128)S(1)}, u32[]{:S(2)}, u32[]{:S(2)}) collective-permute-start(f32[192,128]{1,0:T(8,128)S(1)} %right_sum.3.refs_0_), channel_id=1, source_target_pairs={{0,16},{4,20},{8,24},{12,28},{16,0},{20,4},{24,8},{28,12},{1,17},{... | collective-permute-start | bytes 294920 | tf_op jit(solution)/shard_map/ppermute | solution.py:320
  219.2 15.2 %collective-permute-start.40 = (f32[192,128]{1,0:T(8,128)S(1)}, f32[192,128]{1,0:T(8,128)S(1)}, u32[]{:S(2)}, u32[]{:S(2)}) collective-permute-start(f32[192,128]{1,0:T(8,128)S(1)} %right_sum.3.refs_0_), channel_id=1, source_target_pairs={{0,20},{4,16},{8,28},{12,24},{16,4},{20,0},{24,12},{28,8},{1,21},{... | collective-permute-start | bytes 294920 | tf_op jit(solution)/shard_map/ppermute | solution.py:320
  220.4 14.0 %collective-permute-start.41 = (f32[192,128]{1,0:T(8,128)S(1)}, f32[192,128]{1,0:T(8,128)S(1)}, u32[]{:S(2)}, u32[]{:S(2)}) collective-permute-start(f32[192,128]{1,0:T(8,128)S(1)} %right_sum.3.refs_0_), channel_id=1, source_target_pairs={{0,24},{4,28},{8,16},{12,20},{16,8},{20,12},{24,0},{28,4},{1,25},{... | collective-permute-start | bytes 294920 | tf_op jit(solution)/shard_map/ppermute | solution.py:320
  221.9 12.5 %collective-permute-start.42 = (f32[192,128]{1,0:T(8,128)S(1)}, f32[192,128]{1,0:T(8,128)S(1)}, u32[]{:S(2)}, u32[]{:S(2)}) collective-permute-start(f32[192,128]{1,0:T(8,128)S(1)} %right_sum.3.refs_0_), channel_id=1, source_target_pairs={{0,28},{4,24},{8,20},{12,16},{16,12},{20,8},{24,4},{28,0},{1,29},{... | collective-permute-start | bytes 294920 | tf_op jit(solution)/shard_map/ppermute | solution.py:320
  237.3 20.1 %collective-permute-start.46 = (bf16[576,512]{1,0:T(8,128)(2,1)}, bf16[576,512]{1,0:T(8,128)(2,1)}, u32[]{:S(2)}, u32[]{:S(2)}) collective-permute-start(bf16[576,512]{1,0:T(8,128)(2,1)} %get-tuple-element.174.refs_0_), channel_id=1, source_target_pairs={{0,8},{4,12},{8,16},{12,20},{16,24},{20,28},{24,0},{28,4},{1,9},{5... | collective-permute-start | bytes 1769480 | tf_op jit(solution)/shard_map/ppermute | solution.py:562
  241.1 16.6 %collective-permute-start.47 = (bf16[576,512]{1,0:T(8,128)(2,1)}, bf16[576,512]{1,0:T(8,128)(2,1)}, u32[]{:S(2)}, u32[]{:S(2)}) collective-permute-start(bf16[576,512]{1,0:T(8,128)(2,1)} %get-tuple-element.174.refs_0_), channel_id=1, source_target_pairs={{0,4},{4,0},{8,12},{12,8},{16,20},{20,16},{24,28},{28,24},{1,5},{5... | collective-permute-start | bytes 1769480 | tf_op jit(solution)/shard_map/ppermute | solution.py:320
  242.3 27.1 %collective-permute-start.48 = (bf16[576,512]{1,0:T(8,128)(2,1)}, bf16[576,512]{1,0:T(8,128)(2,1)}, u32[]{:S(2)}, u32[]{:S(2)}) collective-permute-start(bf16[576,512]{1,0:T(8,128)(2,1)} %get-tuple-element.180.refs_1_), channel_id=1, source_target_pairs={{0,8},{4,12},{8,16},{12,20},{16,24},{20,28},{24,0},{28,4},{1,9},{5... | collective-permute-start | bytes 1769480 | tf_op jit(solution)/shard_map/ppermute | solution.py:562
  242.9 27.4 %collective-permute-start.49 = (bf16[576,512]{1,0:T(8,128)(2,1)}, bf16[576,512]{1,0:T(8,128)(2,1)}, u32[]{:S(2)}, u32[]{:S(2)}) collective-permute-start(bf16[576,512]{1,0:T(8,128)(2,1)} %get-tuple-element.180.refs_1_), channel_id=1, source_target_pairs={{0,4},{4,0},{8,12},{12,8},{16,20},{20,16},{24,28},{28,24},{1,5},{5... | collective-permute-start | bytes 1769480 | tf_op jit(solution)/shard_map/ppermute | solution.py:320
  257.7 23.2 %collective-permute-start.50 = (bf16[576,512]{1,0:T(8,128)(2,1)}, bf16[576,512]{1,0:T(8,128)(2,1)S(1)}, u32[]{:S(2)}, u32[]{:S(2)}) collective-permute-start(bf16[576,512]{1,0:T(8,128)(2,1)} %collective-permute-done.46.refs_2_), channel_id=1, source_target_pairs={{0,8},{4,12},{8,16},{12,20},{16,24},{20,28},{24,0},{28,4},{1,9},{5... | collective-permute-start | bytes 1769480 | tf_op jit(solution)/shard_map/ppermute | solution.py:562
  258.4 24.5 %collective-permute-start.51 = (bf16[576,512]{1,0:T(8,128)(2,1)}, bf16[576,512]{1,0:T(8,128)(2,1)S(1)}, u32[]{:S(2)}, u32[]{:S(2)}) collective-permute-start(bf16[576,512]{1,0:T(8,128)(2,1)} %collective-permute-done.46.refs_2_), channel_id=1, source_target_pairs={{0,4},{4,0},{8,12},{12,8},{16,20},{20,16},{24,28},{28,24},{1,5},{5... | collective-permute-start | bytes 1769480 | tf_op jit(solution)/shard_map/ppermute | solution.py:320
  270.4 23.2 %collective-permute-start.52 = (bf16[576,512]{1,0:T(8,128)(2,1)}, bf16[576,512]{1,0:T(8,128)(2,1)S(1)}, u32[]{:S(2)}, u32[]{:S(2)}) collective-permute-start(bf16[576,512]{1,0:T(8,128)(2,1)} %collective-permute-done.48.refs_4_), channel_id=1, source_target_pairs={{0,8},{4,12},{8,16},{12,20},{16,24},{20,28},{24,0},{28,4},{1,9},{5... | collective-permute-start | bytes 1769480 | tf_op jit(solution)/shard_map/ppermute | solution.py:562
  271.0 24.5 %collective-permute-start.53 = (bf16[576,512]{1,0:T(8,128)(2,1)}, bf16[576,512]{1,0:T(8,128)(2,1)S(1)}, u32[]{:S(2)}, u32[]{:S(2)}) collective-permute-start(bf16[576,512]{1,0:T(8,128)(2,1)} %collective-permute-done.48.refs_4_), channel_id=1, source_target_pairs={{0,4},{4,0},{8,12},{12,8},{16,20},{20,16},{24,28},{28,24},{1,5},{5... | collective-permute-start | bytes 1769480 | tf_op jit(solution)/shard_map/ppermute | solution.py:320
  282.9 27.9 %collective-permute-start.54 = (bf16[576,512]{1,0:T(8,128)(2,1)S(1)}, bf16[576,512]{1,0:T(8,128)(2,1)S(1)}, u32[]{:S(2)}, u32[]{:S(2)}) collective-permute-start(bf16[576,512]{1,0:T(8,128)(2,1)S(1)} %collective-permute-done.50.refs_6_), channel_id=1, source_target_pairs={{0,8},{4,12},{8,16},{12,20},{16,24},{20,28},{24,0},{28,4},{1,9},{5... | collective-permute-start | bytes 1769480 | tf_op jit(solution)/shard_map/ppermute | solution.py:562
  283.6 27.2 %collective-permute-start.55 = (bf16[576,512]{1,0:T(8,128)(2,1)S(1)}, bf16[576,512]{1,0:T(8,128)(2,1)S(1)}, u32[]{:S(2)}, u32[]{:S(2)}) collective-permute-start(bf16[576,512]{1,0:T(8,128)(2,1)S(1)} %collective-permute-done.50.refs_6_), channel_id=1, source_target_pairs={{0,4},{4,0},{8,12},{12,8},{16,20},{20,16},{24,28},{28,24},{1,5},{5... | collective-permute-start | bytes 1769480 | tf_op jit(solution)/shard_map/ppermute | solution.py:320
  295.5 20.9 %collective-permute-start.56 = (bf16[576,512]{1,0:T(8,128)(2,1)S(1)}, bf16[576,512]{1,0:T(8,128)(2,1)S(1)}, u32[]{:S(2)}, u32[]{:S(2)}) collective-permute-start(bf16[576,512]{1,0:T(8,128)(2,1)S(1)} %collective-permute-done.52.refs_8_), channel_id=1, source_target_pairs={{0,8},{4,12},{8,16},{12,20},{16,24},{20,28},{24,0},{28,4},{1,9},{5... | collective-permute-start | bytes 1769480 | tf_op jit(solution)/shard_map/ppermute | solution.py:562
  296.2 22.4 %collective-permute-start.57 = (bf16[576,512]{1,0:T(8,128)(2,1)S(1)}, bf16[576,512]{1,0:T(8,128)(2,1)S(1)}, u32[]{:S(2)}, u32[]{:S(2)}) collective-permute-start(bf16[576,512]{1,0:T(8,128)(2,1)S(1)} %collective-permute-done.52.refs_8_), channel_id=1, source_target_pairs={{0,4},{4,0},{8,12},{12,8},{16,20},{20,16},{24,28},{28,24},{1,5},{5... | collective-permute-start | bytes 1769480 | tf_op jit(solution)/shard_map/ppermute | solution.py:320
  318.6 15.0 %collective-permute-start.59 = (bf16[576,512]{1,0:T(8,128)(2,1)S(1)}, bf16[576,512]{1,0:T(8,128)(2,1)S(1)}, u32[]{:S(2)}, u32[]{:S(2)}) collective-permute-start(bf16[576,512]{1,0:T(8,128)(2,1)S(1)} %collective-permute-done.57.refs_1_), channel_id=1, source_target_pairs={{0,8},{4,12},{8,16},{12,20},{16,24},{20,28},{24,0},{28,4},{1,9},{5... | collective-permute-start | bytes 1769480 | tf_op jit(solution)/shard_map/ppermute | solution.py:567
  319.5 14.2 %collective-permute-start.58 = (bf16[576,512]{1,0:T(8,128)(2,1)S(1)}, bf16[576,512]{1,0:T(8,128)(2,1)S(1)}, u32[]{:S(2)}, u32[]{:S(2)}) collective-permute-start(bf16[576,512]{1,0:T(8,128)(2,1)S(1)} %collective-permute-done.54.refs_0_), channel_id=1, source_target_pairs={{0,4},{4,0},{8,12},{12,8},{16,20},{20,16},{24,28},{28,24},{1,5},{5... | collective-permute-start | bytes 1769480 | tf_op jit(solution)/shard_map/ppermute | solution.py:320
  (33 other events, 311.3 us)
